TPU v7x, 32 devices: a whole 2x2x4 slice. The times are simulated.
32 devices in a mesh: grp: 2 (over x), dev: 8 (over z, y), sub: 2 (over core).
Axes of the slice: x: 2, y: 2, z: 4, core: 2. Of those that a mesh axis runs over, the one named last changes fastest.
Arguments:
- tiles: bfloat16 [64, 256, 1536], P(('grp', 'dev')), parts along dimension 0, may hold values from -6 to 6
- counts: int32 [16], P('grp'), parts along dimension 0, may hold values from 1 to 4, as said below
- slide_of: int32 [16], P('grp'), parts along dimension 0, may hold values from 0 to 1, as said below
- rates: int32 [12], replicated, may hold values from 1 to 4
- tile_gain: float32 [1536], replicated, may hold values from 0.1 to 1.9
- gate_weight: bfloat16 [1536, 2048], P('dev', 'sub'), may hold values from -0.15625 to 0.15625
- up_weight: bfloat16 [1536, 2048], P('dev', 'sub'), may hold values from -0.15625 to 0.15625
- embed_proj: bfloat16 [2048, 768], P('sub'), may hold values from -0.5 to 0.5
- slide_gain: float32 [768], replicated, may hold values from 0.1 to 1.9
- slide_wq: bfloat16 [768, 768], P(None, 'sub'), may hold values from -2 to 2
- slide_wk: bfloat16 [768, 768], P(None, 'sub'), may hold values from -2 to 2
- slide_wv: bfloat16 [768, 768], P(None, 'sub'), may hold values from -0.21875 to 0.21875
- slide_wo: bfloat16 [768, 768], P('sub'), may hold values from -0.875 to 0.875
Outputs:
- tile_embed: bfloat16 [64, 2048], P(('grp', 'dev'), 'sub'), parts along dimension 0
- slide_out: bfloat16 [64, 768], P(('grp', 'dev'), 'sub'), parts along dimension 0
There are 2 independent parts, one for each index of `grp`. A program takes and returns all parts, laid end to end along the dimension named above; an argument that names none is the same for every part. Nothing has to cross between parts.
Inputs may be any that keep to these rules, and one draw needn't show every extreme that they name: `counts`: exactly 4 devices of a group hold 4 tiles; every other device holds at most 2. slide_of never falls from one device to the next and names every slide; each slide covers 1 to 6 devices, and exactly one slide of each group covers 8 // 2 + 2.
All inputs are finite; a program needn't handle non-finite values.
Results may differ from a plain program's by a relative error of at most 0.02.
Values may be sent and summed in bfloat16 or wider, within the bound.
No kernel may reach another device: no remote copies, remote signals or barrier semaphores. Data moves between devices by JAX's collectives and lax.ppermute only.
A program may use at most 64 MiB of HBM per device.

v0:
```python
import math

import jax
import jax.numpy as jnp
from jax import lax
from jax.sharding import PartitionSpec as P

HD = 64
SPILL = 1


epsilon = 1e-06
floor_value = -1e30


def normed(rows_in, gains):
    average = jnp.mean(rows_in, axis=-1, keepdims=True)
    centred = rows_in - average
    variance = jnp.mean(centred * centred, axis=-1, keepdims=True)
    return (centred * lax.rsqrt(variance + epsilon) * gains).astype(jnp.bfloat16)


def gated_rows(hidden, gate_weight, up_weight):
    gate_full, up_full = (
        lax.all_gather(gate_weight, "dev", axis=0, tiled=True),
        lax.all_gather(up_weight, "dev", axis=0, tiled=True),
    )
    gate = jnp.dot(hidden, gate_full, preferred_element_type=jnp.float32)
    up_part = jnp.dot(hidden, up_full, preferred_element_type=jnp.float32)
    return (jax.nn.silu(gate) * up_part).astype(jnp.bfloat16)


def on_device(
    tiles,
    counts,
    slide_of,
    rates,
    tile_gain,
    gate_weight,
    up_weight,
    embed_proj,
    slide_gain,
    slide_wq,
    slide_wk,
    slide_wv,
    slide_wo,
):
    slot_count, length, feature_width = tiles.shape
    work_tiles = slot_count - SPILL
    hidden_cols = gate_weight.shape[1]
    n_dev = lax.axis_size("dev")
    my_index = lax.axis_index("dev")
    core_index = lax.axis_index("sub")
    per_tile = n_dev // 2
    block_rows = length // per_tile
    is_busy = counts == slot_count
    busy_flag = is_busy.astype(jnp.int32)
    busy_rank = jnp.cumsum(busy_flag) - 1
    calm_rank = jnp.cumsum(1 - busy_flag) - 1
    i_am_busy = is_busy[my_index]
    receiving = jnp.logical_not(i_am_busy)
    spill_blocks = tiles[slot_count - 1].reshape(per_tile, block_rows, feature_width)
    sending = i_am_busy & jnp.logical_not(is_busy)
    picked = jnp.where(sending, (calm_rank - busy_rank[my_index]) % per_tile, 0)
    send_rows = jnp.where(
        sending[:, None, None], jnp.take(spill_blocks, picked, axis=0), jnp.zeros((), jnp.bfloat16)
    )
    got_rows = lax.all_to_all(send_rows, "dev", split_axis=0, concat_axis=0, tiled=True)
    senders = jnp.argsort(1 - busy_flag, stable=True)[:per_tile]
    in_rows = jnp.take(got_rows, senders, axis=0)
    in_rows = in_rows.reshape(length, feature_width)
    last_rows = jnp.where(receiving, in_rows, tiles[work_tiles - 1])
    kept_rows = tiles[: work_tiles - 1].reshape((work_tiles - 1) * length, feature_width)
    work_rows = jnp.concatenate([kept_rows, last_rows], axis=0)
    gated = gated_rows(normed(work_rows.astype(jnp.float32), tile_gain), gate_weight, up_weight)
    block_sums = jnp.sum(
        gated.reshape(work_tiles, per_tile, block_rows, hidden_cols), axis=2, dtype=jnp.float32
    )
    own_sums = jnp.sum(block_sums, axis=1)
    back_sums = (
        jnp.zeros((n_dev, hidden_cols), jnp.float32).at[senders].set(block_sums[work_tiles - 1])
    )
    back_sums = jnp.where(receiving, back_sums, 0.0)
    returned = lax.all_to_all(
        back_sums.astype(jnp.bfloat16), "dev", split_axis=0, concat_axis=0, tiled=True
    ).astype(back_sums.dtype)
    spill_sum = jnp.sum(returned, axis=0)
    pooled = jnp.concatenate([own_sums, spill_sum[None, :]], axis=0)
    is_valid = jnp.arange(slot_count, dtype=jnp.int32) < counts[my_index]
    tile_embed = jnp.where(is_valid[:, None], pooled / length, 0.0).astype(jnp.bfloat16)
    mixed_rows = lax.psum(
        jnp.dot(tile_embed, embed_proj, preferred_element_type=jnp.float32), "sub"
    )
    hidden = normed(mixed_rows, slide_gain)
    slide_heads = slide_wq.shape[1] // HD
    slide_query = jnp.dot(hidden, slide_wq, preferred_element_type=jnp.float32).astype(jnp.bfloat16)
    slide_keys = jnp.dot(hidden, slide_wk, preferred_element_type=jnp.float32).astype(jnp.bfloat16)
    slide_values = jnp.dot(hidden, slide_wv, preferred_element_type=jnp.float32).astype(
        jnp.bfloat16
    )
    global_heads = core_index * slide_heads + jnp.arange(slide_heads, dtype=jnp.int32)
    dilation = rates[global_heads]
    offset = global_heads % dilation
    my_slide = slide_of[my_index]
    first_dev = jnp.argmax(slide_of == my_slide)
    position = (my_index - first_dev) * slot_count + jnp.arange(slot_count, dtype=jnp.int32)
    chosen = position[:, None] % dilation[None, :] == offset[None, :]
    query_heads = slide_query.reshape(slot_count, slide_heads, HD)
    scale = 1.0 / math.sqrt(HD)
    local_scores = (
        jnp.einsum(
            "ihd,jhd->ijh",
            query_heads,
            slide_keys.reshape(slot_count, slide_heads, HD),
            preferred_element_type=jnp.float32,
        )
        * scale
    )
    near_keys = jnp.broadcast_to(is_valid[None, :, None], local_scores.shape)
    near_masked = jnp.where(near_keys, local_scores, floor_value)
    near_high = jnp.max(near_masked, axis=1)
    near_weights = jnp.where(near_keys, jnp.exp(near_masked - near_high[:, None, :]), 0.0)
    near_total = jnp.sum(near_weights, axis=1)
    near_weighted = jnp.einsum(
        "ijh,jhd->ihd",
        near_weights,
        slide_values.reshape(slot_count, slide_heads, HD).astype(jnp.float32),
    )
    far_high = jnp.full((slot_count, slide_heads), floor_value, jnp.float32)
    piece_keys = lax.all_gather(slide_keys, "dev", axis=0, tiled=True)
    piece_values = lax.all_gather(slide_values, "dev", axis=0, tiled=True)
    piece_rows = piece_keys.shape[0]
    global_row = jnp.arange(piece_rows, dtype=jnp.int32)
    device = global_row // slot_count
    slot_of = global_row % slot_count
    usable = (slot_of < counts[device]) & (slide_of[device] == my_slide)
    key_position = (device - first_dev) * slot_count + slot_of
    key_chosen = key_position[:, None] % dilation[None, :] == offset[None, :]
    allowed = usable[None, :, None] & key_chosen[None, :, :] & chosen[:, None, :]
    scores = (
        jnp.einsum(
            "ihd,jhd->ijh",
            query_heads,
            piece_keys.reshape(piece_rows, slide_heads, HD),
            preferred_element_type=jnp.float32,
        )
        * scale
    )
    masked = jnp.where(allowed, scores, floor_value)
    new_high = jnp.maximum(far_high, jnp.max(masked, axis=1))
    weights = jnp.where(allowed, jnp.exp(masked - new_high[:, None, :]), 0.0)
    new_total = jnp.sum(weights, axis=1)
    new_weighted = jnp.einsum(
        "ijh,jhd->ihd",
        weights,
        piece_values.reshape(piece_rows, slide_heads, HD).astype(jnp.float32),
    )
    overall = jnp.maximum(near_high, new_high)
    near_factor = jnp.exp(near_high - overall)
    far_factor = jnp.exp(new_high - overall)
    all_total = near_total * near_factor + new_total * far_factor
    slide_context = (
        near_weighted * near_factor[..., None] + new_weighted * far_factor[..., None]
    ) / all_total[..., None]
    slide_context = slide_context.reshape(slot_count, slide_heads * HD).astype(jnp.bfloat16)
    out_terms = jnp.dot(slide_context, slide_wo, preferred_element_type=jnp.float32)
    out_half = lax.psum_scatter(out_terms, "sub", scatter_dimension=1, tiled=True)
    half_width = out_half.shape[1]
    base_half = lax.dynamic_slice_in_dim(mixed_rows, core_index * half_width, half_width, 1)
    slide_out = jnp.where(is_valid[:, None], base_half + out_half, 0.0).astype(jnp.bfloat16)
    return (tile_embed, slide_out)


def solution(mesh):
    placed = (
        P(("grp", "dev"), None, None),
        P("grp"),
        P("grp"),
        P(),
        P(),
        P("dev", "sub"),
        P("dev", "sub"),
        P("sub", None),
        P(),
        P(None, "sub"),
        P(None, "sub"),
        P(None, "sub"),
        P("sub", None),
    )
    return jax.shard_map(
        on_device,
        mesh=mesh,
        in_specs=placed,
        out_specs=(P(("grp", "dev"), "sub"), P(("grp", "dev"), "sub")),
        check_vma=False,
    )
```

profile of v0, /device:TPU:0, one launch (start us, length us, event | category | flops | bytes accessed | tf_op | source)
XLA Modules:
  0.0 261.2 jit_solution(18389419514332215756)
XLA Ops:
  11.5 2.0 compare_and_fusion.1
  13.5 1.9 gather_fusion
  15.4 2.9 %select_select_fusion = bf16[8,64,1536]{2,1,0:T(8,128)(2,1)} fusion(bf16[8,64,1536]{2,1,0:T(8,128)(2,1)} %gather_fusion, pred[8]{0:T(512)(128)(4,1)S(1)} %get-tuple-element.13, pred[8]{0:T(512)(128)(4,1)S(1)} %get-tuple-element.15), kind=kLoop, calls=%fused_computation.17 | loop fusion | flops 1572864 | bytes 3145744 | tf_op jit(solution)/shard_map/jit(_where)/select_n | solution.py:65
  18.3 7.4 %all-to-all-start = ((bf16[8,64,1536]{2,1,0:T(8,128)(2,1)}), bf16[8,64,1536]{2,1,0:T(8,128)(2,1)}, u32[]{:S(2)}, u32[]{:S(2)}) async-start(bf16[8,64,1536]{2,1,0:T(8,128)(2,1)} %select_select_fusion), calls=%async_computation | async-start | bytes 3145728 | tf_op jit(solution)/shard_map/all_to_all | solution.py:68
  26.4 1.5 slice.15
  30.5 1.0 sort.17
  31.7 1.3 compare_reduce_fusion
  36.3 54.9 %all-to-all-done = bf16[8,64,1536]{2,1,0:T(8,128)(2,1)} async-done(((bf16[8,64,1536]{2,1,0:T(8,128)(2,1)}), bf16[8,64,1536]{2,1,0:T(8,128)(2,1)}, u32[]{:S(2)}, u32[]{:S(2)}) %all-to-all-start) | async-done | bytes 1572896 | tf_op jit(solution)/shard_map/all_to_all | solution.py:68
  91.2 2.9 %gather_fusion.1 = bf16[4,64,1536]{2,1,0:T(8,128)(2,1)} fusion(bf16[8,64,1536]{2,1,0:T(8,128)(2,1)} %all-to-all-done, s32[1024]{0:T(1024)S(1)} %pad_clamp_fusion.2), kind=kCustom, calls=%fused_computation.1 | custom fusion | bytes 1572880 | tf_op jit(solution)/shard_map/jit(_take)/gather | solution.py:70
  94.2 1.5 bitcast_select_fusion
  96.6 0.8 fusion.2
  97.4 6.5 %fusion.54 = f32[768,1024]{1,0:T(8,128)} fusion(bf16[1536,1024]{1,0:T(8,128)(2,1)} %all-gather.5.cloned.1.call-done, f32[1536]{0:T(1024)S(1)} %copy-done.8, f32[768]{0:T(1024)S(1)} %add_rsqrt_fusion, f32[768]{0:T(1024)S(1)} %broadcast_multiply_fusion, bf16[256,1536]{1,0:T(8,128)(2,1)} %copy-done.4, bf16[512,1536]{1,0:T(8,128)(2,1)S(1)} %bitcast.69), kind=kOutput, calls=%fused_computation.136 | convolution fusion | flops 2425356288 | bytes 8663040 | tf_op jit(solution)/shard_map/dot_general | solution.py:28
  103.9 54.8 %all-gather.7.cloned.1.call-done = bf16[1536,1024]{1,0:T(8,128)(2,1)} async-done(((bf16[192,1024]{1,0:T(8,128)(2,1)}), bf16[1536,1024]{1,0:T(8,128)(2,1)}) %all-gather.7.cloned.1.call-update) | async-done | bytes 3145744 | tf_op jit(solution)/shard_map/all_gather | solution.py:26
  158.7 6.0 %multiply_convert_fusion = bf16[768,1024]{1,0:T(8,128)(2,1)S(1)} fusion(f32[768,1024]{1,0:T(8,128)} %fusion.54, bf16[1536,1024]{1,0:T(8,128)(2,1)} %all-gather.7.cloned.1.call-done, f32[1536]{0:T(1024)S(1)} %copy-done.8, f32[768]{0:T(1024)S(1)} %add_rsqrt_fusion, f32[768]{0:T(1024)S(1)} %broadcast_multiply_fusion, bf16[256,1536]{1,0:T(8,128)(2,1)} %copy-done.4, ...), kind=kOutput, calls=%fused_computation.15 | convolution fusion | flops 2430074880 | bytes 10235904 | tf_op jit(solution)/shard_map/dot_general | solution.py:29
  167.6 3.3 %all-to-all-start.1 = ((bf16[8,2,512]{2,1,0:T(2,128)(2,1)}), bf16[8,2,512]{2,1,0:T(2,128)(2,1)S(1)}, u32[]{:S(2)}, u32[]{:S(2)}) async-start(bf16[8,2,512]{2,1,0:T(2,128)(2,1)} %reshape.503), calls=%async_computation.1 | async-start | bytes 32768 | tf_op jit(solution)/shard_map/all_to_all | solution.py:84
  171.6 5.8 %all-to-all-done.1 = bf16[8,2,512]{2,1,0:T(2,128)(2,1)S(1)} async-done(((bf16[8,2,512]{2,1,0:T(2,128)(2,1)}), bf16[8,2,512]{2,1,0:T(2,128)(2,1)S(1)}, u32[]{:S(2)}, u32[]{:S(2)}) %all-to-all-start.1) | async-done | bytes 16416 | tf_op jit(solution)/shard_map/all_to_all | solution.py:84
  177.9 3.3 %psum.7 = f32[4,768]{1,0:T(4,128)S(1)} all-reduce(f32[4,768]{1,0:T(4,128)S(1)} %fusion.60), channel_id=1, replica_groups=mesh['grp'=2,'dev'=8,'sub'=2] {'sub'}, use_global_device_ids=true, to_apply=%region_9.10 | all-reduce | flops 3072 | bytes 24576 | tf_op jit(solution)/shard_map/psum | solution.py:91
  181.8 1.3 convolution_convert_fusion
  183.2 30.3 %all-gather = bf16[8,4,384]{2,1,0:T(4,128)(2,1)S(1)} all-gather(bf16[1,4,384]{2,1,0:T(4,128)(2,1)S(1)} %bitcast.75), channel_id=1, replica_groups=mesh['grp'=2,'dev'=8,'sub'=2] {'dev'}, dimensions={0}, use_global_device_ids=true | all-gather | bytes 27648 | tf_op jit(solution)/shard_map/all_gather | solution.py:130
  214.0 1.3 convolution_convert_fusion.2
  215.4 30.3 %all-gather.1 = bf16[8,4,384]{2,1,0:T(4,128)(2,1)S(1)} all-gather(bf16[1,4,384]{2,1,0:T(4,128)(2,1)S(1)} %bitcast.76), channel_id=1, replica_groups=mesh['grp'=2,'dev'=8,'sub'=2] {'dev'}, dimensions={0}, use_global_device_ids=true | all-gather | bytes 27648 | tf_op jit(solution)/shard_map/all_gather | solution.py:131
  246.7 1.1 convolution_bitcast_fusion
  247.8 5.2 %reduce-scatter.4.cloned.1.call-done = f32[384,4]{1,0:T(8,128)} async-done(((f32[768,4]{1,0:T(8,128)}), f32[384,4]{1,0:T(8,128)}) %reduce-scatter.4.cloned.1.call-update) | async-done | bytes 6160
  253.0 1.0 copy.49
  (93 shorter events, 17.6 us)
Async XLA Ops:
  7.2 170.4 %copy-start = (bf16[1024,768]{1,0:T(8,128)(2,1)S(1)}, bf16[1024,768]{1,0:T(8,128)(2,1)}, u32[]{:S(2)}) copy-start(bf16[1024,768]{1,0:T(8,128)(2,1)} %param.20) | copy-start | bytes 4718596
  7.2 6.3 %slice-start = ((bf16[4,256,1536]{2,1,0:T(8,128)(2,1)}), bf16[1,256,1536]{2,1,0:T(8,128)(2,1)S(1)}, s32[]{:S(2)}) async-start(bf16[4,256,1536]{2,1,0:T(8,128)(2,1)} %param.13), calls=%async_computation.6 | async-start | bytes 1572864 | tf_op jit(solution)/shard_map/slice | solution.py:62
  7.2 90.2 %all-gather.5.cloned.1.call-start = ((), (), s32[]{:S(2)}) async-start(), calls=%async_computation.3 | async-start | bytes 3538944 | tf_op jit(solution)/shard_map/all_gather | solution.py:25
  7.9 150.8 %all-gather.7.cloned.1.call-start = ((), (), s32[]{:S(2)}) async-start(), calls=%async_computation.4 | async-start | bytes 3538944 | tf_op jit(solution)/shard_map/all_gather | solution.py:26
  18.3 9.6 %copy-start.1 = (s32[8]{0:T(128)S(1)}, s32[8]{0:T(128)}, u32[]{:S(2)}) copy-start(s32[8]{0:T(128)} %param.14) | copy-start | bytes 100
  18.3 10.2 %copy-start.2 = (s32[8]{0:T(128)S(1)}, s32[8]{0:T(128)}, u32[]{:S(2)}) copy-start(s32[8]{0:T(128)} %param.15) | copy-start | bytes 100
  18.3 15.5 %copy-start.3 = (s32[12]{0:T(128)S(1)}, s32[12]{0:T(128)}, u32[]{:S(2)}) copy-start(s32[12]{0:T(128)} %param.16) | copy-start | bytes 148
  18.3 72.9 %all-to-all-start = ((bf16[8,64,1536]{2,1,0:T(8,128)(2,1)}), bf16[8,64,1536]{2,1,0:T(8,128)(2,1)}, u32[]{:S(2)}, u32[]{:S(2)}) async-start(bf16[8,64,1536]{2,1,0:T(8,128)(2,1)} %select_select_fusion), calls=%async_computation | async-start | bytes 3145728 | tf_op jit(solution)/shard_map/all_to_all | solution.py:68
  94.2 3.3 %copy-start.8 = (f32[1536]{0:T(1024)S(1)}, f32[1536]{0:T(1024)}, u32[]{:S(2)}) copy-start(f32[1536]{0:T(1024)} %param.17) | copy-start | bytes 18436
  95.7 0.9 copy-start.4
  164.7 16.8 %copy-start.7 = (bf16[768,384]{1,0:T(8,128)(2,1)S(1)}, bf16[768,384]{1,0:T(8,128)(2,1)}, u32[]{:S(2)}) copy-start(bf16[768,384]{1,0:T(8,128)(2,1)} %param.23) | copy-start | bytes 1769476
  164.7 16.8 %copy-start.9 = (f32[768]{0:T(1024)S(1)}, f32[768]{0:T(1024)}, u32[]{:S(2)}) copy-start(f32[768]{0:T(1024)} %param.21) | copy-start | bytes 9220
  164.7 82.0 %copy-start.5 = (bf16[384,768]{1,0:T(8,128)(2,1)S(1)}, bf16[384,768]{1,0:T(8,128)(2,1)}, u32[]{:S(2)}) copy-start(bf16[384,768]{1,0:T(8,128)(2,1)} %param.25) | copy-start | bytes 1769476
  167.6 9.9 %all-to-all-start.1 = ((bf16[8,2,512]{2,1,0:T(2,128)(2,1)}), bf16[8,2,512]{2,1,0:T(2,128)(2,1)S(1)}, u32[]{:S(2)}, u32[]{:S(2)}) async-start(bf16[8,2,512]{2,1,0:T(2,128)(2,1)} %reshape.503), calls=%async_computation.1 | async-start | bytes 32768 | tf_op jit(solution)/shard_map/all_to_all | solution.py:84
  170.9 82.1 %reduce-scatter.4.cloned.1.call-start = ((), (), s32[]{:S(2)}) async-start(), calls=%async_computation.5 | async-start | bytes 589824
  177.6 77.1 %copy-start.6 = (bf16[4,1024]{1,0:T(4,128)(2,1)}, bf16[4,1024]{1,0:T(4,128)(2,1)S(1)}, u32[]{:S(2)}) copy-start(bf16[4,1024]{1,0:T(4,128)(2,1)S(1)} %fusion.19) | copy-start | bytes 24580
Sparse Core Ops, SparseCore 0:
  10.2 87.1 all-gather.4
  99.6 59.0 all-gather.6
  247.9 4.9 reduce-scatter.3
where the time goes:
time: 262 us; the launch traced here: 261 us
  waiting for transfers between devices  122 us (47%)
  blocking collectives  63.9 us (24%)
  matrix products  17.4 us (7%)
  other arithmetic  16.6 us (6%)
  between operations  15.4 us (6%)
  local copies, waits for them, and re-layouts  14.9 us (6%)
  starting transfers between devices  10.9 us (4%)
    all_to_all x1, waiting for transfers between devices, on_device(): lax.all_to_all(send_rows, 'dev', split_axis=0, concat_axis=0, tiled=True)  54.9 us
    all_gather x1, waiting for transfers between devices, gated_rows(): lax.all_gather(up_weight, 'dev', axis=0, tiled=True)  54.8 us
    all_gather x1, blocking collectives, on_device(): piece_values = lax.all_gather(slide_values, 'dev', axis=0, tiled=True)  30.3 us
    all_gather x1, blocking collectives, on_device(): piece_keys = lax.all_gather(slide_keys, 'dev', axis=0, tiled=True)  30.3 us
    all_to_all x1, starting transfers between devices, on_device(): lax.all_to_all(send_rows, 'dev', split_axis=0, concat_axis=0, tiled=True)  7.41 us
    unnamed x4, waiting for transfers between devices  6.55 us
    dot_general x1, matrix products, gated_rows(): gate = jnp.dot(hidden, gate_full, preferred_element_type=jnp.float32)  6.49 us
    dot_general x1, matrix products, gated_rows(): up_part = jnp.dot(hidden, up_full, preferred_element_type=jnp.float32)  5.95 us
  transfers between devices with their start and end apart: 5, of which 5 were waited for; matrix products, arithmetic and copies ran while one was open for 12% of the time, Pallas kernels for 0%

commit v1 on v0

v1 whole, which is shorter than its diff:
```python
import functools
import math

import jax
import jax.numpy as jnp
from jax import lax
from jax.experimental import pallas as pl
from jax.experimental.pallas import tpu as pltpu
from jax.sharding import PartitionSpec as P

HD = 64
EPSILON = 1e-06
FLOOR = -1e30
CHUNKS = 2
QROWS = 8
VMEM_LIMIT = 48 * 1024 * 1024


def normed(rows_in, gains):
    average = jnp.mean(rows_in, axis=-1, keepdims=True)
    centred = rows_in - average
    variance = jnp.mean(centred * centred, axis=-1, keepdims=True)
    return (centred * lax.rsqrt(variance + EPSILON) * gains).astype(jnp.bfloat16)


def norm_kernel(ids_ref, tiles_ref, gain_ref, out_ref):
    out_ref[...] = normed(tiles_ref[0].astype(jnp.float32), gain_ref[...])


def norm_tiles(ids, tiles, gain, flip):
    slot_count, length, width = tiles.shape
    half = slot_count // 2

    def tile_map(i, ids_ref):
        core = ids_ref[2]
        first = (1 - core if flip else core) * half
        return (first + i, 0, 0)

    return pl.pallas_call(
        norm_kernel,
        grid_spec=pltpu.PrefetchScalarGridSpec(
            num_scalar_prefetch=1,
            grid=(half,),
            in_specs=[
                pl.BlockSpec((1, length, width), tile_map),
                pl.BlockSpec((1, width), lambda i, ids_ref: (0, 0)),
            ],
            out_specs=pl.BlockSpec((length, width), lambda i, ids_ref: (i, 0)),
        ),
        out_shape=jax.ShapeDtypeStruct((half * length, width), jnp.bfloat16),
        compiler_params=pltpu.CompilerParams(vmem_limit_bytes=VMEM_LIMIT),
        cost_estimate=pl.CostEstimate(
            flops=8 * half * length * width,
            bytes_accessed=4 * half * length * width,
            transcendentals=half * length,
        ),
    )(ids, tiles, gain)


def mlp_kernel(n_chunks, n_dev, ny, length, ids_ref, *refs):
    n_blocks = n_dev * n_chunks
    blocks = refs[:n_blocks]
    first_ref, second_ref, out_ref, weights, rows, sums, weight_sems, row_sems = refs[n_blocks:]
    me = ids_ref[1]
    core = ids_ref[2]
    nz = n_dev // ny
    my_z = me // ny
    my_y = me - my_z * ny
    depth = blocks[0].shape[0]
    cols = blocks[0].shape[1] // 2
    row_copies = [
        pltpu.make_async_copy(ref, rows.at[i], row_sems.at[i])
        for i, ref in enumerate((first_ref, second_ref))
    ]
    weight_copies = []
    for c in range(n_chunks):
        copies = []
        for k in range(n_dev):
            step, flip = k // ny, k % ny
            z = my_z - step
            z = jnp.where(z < 0, z + nz, z)
            y = 1 - my_y if flip else my_y
            start = pl.multiple_of((z * ny + y) * depth, depth)
            copies.append(
                pltpu.make_async_copy(
                    blocks[c * n_dev + k], weights.at[c, pl.ds(start, depth)], weight_sems.at[c, k]
                )
            )
        weight_copies.append(copies)
    row_copies[0].start()
    for copy in weight_copies[0]:
        copy.start()
    row_copies[1].start()
    for copies in weight_copies[1:]:
        for copy in copies:
            copy.start()
    half = rows.shape[1] // length
    for c in range(n_chunks):
        for copy in weight_copies[c]:
            copy.wait()
        for i in range(2):
            if c == 0:
                row_copies[i].wait()
            first = (1 - core if i else core) * half

            def one_tile(j, carry):
                start = pl.multiple_of(j * length, length)
                both = jnp.dot(
                    rows[i, pl.ds(start, length), :],
                    weights[c],
                    preferred_element_type=jnp.float32,
                )
                gate, up_part = both[:, :cols], both[:, cols:]
                silu = gate * (0.5 * jnp.tanh(0.5 * gate) + 0.5)
                gated = (silu * up_part).astype(jnp.bfloat16).astype(jnp.float32)
                sums[pl.ds(first + j, 1), c * cols : (c + 1) * cols] = jnp.sum(
                    gated, axis=0, keepdims=True
                )
                return carry

            lax.fori_loop(0, half, one_tile, 0)
    out_ref[...] = (sums[: 2 * half] * (1.0 / length)).astype(jnp.bfloat16)


def mlp(ids, chunks, first, second, length, ny):
    n_chunks, n_dev = len(chunks), len(chunks[0])
    depth, both_cols = chunks[0][0].shape
    width = depth * n_dev
    cols = both_cols // 2
    total_rows = 2 * first.shape[0]
    slot_count = total_rows // length
    any_spec = pl.BlockSpec(memory_space=pl.ANY)
    flat = [block for chunk in chunks for block in chunk]
    return pl.pallas_call(
        functools.partial(mlp_kernel, n_chunks, n_dev, ny, length),
        in_specs=[pl.BlockSpec(memory_space=pltpu.SMEM)] + [any_spec] * (len(flat) + 2),
        out_specs=pl.BlockSpec(memory_space=pltpu.VMEM),
        out_shape=jax.ShapeDtypeStruct((slot_count, n_chunks * cols), jnp.bfloat16),
        scratch_shapes=[
            pltpu.VMEM((n_chunks, width, both_cols), jnp.bfloat16),
            pltpu.VMEM((2, first.shape[0], width), jnp.bfloat16),
            pltpu.VMEM((8, n_chunks * cols), jnp.float32),
            pltpu.SemaphoreType.DMA((n_chunks, n_dev)),
            pltpu.SemaphoreType.DMA((2,)),
        ],
        compiler_params=pltpu.CompilerParams(vmem_limit_bytes=VMEM_LIMIT),
        cost_estimate=pl.CostEstimate(
            flops=2 * total_rows * width * n_chunks * both_cols,
            bytes_accessed=2 * (total_rows * width + n_chunks * width * both_cols),
            transcendentals=total_rows * n_chunks * cols,
        ),
    )(ids, *flat, first, second)


def small_mod(value, rate):
    return jnp.where(
        rate == 1,
        0,
        jnp.where(rate == 2, value & 1, jnp.where(rate == 3, lax.rem(value, 3), value & 3)),
    )


def multiplicity_kernel(n_dev, slot_count, heads, ids_ref, counts_ref, slide_ref, rates_ref, out_ref):
    me, core = ids_ref[1], ids_ref[2]
    shape = out_ref.shape
    row = lax.broadcasted_iota(jnp.int32, shape, 0)
    col = lax.broadcasted_iota(jnp.int32, shape, 1)
    head = row // QROWS + core * (heads // 2)
    head = jnp.where(head >= heads, head - heads, head)
    query = row % QROWS
    step, slot = col // slot_count, col % slot_count
    device = me - step
    device = jnp.where(device < 0, device + n_dev, device)
    rate = jnp.full(shape, 1, jnp.int32)
    for h in range(heads):
        rate = jnp.where(head == h, rates_ref[h], rate)
    my_slide = slide_ref[me]
    first = me
    count = jnp.zeros(shape, jnp.int32)
    slide = jnp.zeros(shape, jnp.int32)
    for k in reversed(range(n_dev)):
        first = jnp.where(slide_ref[k] == my_slide, k, first)
        count = jnp.where(device == k, counts_ref[k], count)
        slide = jnp.where(device == k, slide_ref[k], slide)
    offset = small_mod(head, rate)
    query_position = (me - first) * slot_count + query
    key_position = (device - first) * slot_count + slot
    valid = slot < count
    near = jnp.where((step == 0) & valid, 1.0, 0.0)
    far = jnp.where(
        (slide == my_slide)
        & valid
        & (small_mod(query_position, rate) == offset)
        & (small_mod(key_position, rate) == offset),
        1.0,
        0.0,
    )
    out_ref[...] = near + far


def embed_kernel(ids_ref, counts_ref, mine_ref, theirs_ref, proj_ref, embed_ref, mixed_ref):
    mine, theirs = mine_ref[...], theirs_ref[...]
    low = lax.rem(ids_ref[0], 2) == 0
    rows = jnp.concatenate(
        [jnp.where(low, mine, theirs), jnp.where(low, theirs, mine)], axis=1
    )
    slot = lax.broadcasted_iota(jnp.int32, rows.shape, 0)
    rows = jnp.where(slot < counts_ref[ids_ref[1]], rows.astype(jnp.float32), 0.0)
    rows = rows.astype(jnp.bfloat16)
    embed_ref[...] = rows
    mixed_ref[...] = jnp.dot(rows, proj_ref[...], preferred_element_type=jnp.float32)


def slide_kernel(n_dev, slot_count, heads, ids_ref, counts_ref, *refs):
    terms = refs[: 2 * n_dev]
    (
        many_ref,
        gain_ref,
        wq_ref,
        wq_far_ref,
        wk_ref,
        wk_far_ref,
        wv_ref,
        wv_far_ref,
        wo_ref,
        wo_far_ref,
        out_ref,
        mixed,
    ) = refs[2 * n_dev :]
    core = ids_ref[2]
    for k in range(n_dev):
        mixed[k * slot_count : (k + 1) * slot_count, :] = (
            terms[2 * k][...] + terms[2 * k + 1][...]
        )
    hidden = normed(mixed[...], gain_ref[...])

    def project(rows, near_ref, far_ref):
        return jnp.concatenate(
            [
                jnp.dot(rows, near_ref[...], preferred_element_type=jnp.float32),
                jnp.dot(rows, far_ref[...], preferred_element_type=jnp.float32),
            ],
            axis=1,
        )

    query = project(hidden[:QROWS], wq_ref, wq_far_ref)
    keys = project(hidden, wk_ref, wk_far_ref).astype(jnp.bfloat16)
    values = project(hidden, wv_ref, wv_far_ref).astype(jnp.bfloat16)
    wide = (heads * QROWS, query.shape[1])
    own_head = (
        lax.broadcasted_iota(jnp.int32, wide, 0) // QROWS
        == lax.broadcasted_iota(jnp.int32, wide, 1) // HD
    )
    spread = jnp.where(own_head, jnp.concatenate([query] * heads, axis=0), 0.0)
    scores = lax.dot_general(
        spread.astype(jnp.bfloat16), keys, (((1,), (1,)), ((), ())), preferred_element_type=jnp.float32
    ) * (1.0 / math.sqrt(HD))
    many = many_ref[...]
    masked = jnp.where(many > 0.0, scores, FLOOR)
    weights = many * jnp.exp(masked - jnp.max(masked, axis=1, keepdims=True))
    weights = weights / jnp.sum(weights, axis=1, keepdims=True)
    context = jnp.dot(weights.astype(jnp.bfloat16), values, preferred_element_type=jnp.float32)
    context = jnp.where(own_head, context, 0.0).reshape(heads, QROWS, wide[1])
    context = jnp.sum(context, axis=0).astype(jnp.bfloat16)
    half = wide[1] // 2
    columns = pl.ds(pl.multiple_of(core * half, 128), half)
    attended = jnp.dot(
        context[:, :half], wo_ref[:, columns], preferred_element_type=jnp.float32
    ) + jnp.dot(context[:, half:], wo_far_ref[...], preferred_element_type=jnp.float32)
    total = mixed[:QROWS, columns] + attended
    slot = lax.broadcasted_iota(jnp.int32, total.shape, 0)
    total = jnp.where(slot < counts_ref[ids_ref[1]], total, 0.0)
    out_ref[...] = total[:slot_count].astype(jnp.bfloat16)


def on_device(
    tiles,
    counts,
    slide_of,
    rates,
    tile_gain,
    gate_weight,
    up_weight,
    embed_proj,
    slide_gain,
    slide_wq,
    slide_wk,
    slide_wv,
    slide_wo,
):
    slot_count, length, width = tiles.shape
    hidden_cols = gate_weight.shape[1]
    n_grp, n_dev, n_sub = (lax.axis_size(a) for a in ("grp", "dev", "sub"))
    ny = 2
    nz = n_dev // ny
    heads = slide_wq.shape[1] * n_sub // HD
    group, me, core = (lax.axis_index(a) for a in ("grp", "dev", "sub"))
    ids = jnp.stack([group, me, core]).astype(jnp.int32)

    to_pair = [(g, g ^ 1) for g in range(n_grp)]
    to_sibling = [(s, s ^ 1) for s in range(n_sub)]
    along_z = [(d, (d + ny) % n_dev) for d in range(n_dev)]
    along_y = [(d, d ^ 1) for d in range(n_dev)]

    half_cols = hidden_cols // 2
    cols = half_cols // CHUNKS
    base = (group % 2) * half_cols
    own_blocks = [
        jnp.concatenate(
            [
                lax.dynamic_slice_in_dim(w, base + c * cols, cols, 1)
                for w in (gate_weight, up_weight)
            ],
            axis=1,
        )
        for c in range(CHUNKS)
    ]
    gain_row = tile_gain[None, :]
    first = norm_tiles(ids, tiles, gain_row, False)
    chunks = []
    for block in own_blocks:
        blocks = []
        for step in range(nz):
            if step:
                block = lax.ppermute(block, "dev", along_z)
            blocks += [block, lax.ppermute(block, "dev", along_y)]
        chunks.append(blocks)
    pair_first = lax.ppermute(first, "grp", to_pair)
    pair_second = lax.ppermute(pair_first, "sub", to_sibling)
    second = norm_tiles(ids, tiles, gain_row, True)

    wq_far = lax.ppermute(slide_wq, "sub", to_sibling)
    wk_far = lax.ppermute(slide_wk, "sub", to_sibling)
    wv_far = lax.ppermute(slide_wv, "sub", to_sibling)
    out_cols = slide_wo.shape[1] // n_sub
    wo_far = lax.ppermute(
        lax.dynamic_slice_in_dim(slide_wo, (1 - core) * out_cols, out_cols, 1), "sub", to_sibling
    )

    smem = pl.BlockSpec(memory_space=pltpu.SMEM)
    vmem = pl.BlockSpec(memory_space=pltpu.VMEM)
    many = pl.pallas_call(
        functools.partial(multiplicity_kernel, n_dev, slot_count, heads),
        in_specs=[smem] * 4,
        out_specs=vmem,
        out_shape=jax.ShapeDtypeStruct((heads * QROWS, n_dev * slot_count), jnp.float32),
    )(ids, counts, slide_of, rates)

    own = [mlp(ids, [chunk], first, second, length, ny) for chunk in chunks]
    pair = mlp(ids, chunks, pair_first, pair_second, length, ny)
    theirs = lax.ppermute(pair, "grp", to_pair)
    mine = jnp.concatenate(own, axis=1)

    tile_embed, term = pl.pallas_call(
        embed_kernel,
        in_specs=[smem, smem, vmem, vmem, vmem],
        out_specs=(vmem, vmem),
        out_shape=(
            jax.ShapeDtypeStruct((slot_count, hidden_cols), jnp.bfloat16),
            jax.ShapeDtypeStruct((slot_count, embed_proj.shape[1]), jnp.float32),
        ),
        compiler_params=pltpu.CompilerParams(vmem_limit_bytes=VMEM_LIMIT),
    )(ids, counts, mine, theirs, embed_proj)

    terms = []
    for step in range(n_dev):
        for flip in range(2):
            if step == 0 and flip == 0:
                terms.append(term)
                continue
            perm = [
                (d * n_sub + s, ((d + step) % n_dev) * n_sub + (s ^ flip))
                for d in range(n_dev)
                for s in range(n_sub)
            ]
            terms.append(lax.ppermute(term, ("dev", "sub"), perm))

    slide_out = pl.pallas_call(
        functools.partial(slide_kernel, n_dev, slot_count, heads),
        in_specs=[smem, smem] + [vmem] * (2 * n_dev + 10),
        out_specs=vmem,
        out_shape=jax.ShapeDtypeStruct((slot_count, out_cols), jnp.bfloat16),
        scratch_shapes=[pltpu.VMEM((n_dev * slot_count, embed_proj.shape[1]), jnp.float32)],
        compiler_params=pltpu.CompilerParams(vmem_limit_bytes=VMEM_LIMIT),
    )(
        ids,
        counts,
        *terms,
        many,
        slide_gain[None, :],
        slide_wq,
        wq_far,
        slide_wk,
        wk_far,
        slide_wv,
        wv_far,
        slide_wo,
        wo_far,
    )
    return (tile_embed, slide_out)


def solution(mesh):
    placed = (
        P(("grp", "dev"), None, None),
        P("grp"),
        P("grp"),
        P(),
        P(),
        P("dev", "sub"),
        P("dev", "sub"),
        P("sub", None),
        P(),
        P(None, "sub"),
        P(None, "sub"),
        P(None, "sub"),
        P("sub", None),
    )
    return jax.shard_map(
        on_device,
        mesh=mesh,
        in_specs=placed,
        out_specs=(P(("grp", "dev"), "sub"), P(("grp", "dev"), "sub")),
        check_vma=False,
    )
```

time: 262 us -> 154 us (0.59)
  waiting for transfers between devices: 122 us -> 54.9 us
  blocking collectives: 63.9 us -> 0 us
  starting transfers between devices: 10.9 us -> 38.9 us
  Pallas kernels: 0 us -> 27.7 us
  matrix products: 17.4 us -> 0 us
  other arithmetic: 16.6 us -> 0.11 us
  local copies, waits for them, and re-layouts: 14.9 us -> 29.6 us
  between operations: 15.4 us -> 1.07 us
    all_to_all x2 -> x0, waiting for transfers between devices: 60.7 us -> none  [the longest x1 54.9 us: on_device(): lax.all_to_all(send_rows, 'dev', split_axis=0, concat_axis=0, tiled=True)]
    all_gather x2 -> x0, blocking collectives: 60.7 us -> none  [the longest x1 30.3 us: on_device(): piece_values = lax.all_gather(slide_values, 'dev', axis=0, tiled=True)]
    ppermute x0 -> x36, waiting for transfers between devices: none -> 54.9 us  [the longest x1 33.3 us: on_device(): pair_first = lax.ppermute(first, 'grp', to_pair)]
    all_gather x2 -> x0, waiting for transfers between devices: 54.9 us -> none  [the longest x1 54.8 us: gated_rows(): lax.all_gather(up_weight, 'dev', axis=0, tiled=True)]
    ppermute x0 -> x36, starting transfers between devices: none -> 38.9 us  [the longest x15 19.8 us: on_device(): terms.append(lax.ppermute(term, ('dev', 'sub'), perm))]
    pallas_call x0 -> x8, Pallas kernels: none -> 27.7 us  [the longest x3 19 us: mlp(): pl.pallas_call(functools.partial(mlp_kernel, n_chunks, n_dev, ny, length)...]
    unnamed x23 -> x120, local copies, waits for them, and re-layouts: 2.17 us -> 26.9 us
    dot_general x10 -> x0, matrix products: 16.3 us -> none  [the longest x1 6.49 us: gated_rows(): gate = jnp.dot(hidden, gate_full, preferred_element_type=jnp.float32)]
  transfers between devices with their start and end apart: 5 -> 36, of which waited for: 5 -> 12; matrix products, arithmetic and copies ran while one was open for 12% -> 1% of each run, Pallas kernels for 0% -> 15%
where the time goes in v1:
time: 154 us; the launch traced here: 152 us
  waiting for transfers between devices  54.9 us (36%)
  starting transfers between devices  38.9 us (25%)
  local copies, waits for them, and re-layouts  29.6 us (19%)
  Pallas kernels  27.7 us (18%)
    ppermute x1, waiting for transfers between devices, on_device(): pair_first = lax.ppermute(first, 'grp', to_pair)  33.3 us
    unnamed x120, local copies, waits for them, and re-layouts  26.9 us
    ppermute x15, starting transfers between devices, on_device(): terms.append(lax.ppermute(term, ('dev', 'sub'), perm))  19.8 us
    pallas_call x3, Pallas kernels, mlp(): pl.pallas_call(functools.partial(mlp_kernel, n_chunks, n_dev, ny, length)...  19 us
    ppermute x6, waiting for transfers between devices, on_device(): block = lax.ppermute(block, 'dev', along_z)  13.1 us
    ppermute x8, starting transfers between devices, on_device(): blocks += [block, lax.ppermute(block, 'dev', along_y)]  8.94 us
    ppermute x8, waiting for transfers between devices, on_device(): blocks += [block, lax.ppermute(block, 'dev', along_y)]  5.65 us
    ppermute x6, starting transfers between devices, on_device(): block = lax.ppermute(block, 'dev', along_z)  4.98 us
  transfers between devices with their start and end apart: 36, of which 12 were waited for; matrix products, arithmetic and copies ran while one was open for 1% of the time, Pallas kernels for 15%

profile of v1, /device:TPU:0, one launch (start us, length us, event | category | flops | bytes accessed | tf_op | source)
XLA Modules:
  0.0 152.4 jit_solution(6305721981906455183)
XLA Ops:
  1.4 1.9 %copy-done = bf16[4,256,1536]{2,1,0:T(8,128)(2,1)S(1)} copy-done((bf16[4,256,1536]{2,1,0:T(8,128)(2,1)S(1)}, bf16[4,256,1536]{2,1,0:T(8,128)(2,1)}, u32[]{:S(2)}) %copy-start) | copy-done | bytes 3145752
  3.3 1.6 %shard_map.140.refs_8_ = bf16[512,1536]{1,0:T(8,128)(2,1)S(1)} custom-call(s32[3]{0:T(128)S(1)} %pad_add_fusion.ids_ref, bf16[4,256,1536]{2,1,0:T(8,128)(2,1)S(1)} %copy-done, f32[1,1536]{1,0:T(1,128)S(1)} %broadcast_in_dim.6.gain_ref), custom_call_target="tpu_custom_call" | custom-call | flops 6291456 | bytes 3145728 | tf_op jit(solution)/shard_map/pallas_call | solution.py:39
  4.9 3.0 %collective-permute-start.14 = (bf16[512,1536]{1,0:T(8,128)(2,1)S(1)}, bf16[512,1536]{1,0:T(8,128)(2,1)}, u32[]{:S(2)}, u32[]{:S(2)}) collective-permute-start(bf16[512,1536]{1,0:T(8,128)(2,1)S(1)} %shard_map.140.refs_8_), channel_id=1, source_target_pairs={{0,16},{16,0},{1,17},{17,1},{2,18},{18,2},{3,19},{19,3},{4,20},{20... | collective-permute-start | bytes 4718600 | tf_op jit(solution)/shard_map/ppermute | solution.py:328
  9.1 33.3 %collective-permute-done.14.refs_16_ = bf16[512,1536]{1,0:T(8,128)(2,1)} collective-permute-done((bf16[512,1536]{1,0:T(8,128)(2,1)S(1)}, bf16[512,1536]{1,0:T(8,128)(2,1)}, u32[]{:S(2)}, u32[]{:S(2)}) %collective-permute-start.14) | collective-permute-done | bytes 1572896 | tf_op jit(solution)/shard_map/ppermute | solution.py:328
  43.5 1.9 %collective-permute-start.8 = (bf16[192,512]{1,0:T(8,128)(2,1)S(1)}, bf16[192,512]{1,0:T(8,128)(2,1)S(1)}, u32[]{:S(2)}, u32[]{:S(2)}) collective-permute-start(bf16[192,512]{1,0:T(8,128)(2,1)S(1)} %pad_maximum_fusion.1.refs_0_.refs_8_), channel_id=1, source_target_pairs={{0,4},{2,6},{4,8},{6,10},{8,12},{10,14},{12,0},{14,2},{1,5},{3,7},... | collective-permute-start | bytes 589832 | tf_op jit(solution)/shard_map/ppermute | solution.py:325
  45.4 1.6 %collective-permute-start.1 = (bf16[192,512]{1,0:T(8,128)(2,1)S(1)}, bf16[192,512]{1,0:T(8,128)(2,1)S(1)}, u32[]{:S(2)}, u32[]{:S(2)}) collective-permute-start(bf16[192,512]{1,0:T(8,128)(2,1)S(1)} %pad_maximum_fusion.refs_0_), channel_id=1, source_target_pairs={{0,4},{2,6},{4,8},{6,10},{8,12},{10,14},{12,0},{14,2},{1,5},{3,7},... | collective-permute-start | bytes 589832 | tf_op jit(solution)/shard_map/ppermute | solution.py:325
  49.7 3.4 %collective-permute-done.8.refs_2_.refs_10_ = bf16[192,512]{1,0:T(8,128)(2,1)S(1)} collective-permute-done((bf16[192,512]{1,0:T(8,128)(2,1)S(1)}, bf16[192,512]{1,0:T(8,128)(2,1)S(1)}, u32[]{:S(2)}, u32[]{:S(2)}) %collective-permute-start.8) | collective-permute-done | bytes 196640 | tf_op jit(solution)/shard_map/ppermute | solution.py:325
  53.1 4.0 %collective-permute-done.1.refs_2_ = bf16[192,512]{1,0:T(8,128)(2,1)S(1)} collective-permute-done((bf16[192,512]{1,0:T(8,128)(2,1)S(1)}, bf16[192,512]{1,0:T(8,128)(2,1)S(1)}, u32[]{:S(2)}, u32[]{:S(2)}) %collective-permute-start.1) | collective-permute-done | bytes 196640 | tf_op jit(solution)/shard_map/ppermute | solution.py:325
  62.9 3.2 %collective-permute-done.3.refs_4_ = bf16[192,512]{1,0:T(8,128)(2,1)} collective-permute-done((bf16[192,512]{1,0:T(8,128)(2,1)S(1)}, bf16[192,512]{1,0:T(8,128)(2,1)}, u32[]{:S(2)}, u32[]{:S(2)}) %collective-permute-start.3) | collective-permute-done | bytes 196640 | tf_op jit(solution)/shard_map/ppermute | solution.py:325
  71.9 2.3 %collective-permute-done.5.refs_6_ = bf16[192,512]{1,0:T(8,128)(2,1)} collective-permute-done((bf16[192,512]{1,0:T(8,128)(2,1)}, bf16[192,512]{1,0:T(8,128)(2,1)}, u32[]{:S(2)}, u32[]{:S(2)}) %collective-permute-start.5) | collective-permute-done | bytes 196640 | tf_op jit(solution)/shard_map/ppermute | solution.py:325
  76.7 1.6 %shard_map.141.refs_9_ = bf16[512,1536]{1,0:T(8,128)(2,1)S(1)} custom-call(s32[3]{0:T(128)S(1)} %pad_add_fusion.ids_ref, bf16[4,256,1536]{2,1,0:T(8,128)(2,1)S(1)} %copy-done.1, f32[1,1536]{1,0:T(1,128)S(1)} %broadcast_in_dim.6.gain_ref), custom_call_target="tpu_custom_call" | custom-call | flops 6291456 | bytes 3145728 | tf_op jit(solution)/shard_map/pallas_call | solution.py:39
  79.0 4.2 %collective-permute-done.13.refs_7_.refs_15_ = bf16[192,512]{1,0:T(8,128)(2,1)} collective-permute-done((bf16[192,512]{1,0:T(8,128)(2,1)}, bf16[192,512]{1,0:T(8,128)(2,1)}, u32[]{:S(2)}, u32[]{:S(2)}) %collective-permute-start.13) | collective-permute-done | bytes 196640 | tf_op jit(solution)/shard_map/ppermute | solution.py:326
  84.2 5.4 %shard_map.143 = bf16[4,256]{1,0:T(4,128)(2,1)S(1)} custom-call(s32[3]{0:T(128)S(1)} %pad_add_fusion.ids_ref, bf16[192,512]{1,0:T(8,128)(2,1)S(1)} %copy-done.18, bf16[192,512]{1,0:T(8,128)(2,1)S(1)} %copy-done.51, bf16[192,512]{1,0:T(8,128)(2,1)S(1)} %copy-done.46, bf16[192,512]{1,0:T(8,128)(2,1)S(1)} %copy-done.55, ...), custom_call_target="tpu_custom_call" | custom-call | flops 1610612736 | bytes 4718592 | tf_op jit(solution)/shard_map/pallas_call | solution.py:134
  90.2 5.3 %shard_map.142 = bf16[4,256]{1,0:T(4,128)(2,1)S(1)} custom-call(s32[3]{0:T(128)S(1)} %pad_add_fusion.ids_ref, bf16[192,512]{1,0:T(8,128)(2,1)S(1)} %copy-done.20, bf16[192,512]{1,0:T(8,128)(2,1)S(1)} %copy-done.53, bf16[192,512]{1,0:T(8,128)(2,1)S(1)} %copy-done.49, bf16[192,512]{1,0:T(8,128)(2,1)S(1)} %copy-done.57, ...), custom_call_target="tpu_custom_call" | custom-call | flops 1610612736 | bytes 4718592 | tf_op jit(solution)/shard_map/pallas_call | solution.py:134
  95.6 8.2 %shard_map.144 = bf16[4,512]{1,0:T(4,128)(2,1)S(1)} custom-call(s32[3]{0:T(128)S(1)} %pad_add_fusion.ids_ref, bf16[192,512]{1,0:T(8,128)(2,1)S(1)} %copy-done.20, bf16[192,512]{1,0:T(8,128)(2,1)S(1)} %copy-done.53, bf16[192,512]{1,0:T(8,128)(2,1)S(1)} %copy-done.49, bf16[192,512]{1,0:T(8,128)(2,1)S(1)} %copy-done.57, ...), custom_call_target="tpu_custom_call" | custom-call | flops 3221225472 | bytes 6291456 | tf_op jit(solution)/shard_map/pallas_call | solution.py:134
  103.9 1.5 %collective-permute-start.16 = (bf16[4,512]{1,0:T(4,128)(2,1)S(1)}, bf16[4,512]{1,0:T(4,128)(2,1)S(1)}, u32[]{:S(2)}, u32[]{:S(2)}) collective-permute-start(bf16[4,512]{1,0:T(4,128)(2,1)S(1)} %shard_map.144), channel_id=1, source_target_pairs={{0,16},{16,0},{1,17},{17,1},{2,18},{18,2},{3,19},{19,3},{4,20},{20... | collective-permute-start | bytes 12296 | tf_op jit(solution)/shard_map/ppermute | solution.py:351
  105.4 2.1 %collective-permute-done.16.theirs_ref = bf16[4,512]{1,0:T(4,128)(2,1)S(1)} collective-permute-done((bf16[4,512]{1,0:T(4,128)(2,1)S(1)}, bf16[4,512]{1,0:T(4,128)(2,1)S(1)}, u32[]{:S(2)}, u32[]{:S(2)}) %collective-permute-start.16) | collective-permute-done | bytes 4128 | tf_op jit(solution)/shard_map/ppermute | solution.py:351
  112.3 1.6 %collective-permute-start.20 = (f32[4,768]{1,0:T(4,128)S(1)}, f32[4,768]{1,0:T(4,128)S(1)}, u32[]{:S(2)}, u32[]{:S(2)}) collective-permute-start(f32[4,768]{1,0:T(4,128)S(1)} %get-tuple-element.5.refs_0_), channel_id=1, source_target_pairs={{0,4},{1,5},{2,6},{3,7},{4,8},{5,9},{6,10},{7,11},{8,12},{9,13},{1... | collective-permute-start | bytes 36872 | tf_op jit(solution)/shard_map/ppermute | solution.py:376
  118.9 1.8 %collective-permute-start.23 = (f32[4,768]{1,0:T(4,128)S(1)}, f32[4,768]{1,0:T(4,128)S(1)}, u32[]{:S(2)}, u32[]{:S(2)}) collective-permute-start(f32[4,768]{1,0:T(4,128)S(1)} %get-tuple-element.5.refs_0_), channel_id=1, source_target_pairs={{0,7},{1,6},{2,9},{3,8},{4,11},{5,10},{6,13},{7,12},{8,15},{9,14},... | collective-permute-start | bytes 36872 | tf_op jit(solution)/shard_map/ppermute | solution.py:376
  122.7 1.7 %collective-permute-start.25 = (f32[4,768]{1,0:T(4,128)S(1)}, f32[4,768]{1,0:T(4,128)S(1)}, u32[]{:S(2)}, u32[]{:S(2)}) collective-permute-start(f32[4,768]{1,0:T(4,128)S(1)} %get-tuple-element.5.refs_0_), channel_id=1, source_target_pairs={{0,9},{1,8},{2,11},{3,10},{4,13},{5,12},{6,15},{7,14},{8,1},{9,0},... | collective-permute-start | bytes 36872 | tf_op jit(solution)/shard_map/ppermute | solution.py:376
  125.0 1.9 %collective-permute-start.26 = (f32[4,768]{1,0:T(4,128)S(1)}, f32[4,768]{1,0:T(4,128)S(1)}, u32[]{:S(2)}, u32[]{:S(2)}) collective-permute-start(f32[4,768]{1,0:T(4,128)S(1)} %get-tuple-element.5.refs_0_), channel_id=1, source_target_pairs={{0,10},{1,11},{2,12},{3,13},{4,14},{5,15},{6,0},{7,1},{8,2},{9,3},... | collective-permute-start | bytes 36872 | tf_op jit(solution)/shard_map/ppermute | solution.py:376
  129.4 2.2 %collective-permute-start.28 = (f32[4,768]{1,0:T(4,128)S(1)}, f32[4,768]{1,0:T(4,128)}, u32[]{:S(2)}, u32[]{:S(2)}) collective-permute-start(f32[4,768]{1,0:T(4,128)S(1)} %get-tuple-element.5.refs_0_), channel_id=1, source_target_pairs={{0,12},{1,13},{2,14},{3,15},{4,0},{5,1},{6,2},{7,3},{8,4},{9,5},{1... | collective-permute-start | bytes 36872 | tf_op jit(solution)/shard_map/ppermute | solution.py:376
  132.2 1.6 %collective-permute-start.29 = (f32[4,768]{1,0:T(4,128)S(1)}, f32[4,768]{1,0:T(4,128)}, u32[]{:S(2)}, u32[]{:S(2)}) collective-permute-start(f32[4,768]{1,0:T(4,128)S(1)} %get-tuple-element.5.refs_0_), channel_id=1, source_target_pairs={{0,13},{1,12},{2,15},{3,14},{4,1},{5,0},{6,3},{7,2},{8,5},{9,4},{1... | collective-permute-start | bytes 36872 | tf_op jit(solution)/shard_map/ppermute | solution.py:376
  149.6 2.7 %shard_map.147 = bf16[4,384]{1,0:T(4,128)(2,1)} custom-call(s32[3]{0:T(128)S(1)} %copy-done.22, s32[8]{0:T(128)S(1)} %copy-done.44, f32[4,768]{1,0:T(4,128)S(1)} %get-tuple-element.5.refs_0_, f32[4,768]{1,0:T(4,128)S(1)} %copy-done.24, f32[4,768]{1,0:T(4,128)S(1)} %copy-done.26, f32[4,768]{1,0:T(4,128)S(1)} %copy-done.28, f32[4,768]{1,0:T(4,128)S(1)} %copy-done.30, ...), custom_call_target="tpu_custom_call" | custom-call | tf_op jit(solution)/shard_map/pallas_call | solution.py:378
  (184 shorter events, 53.1 us)
Async XLA Ops:
  4.9 37.5 %collective-permute-start.14 = (bf16[512,1536]{1,0:T(8,128)(2,1)S(1)}, bf16[512,1536]{1,0:T(8,128)(2,1)}, u32[]{:S(2)}, u32[]{:S(2)}) collective-permute-start(bf16[512,1536]{1,0:T(8,128)(2,1)S(1)} %shard_map.140.refs_8_), channel_id=1, source_target_pairs={{0,16},{16,0},{1,17},{17,1},{2,18},{18,2},{3,19},{19,3},{4,20},{20... | collective-permute-start | bytes 4718600 | tf_op jit(solution)/shard_map/ppermute | solution.py:328
  42.4 53.2 %collective-permute-start.15 = (bf16[512,1536]{1,0:T(8,128)(2,1)}, bf16[512,1536]{1,0:T(8,128)(2,1)}, u32[]{:S(2)}, u32[]{:S(2)}) collective-permute-start(bf16[512,1536]{1,0:T(8,128)(2,1)} %collective-permute-done.14.refs_16_), channel_id=1, source_target_pairs={{0,1},{1,0},{2,3},{3,2},{4,5},{5,4},{6,7},{7,6},{8,9},{9,8},{10,11... | collective-permute-start | bytes 4718600 | tf_op jit(solution)/shard_map/ppermute | solution.py:329
  43.5 9.7 %collective-permute-start.8 = (bf16[192,512]{1,0:T(8,128)(2,1)S(1)}, bf16[192,512]{1,0:T(8,128)(2,1)S(1)}, u32[]{:S(2)}, u32[]{:S(2)}) collective-permute-start(bf16[192,512]{1,0:T(8,128)(2,1)S(1)} %pad_maximum_fusion.1.refs_0_.refs_8_), channel_id=1, source_target_pairs={{0,4},{2,6},{4,8},{6,10},{8,12},{10,14},{12,0},{14,2},{1,5},{3,7},... | collective-permute-start | bytes 589832 | tf_op jit(solution)/shard_map/ppermute | solution.py:325
  45.4 11.8 %collective-permute-start.1 = (bf16[192,512]{1,0:T(8,128)(2,1)S(1)}, bf16[192,512]{1,0:T(8,128)(2,1)S(1)}, u32[]{:S(2)}, u32[]{:S(2)}) collective-permute-start(bf16[192,512]{1,0:T(8,128)(2,1)S(1)} %pad_maximum_fusion.refs_0_), channel_id=1, source_target_pairs={{0,4},{2,6},{4,8},{6,10},{8,12},{10,14},{12,0},{14,2},{1,5},{3,7},... | collective-permute-start | bytes 589832 | tf_op jit(solution)/shard_map/ppermute | solution.py:325
  47.0 10.3 %collective-permute-start.7 = (bf16[192,512]{1,0:T(8,128)(2,1)S(1)}, bf16[192,512]{1,0:T(8,128)(2,1)S(1)}, u32[]{:S(2)}, u32[]{:S(2)}) collective-permute-start(bf16[192,512]{1,0:T(8,128)(2,1)S(1)} %pad_maximum_fusion.1.refs_0_.refs_8_), channel_id=1, source_target_pairs={{0,2},{2,0},{4,6},{6,4},{8,10},{10,8},{12,14},{14,12},{1,3},{3,1},... | collective-permute-start | bytes 589832 | tf_op jit(solution)/shard_map/ppermute | solution.py:326
  48.5 11.0 %collective-permute-start = (bf16[192,512]{1,0:T(8,128)(2,1)S(1)}, bf16[192,512]{1,0:T(8,128)(2,1)S(1)}, u32[]{:S(2)}, u32[]{:S(2)}) collective-permute-start(bf16[192,512]{1,0:T(8,128)(2,1)S(1)} %pad_maximum_fusion.refs_0_), channel_id=1, source_target_pairs={{0,2},{2,0},{4,6},{6,4},{8,10},{10,8},{12,14},{14,12},{1,3},{3,1},... | collective-permute-start | bytes 589832 | tf_op jit(solution)/shard_map/ppermute | solution.py:326
  61.6 9.6 %collective-permute-start.12 = (bf16[192,512]{1,0:T(8,128)(2,1)}, bf16[192,512]{1,0:T(8,128)(2,1)}, u32[]{:S(2)}, u32[]{:S(2)}) collective-permute-start(bf16[192,512]{1,0:T(8,128)(2,1)} %collective-permute-done.10.refs_4_.refs_12_), channel_id=1, source_target_pairs={{0,4},{2,6},{4,8},{6,10},{8,12},{10,14},{12,0},{14,2},{1,5},{3,7},... | collective-permute-start | bytes 589832 | tf_op jit(solution)/shard_map/ppermute | solution.py:325
  66.8 11.5 %collective-permute-start.11 = (bf16[192,512]{1,0:T(8,128)(2,1)}, bf16[192,512]{1,0:T(8,128)(2,1)}, u32[]{:S(2)}, u32[]{:S(2)}) collective-permute-start(bf16[192,512]{1,0:T(8,128)(2,1)} %collective-permute-done.10.refs_4_.refs_12_), channel_id=1, source_target_pairs={{0,2},{2,0},{4,6},{6,4},{8,10},{10,8},{12,14},{14,12},{1,3},{3,1},... | collective-permute-start | bytes 589832 | tf_op jit(solution)/shard_map/ppermute | solution.py:326
  69.9 9.2 %collective-permute-start.4 = (bf16[192,512]{1,0:T(8,128)(2,1)}, bf16[192,512]{1,0:T(8,128)(2,1)}, u32[]{:S(2)}, u32[]{:S(2)}) collective-permute-start(bf16[192,512]{1,0:T(8,128)(2,1)} %collective-permute-done.3.refs_4_), channel_id=1, source_target_pairs={{0,2},{2,0},{4,6},{6,4},{8,10},{10,8},{12,14},{14,12},{1,3},{3,1},... | collective-permute-start | bytes 589832 | tf_op jit(solution)/shard_map/ppermute | solution.py:326
  71.1 12.1 %collective-permute-start.13 = (bf16[192,512]{1,0:T(8,128)(2,1)}, bf16[192,512]{1,0:T(8,128)(2,1)}, u32[]{:S(2)}, u32[]{:S(2)}) collective-permute-start(bf16[192,512]{1,0:T(8,128)(2,1)} %collective-permute-done.12.refs_6_.refs_14_), channel_id=1, source_target_pairs={{0,2},{2,0},{4,6},{6,4},{8,10},{10,8},{12,14},{14,12},{1,3},{3,1},... | collective-permute-start | bytes 589832 | tf_op jit(solution)/shard_map/ppermute | solution.py:326
  74.2 15.4 %collective-permute-start.6 = (bf16[192,512]{1,0:T(8,128)(2,1)}, bf16[192,512]{1,0:T(8,128)(2,1)S(1)}, u32[]{:S(2)}, u32[]{:S(2)}) collective-permute-start(bf16[192,512]{1,0:T(8,128)(2,1)} %collective-permute-done.5.refs_6_), channel_id=1, source_target_pairs={{0,2},{2,0},{4,6},{6,4},{8,10},{10,8},{12,14},{14,12},{1,3},{3,1},... | collective-permute-start | bytes 589832 | tf_op jit(solution)/shard_map/ppermute | solution.py:326
  78.4 32.7 %collective-permute-start.32 = (bf16[768,384]{1,0:T(8,128)(2,1)S(1)}, bf16[768,384]{1,0:T(8,128)(2,1)S(1)}, u32[]{:S(2)}, u32[]{:S(2)}) collective-permute-start(bf16[768,384]{1,0:T(8,128)(2,1)S(1)} %copy-done.6), channel_id=1, source_target_pairs={{0,1},{1,0},{2,3},{3,2},{4,5},{5,4},{6,7},{7,6},{8,9},{9,8},{10,11... | collective-permute-start | bytes 1769480 | tf_op jit(solution)/shard_map/ppermute | solution.py:332
  79.0 33.3 %collective-permute-start.33 = (bf16[768,384]{1,0:T(8,128)(2,1)S(1)}, bf16[768,384]{1,0:T(8,128)(2,1)S(1)}, u32[]{:S(2)}, u32[]{:S(2)}) collective-permute-start(bf16[768,384]{1,0:T(8,128)(2,1)S(1)} %copy-done.8), channel_id=1, source_target_pairs={{0,1},{1,0},{2,3},{3,2},{4,5},{5,4},{6,7},{7,6},{8,9},{9,8},{10,11... | collective-permute-start | bytes 1769480 | tf_op jit(solution)/shard_map/ppermute | solution.py:333
  83.2 30.7 %collective-permute-start.34 = (bf16[768,384]{1,0:T(8,128)(2,1)S(1)}, bf16[768,384]{1,0:T(8,128)(2,1)S(1)}, u32[]{:S(2)}, u32[]{:S(2)}) collective-permute-start(bf16[768,384]{1,0:T(8,128)(2,1)S(1)} %copy-done.10), channel_id=1, source_target_pairs={{0,1},{1,0},{2,3},{3,2},{4,5},{5,4},{6,7},{7,6},{8,9},{9,8},{10,11... | collective-permute-start | bytes 1769480 | tf_op jit(solution)/shard_map/ppermute | solution.py:334
  89.7 19.3 %collective-permute-start.35 = (bf16[384,384]{1,0:T(8,128)(2,1)S(1)}, bf16[384,384]{1,0:T(8,128)(2,1)S(1)}, u32[]{:S(2)}, u32[]{:S(2)}) collective-permute-start(bf16[384,384]{1,0:T(8,128)(2,1)S(1)} %constant_dynamic-slice_fusion), channel_id=1, source_target_pairs={{0,1},{1,0},{2,3},{3,2},{4,5},{5,4},{6,7},{7,6},{8,9},{9,8},{10,11... | collective-permute-start | bytes 884744 | tf_op jit(solution)/shard_map/ppermute | solution.py:336
  111.1 9.5 %collective-permute-start.19 = (f32[4,768]{1,0:T(4,128)S(1)}, f32[4,768]{1,0:T(4,128)S(1)}, u32[]{:S(2)}, u32[]{:S(2)}) collective-permute-start(f32[4,768]{1,0:T(4,128)S(1)} %get-tuple-element.5.refs_0_), channel_id=1, source_target_pairs={{0,3},{1,2},{2,5},{3,4},{4,7},{5,6},{6,9},{7,8},{8,11},{9,10},{10,... | collective-permute-start | bytes 36872 | tf_op jit(solution)/shard_map/ppermute | solution.py:376
  112.3 9.8 %collective-permute-start.20 = (f32[4,768]{1,0:T(4,128)S(1)}, f32[4,768]{1,0:T(4,128)S(1)}, u32[]{:S(2)}, u32[]{:S(2)}) collective-permute-start(f32[4,768]{1,0:T(4,128)S(1)} %get-tuple-element.5.refs_0_), channel_id=1, source_target_pairs={{0,4},{1,5},{2,6},{3,7},{4,8},{5,9},{6,10},{7,11},{8,12},{9,13},{1... | collective-permute-start | bytes 36872 | tf_op jit(solution)/shard_map/ppermute | solution.py:376
  114.7 9.7 %collective-permute-start.21 = (f32[4,768]{1,0:T(4,128)S(1)}, f32[4,768]{1,0:T(4,128)S(1)}, u32[]{:S(2)}, u32[]{:S(2)}) collective-permute-start(f32[4,768]{1,0:T(4,128)S(1)} %get-tuple-element.5.refs_0_), channel_id=1, source_target_pairs={{0,5},{1,4},{2,7},{3,6},{4,9},{5,8},{6,11},{7,10},{8,13},{9,12},{1... | collective-permute-start | bytes 36872 | tf_op jit(solution)/shard_map/ppermute | solution.py:376
  116.8 10.0 %collective-permute-start.22 = (f32[4,768]{1,0:T(4,128)S(1)}, f32[4,768]{1,0:T(4,128)S(1)}, u32[]{:S(2)}, u32[]{:S(2)}) collective-permute-start(f32[4,768]{1,0:T(4,128)S(1)} %get-tuple-element.5.refs_0_), channel_id=1, source_target_pairs={{0,6},{1,7},{2,8},{3,9},{4,10},{5,11},{6,12},{7,13},{8,14},{9,15},... | collective-permute-start | bytes 36872 | tf_op jit(solution)/shard_map/ppermute | solution.py:376
  118.9 9.9 %collective-permute-start.23 = (f32[4,768]{1,0:T(4,128)S(1)}, f32[4,768]{1,0:T(4,128)S(1)}, u32[]{:S(2)}, u32[]{:S(2)}) collective-permute-start(f32[4,768]{1,0:T(4,128)S(1)} %get-tuple-element.5.refs_0_), channel_id=1, source_target_pairs={{0,7},{1,6},{2,9},{3,8},{4,11},{5,10},{6,13},{7,12},{8,15},{9,14},... | collective-permute-start | bytes 36872 | tf_op jit(solution)/shard_map/ppermute | solution.py:376
  121.3 10.3 %collective-permute-start.24 = (f32[4,768]{1,0:T(4,128)S(1)}, f32[4,768]{1,0:T(4,128)S(1)}, u32[]{:S(2)}, u32[]{:S(2)}) collective-permute-start(f32[4,768]{1,0:T(4,128)S(1)} %get-tuple-element.5.refs_0_), channel_id=1, source_target_pairs={{0,8},{1,9},{2,10},{3,11},{4,12},{5,13},{6,14},{7,15},{8,0},{9,1},... | collective-permute-start | bytes 36872 | tf_op jit(solution)/shard_map/ppermute | solution.py:376
  122.7 11.1 %collective-permute-start.25 = (f32[4,768]{1,0:T(4,128)S(1)}, f32[4,768]{1,0:T(4,128)S(1)}, u32[]{:S(2)}, u32[]{:S(2)}) collective-permute-start(f32[4,768]{1,0:T(4,128)S(1)} %get-tuple-element.5.refs_0_), channel_id=1, source_target_pairs={{0,9},{1,8},{2,11},{3,10},{4,13},{5,12},{6,15},{7,14},{8,1},{9,0},... | collective-permute-start | bytes 36872 | tf_op jit(solution)/shard_map/ppermute | solution.py:376
  125.0 9.6 %collective-permute-start.26 = (f32[4,768]{1,0:T(4,128)S(1)}, f32[4,768]{1,0:T(4,128)S(1)}, u32[]{:S(2)}, u32[]{:S(2)}) collective-permute-start(f32[4,768]{1,0:T(4,128)S(1)} %get-tuple-element.5.refs_0_), channel_id=1, source_target_pairs={{0,10},{1,11},{2,12},{3,13},{4,14},{5,15},{6,0},{7,1},{8,2},{9,3},... | collective-permute-start | bytes 36872 | tf_op jit(solution)/shard_map/ppermute | solution.py:376
  127.4 10.3 %collective-permute-start.27 = (f32[4,768]{1,0:T(4,128)S(1)}, f32[4,768]{1,0:T(4,128)}, u32[]{:S(2)}, u32[]{:S(2)}) collective-permute-start(f32[4,768]{1,0:T(4,128)S(1)} %get-tuple-element.5.refs_0_), channel_id=1, source_target_pairs={{0,11},{1,10},{2,13},{3,12},{4,15},{5,14},{6,1},{7,0},{8,3},{9,2},... | collective-permute-start | bytes 36872 | tf_op jit(solution)/shard_map/ppermute | solution.py:376
  (72 other events, 661.8 us)

commit v2 on v1

v2 whole, which is shorter than its diff:
```python
import functools
import math

import jax
import jax.numpy as jnp
from jax import lax
from jax.experimental import pallas as pl
from jax.experimental.pallas import tpu as pltpu
from jax.sharding import PartitionSpec as P

HD = 64
EPSILON = 1e-06
FLOOR = -1e30
CHUNKS = (384, 128)
QROWS = 8
VMEM_LIMIT = 60 * 1024 * 1024
SMALL_VMEM = 24 * 1024 * 1024


def normed(rows_in, gains):
    average = jnp.mean(rows_in, axis=-1, keepdims=True)
    centred = rows_in - average
    variance = jnp.mean(centred * centred, axis=-1, keepdims=True)
    return (centred * lax.rsqrt(variance + EPSILON) * gains).astype(jnp.bfloat16)


def norm_kernel(ids_ref, tiles_ref, gain_ref, *out_refs):
    hidden = normed(tiles_ref[0].astype(jnp.float32), gain_ref[...])
    for i, out_ref in enumerate(out_refs):

        @pl.when(pl.program_id(0) == i)
        def _():
            out_ref[...] = hidden


def norm_tiles(ids, tiles, gain, flip):
    slot_count, length, width = tiles.shape
    half = slot_count // 2

    def tile_map(i, ids_ref):
        core = ids_ref[2]
        first = (1 - core if flip else core) * half
        return (first + i, 0, 0)

    return pl.pallas_call(
        norm_kernel,
        grid_spec=pltpu.PrefetchScalarGridSpec(
            num_scalar_prefetch=1,
            grid=(half,),
            in_specs=[
                pl.BlockSpec((1, length, width), tile_map),
                pl.BlockSpec((1, width), lambda i, ids_ref: (0, 0)),
            ],
            out_specs=[pl.BlockSpec((length, width), lambda i, ids_ref: (0, 0))] * half,
        ),
        out_shape=[jax.ShapeDtypeStruct((length, width), jnp.bfloat16)] * half,
        compiler_params=pltpu.CompilerParams(vmem_limit_bytes=VMEM_LIMIT),
        cost_estimate=pl.CostEstimate(
            flops=8 * half * length * width,
            bytes_accessed=4 * half * length * width,
            transcendentals=half * length,
        ),
    )(ids, tiles, gain)


def gate_kernel(value_ref, after_ref, out_ref):
    del value_ref, after_ref, out_ref


def after(value, *others):
    any_spec = pl.BlockSpec(memory_space=pl.ANY)
    for other in others:
        value = pl.pallas_call(
            gate_kernel,
            in_specs=[any_spec, any_spec],
            out_specs=any_spec,
            out_shape=jax.ShapeDtypeStruct(value.shape, value.dtype),
            input_output_aliases={0: 0},
            compiler_params=pltpu.CompilerParams(vmem_limit_bytes=VMEM_LIMIT),
        )(value, other)
    return value


def mlp_kernel(n_dev, ny, n_tiles, length, ids_ref, *refs):
    blocks = refs[:n_dev]
    tile_refs = refs[n_dev : n_dev + n_tiles]
    out_ref, weights, rows, weight_sems, row_sems = refs[n_dev + n_tiles :]
    me = ids_ref[1]
    nz = n_dev // ny
    my_z = me // ny
    my_y = me - my_z * ny
    depth, both_cols = blocks[0].shape
    cols = both_cols // 2
    row_copies = [
        pltpu.make_async_copy(ref, rows.at[pl.ds(i * length, length)], row_sems.at[i])
        for i, ref in enumerate(tile_refs)
    ]
    weight_copies = []
    for k in range(n_dev):
        step, flip = k // ny, k % ny
        z = my_z - step
        z = jnp.where(z < 0, z + nz, z)
        y = 1 - my_y if flip else my_y
        start = pl.multiple_of((z * ny + y) * depth, depth)
        weight_copies.append(
            pltpu.make_async_copy(blocks[k], weights.at[pl.ds(start, depth)], weight_sems.at[k])
        )
    for copy in row_copies[:2] + weight_copies + row_copies[2:]:
        copy.start()
    for copy in weight_copies:
        copy.wait()
    for i in range(0, n_tiles, 2):
        row_copies[i].wait()
        row_copies[i + 1].wait()
        both = jnp.dot(
            rows[i * length : (i + 2) * length, :],
            weights[...],
            preferred_element_type=jnp.float32,
        )
        gate, up_part = both[:, :cols], both[:, cols:]
        silu = gate * (0.5 * jnp.tanh(0.5 * gate) + 0.5)
        gated = (silu * up_part).astype(jnp.bfloat16).astype(jnp.float32)
        for j in range(2):
            out_ref[i + j : i + j + 1, :] = jnp.sum(
                gated[j * length : (j + 1) * length], axis=0, keepdims=True
            ) * (1.0 / length)


def mlp(ids, blocks, tiles, ny):
    n_dev, n_tiles = len(blocks), len(tiles)
    depth, both_cols = blocks[0].shape
    length, width = tiles[0].shape
    cols = both_cols // 2
    any_spec = pl.BlockSpec(memory_space=pl.ANY)
    return pl.pallas_call(
        functools.partial(mlp_kernel, n_dev, ny, n_tiles, length),
        in_specs=[pl.BlockSpec(memory_space=pltpu.SMEM)] + [any_spec] * (n_dev + n_tiles),
        out_specs=pl.BlockSpec(memory_space=pltpu.VMEM),
        out_shape=jax.ShapeDtypeStruct((n_tiles, cols), jnp.float32),
        scratch_shapes=[
            pltpu.VMEM((width, both_cols), jnp.bfloat16),
            pltpu.VMEM((n_tiles * length, width), jnp.bfloat16),
            pltpu.SemaphoreType.DMA((n_dev,)),
            pltpu.SemaphoreType.DMA((n_tiles,)),
        ],
        compiler_params=pltpu.CompilerParams(vmem_limit_bytes=VMEM_LIMIT),
        cost_estimate=pl.CostEstimate(
            flops=2 * n_tiles * length * width * both_cols,
            bytes_accessed=2 * (n_tiles * length * width + width * both_cols),
            transcendentals=n_tiles * length * cols,
        ),
    )(ids, *blocks, *tiles)


def small_mod(value, rate):
    return jnp.where(
        rate == 1,
        0,
        jnp.where(rate == 2, value & 1, jnp.where(rate == 3, lax.rem(value, 3), value & 3)),
    )


def multiplicity_kernel(n_dev, slot_count, heads, ids_ref, counts_ref, slide_ref, rates_ref, out_ref):
    me, core = ids_ref[1], ids_ref[2]
    shape = out_ref.shape
    row = lax.broadcasted_iota(jnp.int32, shape, 0)
    col = lax.broadcasted_iota(jnp.int32, shape, 1)
    head = row // QROWS + core * (heads // 2)
    head = jnp.where(head >= heads, head - heads, head)
    query = row % QROWS
    device, slot = col // slot_count, col % slot_count
    rate = jnp.full(shape, 1, jnp.int32)
    for h in range(heads):
        rate = jnp.where(head == h, rates_ref[h], rate)
    my_slide = slide_ref[me]
    first = me
    count = jnp.zeros(shape, jnp.int32)
    slide = jnp.zeros(shape, jnp.int32)
    for k in reversed(range(n_dev)):
        first = jnp.where(slide_ref[k] == my_slide, k, first)
        count = jnp.where(device == k, counts_ref[k], count)
        slide = jnp.where(device == k, slide_ref[k], slide)
    offset = small_mod(head, rate)
    query_position = (me - first) * slot_count + query
    key_position = (device - first) * slot_count + slot
    valid = slot < count
    near = jnp.where((device == me) & valid, 1.0, 0.0)
    far = jnp.where(
        (slide == my_slide)
        & valid
        & (small_mod(query_position, rate) == offset)
        & (small_mod(key_position, rate) == offset),
        1.0,
        0.0,
    )
    out_ref[...] = near + far


def order_kernel(slot_count, ids_ref, own_ref, even_ref, odd_ref, rest_ref, own_out, pair_out):
    half = slot_count // 2
    low = ids_ref[2] == 0

    def ordered(mine, others):
        return jnp.concatenate(
            [jnp.where(low, mine, others), jnp.where(low, others, mine)], axis=0
        ).astype(jnp.bfloat16)

    own = jnp.concatenate([own_ref[...], rest_ref[:slot_count, :]], axis=1)
    own_out[...] = ordered(own[:half], own[half:])
    sides = []
    for side in range(2):
        large = jnp.concatenate([ref[side : side + 1, :] for ref in (even_ref, odd_ref)], axis=0)
        start = slot_count + side * half
        sides.append(jnp.concatenate([large, rest_ref[start : start + half, :]], axis=1))
    pair_out[...] = ordered(*sides)


def embed_kernel(ids_ref, counts_ref, mine_ref, pair_ref, proj_ref, embed_ref, terms_ref):
    mine, theirs = mine_ref[...], pair_ref[...]
    low = lax.rem(ids_ref[0], 2) == 0
    rows = jnp.concatenate(
        [jnp.where(low, mine, theirs), jnp.where(low, theirs, mine)], axis=1
    )
    slot = lax.broadcasted_iota(jnp.int32, rows.shape, 0)
    rows = jnp.where(slot < counts_ref[ids_ref[1]], rows.astype(jnp.float32), 0.0)
    rows = rows.astype(jnp.bfloat16)
    embed_ref[...] = rows
    mixed = jnp.dot(rows, proj_ref[...], preferred_element_type=jnp.float32)
    half = mixed.shape[1] // 2
    packed = jnp.concatenate([mixed[:, :half], mixed[:, half:]], axis=0)
    for k in range(terms_ref.shape[0]):
        terms_ref[k] = packed


def slide_kernel(n_dev, slot_count, heads, ids_ref, counts_ref, *refs):
    (
        terms_ref,
        many_ref,
        gain_ref,
        wq_ref,
        wq_far_ref,
        wk_ref,
        wk_far_ref,
        wv_ref,
        wv_far_ref,
        wo_ref,
        wo_far_ref,
        out_ref,
        mixed,
    ) = refs
    me, core = ids_ref[1], ids_ref[2]
    for k in range(n_dev):
        packed = terms_ref[2 * k] + terms_ref[2 * k + 1]
        mixed[k * slot_count : (k + 1) * slot_count, :] = jnp.concatenate(
            [packed[:slot_count], packed[slot_count:]], axis=1
        )
    hidden = normed(mixed[...], gain_ref[...])
    per_tile = QROWS // slot_count
    around = mixed[pl.ds(pl.multiple_of(me // per_tile * QROWS, QROWS), QROWS), :]
    mine = around
    for k in range(1, per_tile):
        turned = jnp.concatenate([around[k * slot_count :], around[: k * slot_count]], axis=0)
        mine = jnp.where(lax.rem(me, per_tile) == k, turned, mine)
    my_hidden = normed(mine, gain_ref[...])

    def project(rows, near_ref, far_ref):
        return jnp.concatenate(
            [
                jnp.dot(rows, near_ref[...], preferred_element_type=jnp.float32),
                jnp.dot(rows, far_ref[...], preferred_element_type=jnp.float32),
            ],
            axis=1,
        )

    query = project(my_hidden, wq_ref, wq_far_ref)
    keys = project(hidden, wk_ref, wk_far_ref).astype(jnp.bfloat16)
    values = project(hidden, wv_ref, wv_far_ref).astype(jnp.bfloat16)
    wide = (heads * QROWS, query.shape[1])
    own_head = (
        lax.broadcasted_iota(jnp.int32, wide, 0) // QROWS
        == lax.broadcasted_iota(jnp.int32, wide, 1) // HD
    )
    spread = jnp.where(own_head, jnp.concatenate([query] * heads, axis=0), 0.0)
    scores = lax.dot_general(
        spread.astype(jnp.bfloat16), keys, (((1,), (1,)), ((), ())), preferred_element_type=jnp.float32
    ) * (1.0 / math.sqrt(HD))
    many = many_ref[...]
    masked = jnp.where(many > 0.0, scores, FLOOR)
    weights = many * jnp.exp(masked - jnp.max(masked, axis=1, keepdims=True))
    weights = weights / jnp.sum(weights, axis=1, keepdims=True)
    context = jnp.dot(weights.astype(jnp.bfloat16), values, preferred_element_type=jnp.float32)
    context = jnp.where(own_head, context, 0.0).reshape(heads, QROWS, wide[1])
    context = jnp.sum(context, axis=0).astype(jnp.bfloat16)
    half = wide[1] // 2
    columns = pl.ds(pl.multiple_of(core * half, 128), half)
    attended = jnp.dot(
        context[:, :half], wo_ref[:, columns], preferred_element_type=jnp.float32
    ) + jnp.dot(context[:, half:], wo_far_ref[...], preferred_element_type=jnp.float32)
    total = jnp.where(core == 0, mine[:, :half], mine[:, half:]) + attended
    slot = lax.broadcasted_iota(jnp.int32, total.shape, 0)
    total = jnp.where(slot < counts_ref[ids_ref[1]], total, 0.0)
    out_ref[...] = total[:slot_count].astype(jnp.bfloat16)


def on_device(
    tiles,
    counts,
    slide_of,
    rates,
    tile_gain,
    gate_weight,
    up_weight,
    embed_proj,
    slide_gain,
    slide_wq,
    slide_wk,
    slide_wv,
    slide_wo,
):
    slot_count, length, width = tiles.shape
    hidden_cols = gate_weight.shape[1]
    n_grp, n_dev, n_sub = (lax.axis_size(a) for a in ("grp", "dev", "sub"))
    ny = 2
    nz = n_dev // ny
    heads = slide_wq.shape[1] * n_sub // HD
    group, me, core = (lax.axis_index(a) for a in ("grp", "dev", "sub"))
    ids = jnp.stack([group, me, core]).astype(jnp.int32)

    to_pair = [(g, g ^ 1) for g in range(n_grp)]
    to_sibling = [(s, s ^ 1) for s in range(n_sub)]
    along_z = [(d, (d + ny) % n_dev) for d in range(n_dev)]
    along_y = [(d, d ^ 1) for d in range(n_dev)]

    half_cols = hidden_cols // 2
    base = (group % 2) * half_cols
    own_blocks = []
    for cols in CHUNKS:
        own_blocks.append(
            jnp.concatenate(
                [
                    lax.dynamic_slice_in_dim(w, base, cols, 1)
                    for w in (gate_weight, up_weight)
                ],
                axis=1,
            )
        )
        base = base + cols
    gain_row = tile_gain[None, :]
    first = norm_tiles(ids, tiles, gain_row, False)
    pair_first = [lax.ppermute(rows, "grp", to_pair) for rows in first]
    chunks = []
    for block in own_blocks:
        blocks = []
        for step in range(nz):
            if step:
                block = lax.ppermute(block, "dev", along_z)
            blocks += [block, lax.ppermute(block, "dev", along_y)]
        chunks.append(blocks)
    second = norm_tiles(ids, tiles, gain_row, True)
    pair_first = [after(pair_first[0], chunks[0][n_dev // 2]), after(pair_first[1], chunks[1][-1])]
    pair_second = [lax.ppermute(rows, "sub", to_sibling) for rows in pair_first]

    wq_far = lax.ppermute(slide_wq, "sub", to_sibling)
    wk_far = lax.ppermute(slide_wk, "sub", to_sibling)
    wv_far = lax.ppermute(slide_wv, "sub", to_sibling)
    out_cols = slide_wo.shape[1] // n_sub
    wo_far = lax.ppermute(
        lax.dynamic_slice_in_dim(slide_wo, (1 - core) * out_cols, out_cols, 1), "sub", to_sibling
    )

    smem = pl.BlockSpec(memory_space=pltpu.SMEM)
    vmem = pl.BlockSpec(memory_space=pltpu.VMEM)
    many = pl.pallas_call(
        functools.partial(multiplicity_kernel, n_dev, slot_count, heads),
        in_specs=[smem] * 4,
        out_specs=vmem,
        out_shape=jax.ShapeDtypeStruct((heads * QROWS, n_dev * slot_count), jnp.float32),
    )(ids, counts, slide_of, rates)

    large, small = chunks
    own_large = mlp(ids, large, [*first, *second], ny)
    pair_large = [mlp(ids, large, [p, q], ny) for p, q in zip(pair_first, pair_second)]
    rest = mlp(ids, small, [*first, *second, *pair_first, *pair_second], ny)
    own, pair = pl.pallas_call(
        functools.partial(order_kernel, slot_count),
        in_specs=[smem] + [vmem] * 4,
        out_specs=(vmem, vmem),
        out_shape=(
            jax.ShapeDtypeStruct((slot_count, half_cols), jnp.bfloat16),
            jax.ShapeDtypeStruct((slot_count, half_cols), jnp.bfloat16),
        ),
    )(ids, own_large, *pair_large, rest)
    theirs = lax.ppermute(pair, "grp", to_pair)

    n_rows, out_width = slot_count, embed_proj.shape[1]
    packed = (n_dev * n_sub, 2 * n_rows, out_width // 2)
    tile_embed, terms = pl.pallas_call(
        embed_kernel,
        in_specs=[smem, smem, vmem, vmem, vmem],
        out_specs=(vmem, vmem),
        out_shape=(
            jax.ShapeDtypeStruct((slot_count, hidden_cols), jnp.bfloat16),
            jax.ShapeDtypeStruct(packed, jnp.float32),
        ),
        compiler_params=pltpu.CompilerParams(vmem_limit_bytes=SMALL_VMEM),
    )(ids, counts, own, theirs, embed_proj)
    terms = lax.all_to_all(terms, ("dev", "sub"), split_axis=0, concat_axis=0, tiled=True)

    slide_out = pl.pallas_call(
        functools.partial(slide_kernel, n_dev, slot_count, heads),
        in_specs=[smem, smem] + [vmem] * 11,
        out_specs=vmem,
        out_shape=jax.ShapeDtypeStruct((slot_count, out_cols), jnp.bfloat16),
        scratch_shapes=[pltpu.VMEM((n_dev * slot_count, out_width), jnp.float32)],
        compiler_params=pltpu.CompilerParams(vmem_limit_bytes=SMALL_VMEM),
    )(
        ids,
        counts,
        terms,
        many,
        slide_gain[None, :],
        slide_wq,
        wq_far,
        slide_wk,
        wk_far,
        slide_wv,
        wv_far,
        slide_wo,
        wo_far,
    )
    return (tile_embed, slide_out)


def solution(mesh):
    placed = (
        P(("grp", "dev"), None, None),
        P("grp"),
        P("grp"),
        P(),
        P(),
        P("dev", "sub"),
        P("dev", "sub"),
        P("sub", None),
        P(),
        P(None, "sub"),
        P(None, "sub"),
        P(None, "sub"),
        P("sub", None),
    )
    return jax.shard_map(
        on_device,
        mesh=mesh,
        in_specs=placed,
        out_specs=(P(("grp", "dev"), "sub"), P(("grp", "dev"), "sub")),
        check_vma=False,
    )
```

time: 154 us -> 127 us (0.82)
  local copies, waits for them, and re-layouts: 29.6 us -> 8.17 us
  starting transfers between devices: 38.9 us -> 24.5 us
  Pallas kernels: 27.7 us -> 41.2 us
  waiting for transfers between devices: 54.9 us -> 51.1 us
    ppermute x17 -> x4, waiting for transfers between devices: 34 us -> 1.07 us  [the longest x2 1.07 us: on_device(): pair_first = [lax.ppermute(rows, 'grp', to_pair) for rows in first]]
    unnamed x120 -> x56, local copies, waits for them, and re-layouts: 26.9 us -> 6.71 us
    ppermute x17 -> x4, starting transfers between devices: 22.8 us -> 3.48 us  [the longest x2 2.97 us: on_device(): pair_first = [lax.ppermute(rows, 'grp', to_pair) for rows in first]]
    ppermute x6, waiting for transfers between devices: 13.1 us -> 25.2 us  [on_device(): block = lax.ppermute(block, 'dev', along_z)]
    ppermute x8, waiting for transfers between devices: 5.65 us -> 15.4 us  [on_device(): blocks += [block, lax.ppermute(block, 'dev', along_y)]]
    pallas_call x3 -> x7, Pallas kernels: 19 us -> 26.4 us  [the longest x4 25 us: mlp(): pl.pallas_call(functools.partial(mlp_kernel, n_dev, ny, n_tiles, length),...]
    all_to_all x0 -> x1, waiting for transfers between devices: none -> 6.99 us  [on_device(): lax.all_to_all(terms, ('dev', 'sub'), split_axis=0, concat_axis=0, tiled=...]
    all_to_all x0 -> x1, starting transfers between devices: none -> 5.59 us  [on_device(): lax.all_to_all(terms, ('dev', 'sub'), split_axis=0, concat_axis=0, tiled=...]
  transfers between devices with their start and end apart: 36 -> 24, of which waited for: 12 -> 12; matrix products, arithmetic and copies ran while one was open for 1% -> 0% of each run, Pallas kernels for 15% -> 26%
where the time goes in v2:
time: 127 us
  waiting for transfers between devices  51.1 us (40%)
  Pallas kernels  41.2 us (32%)
  starting transfers between devices  24.5 us (19%)
  local copies, waits for them, and re-layouts  8.17 us (6%)
    ppermute x6, waiting for transfers between devices, on_device(): block = lax.ppermute(block, 'dev', along_z)  25.2 us
    pallas_call x4, Pallas kernels, mlp(): pl.pallas_call(functools.partial(mlp_kernel, n_dev, ny, n_tiles, length),...  25 us
    ppermute x8, waiting for transfers between devices, on_device(): blocks += [block, lax.ppermute(block, 'dev', along_y)]  15.4 us
    ppermute x8, starting transfers between devices, on_device(): blocks += [block, lax.ppermute(block, 'dev', along_y)]  9.27 us
    pallas_call x2, Pallas kernels, norm_tiles(): pl.pallas_call(norm_kernel, grid_spec=pltpu.PrefetchScalarGridSpec(num_sc...  8.29 us
    all_to_all x1, waiting for transfers between devices, on_device(): lax.all_to_all(terms, ('dev', 'sub'), split_axis=0, concat_axis=0, tiled=...  6.99 us
    unnamed x56, local copies, waits for them, and re-layouts  6.71 us
    all_to_all x1, starting transfers between devices, on_device(): lax.all_to_all(terms, ('dev', 'sub'), split_axis=0, concat_axis=0, tiled=...  5.59 us
  transfers between devices with their start and end apart: 24, of which 12 were waited for; matrix products, arithmetic and copies ran while one was open for 0% of the time, Pallas kernels for 26%

profile of v2, /device:TPU:0, one launch (start us, length us, event | category | flops | bytes accessed | tf_op | source)
XLA Modules:
  0.0 126.6 jit_solution(10742565942298752515)
XLA Ops:
  2.6 4.2 %shard_map.140 = (bf16[256,1536]{1,0:T(8,128)(2,1)}, bf16[256,1536]{1,0:T(8,128)(2,1)}) custom-call(s32[3]{0:T(128)} %pad_add_fusion.ids_ref, bf16[4,256,1536]{2,1,0:T(8,128)(2,1)} %tiles_ref.3, f32[1,1536]{1,0:T(1,128)} %broadcast_in_dim.6.gain_ref), custom_call_target="tpu_custom_call" | custom-call | flops 6291456 | bytes 3145728 | tf_op jit(solution)/shard_map/pallas_call | solution.py:45
  6.7 2.9 %collective-permute-start.7 = (bf16[256,1536]{1,0:T(8,128)(2,1)}, bf16[256,1536]{1,0:T(8,128)(2,1)S(1)}, u32[]{:S(2)}, u32[]{:S(2)}) collective-permute-start(bf16[256,1536]{1,0:T(8,128)(2,1)} %get-tuple-element.10.refs_8_), channel_id=1, source_target_pairs={{0,16},{16,0},{1,17},{17,1},{2,18},{18,2},{3,19},{19,3},{4,20},{20... | collective-permute-start | bytes 2359304 | tf_op jit(solution)/shard_map/ppermute | solution.py:350
  9.8 2.1 %collective-permute-start.1 = (bf16[192,768]{1,0:T(8,128)(2,1)S(1)}, bf16[192,768]{1,0:T(8,128)(2,1)}, u32[]{:S(2)}, u32[]{:S(2)}) collective-permute-start(bf16[192,768]{1,0:T(8,128)(2,1)S(1)} %pad_maximum_fusion.refs_0_), channel_id=1, source_target_pairs={{0,4},{2,6},{4,8},{6,10},{8,12},{10,14},{12,0},{14,2},{1,5},{3,7},... | collective-permute-start | bytes 884744 | tf_op jit(solution)/shard_map/ppermute | solution.py:356
  12.0 1.6 %collective-permute-start.10 = (bf16[192,256]{1,0:T(8,128)(2,1)S(1)}, bf16[192,256]{1,0:T(8,128)(2,1)S(1)}, u32[]{:S(2)}, u32[]{:S(2)}) collective-permute-start(bf16[192,256]{1,0:T(8,128)(2,1)S(1)} %pad_maximum_fusion.1.refs_0_), channel_id=1, source_target_pairs={{0,4},{2,6},{4,8},{6,10},{8,12},{10,14},{12,0},{14,2},{1,5},{3,7},... | collective-permute-start | bytes 294920 | tf_op jit(solution)/shard_map/ppermute | solution.py:356
  13.6 7.9 %collective-permute-done.1.refs_2_ = bf16[192,768]{1,0:T(8,128)(2,1)} collective-permute-done((bf16[192,768]{1,0:T(8,128)(2,1)S(1)}, bf16[192,768]{1,0:T(8,128)(2,1)}, u32[]{:S(2)}, u32[]{:S(2)}) %collective-permute-start.1) | collective-permute-done | bytes 294944 | tf_op jit(solution)/shard_map/ppermute | solution.py:356
  22.9 9.3 %collective-permute-done.11.refs_4_ = bf16[192,256]{1,0:T(8,128)(2,1)S(1)} collective-permute-done((bf16[192,256]{1,0:T(8,128)(2,1)S(1)}, bf16[192,256]{1,0:T(8,128)(2,1)S(1)}, u32[]{:S(2)}, u32[]{:S(2)}) %collective-permute-start.11) | collective-permute-done | bytes 98336 | tf_op jit(solution)/shard_map/ppermute | solution.py:356
  32.2 6.4 %collective-permute-done.12.refs_6_ = bf16[192,256]{1,0:T(8,128)(2,1)S(1)} collective-permute-done((bf16[192,256]{1,0:T(8,128)(2,1)S(1)}, bf16[192,256]{1,0:T(8,128)(2,1)S(1)}, u32[]{:S(2)}, u32[]{:S(2)}) %collective-permute-start.12) | collective-permute-done | bytes 98336 | tf_op jit(solution)/shard_map/ppermute | solution.py:356
  40.6 2.6 %collective-permute-done.13.after_ref.refs_7_ = bf16[192,256]{1,0:T(8,128)(2,1)S(1)} collective-permute-done((bf16[192,256]{1,0:T(8,128)(2,1)S(1)}, bf16[192,256]{1,0:T(8,128)(2,1)S(1)}, u32[]{:S(2)}, u32[]{:S(2)}) %collective-permute-start.13) | collective-permute-done | bytes 98336 | tf_op jit(solution)/shard_map/ppermute | solution.py:357
  46.6 1.8 %collective-permute-start.2 = (bf16[192,768]{1,0:T(8,128)(2,1)}, bf16[192,768]{1,0:T(8,128)(2,1)}, u32[]{:S(2)}, u32[]{:S(2)}) collective-permute-start(bf16[192,768]{1,0:T(8,128)(2,1)} %collective-permute-done.1.refs_2_), channel_id=1, source_target_pairs={{0,2},{2,0},{4,6},{6,4},{8,10},{10,8},{12,14},{14,12},{1,3},{3,1},... | collective-permute-start | bytes 884744 | tf_op jit(solution)/shard_map/ppermute | solution.py:357
  50.6 4.1 %shard_map.141 = (bf16[256,1536]{1,0:T(8,128)(2,1)}, bf16[256,1536]{1,0:T(8,128)(2,1)}) custom-call(s32[3]{0:T(128)} %pad_add_fusion.ids_ref, bf16[4,256,1536]{2,1,0:T(8,128)(2,1)} %tiles_ref.3, f32[1,1536]{1,0:T(1,128)} %broadcast_in_dim.6.gain_ref), custom_call_target="tpu_custom_call" | custom-call | flops 6291456 | bytes 3145728 | tf_op jit(solution)/shard_map/pallas_call | solution.py:45
  54.7 2.1 %collective-permute-done.2.refs_3_ = bf16[192,768]{1,0:T(8,128)(2,1)} collective-permute-done((bf16[192,768]{1,0:T(8,128)(2,1)}, bf16[192,768]{1,0:T(8,128)(2,1)}, u32[]{:S(2)}, u32[]{:S(2)}) %collective-permute-start.2) | collective-permute-done | bytes 294944 | tf_op jit(solution)/shard_map/ppermute | solution.py:357
  56.8 1.8 %collective-permute-start.15 = (bf16[192,256]{1,0:T(8,128)(2,1)S(1)}, bf16[192,256]{1,0:T(8,128)(2,1)S(1)}, u32[]{:S(2)}, u32[]{:S(2)}) collective-permute-start(bf16[192,256]{1,0:T(8,128)(2,1)S(1)} %pad_maximum_fusion.1.refs_0_), channel_id=1, source_target_pairs={{0,2},{2,0},{4,6},{6,4},{8,10},{10,8},{12,14},{14,12},{1,3},{3,1},... | collective-permute-start | bytes 294920 | tf_op jit(solution)/shard_map/ppermute | solution.py:357
  58.6 4.5 %collective-permute-done.4.refs_5_ = bf16[192,768]{1,0:T(8,128)(2,1)} collective-permute-done((bf16[192,768]{1,0:T(8,128)(2,1)}, bf16[192,768]{1,0:T(8,128)(2,1)}, u32[]{:S(2)}, u32[]{:S(2)}) %collective-permute-start.4) | collective-permute-done | bytes 294944 | tf_op jit(solution)/shard_map/ppermute | solution.py:357
  63.1 6.2 %collective-permute-done.6.refs_7_ = bf16[192,768]{1,0:T(8,128)(2,1)S(1)} collective-permute-done((bf16[192,768]{1,0:T(8,128)(2,1)}, bf16[192,768]{1,0:T(8,128)(2,1)S(1)}, u32[]{:S(2)}, u32[]{:S(2)}) %collective-permute-start.6) | collective-permute-done | bytes 294944 | tf_op jit(solution)/shard_map/ppermute | solution.py:357
  70.0 7.3 %shard_map.142.own_ref = f32[4,384]{1,0:T(4,128)} custom-call(s32[3]{0:T(128)} %pad_add_fusion.ids_ref, bf16[192,768]{1,0:T(8,128)(2,1)} %copy-done.17, bf16[192,768]{1,0:T(8,128)(2,1)} %collective-permute-done.refs_1_, bf16[192,768]{1,0:T(8,128)(2,1)} %collective-permute-done.1.refs_2_, bf16[192,768]{1,0:T(8,128)(2,1)} %collective-permute-done.2.refs_3_, ...), custom_call_target="tpu_custom_call" | custom-call | flops 2415919104 | bytes 5505024 | tf_op jit(solution)/shard_map/pallas_call | solution.py:135
  78.2 4.8 %shard_map.146.odd_ref = f32[2,384]{1,0:T(2,128)} custom-call(s32[3]{0:T(128)} %pad_add_fusion.ids_ref, bf16[192,768]{1,0:T(8,128)(2,1)} %copy-done.17, bf16[192,768]{1,0:T(8,128)(2,1)} %collective-permute-done.refs_1_, bf16[192,768]{1,0:T(8,128)(2,1)} %collective-permute-done.1.refs_2_, bf16[192,768]{1,0:T(8,128)(2,1)} %collective-permute-done.2.refs_3_, ...), custom_call_target="tpu_custom_call" | custom-call | flops 1207959552 | bytes 3932160 | tf_op jit(solution)/shard_map/pallas_call | solution.py:135
  83.1 1.8 %collective-permute-start.16 = (bf16[192,256]{1,0:T(8,128)(2,1)S(1)}, bf16[192,256]{1,0:T(8,128)(2,1)S(1)}, u32[]{:S(2)}, u32[]{:S(2)}) collective-permute-start(bf16[192,256]{1,0:T(8,128)(2,1)S(1)} %collective-permute-done.10.refs_2_), channel_id=1, source_target_pairs={{0,2},{2,0},{4,6},{6,4},{8,10},{10,8},{12,14},{14,12},{1,3},{3,1},... | collective-permute-start | bytes 294920 | tf_op jit(solution)/shard_map/ppermute | solution.py:357
  85.9 4.8 %shard_map.144.even_ref = f32[2,384]{1,0:T(2,128)} custom-call(s32[3]{0:T(128)} %pad_add_fusion.ids_ref, bf16[192,768]{1,0:T(8,128)(2,1)} %copy-done.17, bf16[192,768]{1,0:T(8,128)(2,1)} %collective-permute-done.refs_1_, bf16[192,768]{1,0:T(8,128)(2,1)} %collective-permute-done.1.refs_2_, bf16[192,768]{1,0:T(8,128)(2,1)} %collective-permute-done.2.refs_3_, ...), custom_call_target="tpu_custom_call" | custom-call | flops 1207959552 | bytes 3932160 | tf_op jit(solution)/shard_map/pallas_call | solution.py:135
  92.1 8.1 %shard_map.147.rest_ref = f32[8,128]{1,0:T(8,128)} custom-call(s32[3]{0:T(128)} %pad_add_fusion.ids_ref, bf16[192,256]{1,0:T(8,128)(2,1)} %copy-done.15, bf16[192,256]{1,0:T(8,128)(2,1)} %copy-done.23, bf16[192,256]{1,0:T(8,128)(2,1)} %copy-done.20, bf16[192,256]{1,0:T(8,128)(2,1)} %copy-done.24, bf16[192,256]{1,0:T(8,128)(2,1)} %copy-done.21, ...), custom_call_target="tpu_custom_call" | custom-call | flops 1610612736 | bytes 7077888 | tf_op jit(solution)/shard_map/pallas_call | solution.py:135
  103.0 2.3 %collective-permute-done.18.pair_ref = bf16[4,512]{1,0:T(4,128)(2,1)S(1)} collective-permute-done((bf16[4,512]{1,0:T(4,128)(2,1)}, bf16[4,512]{1,0:T(4,128)(2,1)S(1)}, u32[]{:S(2)}, u32[]{:S(2)}) %collective-permute-start.18) | collective-permute-done | bytes 4128 | tf_op jit(solution)/shard_map/ppermute | solution.py:393
  106.0 1.6 %shard_map.149 = (bf16[4,1024]{1,0:T(4,128)(2,1)}, f32[16,8,384]{2,1,0:T(8,128)}) custom-call(s32[3]{0:T(128)S(1)} %copy-done.5, s32[8]{0:T(128)S(1)} %copy-done.7, bf16[4,512]{1,0:T(4,128)(2,1)S(1)} %copy-done.9, bf16[4,512]{1,0:T(4,128)(2,1)S(1)} %collective-permute-done.18.pair_ref, bf16[1024,768]{1,0:T(8,128)(2,1)S(1)} %copy-done), custom_call_target="tpu_custom_call" | custom-call | tf_op jit(solution)/shard_map/pallas_call | solution.py:397
  107.6 5.6 %all-to-all-start = ((f32[16,8,384]{2,1,0:T(8,128)}), f32[16,8,384]{2,1,0:T(8,128)S(1)}, u32[]{:S(2)}, u32[]{:S(2)}) async-start(f32[16,8,384]{2,1,0:T(8,128)} %get-tuple-element.17), calls=%async_computation | async-start | bytes 393216 | tf_op jit(solution)/shard_map/all_to_all | solution.py:407
  115.2 7.0 %all-to-all-done.refs_0_ = f32[16,8,384]{2,1,0:T(8,128)S(1)} async-done(((f32[16,8,384]{2,1,0:T(8,128)}), f32[16,8,384]{2,1,0:T(8,128)S(1)}, u32[]{:S(2)}, u32[]{:S(2)}) %all-to-all-start) | async-done | bytes 196640 | tf_op jit(solution)/shard_map/all_to_all | solution.py:407
  123.0 3.6 %shard_map.151 = bf16[4,384]{1,0:T(4,128)(2,1)} custom-call(s32[3]{0:T(128)S(1)} %copy-done.6, s32[8]{0:T(128)S(1)} %copy-done.8, f32[16,8,384]{2,1,0:T(8,128)S(1)} %all-to-all-done.refs_0_, f32[96,32]{1,0:T(8,128)S(1)} %copy-done.4, f32[1,768]{1,0:T(1,128)S(1)} %broadcast_in_dim.7.refs_2_, bf16[768,384]{1,0:T(8,128)(2,1)S(1)} %copy-done.2, ...), custom_call_target="tpu_custom_call" | custom-call | tf_op jit(solution)/shard_map/pallas_call | solution.py:409
  (100 shorter events, 21.1 us)
Async XLA Ops:
  6.7 38.5 %collective-permute-start.7 = (bf16[256,1536]{1,0:T(8,128)(2,1)}, bf16[256,1536]{1,0:T(8,128)(2,1)S(1)}, u32[]{:S(2)}, u32[]{:S(2)}) collective-permute-start(bf16[256,1536]{1,0:T(8,128)(2,1)} %get-tuple-element.10.refs_8_), channel_id=1, source_target_pairs={{0,16},{16,0},{1,17},{17,1},{2,18},{18,2},{3,19},{19,3},{4,20},{20... | collective-permute-start | bytes 2359304 | tf_op jit(solution)/shard_map/ppermute | solution.py:350
  9.7 34.6 %collective-permute-start.9 = (bf16[256,1536]{1,0:T(8,128)(2,1)}, bf16[256,1536]{1,0:T(8,128)(2,1)S(1)}, u32[]{:S(2)}, u32[]{:S(2)}) collective-permute-start(bf16[256,1536]{1,0:T(8,128)(2,1)} %get-tuple-element.11.refs_9_), channel_id=1, source_target_pairs={{0,16},{16,0},{1,17},{17,1},{2,18},{18,2},{3,19},{19,3},{4,20},{20... | collective-permute-start | bytes 2359304 | tf_op jit(solution)/shard_map/ppermute | solution.py:350
  9.8 11.8 %collective-permute-start.1 = (bf16[192,768]{1,0:T(8,128)(2,1)S(1)}, bf16[192,768]{1,0:T(8,128)(2,1)}, u32[]{:S(2)}, u32[]{:S(2)}) collective-permute-start(bf16[192,768]{1,0:T(8,128)(2,1)S(1)} %pad_maximum_fusion.refs_0_), channel_id=1, source_target_pairs={{0,4},{2,6},{4,8},{6,10},{8,12},{10,14},{12,0},{14,2},{1,5},{3,7},... | collective-permute-start | bytes 884744 | tf_op jit(solution)/shard_map/ppermute | solution.py:356
  12.0 10.5 %collective-permute-start.10 = (bf16[192,256]{1,0:T(8,128)(2,1)S(1)}, bf16[192,256]{1,0:T(8,128)(2,1)S(1)}, u32[]{:S(2)}, u32[]{:S(2)}) collective-permute-start(bf16[192,256]{1,0:T(8,128)(2,1)S(1)} %pad_maximum_fusion.1.refs_0_), channel_id=1, source_target_pairs={{0,4},{2,6},{4,8},{6,10},{8,12},{10,14},{12,0},{14,2},{1,5},{3,7},... | collective-permute-start | bytes 294920 | tf_op jit(solution)/shard_map/ppermute | solution.py:356
  21.6 19.1 %collective-permute-start.3 = (bf16[192,768]{1,0:T(8,128)(2,1)}, bf16[192,768]{1,0:T(8,128)(2,1)S(1)}, u32[]{:S(2)}, u32[]{:S(2)}) collective-permute-start(bf16[192,768]{1,0:T(8,128)(2,1)} %collective-permute-done.1.refs_2_), channel_id=1, source_target_pairs={{0,4},{2,6},{4,8},{6,10},{8,12},{10,14},{12,0},{14,2},{1,5},{3,7},... | collective-permute-start | bytes 884744 | tf_op jit(solution)/shard_map/ppermute | solution.py:356
  22.5 9.7 %collective-permute-start.11 = (bf16[192,256]{1,0:T(8,128)(2,1)S(1)}, bf16[192,256]{1,0:T(8,128)(2,1)S(1)}, u32[]{:S(2)}, u32[]{:S(2)}) collective-permute-start(bf16[192,256]{1,0:T(8,128)(2,1)S(1)} %collective-permute-done.10.refs_2_), channel_id=1, source_target_pairs={{0,4},{2,6},{4,8},{6,10},{8,12},{10,14},{12,0},{14,2},{1,5},{3,7},... | collective-permute-start | bytes 294920 | tf_op jit(solution)/shard_map/ppermute | solution.py:356
  32.2 6.4 %collective-permute-start.12 = (bf16[192,256]{1,0:T(8,128)(2,1)S(1)}, bf16[192,256]{1,0:T(8,128)(2,1)S(1)}, u32[]{:S(2)}, u32[]{:S(2)}) collective-permute-start(bf16[192,256]{1,0:T(8,128)(2,1)S(1)} %collective-permute-done.11.refs_4_), channel_id=1, source_target_pairs={{0,4},{2,6},{4,8},{6,10},{8,12},{10,14},{12,0},{14,2},{1,5},{3,7},... | collective-permute-start | bytes 294920 | tf_op jit(solution)/shard_map/ppermute | solution.py:356
  38.6 4.6 %collective-permute-start.13 = (bf16[192,256]{1,0:T(8,128)(2,1)S(1)}, bf16[192,256]{1,0:T(8,128)(2,1)S(1)}, u32[]{:S(2)}, u32[]{:S(2)}) collective-permute-start(bf16[192,256]{1,0:T(8,128)(2,1)S(1)} %collective-permute-done.12.refs_6_), channel_id=1, source_target_pairs={{0,2},{2,0},{4,6},{6,4},{8,10},{10,8},{12,14},{14,12},{1,3},{3,1},... | collective-permute-start | bytes 294920 | tf_op jit(solution)/shard_map/ppermute | solution.py:357
  39.9 8.5 %collective-permute-start = (bf16[192,768]{1,0:T(8,128)(2,1)S(1)}, bf16[192,768]{1,0:T(8,128)(2,1)}, u32[]{:S(2)}, u32[]{:S(2)}) collective-permute-start(bf16[192,768]{1,0:T(8,128)(2,1)S(1)} %pad_maximum_fusion.refs_0_), channel_id=1, source_target_pairs={{0,2},{2,0},{4,6},{6,4},{8,10},{10,8},{12,14},{14,12},{1,3},{3,1},... | collective-permute-start | bytes 884744 | tf_op jit(solution)/shard_map/ppermute | solution.py:357
  40.6 8.6 %collective-permute-start.5 = (bf16[192,768]{1,0:T(8,128)(2,1)S(1)}, bf16[192,768]{1,0:T(8,128)(2,1)}, u32[]{:S(2)}, u32[]{:S(2)}) collective-permute-start(bf16[192,768]{1,0:T(8,128)(2,1)S(1)} %collective-permute-done.3.refs_4_.after_ref), channel_id=1, source_target_pairs={{0,4},{2,6},{4,8},{6,10},{8,12},{10,14},{12,0},{14,2},{1,5},{3,7},... | collective-permute-start | bytes 884744 | tf_op jit(solution)/shard_map/ppermute | solution.py:356
  45.2 32.1 %collective-permute-start.14 = (bf16[256,1536]{1,0:T(8,128)(2,1)}, bf16[256,1536]{1,0:T(8,128)(2,1)S(1)}, u32[]{:S(2)}, u32[]{:S(2)}) collective-permute-start(bf16[256,1536]{1,0:T(8,128)(2,1)} %shard_map.145.refs_8_.refs_13_), channel_id=1, source_target_pairs={{0,1},{1,0},{2,3},{3,2},{4,5},{5,4},{6,7},{7,6},{8,9},{9,8},{10,11... | collective-permute-start | bytes 2359304 | tf_op jit(solution)/shard_map/ppermute | solution.py:361
  46.1 38.8 %collective-permute-start.8 = (bf16[256,1536]{1,0:T(8,128)(2,1)}, bf16[256,1536]{1,0:T(8,128)(2,1)S(1)}, u32[]{:S(2)}, u32[]{:S(2)}) collective-permute-start(bf16[256,1536]{1,0:T(8,128)(2,1)} %shard_map.143.refs_8_.refs_12_), channel_id=1, source_target_pairs={{0,1},{1,0},{2,3},{3,2},{4,5},{5,4},{6,7},{7,6},{8,9},{9,8},{10,11... | collective-permute-start | bytes 2359304 | tf_op jit(solution)/shard_map/ppermute | solution.py:361
  46.6 10.2 %collective-permute-start.2 = (bf16[192,768]{1,0:T(8,128)(2,1)}, bf16[192,768]{1,0:T(8,128)(2,1)}, u32[]{:S(2)}, u32[]{:S(2)}) collective-permute-start(bf16[192,768]{1,0:T(8,128)(2,1)} %collective-permute-done.1.refs_2_), channel_id=1, source_target_pairs={{0,2},{2,0},{4,6},{6,4},{8,10},{10,8},{12,14},{14,12},{1,3},{3,1},... | collective-permute-start | bytes 884744 | tf_op jit(solution)/shard_map/ppermute | solution.py:357
  48.4 14.7 %collective-permute-start.4 = (bf16[192,768]{1,0:T(8,128)(2,1)}, bf16[192,768]{1,0:T(8,128)(2,1)}, u32[]{:S(2)}, u32[]{:S(2)}) collective-permute-start(bf16[192,768]{1,0:T(8,128)(2,1)} %copy-done.16), channel_id=1, source_target_pairs={{0,2},{2,0},{4,6},{6,4},{8,10},{10,8},{12,14},{14,12},{1,3},{3,1},... | collective-permute-start | bytes 884744 | tf_op jit(solution)/shard_map/ppermute | solution.py:357
  49.3 20.1 %collective-permute-start.6 = (bf16[192,768]{1,0:T(8,128)(2,1)}, bf16[192,768]{1,0:T(8,128)(2,1)S(1)}, u32[]{:S(2)}, u32[]{:S(2)}) collective-permute-start(bf16[192,768]{1,0:T(8,128)(2,1)} %collective-permute-done.5.refs_6_), channel_id=1, source_target_pairs={{0,2},{2,0},{4,6},{6,4},{8,10},{10,8},{12,14},{14,12},{1,3},{3,1},... | collective-permute-start | bytes 884744 | tf_op jit(solution)/shard_map/ppermute | solution.py:357
  56.8 26.3 %collective-permute-start.15 = (bf16[192,256]{1,0:T(8,128)(2,1)S(1)}, bf16[192,256]{1,0:T(8,128)(2,1)S(1)}, u32[]{:S(2)}, u32[]{:S(2)}) collective-permute-start(bf16[192,256]{1,0:T(8,128)(2,1)S(1)} %pad_maximum_fusion.1.refs_0_), channel_id=1, source_target_pairs={{0,2},{2,0},{4,6},{6,4},{8,10},{10,8},{12,14},{14,12},{1,3},{3,1},... | collective-permute-start | bytes 294920 | tf_op jit(solution)/shard_map/ppermute | solution.py:357
  63.1 52.1 %collective-permute-start.19 = (bf16[768,384]{1,0:T(8,128)(2,1)S(1)}, bf16[768,384]{1,0:T(8,128)(2,1)}, u32[]{:S(2)}, u32[]{:S(2)}) collective-permute-start(bf16[768,384]{1,0:T(8,128)(2,1)S(1)} %copy-done.2), channel_id=1, source_target_pairs={{0,1},{1,0},{2,3},{3,2},{4,5},{5,4},{6,7},{7,6},{8,9},{9,8},{10,11... | collective-permute-start | bytes 1769480 | tf_op jit(solution)/shard_map/ppermute | solution.py:363
  69.3 45.9 %collective-permute-start.20 = (bf16[768,384]{1,0:T(8,128)(2,1)S(1)}, bf16[768,384]{1,0:T(8,128)(2,1)}, u32[]{:S(2)}, u32[]{:S(2)}) collective-permute-start(bf16[768,384]{1,0:T(8,128)(2,1)S(1)} %copy-done.3), channel_id=1, source_target_pairs={{0,1},{1,0},{2,3},{3,2},{4,5},{5,4},{6,7},{7,6},{8,9},{9,8},{10,11... | collective-permute-start | bytes 1769480 | tf_op jit(solution)/shard_map/ppermute | solution.py:364
  77.3 37.9 %collective-permute-start.21 = (bf16[768,384]{1,0:T(8,128)(2,1)}, bf16[768,384]{1,0:T(8,128)(2,1)}, u32[]{:S(2)}, u32[]{:S(2)}) collective-permute-start(bf16[768,384]{1,0:T(8,128)(2,1)} %refs_7_.1), channel_id=1, source_target_pairs={{0,1},{1,0},{2,3},{3,2},{4,5},{5,4},{6,7},{7,6},{8,9},{9,8},{10,11... | collective-permute-start | bytes 1769480 | tf_op jit(solution)/shard_map/ppermute | solution.py:365
  83.1 7.7 %collective-permute-start.16 = (bf16[192,256]{1,0:T(8,128)(2,1)S(1)}, bf16[192,256]{1,0:T(8,128)(2,1)S(1)}, u32[]{:S(2)}, u32[]{:S(2)}) collective-permute-start(bf16[192,256]{1,0:T(8,128)(2,1)S(1)} %collective-permute-done.10.refs_2_), channel_id=1, source_target_pairs={{0,2},{2,0},{4,6},{6,4},{8,10},{10,8},{12,14},{14,12},{1,3},{3,1},... | collective-permute-start | bytes 294920 | tf_op jit(solution)/shard_map/ppermute | solution.py:357
  84.9 5.8 %collective-permute-start.17 = (bf16[192,256]{1,0:T(8,128)(2,1)S(1)}, bf16[192,256]{1,0:T(8,128)(2,1)S(1)}, u32[]{:S(2)}, u32[]{:S(2)}) collective-permute-start(bf16[192,256]{1,0:T(8,128)(2,1)S(1)} %collective-permute-done.11.refs_4_), channel_id=1, source_target_pairs={{0,2},{2,0},{4,6},{6,4},{8,10},{10,8},{12,14},{14,12},{1,3},{3,1},... | collective-permute-start | bytes 294920 | tf_op jit(solution)/shard_map/ppermute | solution.py:357
  101.5 3.8 %collective-permute-start.18 = (bf16[4,512]{1,0:T(4,128)(2,1)}, bf16[4,512]{1,0:T(4,128)(2,1)S(1)}, u32[]{:S(2)}, u32[]{:S(2)}) collective-permute-start(bf16[4,512]{1,0:T(4,128)(2,1)} %get-tuple-element.15), channel_id=1, source_target_pairs={{0,16},{16,0},{1,17},{17,1},{2,18},{18,2},{3,19},{19,3},{4,20},{20... | collective-permute-start | bytes 12296 | tf_op jit(solution)/shard_map/ppermute | solution.py:393
  107.6 14.6 %all-to-all-start = ((f32[16,8,384]{2,1,0:T(8,128)}), f32[16,8,384]{2,1,0:T(8,128)S(1)}, u32[]{:S(2)}, u32[]{:S(2)}) async-start(f32[16,8,384]{2,1,0:T(8,128)} %get-tuple-element.17), calls=%async_computation | async-start | bytes 393216 | tf_op jit(solution)/shard_map/all_to_all | solution.py:407
  113.3 1.9 %collective-permute-start.22 = (bf16[384,384]{1,0:T(8,128)(2,1)S(1)}, bf16[384,384]{1,0:T(8,128)(2,1)S(1)}, u32[]{:S(2)}, u32[]{:S(2)}) collective-permute-start(bf16[384,384]{1,0:T(8,128)(2,1)S(1)} %constant_dynamic-slice_fusion), channel_id=1, source_target_pairs={{0,1},{1,0},{2,3},{3,2},{4,5},{5,4},{6,7},{7,6},{8,9},{9,8},{10,11... | collective-permute-start | bytes 884744 | tf_op jit(solution)/shard_map/ppermute | solution.py:367
  (28 other events, 573.2 us)

commit v3 on v2

v3 whole, which is shorter than its diff:
```python
import functools
import math

import jax
import jax.numpy as jnp
from jax import lax
from jax.experimental import pallas as pl
from jax.experimental.pallas import tpu as pltpu
from jax.sharding import PartitionSpec as P

HD = 64
EPSILON = 1e-06
FLOOR = -1e30
CHUNKS = (256, 256)
QROWS = 8
NORM_ROWS = 16
LANES = 128
BLOCK_TILES = 4
VMEM_LIMIT = 28 * 1024 * 1024
SMALL_VMEM = 16 * 1024 * 1024
GATE_VMEM = 1024 * 1024


def normed(rows_in, gains):
    average = jnp.mean(rows_in, axis=-1, keepdims=True)
    centred = rows_in - average
    variance = jnp.mean(centred * centred, axis=-1, keepdims=True)
    return (centred * lax.rsqrt(variance + EPSILON) * gains).astype(jnp.bfloat16)


def norm_kernel(flip, tiles_ref, gain_ref, *refs):
    out_refs, (rows, sems) = refs[:-2], refs[-2:]
    core = lax.axis_index("sub")
    half = len(out_refs)
    first = (1 - core if flip else core) * half
    copies = [
        pltpu.make_async_copy(tiles_ref.at[first + i], rows.at[i], sems.at[i]) for i in range(half)
    ]
    for copy in copies:
        copy.start()
    gain = gain_ref[...].reshape(1, -1)
    for i, out_ref in enumerate(out_refs):
        copies[i].wait()

        def some_rows(j, carry):
            here = pl.ds(pl.multiple_of(j * NORM_ROWS, NORM_ROWS), NORM_ROWS)
            out_ref[here, :] = normed(rows[i, here, :].astype(jnp.float32), gain)
            return carry

        lax.fori_loop(0, out_ref.shape[0] // NORM_ROWS, some_rows, 0, unroll=2)


def norm_tiles(tiles, gain, flip):
    slot_count, length, width = tiles.shape
    half = slot_count // 2
    vmem = pl.BlockSpec(memory_space=pltpu.VMEM)
    return pl.pallas_call(
        functools.partial(norm_kernel, flip),
        in_specs=[pl.BlockSpec(memory_space=pl.ANY), vmem],
        out_specs=[vmem] * half,
        out_shape=[jax.ShapeDtypeStruct((length, width), jnp.bfloat16)] * half,
        scratch_shapes=[
            pltpu.VMEM((half, length, width), jnp.bfloat16),
            pltpu.SemaphoreType.DMA((half,)),
        ],
        compiler_params=pltpu.CompilerParams(vmem_limit_bytes=SMALL_VMEM),
        cost_estimate=pl.CostEstimate(
            flops=8 * half * length * width,
            bytes_accessed=4 * half * length * width,
            transcendentals=half * length,
        ),
    )(tiles, gain)


def gate_kernel(*refs):
    del refs


def after(value, *others):
    any_spec = pl.BlockSpec(memory_space=pl.ANY)
    return pl.pallas_call(
        gate_kernel,
        in_specs=[any_spec] * (1 + len(others)),
        out_specs=any_spec,
        out_shape=jax.ShapeDtypeStruct(value.shape, value.dtype),
        input_output_aliases={0: 0},
        compiler_params=pltpu.CompilerParams(vmem_limit_bytes=GATE_VMEM),
    )(value, *others)


class Mlp:
    def __init__(self, blocks, tile_refs, weights, rows, weight_sems, row_sems, ny):
        n_dev = len(blocks)
        self.length = tile_refs[0].shape[0]
        self.n_tiles = len(tile_refs)
        self.weights, self.rows = weights, rows
        me = lax.axis_index("dev")
        nz = n_dev // ny
        my_z = me // ny
        my_y = me - my_z * ny
        depth = blocks[0].shape[0]
        self.row_copies = [
            pltpu.make_async_copy(
                ref, rows.at[pl.ds(i * self.length, self.length)], row_sems.at[i]
            )
            for i, ref in enumerate(tile_refs)
        ]
        self.weight_copies = []
        for k in range(n_dev):
            step, flip = k // ny, k % ny
            z = my_z - step
            z = jnp.where(z < 0, z + nz, z)
            y = 1 - my_y if flip else my_y
            start = pl.multiple_of((z * ny + y) * depth, depth)
            self.weight_copies.append(
                pltpu.make_async_copy(blocks[k], weights.at[pl.ds(start, depth)], weight_sems.at[k])
            )

    def start(self):
        for copy in self.weight_copies + self.row_copies:
            copy.start()

    def run(self, out_ref):
        cols = self.weights.shape[1] // 2
        length = self.length
        for copy in self.weight_copies:
            copy.wait()
        for first in range(0, self.n_tiles, BLOCK_TILES):
            last = min(first + BLOCK_TILES, self.n_tiles)
            for i in range(first, last):
                self.row_copies[i].wait()
            both = jnp.dot(
                self.rows[first * length : last * length, :],
                self.weights[...],
                preferred_element_type=jnp.float32,
            )
            gate, up_part = both[:, :cols], both[:, cols:]
            silu = gate * (0.5 * jnp.tanh(0.5 * gate) + 0.5)
            gated = (silu * up_part).astype(jnp.bfloat16).astype(jnp.float32)
            for i in range(first, last):
                here = slice((i - first) * length, (i - first + 1) * length)
                out_ref[i : i + 1, :] = jnp.sum(gated[here], axis=0, keepdims=True) * (1.0 / length)


def mlp_scratch(n_dev, blocks, tiles):
    depth, both_cols = blocks[0].shape
    length, width = tiles[0].shape
    return [
        pltpu.VMEM((width, both_cols), jnp.bfloat16),
        pltpu.VMEM((len(tiles) * length, width), jnp.bfloat16),
        pltpu.SemaphoreType.DMA((n_dev,)),
        pltpu.SemaphoreType.DMA((len(tiles),)),
    ]


def mlp_cost(blocks, n_tiles, tiles):
    both_cols = blocks[0].shape[1]
    length, width = tiles[0].shape
    return pl.CostEstimate(
        flops=2 * n_tiles * length * width * both_cols,
        bytes_accessed=2 * (n_tiles * length * width + width * both_cols),
        transcendentals=n_tiles * length * both_cols // 2,
    )


def mlp_kernel(n_dev, ny, n_tiles, after_ref, *refs):
    del after_ref
    out_ref, *scratch = refs[n_dev + n_tiles :]
    part = Mlp(refs[:n_dev], refs[n_dev : n_dev + n_tiles], *scratch, ny)
    part.start()
    part.run(out_ref)


def mlp(after_this, blocks, tiles, ny):
    n_dev, n_tiles = len(blocks), len(tiles)
    any_spec = pl.BlockSpec(memory_space=pl.ANY)
    return pl.pallas_call(
        functools.partial(mlp_kernel, n_dev, ny, n_tiles),
        in_specs=[any_spec] * (1 + n_dev + n_tiles),
        out_specs=pl.BlockSpec(memory_space=pltpu.VMEM),
        out_shape=jax.ShapeDtypeStruct((n_tiles, blocks[0].shape[1] // 2), jnp.float32),
        scratch_shapes=mlp_scratch(n_dev, blocks, tiles),
        compiler_params=pltpu.CompilerParams(vmem_limit_bytes=VMEM_LIMIT),
        cost_estimate=mlp_cost(blocks, n_tiles, tiles),
    )(after_this, *blocks, *tiles)


def last_mlp_kernel(n_dev, n_grp, n_sub, ny, slot_count, own_ref, even_ref, *refs):
    n_tiles = 2 * slot_count
    half = slot_count // 2
    blocks, tile_refs = refs[: 2 * n_dev], refs[2 * n_dev : 2 * n_dev + n_tiles]
    out_ref, weights0, rows0, wsem0, rsem0, weights1, rows1, wsem1, rsem1, odd, rest = refs[
        2 * n_dev + n_tiles :
    ]
    late = [tile_refs[slot_count + 1], tile_refs[slot_count + half + 1]]
    part1 = Mlp(blocks[n_dev:], tile_refs, weights1, rows1, wsem1, rsem1, ny)
    part0 = Mlp(blocks[:n_dev], late, weights0, rows0, wsem0, rsem0, ny)
    part1.start()
    part0.start()
    part1.run(rest)
    part0.run(odd)

    group, core = lax.axis_index("grp"), lax.axis_index("sub")
    low = core == 0

    def packed(mine, others):
        rows = jnp.concatenate(
            [jnp.where(low, mine, others), jnp.where(low, others, mine)], axis=0
        )
        return jnp.concatenate(
            [rows[:, k : k + LANES] for k in range(0, rows.shape[1], LANES)], axis=0
        ).astype(jnp.bfloat16)

    own = jnp.concatenate([own_ref[...], rest[:slot_count, :]], axis=1)
    own = packed(own[:half], own[half:])
    sides = []
    for side in range(2):
        first = jnp.concatenate([ref[side : side + 1, :] for ref in (even_ref, odd)], axis=0)
        start = slot_count + side * half
        sides.append(jnp.concatenate([first, rest[start : start + half, :]], axis=1))
    pair = packed(*sides)
    for g in range(n_grp):
        rows = jnp.where(group == g, own.astype(jnp.float32), pair.astype(jnp.float32))
        for s in range(n_sub):
            out_ref[g * n_sub + s] = rows.astype(jnp.bfloat16)


def last_mlp(own, even, chunks, tiles, slot_count, n_grp, n_sub, ny):
    n_dev = len(chunks[0])
    half = slot_count // 2
    cols = sum(blocks[0].shape[1] // 2 for blocks in chunks)
    late = [tiles[slot_count + 1], tiles[slot_count + half + 1]]
    any_spec = pl.BlockSpec(memory_space=pl.ANY)
    vmem = pl.BlockSpec(memory_space=pltpu.VMEM)
    return pl.pallas_call(
        functools.partial(last_mlp_kernel, n_dev, n_grp, n_sub, ny, slot_count),
        in_specs=[vmem, vmem] + [any_spec] * (2 * n_dev + len(tiles)),
        out_specs=vmem,
        out_shape=jax.ShapeDtypeStruct(
            (n_grp * n_sub, slot_count * cols // LANES, LANES), jnp.bfloat16
        ),
        scratch_shapes=[
            *mlp_scratch(n_dev, chunks[0], late),
            *mlp_scratch(n_dev, chunks[1], tiles),
            pltpu.VMEM((len(late), chunks[0][0].shape[1] // 2), jnp.float32),
            pltpu.VMEM((len(tiles), chunks[1][0].shape[1] // 2), jnp.float32),
        ],
        compiler_params=pltpu.CompilerParams(vmem_limit_bytes=VMEM_LIMIT),
        cost_estimate=mlp_cost(chunks[1], len(tiles) + 2, tiles),
    )(own, even, *chunks[0], *chunks[1], *tiles)


def small_mod(value, rate):
    return jnp.where(
        rate == 1,
        0,
        jnp.where(rate == 2, value & 1, jnp.where(rate == 3, lax.rem(value, 3), value & 3)),
    )


def multiplicity_kernel(n_dev, slot_count, heads, counts_ref, slide_ref, rates_ref, out_ref):
    me, core = lax.axis_index("dev"), lax.axis_index("sub")
    shape = out_ref.shape
    row = lax.broadcasted_iota(jnp.int32, shape, 0)
    col = lax.broadcasted_iota(jnp.int32, shape, 1)
    head = row // QROWS + core * (heads // 2)
    head = jnp.where(head >= heads, head - heads, head)
    query = row % QROWS
    device, slot = col // slot_count, col % slot_count
    rate = jnp.full(shape, 1, jnp.int32)
    for h in range(heads):
        rate = jnp.where(head == h, rates_ref[h], rate)
    my_slide = slide_ref[me]
    first = me
    count = jnp.zeros(shape, jnp.int32)
    slide = jnp.zeros(shape, jnp.int32)
    for k in reversed(range(n_dev)):
        first = jnp.where(slide_ref[k] == my_slide, k, first)
        count = jnp.where(device == k, counts_ref[k], count)
        slide = jnp.where(device == k, slide_ref[k], slide)
    offset = small_mod(head, rate)
    query_position = (me - first) * slot_count + query
    key_position = (device - first) * slot_count + slot
    valid = slot < count
    near = jnp.where((device == me) & valid, 1.0, 0.0)
    far = jnp.where(
        (slide == my_slide)
        & valid
        & (small_mod(query_position, rate) == offset)
        & (small_mod(key_position, rate) == offset),
        1.0,
        0.0,
    )
    out_ref[...] = near + far


def embed_kernel(
    n_sub, counts_ref, parts_ref, gain_ref, near_ref, far_ref, embed_ref, mixed_ref, sent_ref
):
    slot_count, half = embed_ref.shape
    n_blocks = half // 2 // LANES
    group, core = lax.axis_index("grp"), lax.axis_index("sub")
    count = counts_ref[lax.axis_index("dev")]
    base = group // 2 * 2
    halves = []
    for s in range(n_sub):
        pieces = []
        for x in range(2):
            part = parts_ref[(base + x) * n_sub + s].astype(jnp.float32)
            pieces += [part[k * slot_count : (k + 1) * slot_count] for k in range(n_blocks)]
        rows = jnp.concatenate(pieces, axis=1)
        slot = lax.broadcasted_iota(jnp.int32, rows.shape, 0)
        halves.append(jnp.where(slot < count, rows, 0.0))
    low = core == 0
    near = jnp.where(low, halves[0], halves[1]).astype(jnp.bfloat16)
    far = jnp.where(low, halves[1], halves[0]).astype(jnp.bfloat16)
    embed_ref[...] = near
    mixed = jnp.dot(near, near_ref[...], preferred_element_type=jnp.float32) + jnp.dot(
        far, far_ref[...], preferred_element_type=jnp.float32
    )
    mixed_ref[...] = jnp.concatenate([mixed, mixed], axis=0)
    hidden = normed(mixed, gain_ref[...].reshape(1, -1)).astype(jnp.float32)
    width = sent_ref.shape[2]
    pieces = [hidden[:, k : k + width] for k in range(0, hidden.shape[1], width)]
    pieces += [jnp.zeros_like(pieces[0])] * (sent_ref.shape[1] // slot_count - len(pieces))
    sent = jnp.concatenate(pieces, axis=0).astype(jnp.bfloat16)
    for k in range(sent_ref.shape[0]):
        sent_ref[k] = sent


def project(rows, near_ref, far_ref):
    return jnp.concatenate(
        [
            jnp.dot(rows, near_ref[...], preferred_element_type=jnp.float32),
            jnp.dot(rows, far_ref[...], preferred_element_type=jnp.float32),
        ],
        axis=1,
    )


def heads_of(shape):
    return (
        lax.broadcasted_iota(jnp.int32, shape, 0) // QROWS
        == lax.broadcasted_iota(jnp.int32, shape, 1) // HD
    )


def query_kernel(heads, mixed_ref, gain_ref, wq_ref, wq_far_ref, out_ref):
    hidden = normed(mixed_ref[...], gain_ref[...].reshape(1, -1))
    query = project(hidden, wq_ref, wq_far_ref)
    spread = jnp.concatenate([query] * heads, axis=0)
    out_ref[...] = jnp.where(heads_of(spread.shape), spread, 0.0).astype(jnp.bfloat16)


def slide_kernel(
    heads,
    counts_ref,
    sent_ref,
    mixed_ref,
    query_ref,
    many_ref,
    wk_ref,
    wk_far_ref,
    wv_ref,
    wv_far_ref,
    wo_ref,
    wo_far_ref,
    out_ref,
    rows,
):
    slot_count, half = out_ref.shape
    core = lax.axis_index("sub")
    count = counts_ref[lax.axis_index("dev")]
    width = sent_ref.shape[2]
    for k in range(sent_ref.shape[0]):
        sent = sent_ref[k].astype(jnp.float32)
        rows[k * slot_count : (k + 1) * slot_count, :] = jnp.concatenate(
            [
                sent[j * slot_count : (j + 1) * slot_count]
                for j in range(rows.shape[1] // width)
            ],
            axis=1,
        )
    hidden = rows[...].astype(jnp.bfloat16)
    keys = project(hidden, wk_ref, wk_far_ref).astype(jnp.bfloat16)
    scores = lax.dot_general(
        query_ref[...], keys, (((1,), (1,)), ((), ())), preferred_element_type=jnp.float32
    ) * (1.0 / math.sqrt(HD))
    values = project(hidden, wv_ref, wv_far_ref).astype(jnp.bfloat16)
    many = many_ref[...]
    masked = jnp.where(many > 0.0, scores, FLOOR)
    weights = many * jnp.exp(masked - jnp.max(masked, axis=1, keepdims=True))
    weights = weights / jnp.sum(weights, axis=1, keepdims=True)
    context = jnp.dot(weights.astype(jnp.bfloat16), values, preferred_element_type=jnp.float32)
    context = jnp.where(heads_of(context.shape), context, 0.0)
    context = context.reshape(heads, QROWS, context.shape[1])
    context = jnp.sum(context, axis=0).astype(jnp.bfloat16)
    columns = pl.ds(pl.multiple_of(core * half, LANES), half)
    attended = jnp.dot(
        context[:, :half], wo_ref[:, columns], preferred_element_type=jnp.float32
    ) + jnp.dot(context[:, half:], wo_far_ref[...], preferred_element_type=jnp.float32)
    total = mixed_ref[:, columns] + attended
    slot = lax.broadcasted_iota(jnp.int32, total.shape, 0)
    total = jnp.where(slot < count, total, 0.0)
    out_ref[...] = total[:slot_count].astype(jnp.bfloat16)


def on_device(
    tiles,
    counts,
    slide_of,
    rates,
    tile_gain,
    gate_weight,
    up_weight,
    embed_proj,
    slide_gain,
    slide_wq,
    slide_wk,
    slide_wv,
    slide_wo,
):
    slot_count, length, width = tiles.shape
    hidden_cols = gate_weight.shape[1]
    n_grp, n_dev, n_sub = (lax.axis_size(a) for a in ("grp", "dev", "sub"))
    ny = 2
    nz = n_dev // ny
    heads = slide_wq.shape[1] * n_sub // HD
    group, core = lax.axis_index("grp"), lax.axis_index("sub")

    to_pair = [(g, g ^ 1) for g in range(n_grp)]
    to_sibling = [(s, s ^ 1) for s in range(n_sub)]
    along_z = [(d, (d + ny) % n_dev) for d in range(n_dev)]
    along_y = [(d, d ^ 1) for d in range(n_dev)]

    half_cols = hidden_cols // 2
    base = (group % 2) * half_cols
    own_blocks = []
    for cols in CHUNKS:
        own_blocks.append(
            jnp.concatenate(
                [
                    lax.dynamic_slice_in_dim(w, base, cols, 1)
                    for w in (gate_weight, up_weight)
                ],
                axis=1,
            )
        )
        base = base + cols
    first = norm_tiles(tiles, tile_gain, False)
    second = norm_tiles(tiles, tile_gain, True)
    pair_first = [lax.ppermute(rows, "grp", to_pair) for rows in first]

    proj_far = lax.ppermute(embed_proj, "sub", to_sibling)
    wq_far = lax.ppermute(slide_wq, "sub", to_sibling)
    wk_far = lax.ppermute(slide_wk, "sub", to_sibling)
    wv_far = lax.ppermute(slide_wv, "sub", to_sibling)
    out_cols = slide_wo.shape[1] // n_sub
    wo_far = lax.ppermute(
        lax.dynamic_slice_in_dim(slide_wo, (1 - core) * out_cols, out_cols, 1), "sub", to_sibling
    )
    smem = pl.BlockSpec(memory_space=pltpu.SMEM)
    vmem = pl.BlockSpec(memory_space=pltpu.VMEM)
    many = pl.pallas_call(
        functools.partial(multiplicity_kernel, n_dev, slot_count, heads),
        in_specs=[smem] * 3,
        out_specs=vmem,
        out_shape=jax.ShapeDtypeStruct((heads * QROWS, n_dev * slot_count), jnp.float32),
    )(counts, slide_of, rates)

    beside = {
        (1, 0): [many, first[0]],
        (1, 1): [second[0]],
        (2, 0): [proj_far],
        (2, 1): [wq_far, wk_far, pair_first[0]],
        (3, 0): [wv_far, wo_far],
    }
    chunks = [[] for _ in own_blocks]
    held = list(own_blocks)
    last = None
    for step in range(nz):
        for c, blocks in enumerate(chunks):
            if step:
                arrived = lax.ppermute(held[c], "dev", along_z)
                others = beside.get((step, c), [])
                if last is not None:
                    others = [last, *others]
                held[c] = after(arrived, blocks[-1], *others)
                last = held[c]
            blocks += [held[c], lax.ppermute(held[c], "dev", along_y)]
    pair_first[1] = after(pair_first[1], last)
    pair_second = [lax.ppermute(rows, "sub", to_sibling) for rows in pair_first]

    own = mlp(last, chunks[0], [*first, *second], ny)
    even = mlp(last, chunks[0], [pair_first[0], pair_second[0]], ny)
    every = [*first, *second, *pair_first, *pair_second]
    parts = last_mlp(own, even, chunks, every, slot_count, n_grp, n_sub, ny)
    parts = lax.all_to_all(parts, ("grp", "sub"), split_axis=0, concat_axis=0, tiled=True)

    out_width = embed_proj.shape[1]
    sent_rows = 16
    sent_cols = 2 * LANES
    small = pltpu.CompilerParams(vmem_limit_bytes=SMALL_VMEM)
    tile_embed, mixed, sent = pl.pallas_call(
        functools.partial(embed_kernel, n_sub),
        in_specs=[smem] + [vmem] * 4,
        out_specs=(vmem, vmem, vmem),
        out_shape=(
            jax.ShapeDtypeStruct((slot_count, hidden_cols), jnp.bfloat16),
            jax.ShapeDtypeStruct((QROWS, out_width), jnp.float32),
            jax.ShapeDtypeStruct((n_dev, sent_rows, sent_cols), jnp.bfloat16),
        ),
        compiler_params=small,
    )(counts, parts, slide_gain, embed_proj, proj_far)
    sent = lax.all_to_all(sent, "dev", split_axis=0, concat_axis=0, tiled=True)
    query = pl.pallas_call(
        functools.partial(query_kernel, heads),
        in_specs=[vmem] * 4,
        out_specs=vmem,
        out_shape=jax.ShapeDtypeStruct((heads * QROWS, out_width), jnp.bfloat16),
        compiler_params=small,
    )(mixed, slide_gain, slide_wq, wq_far)
    slide_out = pl.pallas_call(
        functools.partial(slide_kernel, heads),
        in_specs=[smem] + [vmem] * 10,
        out_specs=vmem,
        out_shape=jax.ShapeDtypeStruct((slot_count, out_cols), jnp.bfloat16),
        scratch_shapes=[pltpu.VMEM((n_dev * slot_count, out_width), jnp.float32)],
        compiler_params=small,
    )(counts, sent, mixed, query, many, slide_wk, wk_far, slide_wv, wv_far, slide_wo, wo_far)
    return (tile_embed, slide_out)


def solution(mesh):
    placed = (
        P(("grp", "dev"), None, None),
        P("grp"),
        P("grp"),
        P(),
        P(),
        P("dev", "sub"),
        P("dev", "sub"),
        P("sub", None),
        P(),
        P(None, "sub"),
        P(None, "sub"),
        P(None, "sub"),
        P("sub", None),
    )
    return jax.shard_map(
        on_device,
        mesh=mesh,
        in_specs=placed,
        out_specs=(P(("grp", "dev"), "sub"), P(("grp", "dev"), "sub")),
        check_vma=False,
    )
```

time: 127 us -> 123 us (0.969)
  waiting for transfers between devices: 51.1 us -> 33 us
  local copies, waits for them, and re-layouts: 8.17 us -> 18.2 us
  Pallas kernels: 41.2 us -> 34.3 us
  blocking collectives: 0 us -> 6.42 us
  starting transfers between devices: 24.5 us -> 29.2 us
    ppermute x15, waiting for transfers between devices: 43 us -> 26.3 us  [the longest x6 15.6 us: on_device(): arrived = lax.ppermute(held[c], 'dev', along_z)]
    unnamed x56 -> x88, local copies, waits for them, and re-layouts: 6.71 us -> 16.1 us
    pallas_call x11 -> x15, Pallas kernels: 39.8 us -> 32.9 us  [the longest x1 9.9 us: last_mlp(): pl.pallas_call(functools.partial(last_mlp_kernel, n_dev, n_grp, n_sub, ny...]
    all_to_all x0 -> x1, blocking collectives: none -> 6.42 us  [on_device(): lax.all_to_all(parts, ('grp', 'sub'), split_axis=0, concat_axis=0, tiled=...]
    ppermute x15, starting transfers between devices: 14.9 us -> 19.7 us  [the longest x8 9.83 us: on_device(): blocks += [held[c], lax.ppermute(held[c], 'dev', along_y)]]
    all_to_all x1, waiting for transfers between devices: 6.99 us -> 4.69 us  [on_device(): sent = lax.all_to_all(sent, 'dev', split_axis=0, concat_axis=0, tiled=True)]
    broadcast_in_dim x2 -> x0, local copies, waits for them, and re-layouts: 1.37 us -> none  [the longest x1 1.36 us: on_device(): gain_row = tile_gain[None, :]]
  transfers between devices with their start and end apart: 24 -> 24, of which waited for: 12 -> 9; matrix products, arithmetic and copies ran while one was open for 0% -> 2% of each run, Pallas kernels for 26% -> 16%
where the time goes in v3:
time: 123 us; the launch traced here: 122 us
  Pallas kernels  34.3 us (28%)
  waiting for transfers between devices  33 us (27%)
  starting transfers between devices  29.2 us (24%)
  local copies, waits for them, and re-layouts  18.2 us (15%)
  blocking collectives  6.42 us (5%)
    unnamed x88, local copies, waits for them, and re-layouts  16.1 us
    ppermute x6, waiting for transfers between devices, on_device(): arrived = lax.ppermute(held[c], 'dev', along_z)  15.6 us
    ppermute x8, waiting for transfers between devices, on_device(): blocks += [held[c], lax.ppermute(held[c], 'dev', along_y)]  10.7 us
    pallas_call x1, Pallas kernels, last_mlp(): pl.pallas_call(functools.partial(last_mlp_kernel, n_dev, n_grp, n_sub, ny...  9.9 us
    ppermute x8, starting transfers between devices, on_device(): blocks += [held[c], lax.ppermute(held[c], 'dev', along_y)]  9.83 us
    ppermute x6, starting transfers between devices, on_device(): arrived = lax.ppermute(held[c], 'dev', along_z)  9.3 us
    pallas_call x2, Pallas kernels, mlp(): pl.pallas_call(functools.partial(mlp_kernel, n_dev, ny, n_tiles), in_spec...  8.78 us
    pallas_call x2, Pallas kernels, norm_tiles(): pl.pallas_call(functools.partial(norm_kernel, flip), in_specs=[pl.BlockSp...  7.89 us
  transfers between devices with their start and end apart: 24, of which 9 were waited for; matrix products, arithmetic and copies ran while one was open for 2% of the time, Pallas kernels for 16%

profile of v3, /device:TPU:0, one launch (start us, length us, event | category | flops | bytes accessed | tf_op | source)
XLA Modules:
  0.0 122.3 jit_solution(17500004784482205260)
XLA Ops:
  2.3 2.6 %collective-permute-start.3 = (bf16[192,512]{1,0:T(8,128)(2,1)S(1)}, bf16[192,512]{1,0:T(8,128)(2,1)S(1)}, u32[]{:S(2)}, u32[]{:S(2)}) collective-permute-start(bf16[192,512]{1,0:T(8,128)(2,1)S(1)} %pad_maximum_fusion.1.refs_0_), channel_id=1, source_target_pairs={{0,2},{2,0},{4,6},{6,4},{8,10},{10,8},{12,14},{14,12},{1,3},{3,1},... | collective-permute-start | bytes 589832 | tf_op jit(solution)/shard_map/ppermute | solution.py:490
  8.6 2.0 %collective-permute-done.3.refs_1_ = bf16[192,512]{1,0:T(8,128)(2,1)S(1)} collective-permute-done((bf16[192,512]{1,0:T(8,128)(2,1)S(1)}, bf16[192,512]{1,0:T(8,128)(2,1)S(1)}, u32[]{:S(2)}, u32[]{:S(2)}) %collective-permute-start.3) | collective-permute-done | bytes 196640 | tf_op jit(solution)/shard_map/ppermute | solution.py:490
  12.1 1.9 %copy-done = bf16[4,256,1536]{2,1,0:T(8,128)(2,1)S(1)} copy-done((bf16[4,256,1536]{2,1,0:T(8,128)(2,1)S(1)}, bf16[4,256,1536]{2,1,0:T(8,128)(2,1)}, u32[]{:S(2)}) %copy-start) | copy-done | bytes 3145752
  14.0 3.5 %shard_map.143 = (bf16[256,1536]{1,0:T(8,128)(2,1)S(1)}, bf16[256,1536]{1,0:T(8,128)(2,1)S(1)}) custom-call(bf16[4,256,1536]{2,1,0:T(8,128)(2,1)S(1)} %copy-done, f32[1536]{0:T(1024)S(1)} %copy-done.39), custom_call_target="tpu_custom_call" | custom-call | flops 6291456 | bytes 3145728 | tf_op jit(solution)/shard_map/pallas_call | solution.py:57
  18.4 4.4 %shard_map.141 = (bf16[256,1536]{1,0:T(8,128)(2,1)}, bf16[256,1536]{1,0:T(8,128)(2,1)}) custom-call(bf16[4,256,1536]{2,1,0:T(8,128)(2,1)S(1)} %copy-done, f32[1536]{0:T(1024)S(1)} %copy-done.39), custom_call_target="tpu_custom_call" | custom-call | flops 6291456 | bytes 3145728 | tf_op jit(solution)/shard_map/pallas_call | solution.py:57
  22.9 2.0 %collective-permute-start.5 = (bf16[192,512]{1,0:T(8,128)(2,1)S(1)}, bf16[192,512]{1,0:T(8,128)(2,1)S(1)}, u32[]{:S(2)}, u32[]{:S(2)}) collective-permute-start(bf16[192,512]{1,0:T(8,128)(2,1)S(1)} %shard_map.144.refs_2_.refs_10_), channel_id=1, source_target_pairs={{0,2},{2,0},{4,6},{6,4},{8,10},{10,8},{12,14},{14,12},{1,3},{3,1},... | collective-permute-start | bytes 589832 | tf_op jit(solution)/shard_map/ppermute | solution.py:490
  27.7 3.1 %collective-permute-done.5.refs_1_.refs_11_ = bf16[192,512]{1,0:T(8,128)(2,1)S(1)} collective-permute-done((bf16[192,512]{1,0:T(8,128)(2,1)S(1)}, bf16[192,512]{1,0:T(8,128)(2,1)S(1)}, u32[]{:S(2)}, u32[]{:S(2)}) %collective-permute-start.5) | collective-permute-done | bytes 196640 | tf_op jit(solution)/shard_map/ppermute | solution.py:490
  31.4 1.8 %collective-permute-start.11 = (bf16[256,1536]{1,0:T(8,128)(2,1)}, bf16[256,1536]{1,0:T(8,128)(2,1)S(1)}, u32[]{:S(2)}, u32[]{:S(2)}) collective-permute-start(bf16[256,1536]{1,0:T(8,128)(2,1)} %get-tuple-element.9.refs_3_.refs_8_.refs_16_), channel_id=1, source_target_pairs={{0,16},{16,0},{1,17},{17,1},{2,18},{18,2},{3,19},{19,3},{4,20},{20... | collective-permute-start | bytes 2359304 | tf_op jit(solution)/shard_map/ppermute | solution.py:452
  36.2 6.3 %collective-permute-done.6.refs_0_ = bf16[192,512]{1,0:T(8,128)(2,1)S(1)} collective-permute-done((bf16[192,512]{1,0:T(8,128)(2,1)S(1)}, bf16[192,512]{1,0:T(8,128)(2,1)S(1)}, u32[]{:S(2)}, u32[]{:S(2)}) %collective-permute-start.6) | collective-permute-done | bytes 196640 | tf_op jit(solution)/shard_map/ppermute | solution.py:484
  50.1 2.0 %collective-permute-done.11.refs_5_.refs_8_.refs_20_ = bf16[256,1536]{1,0:T(8,128)(2,1)S(1)} collective-permute-done((bf16[256,1536]{1,0:T(8,128)(2,1)}, bf16[256,1536]{1,0:T(8,128)(2,1)S(1)}, u32[]{:S(2)}, u32[]{:S(2)}) %collective-permute-start.11) | collective-permute-done | bytes 786464 | tf_op jit(solution)/shard_map/ppermute | solution.py:452
  54.0 1.9 %collective-permute-start.14 = (bf16[192,512]{1,0:T(8,128)(2,1)S(1)}, bf16[192,512]{1,0:T(8,128)(2,1)S(1)}, u32[]{:S(2)}, u32[]{:S(2)}) collective-permute-start(bf16[192,512]{1,0:T(8,128)(2,1)S(1)} %copy-done.7), channel_id=1, source_target_pairs={{0,4},{2,6},{4,8},{6,10},{8,12},{10,14},{12,0},{14,2},{1,5},{3,7},... | collective-permute-start | bytes 589832 | tf_op jit(solution)/shard_map/ppermute | solution.py:484
  57.4 1.6 %collective-permute-start.12 = (bf16[192,512]{1,0:T(8,128)(2,1)S(1)}, bf16[192,512]{1,0:T(8,128)(2,1)S(1)}, u32[]{:S(2)}, u32[]{:S(2)}) collective-permute-start(bf16[192,512]{1,0:T(8,128)(2,1)S(1)} %shard_map.146.refs_2_.refs_12_), channel_id=1, source_target_pairs={{0,4},{2,6},{4,8},{6,10},{8,12},{10,14},{12,0},{14,2},{1,5},{3,7},... | collective-permute-start | bytes 589832 | tf_op jit(solution)/shard_map/ppermute | solution.py:484
  59.0 4.7 %collective-permute-done.14.refs_0_ = bf16[192,512]{1,0:T(8,128)(2,1)S(1)} collective-permute-done((bf16[192,512]{1,0:T(8,128)(2,1)S(1)}, bf16[192,512]{1,0:T(8,128)(2,1)S(1)}, u32[]{:S(2)}, u32[]{:S(2)}) %collective-permute-start.14) | collective-permute-done | bytes 196640 | tf_op jit(solution)/shard_map/ppermute | solution.py:484
  63.7 4.0 %collective-permute-done.12.refs_0_ = bf16[192,512]{1,0:T(8,128)(2,1)S(1)} collective-permute-done((bf16[192,512]{1,0:T(8,128)(2,1)S(1)}, bf16[192,512]{1,0:T(8,128)(2,1)S(1)}, u32[]{:S(2)}, u32[]{:S(2)}) %collective-permute-start.12) | collective-permute-done | bytes 196640 | tf_op jit(solution)/shard_map/ppermute | solution.py:484
  67.8 1.6 %collective-permute-start.18 = (bf16[192,512]{1,0:T(8,128)(2,1)S(1)}, bf16[192,512]{1,0:T(8,128)(2,1)S(1)}, u32[]{:S(2)}, u32[]{:S(2)}) collective-permute-start(bf16[192,512]{1,0:T(8,128)(2,1)S(1)} %shard_map.147.refs_2_.refs_6_), channel_id=1, source_target_pairs={{0,2},{2,0},{4,6},{6,4},{8,10},{10,8},{12,14},{14,12},{1,3},{3,1},... | collective-permute-start | bytes 589832 | tf_op jit(solution)/shard_map/ppermute | solution.py:490
  69.9 5.7 %collective-permute-done.18.refs_7_ = bf16[192,512]{1,0:T(8,128)(2,1)S(1)} collective-permute-done((bf16[192,512]{1,0:T(8,128)(2,1)S(1)}, bf16[192,512]{1,0:T(8,128)(2,1)S(1)}, u32[]{:S(2)}, u32[]{:S(2)}) %collective-permute-start.18) | collective-permute-done | bytes 196640 | tf_op jit(solution)/shard_map/ppermute | solution.py:490
  75.6 3.3 %shard_map.150.even_ref = f32[2,256]{1,0:T(2,128)S(1)} custom-call(bf16[192,512]{1,0:T(8,128)(2,1)S(1)} %shard_map.148.after_ref.refs_1_.refs_14_, bf16[192,512]{1,0:T(8,128)(2,1)S(1)} %copy-done.19, bf16[192,512]{1,0:T(8,128)(2,1)S(1)} %copy-done.23, bf16[192,512]{1,0:T(8,128)(2,1)S(1)} %copy-done.2, bf16[192,512]{1,0:T(8,128)(2,1)S(1)} %copy-done.14, ...), custom_call_target="tpu_custom_call" | custom-call | flops 805306368 | bytes 3145728 | tf_op jit(solution)/shard_map/pallas_call | solution.py:177
  79.0 5.4 %shard_map.149.own_ref = f32[4,256]{1,0:T(4,128)S(1)} custom-call(bf16[192,512]{1,0:T(8,128)(2,1)S(1)} %shard_map.148.after_ref.refs_1_.refs_14_, bf16[192,512]{1,0:T(8,128)(2,1)S(1)} %copy-done.19, bf16[192,512]{1,0:T(8,128)(2,1)S(1)} %copy-done.23, bf16[192,512]{1,0:T(8,128)(2,1)S(1)} %copy-done.2, bf16[192,512]{1,0:T(8,128)(2,1)S(1)} %copy-done.14, ...), custom_call_target="tpu_custom_call" | custom-call | flops 1610612736 | bytes 4718592 | tf_op jit(solution)/shard_map/pallas_call | solution.py:177
  84.6 9.9 %shard_map.152 = bf16[4,16,128]{2,1,0:T(8,128)(2,1)S(1)} custom-call(f32[4,256]{1,0:T(4,128)S(1)} %shard_map.149.own_ref, f32[2,256]{1,0:T(2,128)S(1)} %shard_map.150.even_ref, bf16[192,512]{1,0:T(8,128)(2,1)S(1)} %copy-done.19, bf16[192,512]{1,0:T(8,128)(2,1)S(1)} %copy-done.23, bf16[192,512]{1,0:T(8,128)(2,1)S(1)} %copy-done.2, ...), custom_call_target="tpu_custom_call" | custom-call | flops 4026531840 | bytes 9437184 | tf_op jit(solution)/shard_map/pallas_call | solution.py:235
  94.5 6.4 %all_to_all.10.parts_ref = bf16[4,16,128]{2,1,0:T(8,128)(2,1)S(1)} all-to-all(bf16[4,16,128]{2,1,0:T(8,128)(2,1)S(1)} %shard_map.152), channel_id=1, replica_groups=mesh['grp'=2,'dev'=8,'sub'=2] {'grp','sub'}, dimensions={0} | all-to-all | bytes 32768 | tf_op jit(solution)/shard_map/all_to_all | solution.py:498
  100.9 1.9 %shard_map.153 = (bf16[4,1024]{1,0:T(4,128)(2,1)}, f32[8,768]{1,0:T(8,128)S(1)}, bf16[8,16,256]{2,1,0:T(8,128)(2,1)}) custom-call(s32[8]{0:T(128)S(1)} %copy-done.41, bf16[4,16,128]{2,1,0:T(8,128)(2,1)S(1)} %all_to_all.10.parts_ref, f32[768]{0:T(1024)S(1)} %copy-done.40, bf16[1024,768]{1,0:T(8,128)(2,1)S(1)} %copy-done.8, ...), custom_call_target="tpu_custom_call" | custom-call | tf_op jit(solution)/shard_map/pallas_call | solution.py:504
  103.4 5.8 %all-to-all-start.1 = ((bf16[8,16,256]{2,1,0:T(8,128)(2,1)}), bf16[8,16,256]{2,1,0:T(8,128)(2,1)S(1)}, u32[]{:S(2)}, u32[]{:S(2)}) async-start(bf16[8,16,256]{2,1,0:T(8,128)(2,1)} %get-tuple-element.14), calls=%async_computation.1 | async-start | bytes 131072 | tf_op jit(solution)/shard_map/all_to_all | solution.py:515
  111.4 4.7 %all-to-all-done.1.sent_ref = bf16[8,16,256]{2,1,0:T(8,128)(2,1)S(1)} async-done(((bf16[8,16,256]{2,1,0:T(8,128)(2,1)}), bf16[8,16,256]{2,1,0:T(8,128)(2,1)S(1)}, u32[]{:S(2)}, u32[]{:S(2)}) %all-to-all-start.1) | async-done | bytes 65568 | tf_op jit(solution)/shard_map/all_to_all | solution.py:515
  119.3 3.0 %shard_map.155 = bf16[4,384]{1,0:T(4,128)(2,1)} custom-call(s32[8]{0:T(128)S(1)} %copy-done.41, bf16[8,16,256]{2,1,0:T(8,128)(2,1)S(1)} %copy-done.29, f32[8,768]{1,0:T(8,128)S(1)} %copy-done.38, bf16[96,768]{1,0:T(8,128)(2,1)S(1)} %shard_map.154.query_ref, f32[96,32]{1,0:T(8,128)S(1)} %copy-done.27, bf16[768,384]{1,0:T(8,128)(2,1)} %wk_ref.1, ...), custom_call_target="tpu_custom_call" | custom-call | tf_op jit(solution)/shard_map/pallas_call | solution.py:523
  (133 shorter events, 31.6 us)
Async XLA Ops:
  0.6 45.2 %collective-permute-start.8 = (bf16[1024,768]{1,0:T(8,128)(2,1)}, bf16[1024,768]{1,0:T(8,128)(2,1)S(1)}, u32[]{:S(2)}, u32[]{:S(2)}) collective-permute-start(bf16[1024,768]{1,0:T(8,128)(2,1)} %near_ref.1), channel_id=1, source_target_pairs={{0,1},{1,0},{2,3},{3,2},{4,5},{5,4},{6,7},{7,6},{8,9},{9,8},{10,11... | collective-permute-start | bytes 4718600 | tf_op jit(solution)/shard_map/ppermute | solution.py:454
  2.3 8.4 %collective-permute-start.3 = (bf16[192,512]{1,0:T(8,128)(2,1)S(1)}, bf16[192,512]{1,0:T(8,128)(2,1)S(1)}, u32[]{:S(2)}, u32[]{:S(2)}) collective-permute-start(bf16[192,512]{1,0:T(8,128)(2,1)S(1)} %pad_maximum_fusion.1.refs_0_), channel_id=1, source_target_pairs={{0,2},{2,0},{4,6},{6,4},{8,10},{10,8},{12,14},{14,12},{1,3},{3,1},... | collective-permute-start | bytes 589832 | tf_op jit(solution)/shard_map/ppermute | solution.py:490
  4.9 17.9 %collective-permute-start.2 = (bf16[192,512]{1,0:T(8,128)(2,1)S(1)}, bf16[192,512]{1,0:T(8,128)(2,1)S(1)}, u32[]{:S(2)}, u32[]{:S(2)}) collective-permute-start(bf16[192,512]{1,0:T(8,128)(2,1)S(1)} %pad_maximum_fusion.1.refs_0_), channel_id=1, source_target_pairs={{0,4},{2,6},{4,8},{6,10},{8,12},{10,14},{12,0},{14,2},{1,5},{3,7},... | collective-permute-start | bytes 589832 | tf_op jit(solution)/shard_map/ppermute | solution.py:484
  6.5 16.4 %collective-permute-start.1 = (bf16[192,512]{1,0:T(8,128)(2,1)S(1)}, bf16[192,512]{1,0:T(8,128)(2,1)S(1)}, u32[]{:S(2)}, u32[]{:S(2)}) collective-permute-start(bf16[192,512]{1,0:T(8,128)(2,1)S(1)} %pad_maximum_fusion.refs_8_), channel_id=1, source_target_pairs={{0,2},{2,0},{4,6},{6,4},{8,10},{10,8},{12,14},{14,12},{1,3},{3,1},... | collective-permute-start | bytes 589832 | tf_op jit(solution)/shard_map/ppermute | solution.py:490
  7.1 15.8 %collective-permute-start = (bf16[192,512]{1,0:T(8,128)(2,1)S(1)}, bf16[192,512]{1,0:T(8,128)(2,1)S(1)}, u32[]{:S(2)}, u32[]{:S(2)}) collective-permute-start(bf16[192,512]{1,0:T(8,128)(2,1)S(1)} %pad_maximum_fusion.refs_8_), channel_id=1, source_target_pairs={{0,4},{2,6},{4,8},{6,10},{8,12},{10,14},{12,0},{14,2},{1,5},{3,7},... | collective-permute-start | bytes 589832 | tf_op jit(solution)/shard_map/ppermute | solution.py:484
  10.6 32.6 %collective-permute-start.9 = (bf16[768,384]{1,0:T(8,128)(2,1)}, bf16[768,384]{1,0:T(8,128)(2,1)S(1)}, u32[]{:S(2)}, u32[]{:S(2)}) collective-permute-start(bf16[768,384]{1,0:T(8,128)(2,1)} %wq_ref.1), channel_id=1, source_target_pairs={{0,1},{1,0},{2,3},{3,2},{4,5},{5,4},{6,7},{7,6},{8,9},{9,8},{10,11... | collective-permute-start | bytes 1769480 | tf_op jit(solution)/shard_map/ppermute | solution.py:455
  22.9 7.8 %collective-permute-start.5 = (bf16[192,512]{1,0:T(8,128)(2,1)S(1)}, bf16[192,512]{1,0:T(8,128)(2,1)S(1)}, u32[]{:S(2)}, u32[]{:S(2)}) collective-permute-start(bf16[192,512]{1,0:T(8,128)(2,1)S(1)} %shard_map.144.refs_2_.refs_10_), channel_id=1, source_target_pairs={{0,2},{2,0},{4,6},{6,4},{8,10},{10,8},{12,14},{14,12},{1,3},{3,1},... | collective-permute-start | bytes 589832 | tf_op jit(solution)/shard_map/ppermute | solution.py:490
  24.9 8.9 %collective-permute-start.4 = (bf16[192,512]{1,0:T(8,128)(2,1)S(1)}, bf16[192,512]{1,0:T(8,128)(2,1)S(1)}, u32[]{:S(2)}, u32[]{:S(2)}) collective-permute-start(bf16[192,512]{1,0:T(8,128)(2,1)S(1)} %shard_map.144.refs_2_.refs_10_), channel_id=1, source_target_pairs={{0,4},{2,6},{4,8},{6,10},{8,12},{10,14},{12,0},{14,2},{1,5},{3,7},... | collective-permute-start | bytes 589832 | tf_op jit(solution)/shard_map/ppermute | solution.py:484
  27.2 8.4 %collective-permute-start.7 = (bf16[192,512]{1,0:T(8,128)(2,1)S(1)}, bf16[192,512]{1,0:T(8,128)(2,1)S(1)}, u32[]{:S(2)}, u32[]{:S(2)}) collective-permute-start(bf16[192,512]{1,0:T(8,128)(2,1)S(1)} %shard_map.142.refs_2_), channel_id=1, source_target_pairs={{0,2},{2,0},{4,6},{6,4},{8,10},{10,8},{12,14},{14,12},{1,3},{3,1},... | collective-permute-start | bytes 589832 | tf_op jit(solution)/shard_map/ppermute | solution.py:490
  31.4 20.7 %collective-permute-start.11 = (bf16[256,1536]{1,0:T(8,128)(2,1)}, bf16[256,1536]{1,0:T(8,128)(2,1)S(1)}, u32[]{:S(2)}, u32[]{:S(2)}) collective-permute-start(bf16[256,1536]{1,0:T(8,128)(2,1)} %get-tuple-element.9.refs_3_.refs_8_.refs_16_), channel_id=1, source_target_pairs={{0,16},{16,0},{1,17},{17,1},{2,18},{18,2},{3,19},{19,3},{4,20},{20... | collective-permute-start | bytes 2359304 | tf_op jit(solution)/shard_map/ppermute | solution.py:452
  34.5 8.1 %collective-permute-start.6 = (bf16[192,512]{1,0:T(8,128)(2,1)S(1)}, bf16[192,512]{1,0:T(8,128)(2,1)S(1)}, u32[]{:S(2)}, u32[]{:S(2)}) collective-permute-start(bf16[192,512]{1,0:T(8,128)(2,1)S(1)} %shard_map.142.refs_2_), channel_id=1, source_target_pairs={{0,4},{2,6},{4,8},{6,10},{8,12},{10,14},{12,0},{14,2},{1,5},{3,7},... | collective-permute-start | bytes 589832 | tf_op jit(solution)/shard_map/ppermute | solution.py:484
  36.2 13.3 %collective-permute-start.10 = (bf16[768,384]{1,0:T(8,128)(2,1)}, bf16[768,384]{1,0:T(8,128)(2,1)}, u32[]{:S(2)}, u32[]{:S(2)}) collective-permute-start(bf16[768,384]{1,0:T(8,128)(2,1)} %wk_ref.1), channel_id=1, source_target_pairs={{0,1},{1,0},{2,3},{3,2},{4,5},{5,4},{6,7},{7,6},{8,9},{9,8},{10,11... | collective-permute-start | bytes 1769480 | tf_op jit(solution)/shard_map/ppermute | solution.py:456
  43.3 12.7 %collective-permute-start.16 = (bf16[768,384]{1,0:T(8,128)(2,1)}, bf16[768,384]{1,0:T(8,128)(2,1)S(1)}, u32[]{:S(2)}, u32[]{:S(2)}) collective-permute-start(bf16[768,384]{1,0:T(8,128)(2,1)} %wv_ref.1), channel_id=1, source_target_pairs={{0,1},{1,0},{2,3},{3,2},{4,5},{5,4},{6,7},{7,6},{8,9},{9,8},{10,11... | collective-permute-start | bytes 1769480 | tf_op jit(solution)/shard_map/ppermute | solution.py:457
  43.3 24.5 %collective-permute-start.21 = (bf16[256,1536]{1,0:T(8,128)(2,1)}, bf16[256,1536]{1,0:T(8,128)(2,1)}, u32[]{:S(2)}, u32[]{:S(2)}) collective-permute-start(bf16[256,1536]{1,0:T(8,128)(2,1)} %get-tuple-element.11.refs_9_.refs_17_), channel_id=1, source_target_pairs={{0,16},{16,0},{1,17},{17,1},{2,18},{18,2},{3,19},{19,3},{4,20},{20... | collective-permute-start | bytes 2359304 | tf_op jit(solution)/shard_map/ppermute | solution.py:452
  45.8 7.2 %collective-permute-start.17 = (bf16[384,384]{1,0:T(8,128)(2,1)S(1)}, bf16[384,384]{1,0:T(8,128)(2,1)S(1)}, u32[]{:S(2)}, u32[]{:S(2)}) collective-permute-start(bf16[384,384]{1,0:T(8,128)(2,1)S(1)} %constant_dynamic-slice_fusion), channel_id=1, source_target_pairs={{0,1},{1,0},{2,3},{3,2},{4,5},{5,4},{6,7},{7,6},{8,9},{9,8},{10,11... | collective-permute-start | bytes 884744 | tf_op jit(solution)/shard_map/ppermute | solution.py:459
  49.6 7.9 %collective-permute-start.15 = (bf16[192,512]{1,0:T(8,128)(2,1)}, bf16[192,512]{1,0:T(8,128)(2,1)S(1)}, u32[]{:S(2)}, u32[]{:S(2)}) collective-permute-start(bf16[192,512]{1,0:T(8,128)(2,1)} %copy-done.5), channel_id=1, source_target_pairs={{0,2},{2,0},{4,6},{6,4},{8,10},{10,8},{12,14},{14,12},{1,3},{3,1},... | collective-permute-start | bytes 589832 | tf_op jit(solution)/shard_map/ppermute | solution.py:490
  52.1 17.8 %collective-permute-start.19 = (bf16[256,1536]{1,0:T(8,128)(2,1)S(1)}, bf16[256,1536]{1,0:T(8,128)(2,1)S(1)}, u32[]{:S(2)}, u32[]{:S(2)}) collective-permute-start(bf16[256,1536]{1,0:T(8,128)(2,1)S(1)} %collective-permute-done.11.refs_5_.refs_8_.refs_20_), channel_id=1, source_target_pairs={{0,1},{1,0},{2,3},{3,2},{4,5},{5,4},{6,7},{7,6},{8,9},{9,8},{10,11... | collective-permute-start | bytes 2359304 | tf_op jit(solution)/shard_map/ppermute | solution.py:492
  54.0 9.7 %collective-permute-start.14 = (bf16[192,512]{1,0:T(8,128)(2,1)S(1)}, bf16[192,512]{1,0:T(8,128)(2,1)S(1)}, u32[]{:S(2)}, u32[]{:S(2)}) collective-permute-start(bf16[192,512]{1,0:T(8,128)(2,1)S(1)} %copy-done.7), channel_id=1, source_target_pairs={{0,4},{2,6},{4,8},{6,10},{8,12},{10,14},{12,0},{14,2},{1,5},{3,7},... | collective-permute-start | bytes 589832 | tf_op jit(solution)/shard_map/ppermute | solution.py:484
  55.9 7.8 %collective-permute-start.13 = (bf16[192,512]{1,0:T(8,128)(2,1)S(1)}, bf16[192,512]{1,0:T(8,128)(2,1)S(1)}, u32[]{:S(2)}, u32[]{:S(2)}) collective-permute-start(bf16[192,512]{1,0:T(8,128)(2,1)S(1)} %shard_map.146.refs_2_.refs_12_), channel_id=1, source_target_pairs={{0,2},{2,0},{4,6},{6,4},{8,10},{10,8},{12,14},{14,12},{1,3},{3,1},... | collective-permute-start | bytes 589832 | tf_op jit(solution)/shard_map/ppermute | solution.py:490
  57.4 10.3 %collective-permute-start.12 = (bf16[192,512]{1,0:T(8,128)(2,1)S(1)}, bf16[192,512]{1,0:T(8,128)(2,1)S(1)}, u32[]{:S(2)}, u32[]{:S(2)}) collective-permute-start(bf16[192,512]{1,0:T(8,128)(2,1)S(1)} %shard_map.146.refs_2_.refs_12_), channel_id=1, source_target_pairs={{0,4},{2,6},{4,8},{6,10},{8,12},{10,14},{12,0},{14,2},{1,5},{3,7},... | collective-permute-start | bytes 589832 | tf_op jit(solution)/shard_map/ppermute | solution.py:484
  67.8 16.8 %collective-permute-start.22 = (bf16[256,1536]{1,0:T(8,128)(2,1)}, bf16[256,1536]{1,0:T(8,128)(2,1)S(1)}, u32[]{:S(2)}, u32[]{:S(2)}) collective-permute-start(bf16[256,1536]{1,0:T(8,128)(2,1)} %shard_map.151.refs_21_), channel_id=1, source_target_pairs={{0,1},{1,0},{2,3},{3,2},{4,5},{5,4},{6,7},{7,6},{8,9},{9,8},{10,11... | collective-permute-start | bytes 2359304 | tf_op jit(solution)/shard_map/ppermute | solution.py:492
  67.8 7.8 %collective-permute-start.18 = (bf16[192,512]{1,0:T(8,128)(2,1)S(1)}, bf16[192,512]{1,0:T(8,128)(2,1)S(1)}, u32[]{:S(2)}, u32[]{:S(2)}) collective-permute-start(bf16[192,512]{1,0:T(8,128)(2,1)S(1)} %shard_map.147.refs_2_.refs_6_), channel_id=1, source_target_pairs={{0,2},{2,0},{4,6},{6,4},{8,10},{10,8},{12,14},{14,12},{1,3},{3,1},... | collective-permute-start | bytes 589832 | tf_op jit(solution)/shard_map/ppermute | solution.py:490
  69.4 15.1 %collective-permute-start.20 = (bf16[192,512]{1,0:T(8,128)(2,1)S(1)}, bf16[192,512]{1,0:T(8,128)(2,1)S(1)}, u32[]{:S(2)}, u32[]{:S(2)}) collective-permute-start(bf16[192,512]{1,0:T(8,128)(2,1)S(1)} %shard_map.148.after_ref.refs_1_.refs_14_), channel_id=1, source_target_pairs={{0,2},{2,0},{4,6},{6,4},{8,10},{10,8},{12,14},{14,12},{1,3},{3,1},... | collective-permute-start | bytes 589832 | tf_op jit(solution)/shard_map/ppermute | solution.py:490
  103.4 12.7 %all-to-all-start.1 = ((bf16[8,16,256]{2,1,0:T(8,128)(2,1)}), bf16[8,16,256]{2,1,0:T(8,128)(2,1)S(1)}, u32[]{:S(2)}, u32[]{:S(2)}) async-start(bf16[8,16,256]{2,1,0:T(8,128)(2,1)} %get-tuple-element.14), calls=%async_computation.1 | async-start | bytes 131072 | tf_op jit(solution)/shard_map/all_to_all | solution.py:515
  (44 other events, 289.2 us)

commit v4 on v3

--- a/solution.py
+++ b/solution.py
@@ -15,10 +15,11 @@
 QROWS = 8
 NORM_ROWS = 16
 LANES = 128
-BLOCK_TILES = 4
-VMEM_LIMIT = 28 * 1024 * 1024
-SMALL_VMEM = 16 * 1024 * 1024
-GATE_VMEM = 1024 * 1024
+UNIT_TILES = 2
+UNIT_ROWS = 16
+MLP_VMEM = 24 * 1024 * 1024
+NORM_VMEM = 8 * 1024 * 1024
+SMALL_VMEM = 4 * 1024 * 1024
 
 
 def normed(rows_in, gains):
@@ -29,41 +30,50 @@
 
 
 def norm_kernel(flip, tiles_ref, gain_ref, *refs):
-    out_refs, (rows, sems) = refs[:-2], refs[-2:]
+    out_refs, (rows, hidden, in_sems, out_sems) = refs[:-4], refs[-4:]
     core = lax.axis_index("sub")
     half = len(out_refs)
     first = (1 - core if flip else core) * half
     copies = [
-        pltpu.make_async_copy(tiles_ref.at[first + i], rows.at[i], sems.at[i]) for i in range(half)
+        pltpu.make_async_copy(tiles_ref.at[first + i], rows.at[i], in_sems.at[i])
+        for i in range(half)
+    ]
+    stores = [
+        pltpu.make_async_copy(hidden.at[i], out_refs[i], out_sems.at[i]) for i in range(half)
     ]
     for copy in copies:
         copy.start()
     gain = gain_ref[...].reshape(1, -1)
-    for i, out_ref in enumerate(out_refs):
+    for i in range(half):
         copies[i].wait()
 
         def some_rows(j, carry):
             here = pl.ds(pl.multiple_of(j * NORM_ROWS, NORM_ROWS), NORM_ROWS)
-            out_ref[here, :] = normed(rows[i, here, :].astype(jnp.float32), gain)
+            hidden[i, here, :] = normed(rows[i, here, :].astype(jnp.float32), gain)
             return carry
 
-        lax.fori_loop(0, out_ref.shape[0] // NORM_ROWS, some_rows, 0, unroll=2)
+        lax.fori_loop(0, rows.shape[1] // NORM_ROWS, some_rows, 0, unroll=4)
+        stores[i].start()
+    for store in stores:
+        store.wait()
 
 
 def norm_tiles(tiles, gain, flip):
     slot_count, length, width = tiles.shape
     half = slot_count // 2
-    vmem = pl.BlockSpec(memory_space=pltpu.VMEM)
+    hbm = pl.BlockSpec(memory_space=pltpu.HBM)
     return pl.pallas_call(
         functools.partial(norm_kernel, flip),
-        in_specs=[pl.BlockSpec(memory_space=pl.ANY), vmem],
-        out_specs=[vmem] * half,
+        in_specs=[hbm, pl.BlockSpec(memory_space=pltpu.VMEM)],
+        out_specs=[hbm] * half,
         out_shape=[jax.ShapeDtypeStruct((length, width), jnp.bfloat16)] * half,
         scratch_shapes=[
             pltpu.VMEM((half, length, width), jnp.bfloat16),
+            pltpu.VMEM((half, length, width), jnp.bfloat16),
+            pltpu.SemaphoreType.DMA((half,)),
             pltpu.SemaphoreType.DMA((half,)),
         ],
-        compiler_params=pltpu.CompilerParams(vmem_limit_bytes=SMALL_VMEM),
+        compiler_params=pltpu.CompilerParams(vmem_limit_bytes=NORM_VMEM),
         cost_estimate=pl.CostEstimate(
             flops=8 * half * length * width,
             bytes_accessed=4 * half * length * width,
@@ -72,84 +82,77 @@
     )(tiles, gain)
 
 
-def gate_kernel(*refs):
-    del refs
-
-
 def after(value, *others):
-    any_spec = pl.BlockSpec(memory_space=pl.ANY)
-    return pl.pallas_call(
-        gate_kernel,
-        in_specs=[any_spec] * (1 + len(others)),
-        out_specs=any_spec,
-        out_shape=jax.ShapeDtypeStruct(value.shape, value.dtype),
-        input_output_aliases={0: 0},
-        compiler_params=pltpu.CompilerParams(vmem_limit_bytes=GATE_VMEM),
-    )(value, *others)
-
-
-class Mlp:
-    def __init__(self, blocks, tile_refs, weights, rows, weight_sems, row_sems, ny):
-        n_dev = len(blocks)
-        self.length = tile_refs[0].shape[0]
-        self.n_tiles = len(tile_refs)
-        self.weights, self.rows = weights, rows
-        me = lax.axis_index("dev")
-        nz = n_dev // ny
-        my_z = me // ny
-        my_y = me - my_z * ny
-        depth = blocks[0].shape[0]
-        self.row_copies = [
-            pltpu.make_async_copy(
-                ref, rows.at[pl.ds(i * self.length, self.length)], row_sems.at[i]
-            )
-            for i, ref in enumerate(tile_refs)
-        ]
-        self.weight_copies = []
-        for k in range(n_dev):
-            step, flip = k // ny, k % ny
-            z = my_z - step
-            z = jnp.where(z < 0, z + nz, z)
-            y = 1 - my_y if flip else my_y
-            start = pl.multiple_of((z * ny + y) * depth, depth)
-            self.weight_copies.append(
-                pltpu.make_async_copy(blocks[k], weights.at[pl.ds(start, depth)], weight_sems.at[k])
-            )
-
-    def start(self):
-        for copy in self.weight_copies + self.row_copies:
-            copy.start()
-
-    def run(self, out_ref):
-        cols = self.weights.shape[1] // 2
-        length = self.length
-        for copy in self.weight_copies:
-            copy.wait()
-        for first in range(0, self.n_tiles, BLOCK_TILES):
-            last = min(first + BLOCK_TILES, self.n_tiles)
-            for i in range(first, last):
-                self.row_copies[i].wait()
-            both = jnp.dot(
-                self.rows[first * length : last * length, :],
-                self.weights[...],
-                preferred_element_type=jnp.float32,
-            )
-            gate, up_part = both[:, :cols], both[:, cols:]
+    return lax.optimization_barrier((value, *others))[0]
+
+
+def block_copies(blocks, weights, sems, ny):
+    n_dev = len(blocks)
+    me = lax.axis_index("dev")
+    nz = n_dev // ny
+    my_z = me // ny
+    my_y = me - my_z * ny
+    depth = blocks[0].shape[0]
+    copies = []
+    for k in range(n_dev):
+        step, flip = k // ny, k % ny
+        z = my_z - step
+        z = jnp.where(z < 0, z + nz, z)
+        y = 1 - my_y if flip else my_y
+        start = pl.multiple_of((z * ny + y) * depth, depth)
+        copies.append(
+            pltpu.make_async_copy(blocks[k], weights.at[pl.ds(start, depth)], sems.at[k])
+        )
+    return copies
+
+
+def tile_copies(tile_refs, rows, sems):
+    length = tile_refs[0].shape[0]
+    return [
+        pltpu.make_async_copy(ref, rows.at[pl.ds(i * length, length)], sems.at[i])
+        for i, ref in enumerate(tile_refs)
+    ]
+
+
+def gated_means(both, out_ref, at, length):
+    cols = both.shape[1] // 2
+    for tile in range(both.shape[0] // length):
+        total = jnp.zeros((8, cols), jnp.float32)
+        for first in range(tile * length, (tile + 1) * length, UNIT_ROWS):
+            gate = both[first : first + UNIT_ROWS, :cols]
+            up_part = both[first : first + UNIT_ROWS, cols:]
             silu = gate * (0.5 * jnp.tanh(0.5 * gate) + 0.5)
             gated = (silu * up_part).astype(jnp.bfloat16).astype(jnp.float32)
-            for i in range(first, last):
-                here = slice((i - first) * length, (i - first + 1) * length)
-                out_ref[i : i + 1, :] = jnp.sum(gated[here], axis=0, keepdims=True) * (1.0 / length)
-
-
-def mlp_scratch(n_dev, blocks, tiles):
-    depth, both_cols = blocks[0].shape
-    length, width = tiles[0].shape
+            total = total + jnp.sum(gated.reshape(UNIT_ROWS // 8, 8, cols), axis=0)
+        out_ref[at + tile : at + tile + 1, :] = jnp.sum(total, axis=0, keepdims=True) * (
+            1.0 / length
+        )
+
+
+def run_units(units, products, length):
+    pending = None
+    for i, (waits, rows, weights, out_ref, at) in enumerate(units):
+        for copy in waits:
+            copy.wait()
+        both = products[i % 2]
+        both[...] = jnp.dot(rows[...], weights[...], preferred_element_type=jnp.float32)
+        if pending is not None:
+            gated_means(*pending, length)
+        pending = (both, out_ref, at)
+    gated_means(*pending, length)
+
+
+def mlp_scratch(n_dev, chunks, n_tiles, length):
+    depth, both_cols = chunks[0][0].shape
+    width = n_dev * depth
+    unit = (UNIT_TILES * length, both_cols)
     return [
-        pltpu.VMEM((width, both_cols), jnp.bfloat16),
-        pltpu.VMEM((len(tiles) * length, width), jnp.bfloat16),
-        pltpu.SemaphoreType.DMA((n_dev,)),
-        pltpu.SemaphoreType.DMA((len(tiles),)),
+        pltpu.VMEM((len(chunks), width, both_cols), jnp.bfloat16),
+        pltpu.VMEM((n_tiles * length, width), jnp.bfloat16),
+        pltpu.VMEM(unit, jnp.float32),
+        pltpu.VMEM(unit, jnp.float32),
+        pltpu.SemaphoreType.DMA((len(chunks), n_dev)),
+        pltpu.SemaphoreType.DMA((n_tiles,)),
     ]
 
 
@@ -163,42 +166,59 @@
     )
 
 
-def mlp_kernel(n_dev, ny, n_tiles, after_ref, *refs):
+def first_mlp_kernel(n_dev, ny, n_tiles, after_ref, *refs):
     del after_ref
-    out_ref, *scratch = refs[n_dev + n_tiles :]
-    part = Mlp(refs[:n_dev], refs[n_dev : n_dev + n_tiles], *scratch, ny)
-    part.start()
-    part.run(out_ref)
-
-
-def mlp(after_this, blocks, tiles, ny):
+    blocks, tile_refs = refs[:n_dev], refs[n_dev : n_dev + n_tiles]
+    out_ref, weights, rows, even, odd, weight_sems, row_sems = refs[n_dev + n_tiles :]
+    length = tile_refs[0].shape[0]
+    loads = block_copies(blocks, weights.at[0], weight_sems.at[0], ny)
+    row_loads = tile_copies(tile_refs, rows, row_sems)
+    for copy in loads + row_loads:
+        copy.start()
+    units = []
+    for i in range(0, n_tiles, UNIT_TILES):
+        here = slice(i * length, (i + UNIT_TILES) * length)
+        waits = row_loads[i : i + UNIT_TILES] + (loads if i == 0 else [])
+        units.append((waits, rows.at[here], weights.at[0], out_ref, i))
+    run_units(units, (even, odd), length)
+
+
+def first_mlp(after_this, blocks, tiles, ny):
     n_dev, n_tiles = len(blocks), len(tiles)
-    any_spec = pl.BlockSpec(memory_space=pl.ANY)
+    hbm = pl.BlockSpec(memory_space=pltpu.HBM)
     return pl.pallas_call(
-        functools.partial(mlp_kernel, n_dev, ny, n_tiles),
-        in_specs=[any_spec] * (1 + n_dev + n_tiles),
+        functools.partial(first_mlp_kernel, n_dev, ny, n_tiles),
+        in_specs=[hbm] * (1 + n_dev + n_tiles),
         out_specs=pl.BlockSpec(memory_space=pltpu.VMEM),
         out_shape=jax.ShapeDtypeStruct((n_tiles, blocks[0].shape[1] // 2), jnp.float32),
-        scratch_shapes=mlp_scratch(n_dev, blocks, tiles),
-        compiler_params=pltpu.CompilerParams(vmem_limit_bytes=VMEM_LIMIT),
+        scratch_shapes=mlp_scratch(n_dev, [blocks], n_tiles, tiles[0].shape[0]),
+        compiler_params=pltpu.CompilerParams(vmem_limit_bytes=MLP_VMEM),
         cost_estimate=mlp_cost(blocks, n_tiles, tiles),
     )(after_this, *blocks, *tiles)
 
 
-def last_mlp_kernel(n_dev, n_grp, n_sub, ny, slot_count, own_ref, even_ref, *refs):
+def last_mlp_kernel(n_dev, n_grp, n_sub, ny, slot_count, first_ref, *refs):
     n_tiles = 2 * slot_count
     half = slot_count // 2
     blocks, tile_refs = refs[: 2 * n_dev], refs[2 * n_dev : 2 * n_dev + n_tiles]
-    out_ref, weights0, rows0, wsem0, rsem0, weights1, rows1, wsem1, rsem1, odd, rest = refs[
+    out_ref, weights, rows, even, odd, weight_sems, row_sems, late, rest = refs[
         2 * n_dev + n_tiles :
     ]
-    late = [tile_refs[slot_count + 1], tile_refs[slot_count + half + 1]]
-    part1 = Mlp(blocks[n_dev:], tile_refs, weights1, rows1, wsem1, rsem1, ny)
-    part0 = Mlp(blocks[:n_dev], late, weights0, rows0, wsem0, rsem0, ny)
-    part1.start()
-    part0.start()
-    part1.run(rest)
-    part0.run(odd)
+    length = tile_refs[0].shape[0]
+    loads = [
+        block_copies(blocks[c * n_dev : (c + 1) * n_dev], weights.at[c], weight_sems.at[c], ny)
+        for c in range(2)
+    ]
+    row_loads = tile_copies(tile_refs, rows, row_sems)
+    for copy in loads[1] + row_loads + loads[0]:
+        copy.start()
+    units = []
+    for i in range(0, n_tiles, UNIT_TILES):
+        here = slice(i * length, (i + UNIT_TILES) * length)
+        waits = row_loads[i : i + UNIT_TILES] + (loads[1] if i == 0 else [])
+        units.append((waits, rows.at[here], weights.at[1], rest, i))
+    units.append((loads[0], units[-1][1], weights.at[0], late, 0))
+    run_units(units, (even, odd), length)
 
     group, core = lax.axis_index("grp"), lax.axis_index("sub")
     low = core == 0
@@ -209,45 +229,49 @@
         )
         return jnp.concatenate(
             [rows[:, k : k + LANES] for k in range(0, rows.shape[1], LANES)], axis=0
-        ).astype(jnp.bfloat16)
-
-    own = jnp.concatenate([own_ref[...], rest[:slot_count, :]], axis=1)
-    own = packed(own[:half], own[half:])
-    sides = []
-    for side in range(2):
-        first = jnp.concatenate([ref[side : side + 1, :] for ref in (even_ref, odd)], axis=0)
-        start = slot_count + side * half
-        sides.append(jnp.concatenate([first, rest[start : start + half, :]], axis=1))
-    pair = packed(*sides)
+        )
+
+    def features(ref, at):
+        return jnp.concatenate([ref[at : at + 1, :], rest[at : at + 1, :]], axis=1)
+
+    own = [features(first_ref, i) for i in range(slot_count)]
+    own = packed(jnp.concatenate(own[:half], axis=0), jnp.concatenate(own[half:], axis=0))
+    at = slot_count
+    early = [features(first_ref, at), features(first_ref, at + 1)]
+    at += 2
+    last = [
+        jnp.concatenate([late[i : i + 1, :], rest[at + i : at + i + 1, :]], axis=1)
+        for i in range(2)
+    ]
+    pair = packed(
+        jnp.concatenate([early[0], last[0]], axis=0), jnp.concatenate([early[1], last[1]], axis=0)
+    )
     for g in range(n_grp):
-        rows = jnp.where(group == g, own.astype(jnp.float32), pair.astype(jnp.float32))
+        chosen = jnp.where(group == g, own, pair).astype(jnp.bfloat16)
         for s in range(n_sub):
-            out_ref[g * n_sub + s] = rows.astype(jnp.bfloat16)
-
-
-def last_mlp(own, even, chunks, tiles, slot_count, n_grp, n_sub, ny):
+            out_ref[g * n_sub + s] = chosen
+
+
+def last_mlp(first_means, chunks, tiles, slot_count, n_grp, n_sub, ny):
     n_dev = len(chunks[0])
-    half = slot_count // 2
     cols = sum(blocks[0].shape[1] // 2 for blocks in chunks)
-    late = [tiles[slot_count + 1], tiles[slot_count + half + 1]]
-    any_spec = pl.BlockSpec(memory_space=pl.ANY)
+    hbm = pl.BlockSpec(memory_space=pltpu.HBM)
     vmem = pl.BlockSpec(memory_space=pltpu.VMEM)
     return pl.pallas_call(
         functools.partial(last_mlp_kernel, n_dev, n_grp, n_sub, ny, slot_count),
-        in_specs=[vmem, vmem] + [any_spec] * (2 * n_dev + len(tiles)),
+        in_specs=[vmem] + [hbm] * (2 * n_dev + len(tiles)),
         out_specs=vmem,
         out_shape=jax.ShapeDtypeStruct(
             (n_grp * n_sub, slot_count * cols // LANES, LANES), jnp.bfloat16
         ),
         scratch_shapes=[
-            *mlp_scratch(n_dev, chunks[0], late),
-            *mlp_scratch(n_dev, chunks[1], tiles),
-            pltpu.VMEM((len(late), chunks[0][0].shape[1] // 2), jnp.float32),
+            *mlp_scratch(n_dev, chunks, len(tiles), tiles[0].shape[0]),
+            pltpu.VMEM((UNIT_TILES, chunks[0][0].shape[1] // 2), jnp.float32),
             pltpu.VMEM((len(tiles), chunks[1][0].shape[1] // 2), jnp.float32),
         ],
-        compiler_params=pltpu.CompilerParams(vmem_limit_bytes=VMEM_LIMIT),
-        cost_estimate=mlp_cost(chunks[1], len(tiles) + 2, tiles),
-    )(own, even, *chunks[0], *chunks[1], *tiles)
+        compiler_params=pltpu.CompilerParams(vmem_limit_bytes=MLP_VMEM),
+        cost_estimate=mlp_cost(chunks[1], len(tiles) + UNIT_TILES, tiles),
+    )(first_means, *chunks[0], *chunks[1], *tiles)
 
 
 def small_mod(value, rate):
@@ -466,14 +490,16 @@
         in_specs=[smem] * 3,
         out_specs=vmem,
         out_shape=jax.ShapeDtypeStruct((heads * QROWS, n_dev * slot_count), jnp.float32),
+        compiler_params=pltpu.CompilerParams(vmem_limit_bytes=SMALL_VMEM),
     )(counts, slide_of, rates)
 
+    own_blocks[1] = after(own_blocks[1], first[0])
     beside = {
-        (1, 0): [many, first[0]],
         (1, 1): [second[0]],
         (2, 0): [proj_far],
-        (2, 1): [wq_far, wk_far, pair_first[0]],
-        (3, 0): [wv_far, wo_far],
+        (2, 1): [wq_far, pair_first[0]],
+        (3, 0): [wk_far, wv_far],
+        (3, 1): [wo_far, many],
     }
     chunks = [[] for _ in own_blocks]
     held = list(own_blocks)
@@ -491,10 +517,10 @@
     pair_first[1] = after(pair_first[1], last)
     pair_second = [lax.ppermute(rows, "sub", to_sibling) for rows in pair_first]
 
-    own = mlp(last, chunks[0], [*first, *second], ny)
-    even = mlp(last, chunks[0], [pair_first[0], pair_second[0]], ny)
-    every = [*first, *second, *pair_first, *pair_second]
-    parts = last_mlp(own, even, chunks, every, slot_count, n_grp, n_sub, ny)
+    pieces = [rows for piece in zip(pair_first, pair_second) for rows in piece]
+    own_tiles = [*first, *second]
+    first_means = first_mlp(last, chunks[0], own_tiles + pieces[:2], ny)
+    parts = last_mlp(first_means, chunks, own_tiles + pieces, slot_count, n_grp, n_sub, ny)
     parts = lax.all_to_all(parts, ("grp", "sub"), split_axis=0, concat_axis=0, tiled=True)
 
     out_width = embed_proj.shape[1]

time: 123 us -> 114 us (0.927)
  Pallas kernels: 34.3 us -> 28.8 us
  starting transfers between devices: 29.2 us -> 25.5 us
  waiting for transfers between devices: 33 us -> 35 us
  local copies, waits for them, and re-layouts: 18.2 us -> 16.3 us
    ppermute x2, waiting for transfers between devices: 2.02 us -> 13.9 us  [on_device(): pair_first = [lax.ppermute(rows, 'grp', to_pair) for rows in first]]
    ppermute x6, waiting for transfers between devices: 15.6 us -> 8.28 us  [on_device(): arrived = lax.ppermute(held[c], 'dev', along_z)]
    pallas_call x11 -> x3, Pallas kernels: 16.7 us -> 11.6 us  [the longest x1 6.64 us: first_mlp(): pl.pallas_call(functools.partial(first_mlp_kernel, n_dev, ny, n_tiles), i...]
    ppermute x8, waiting for transfers between devices: 10.7 us -> 7.36 us  [on_device(): blocks += [held[c], lax.ppermute(held[c], 'dev', along_y)]]
    ppermute x6, starting transfers between devices: 9.3 us -> 6.47 us  [on_device(): arrived = lax.ppermute(held[c], 'dev', along_z)]
    unnamed x88 -> x74, local copies, waits for them, and re-layouts: 16.1 us -> 15.2 us
  transfers between devices with their start and end apart: 24 -> 24, of which waited for: 9 -> 9; matrix products, arithmetic and copies ran while one was open for 2% -> 1% of each run, Pallas kernels for 16% -> 12%
where the time goes in v4:
time: 114 us; the launch traced here: 113 us
  waiting for transfers between devices  35 us (31%)
  Pallas kernels  28.8 us (25%)
  starting transfers between devices  25.5 us (22%)
  local copies, waits for them, and re-layouts  16.3 us (14%)
  blocking collectives  6.42 us (6%)
    unnamed x74, local copies, waits for them, and re-layouts  15.2 us
    ppermute x2, waiting for transfers between devices, on_device(): pair_first = [lax.ppermute(rows, 'grp', to_pair) for rows in first]  13.9 us
    pallas_call x1, Pallas kernels, last_mlp(): pl.pallas_call(functools.partial(last_mlp_kernel, n_dev, n_grp, n_sub, ny...  10.2 us
    ppermute x8, starting transfers between devices, on_device(): blocks += [held[c], lax.ppermute(held[c], 'dev', along_y)]  9.42 us
    ppermute x6, waiting for transfers between devices, on_device(): arrived = lax.ppermute(held[c], 'dev', along_z)  8.28 us
    ppermute x8, waiting for transfers between devices, on_device(): blocks += [held[c], lax.ppermute(held[c], 'dev', along_y)]  7.36 us
    pallas_call x1, Pallas kernels, first_mlp(): pl.pallas_call(functools.partial(first_mlp_kernel, n_dev, ny, n_tiles), i...  6.64 us
    ppermute x6, starting transfers between devices, on_device(): arrived = lax.ppermute(held[c], 'dev', along_z)  6.47 us
  transfers between devices with their start and end apart: 24, of which 9 were waited for; matrix products, arithmetic and copies ran while one was open for 1% of the time, Pallas kernels for 12%

profile of v4, /device:TPU:0, one launch (start us, length us, event | category | flops | bytes accessed | tf_op | source)
XLA Modules:
  0.0 113.0 jit_solution(6642761427814329901)
XLA Ops:
  2.2 2.6 %collective-permute-start.3 = (bf16[192,512]{1,0:T(8,128)(2,1)S(1)}, bf16[192,512]{1,0:T(8,128)(2,1)S(1)}, u32[]{:S(2)}, u32[]{:S(2)}) collective-permute-start(bf16[192,512]{1,0:T(8,128)(2,1)S(1)} %pad_maximum_fusion.1.refs_0_), channel_id=1, source_target_pairs={{0,2},{2,0},{4,6},{6,4},{8,10},{10,8},{12,14},{14,12},{1,3},{3,1},... | collective-permute-start | bytes 589832 | tf_op jit(solution)/shard_map/ppermute | solution.py:516
  4.9 1.6 %collective-permute-start.2 = (bf16[192,512]{1,0:T(8,128)(2,1)S(1)}, bf16[192,512]{1,0:T(8,128)(2,1)S(1)}, u32[]{:S(2)}, u32[]{:S(2)}) collective-permute-start(bf16[192,512]{1,0:T(8,128)(2,1)S(1)} %pad_maximum_fusion.1.refs_0_), channel_id=1, source_target_pairs={{0,4},{2,6},{4,8},{6,10},{8,12},{10,14},{12,0},{14,2},{1,5},{3,7},... | collective-permute-start | bytes 589832 | tf_op jit(solution)/shard_map/ppermute | solution.py:510
  6.5 1.9 %copy-done = bf16[4,256,1536]{2,1,0:T(8,128)(2,1)S(1)} copy-done((bf16[4,256,1536]{2,1,0:T(8,128)(2,1)S(1)}, bf16[4,256,1536]{2,1,0:T(8,128)(2,1)}, u32[]{:S(2)}) %copy-start) | copy-done | bytes 3145752
  8.4 2.9 %shard_map.140 = (bf16[256,1536]{1,0:T(8,128)(2,1)}, bf16[256,1536]{1,0:T(8,128)(2,1)}) custom-call(bf16[4,256,1536]{2,1,0:T(8,128)(2,1)S(1)} %copy-done, f32[1536]{0:T(1024)S(1)} %copy-done.11), custom_call_target="tpu_custom_call" | custom-call | flops 6291456 | bytes 3145728 | tf_op jit(solution)/shard_map/pallas_call | solution.py:65
  11.9 1.6 %collective-permute-start = (bf16[192,512]{1,0:T(8,128)(2,1)S(1)}, bf16[192,512]{1,0:T(8,128)(2,1)S(1)}, u32[]{:S(2)}, u32[]{:S(2)}) collective-permute-start(bf16[192,512]{1,0:T(8,128)(2,1)S(1)} %pad_maximum_fusion.refs_8_), channel_id=1, source_target_pairs={{0,4},{2,6},{4,8},{6,10},{8,12},{10,14},{12,0},{14,2},{1,5},{3,7},... | collective-permute-start | bytes 589832 | tf_op jit(solution)/shard_map/ppermute | solution.py:510
  15.1 2.1 %shard_map.141 = (bf16[256,1536]{1,0:T(8,128)(2,1)S(1)}, bf16[256,1536]{1,0:T(8,128)(2,1)S(1)}) custom-call(bf16[4,256,1536]{2,1,0:T(8,128)(2,1)S(1)} %copy-done, f32[1536]{0:T(1024)S(1)} %copy-done.11), custom_call_target="tpu_custom_call" | custom-call | flops 6291456 | bytes 3145728 | tf_op jit(solution)/shard_map/pallas_call | solution.py:65
  19.0 1.6 %collective-permute-start.6 = (bf16[192,512]{1,0:T(8,128)(2,1)S(1)}, bf16[192,512]{1,0:T(8,128)(2,1)S(1)}, u32[]{:S(2)}, u32[]{:S(2)}) collective-permute-start(bf16[192,512]{1,0:T(8,128)(2,1)S(1)} %collective-permute-done.2.refs_2_), channel_id=1, source_target_pairs={{0,4},{2,6},{4,8},{6,10},{8,12},{10,14},{12,0},{14,2},{1,5},{3,7},... | collective-permute-start | bytes 589832 | tf_op jit(solution)/shard_map/ppermute | solution.py:510
  23.3 1.6 %collective-permute-start.10 = (bf16[256,1536]{1,0:T(8,128)(2,1)}, bf16[256,1536]{1,0:T(8,128)(2,1)}, u32[]{:S(2)}, u32[]{:S(2)}) collective-permute-start(bf16[256,1536]{1,0:T(8,128)(2,1)} %get-tuple-element.17.refs_8_.refs_16_), channel_id=1, source_target_pairs={{0,16},{16,0},{1,17},{17,1},{2,18},{18,2},{3,19},{19,3},{4,20},{20... | collective-permute-start | bytes 2359304 | tf_op jit(solution)/shard_map/ppermute | solution.py:476
  24.8 3.8 %collective-permute-done.6.refs_4_ = bf16[192,512]{1,0:T(8,128)(2,1)S(1)} collective-permute-done((bf16[192,512]{1,0:T(8,128)(2,1)S(1)}, bf16[192,512]{1,0:T(8,128)(2,1)S(1)}, u32[]{:S(2)}, u32[]{:S(2)}) %collective-permute-start.6) | collective-permute-done | bytes 196640 | tf_op jit(solution)/shard_map/ppermute | solution.py:510
  31.6 1.5 %collective-permute-start.21 = (bf16[256,1536]{1,0:T(8,128)(2,1)}, bf16[256,1536]{1,0:T(8,128)(2,1)}, u32[]{:S(2)}, u32[]{:S(2)}) collective-permute-start(bf16[256,1536]{1,0:T(8,128)(2,1)} %get-tuple-element.26.refs_9_.refs_17_), channel_id=1, source_target_pairs={{0,16},{16,0},{1,17},{17,1},{2,18},{18,2},{3,19},{19,3},{4,20},{20... | collective-permute-start | bytes 2359304 | tf_op jit(solution)/shard_map/ppermute | solution.py:476
  34.0 10.1 %collective-permute-done.10.refs_12_.refs_20_ = bf16[256,1536]{1,0:T(8,128)(2,1)} collective-permute-done((bf16[256,1536]{1,0:T(8,128)(2,1)}, bf16[256,1536]{1,0:T(8,128)(2,1)}, u32[]{:S(2)}, u32[]{:S(2)}) %collective-permute-start.10) | collective-permute-done | bytes 786464 | tf_op jit(solution)/shard_map/ppermute | solution.py:476
  44.1 1.6 %collective-permute-start.12 = (bf16[192,512]{1,0:T(8,128)(2,1)}, bf16[192,512]{1,0:T(8,128)(2,1)S(1)}, u32[]{:S(2)}, u32[]{:S(2)}) collective-permute-start(bf16[192,512]{1,0:T(8,128)(2,1)} %copy-done.35), channel_id=1, source_target_pairs={{0,2},{2,0},{4,6},{6,4},{8,10},{10,8},{12,14},{14,12},{1,3},{3,1},... | collective-permute-start | bytes 589832 | tf_op jit(solution)/shard_map/ppermute | solution.py:516
  45.7 1.6 %collective-permute-start.11 = (bf16[192,512]{1,0:T(8,128)(2,1)}, bf16[192,512]{1,0:T(8,128)(2,1)S(1)}, u32[]{:S(2)}, u32[]{:S(2)}) collective-permute-start(bf16[192,512]{1,0:T(8,128)(2,1)} %copy-done.35), channel_id=1, source_target_pairs={{0,4},{2,6},{4,8},{6,10},{8,12},{10,14},{12,0},{14,2},{1,5},{3,7},... | collective-permute-start | bytes 589832 | tf_op jit(solution)/shard_map/ppermute | solution.py:510
  49.9 1.7 %collective-permute-done.12.refs_13_ = bf16[192,512]{1,0:T(8,128)(2,1)S(1)} collective-permute-done((bf16[192,512]{1,0:T(8,128)(2,1)}, bf16[192,512]{1,0:T(8,128)(2,1)S(1)}, u32[]{:S(2)}, u32[]{:S(2)}) %collective-permute-start.12) | collective-permute-done | bytes 196640 | tf_op jit(solution)/shard_map/ppermute | solution.py:516
  51.6 3.2 %collective-permute-done.11.after_ref.refs_14_ = bf16[192,512]{1,0:T(8,128)(2,1)S(1)} collective-permute-done((bf16[192,512]{1,0:T(8,128)(2,1)}, bf16[192,512]{1,0:T(8,128)(2,1)S(1)}, u32[]{:S(2)}, u32[]{:S(2)}) %collective-permute-start.11) | collective-permute-done | bytes 196640 | tf_op jit(solution)/shard_map/ppermute | solution.py:510
  54.8 3.8 %collective-permute-done.21.refs_22_ = bf16[256,1536]{1,0:T(8,128)(2,1)} collective-permute-done((bf16[256,1536]{1,0:T(8,128)(2,1)}, bf16[256,1536]{1,0:T(8,128)(2,1)}, u32[]{:S(2)}, u32[]{:S(2)}) %collective-permute-start.21) | collective-permute-done | bytes 786464 | tf_op jit(solution)/shard_map/ppermute | solution.py:476
  60.7 5.7 %collective-permute-done.18.refs_7_ = bf16[192,512]{1,0:T(8,128)(2,1)S(1)} collective-permute-done((bf16[192,512]{1,0:T(8,128)(2,1)S(1)}, bf16[192,512]{1,0:T(8,128)(2,1)S(1)}, u32[]{:S(2)}, u32[]{:S(2)}) %collective-permute-start.18) | collective-permute-done | bytes 196640 | tf_op jit(solution)/shard_map/ppermute | solution.py:516
  72.4 6.6 %shard_map.143.first_ref = f32[6,256]{1,0:T(8,128)S(1)} custom-call(bf16[192,512]{1,0:T(8,128)(2,1)S(1)} %collective-permute-done.11.after_ref.refs_14_, bf16[192,512]{1,0:T(8,128)(2,1)S(1)} %pad_maximum_fusion.1.refs_0_, bf16[192,512]{1,0:T(8,128)(2,1)S(1)} %copy-done.21, bf16[192,512]{1,0:T(8,128)(2,1)S(1)} %copy-done.23, bf16[192,512]{1,0:T(8,128)(2,1)S(1)} %copy-done.29, ...), custom_call_target="tpu_custom_call" | custom-call | flops 2415919104 | bytes 6291456 | tf_op jit(solution)/shard_map/pallas_call | solution.py:189
  79.1 10.2 %shard_map.144 = bf16[4,16,128]{2,1,0:T(8,128)(2,1)S(1)} custom-call(f32[6,256]{1,0:T(8,128)S(1)} %shard_map.143.first_ref, bf16[192,512]{1,0:T(8,128)(2,1)S(1)} %pad_maximum_fusion.1.refs_0_, bf16[192,512]{1,0:T(8,128)(2,1)S(1)} %copy-done.21, bf16[192,512]{1,0:T(8,128)(2,1)S(1)} %copy-done.23, bf16[192,512]{1,0:T(8,128)(2,1)S(1)} %copy-done.29, ...), custom_call_target="tpu_custom_call" | custom-call | flops 4026531840 | bytes 9437184 | tf_op jit(solution)/shard_map/pallas_call | solution.py:260
  89.3 6.4 %all_to_all.10.parts_ref = bf16[4,16,128]{2,1,0:T(8,128)(2,1)S(1)} all-to-all(bf16[4,16,128]{2,1,0:T(8,128)(2,1)S(1)} %shard_map.144), channel_id=1, replica_groups=mesh['grp'=2,'dev'=8,'sub'=2] {'grp','sub'}, dimensions={0} | all-to-all | bytes 32768 | tf_op jit(solution)/shard_map/all_to_all | solution.py:524
  95.7 1.9 %shard_map.145 = (bf16[4,1024]{1,0:T(4,128)(2,1)}, f32[8,768]{1,0:T(8,128)S(1)}, bf16[8,16,256]{2,1,0:T(8,128)(2,1)}) custom-call(s32[8]{0:T(128)S(1)} %copy-done.13, bf16[4,16,128]{2,1,0:T(8,128)(2,1)S(1)} %all_to_all.10.parts_ref, f32[768]{0:T(1024)S(1)} %copy-done.12, bf16[1024,768]{1,0:T(8,128)(2,1)S(1)} %copy-done.1, ...), custom_call_target="tpu_custom_call" | custom-call | tf_op jit(solution)/shard_map/pallas_call | solution.py:530
  97.6 5.5 %all-to-all-start.1 = ((bf16[8,16,256]{2,1,0:T(8,128)(2,1)}), bf16[8,16,256]{2,1,0:T(8,128)(2,1)S(1)}, u32[]{:S(2)}, u32[]{:S(2)}) async-start(bf16[8,16,256]{2,1,0:T(8,128)(2,1)} %get-tuple-element.30), calls=%async_computation.1 | async-start | bytes 131072 | tf_op jit(solution)/shard_map/all_to_all | solution.py:541
  104.6 5.4 %all-to-all-done.1.sent_ref = bf16[8,16,256]{2,1,0:T(8,128)(2,1)S(1)} async-done(((bf16[8,16,256]{2,1,0:T(8,128)(2,1)}), bf16[8,16,256]{2,1,0:T(8,128)(2,1)S(1)}, u32[]{:S(2)}, u32[]{:S(2)}) %all-to-all-start.1) | async-done | bytes 65568 | tf_op jit(solution)/shard_map/all_to_all | solution.py:541
  110.0 3.0 %shard_map.147 = bf16[4,384]{1,0:T(4,128)(2,1)} custom-call(s32[8]{0:T(128)S(1)} %copy-done.13, bf16[8,16,256]{2,1,0:T(8,128)(2,1)S(1)} %all-to-all-done.1.sent_ref, f32[8,768]{1,0:T(8,128)S(1)} %get-tuple-element.31.mixed_ref, bf16[96,768]{1,0:T(8,128)(2,1)S(1)} %shard_map.146.query_ref, f32[96,32]{1,0:T(8,128)S(1)} %copy-done.10, ...), custom_call_target="tpu_custom_call" | custom-call | tf_op jit(solution)/shard_map/pallas_call | solution.py:549
  (111 shorter events, 24.3 us)
Async XLA Ops:
  0.6 30.2 %collective-permute-start.8 = (bf16[1024,768]{1,0:T(8,128)(2,1)}, bf16[1024,768]{1,0:T(8,128)(2,1)S(1)}, u32[]{:S(2)}, u32[]{:S(2)}) collective-permute-start(bf16[1024,768]{1,0:T(8,128)(2,1)} %near_ref.1), channel_id=1, source_target_pairs={{0,1},{1,0},{2,3},{3,2},{4,5},{5,4},{6,7},{7,6},{8,9},{9,8},{10,11... | collective-permute-start | bytes 4718600 | tf_op jit(solution)/shard_map/ppermute | solution.py:478
  2.2 11.2 %collective-permute-start.3 = (bf16[192,512]{1,0:T(8,128)(2,1)S(1)}, bf16[192,512]{1,0:T(8,128)(2,1)S(1)}, u32[]{:S(2)}, u32[]{:S(2)}) collective-permute-start(bf16[192,512]{1,0:T(8,128)(2,1)S(1)} %pad_maximum_fusion.1.refs_0_), channel_id=1, source_target_pairs={{0,2},{2,0},{4,6},{6,4},{8,10},{10,8},{12,14},{14,12},{1,3},{3,1},... | collective-permute-start | bytes 589832 | tf_op jit(solution)/shard_map/ppermute | solution.py:516
  4.9 8.9 %collective-permute-start.2 = (bf16[192,512]{1,0:T(8,128)(2,1)S(1)}, bf16[192,512]{1,0:T(8,128)(2,1)S(1)}, u32[]{:S(2)}, u32[]{:S(2)}) collective-permute-start(bf16[192,512]{1,0:T(8,128)(2,1)S(1)} %pad_maximum_fusion.1.refs_0_), channel_id=1, source_target_pairs={{0,4},{2,6},{4,8},{6,10},{8,12},{10,14},{12,0},{14,2},{1,5},{3,7},... | collective-permute-start | bytes 589832 | tf_op jit(solution)/shard_map/ppermute | solution.py:510
  11.3 9.3 %collective-permute-start.1 = (bf16[192,512]{1,0:T(8,128)(2,1)S(1)}, bf16[192,512]{1,0:T(8,128)(2,1)S(1)}, u32[]{:S(2)}, u32[]{:S(2)}) collective-permute-start(bf16[192,512]{1,0:T(8,128)(2,1)S(1)} %pad_maximum_fusion.refs_8_), channel_id=1, source_target_pairs={{0,2},{2,0},{4,6},{6,4},{8,10},{10,8},{12,14},{14,12},{1,3},{3,1},... | collective-permute-start | bytes 589832 | tf_op jit(solution)/shard_map/ppermute | solution.py:516
  11.9 9.4 %collective-permute-start = (bf16[192,512]{1,0:T(8,128)(2,1)S(1)}, bf16[192,512]{1,0:T(8,128)(2,1)S(1)}, u32[]{:S(2)}, u32[]{:S(2)}) collective-permute-start(bf16[192,512]{1,0:T(8,128)(2,1)S(1)} %pad_maximum_fusion.refs_8_), channel_id=1, source_target_pairs={{0,4},{2,6},{4,8},{6,10},{8,12},{10,14},{12,0},{14,2},{1,5},{3,7},... | collective-permute-start | bytes 589832 | tf_op jit(solution)/shard_map/ppermute | solution.py:510
  13.7 8.9 %collective-permute-start.7 = (bf16[192,512]{1,0:T(8,128)(2,1)S(1)}, bf16[192,512]{1,0:T(8,128)(2,1)S(1)}, u32[]{:S(2)}, u32[]{:S(2)}) collective-permute-start(bf16[192,512]{1,0:T(8,128)(2,1)S(1)} %collective-permute-done.2.refs_2_), channel_id=1, source_target_pairs={{0,2},{2,0},{4,6},{6,4},{8,10},{10,8},{12,14},{14,12},{1,3},{3,1},... | collective-permute-start | bytes 589832 | tf_op jit(solution)/shard_map/ppermute | solution.py:516
  19.0 9.6 %collective-permute-start.6 = (bf16[192,512]{1,0:T(8,128)(2,1)S(1)}, bf16[192,512]{1,0:T(8,128)(2,1)S(1)}, u32[]{:S(2)}, u32[]{:S(2)}) collective-permute-start(bf16[192,512]{1,0:T(8,128)(2,1)S(1)} %collective-permute-done.2.refs_2_), channel_id=1, source_target_pairs={{0,4},{2,6},{4,8},{6,10},{8,12},{10,14},{12,0},{14,2},{1,5},{3,7},... | collective-permute-start | bytes 589832 | tf_op jit(solution)/shard_map/ppermute | solution.py:510
  21.2 7.4 %collective-permute-start.5 = (bf16[192,512]{1,0:T(8,128)(2,1)S(1)}, bf16[192,512]{1,0:T(8,128)(2,1)S(1)}, u32[]{:S(2)}, u32[]{:S(2)}) collective-permute-start(bf16[192,512]{1,0:T(8,128)(2,1)S(1)} %collective-permute-done.refs_10_), channel_id=1, source_target_pairs={{0,2},{2,0},{4,6},{6,4},{8,10},{10,8},{12,14},{14,12},{1,3},{3,1},... | collective-permute-start | bytes 589832 | tf_op jit(solution)/shard_map/ppermute | solution.py:516
  21.7 9.1 %collective-permute-start.4 = (bf16[192,512]{1,0:T(8,128)(2,1)S(1)}, bf16[192,512]{1,0:T(8,128)(2,1)S(1)}, u32[]{:S(2)}, u32[]{:S(2)}) collective-permute-start(bf16[192,512]{1,0:T(8,128)(2,1)S(1)} %collective-permute-done.refs_10_), channel_id=1, source_target_pairs={{0,4},{2,6},{4,8},{6,10},{8,12},{10,14},{12,0},{14,2},{1,5},{3,7},... | collective-permute-start | bytes 589832 | tf_op jit(solution)/shard_map/ppermute | solution.py:510
  23.3 20.8 %collective-permute-start.10 = (bf16[256,1536]{1,0:T(8,128)(2,1)}, bf16[256,1536]{1,0:T(8,128)(2,1)}, u32[]{:S(2)}, u32[]{:S(2)}) collective-permute-start(bf16[256,1536]{1,0:T(8,128)(2,1)} %get-tuple-element.17.refs_8_.refs_16_), channel_id=1, source_target_pairs={{0,16},{16,0},{1,17},{17,1},{2,18},{18,2},{3,19},{19,3},{4,20},{20... | collective-permute-start | bytes 2359304 | tf_op jit(solution)/shard_map/ppermute | solution.py:476
  28.6 4.4 %collective-permute-start.9 = (bf16[768,384]{1,0:T(8,128)(2,1)S(1)}, bf16[768,384]{1,0:T(8,128)(2,1)}, u32[]{:S(2)}, u32[]{:S(2)}) collective-permute-start(bf16[768,384]{1,0:T(8,128)(2,1)S(1)} %copy-done.3), channel_id=1, source_target_pairs={{0,1},{1,0},{2,3},{3,2},{4,5},{5,4},{6,7},{7,6},{8,9},{9,8},{10,11... | collective-permute-start | bytes 1769480 | tf_op jit(solution)/shard_map/ppermute | solution.py:479
  29.4 4.4 %collective-permute-start.15 = (bf16[768,384]{1,0:T(8,128)(2,1)S(1)}, bf16[768,384]{1,0:T(8,128)(2,1)}, u32[]{:S(2)}, u32[]{:S(2)}) collective-permute-start(bf16[768,384]{1,0:T(8,128)(2,1)S(1)} %copy-done.4), channel_id=1, source_target_pairs={{0,1},{1,0},{2,3},{3,2},{4,5},{5,4},{6,7},{7,6},{8,9},{9,8},{10,11... | collective-permute-start | bytes 1769480 | tf_op jit(solution)/shard_map/ppermute | solution.py:480
  30.9 3.0 %collective-permute-start.16 = (bf16[768,384]{1,0:T(8,128)(2,1)}, bf16[768,384]{1,0:T(8,128)(2,1)}, u32[]{:S(2)}, u32[]{:S(2)}) collective-permute-start(bf16[768,384]{1,0:T(8,128)(2,1)} %wv_ref.1), channel_id=1, source_target_pairs={{0,1},{1,0},{2,3},{3,2},{4,5},{5,4},{6,7},{7,6},{8,9},{9,8},{10,11... | collective-permute-start | bytes 1769480 | tf_op jit(solution)/shard_map/ppermute | solution.py:481
  31.6 27.1 %collective-permute-start.21 = (bf16[256,1536]{1,0:T(8,128)(2,1)}, bf16[256,1536]{1,0:T(8,128)(2,1)}, u32[]{:S(2)}, u32[]{:S(2)}) collective-permute-start(bf16[256,1536]{1,0:T(8,128)(2,1)} %get-tuple-element.26.refs_9_.refs_17_), channel_id=1, source_target_pairs={{0,16},{16,0},{1,17},{17,1},{2,18},{18,2},{3,19},{19,3},{4,20},{20... | collective-permute-start | bytes 2359304 | tf_op jit(solution)/shard_map/ppermute | solution.py:476
  33.1 11.0 %collective-permute-start.14 = (bf16[192,512]{1,0:T(8,128)(2,1)}, bf16[192,512]{1,0:T(8,128)(2,1)S(1)}, u32[]{:S(2)}, u32[]{:S(2)}) collective-permute-start(bf16[192,512]{1,0:T(8,128)(2,1)} %copy-done.30), channel_id=1, source_target_pairs={{0,2},{2,0},{4,6},{6,4},{8,10},{10,8},{12,14},{14,12},{1,3},{3,1},... | collective-permute-start | bytes 589832 | tf_op jit(solution)/shard_map/ppermute | solution.py:516
  33.8 11.8 %collective-permute-start.13 = (bf16[192,512]{1,0:T(8,128)(2,1)}, bf16[192,512]{1,0:T(8,128)(2,1)S(1)}, u32[]{:S(2)}, u32[]{:S(2)}) collective-permute-start(bf16[192,512]{1,0:T(8,128)(2,1)} %copy-done.30), channel_id=1, source_target_pairs={{0,4},{2,6},{4,8},{6,10},{8,12},{10,14},{12,0},{14,2},{1,5},{3,7},... | collective-permute-start | bytes 589832 | tf_op jit(solution)/shard_map/ppermute | solution.py:510
  33.9 15.3 %collective-permute-start.17 = (bf16[384,384]{1,0:T(8,128)(2,1)S(1)}, bf16[384,384]{1,0:T(8,128)(2,1)S(1)}, u32[]{:S(2)}, u32[]{:S(2)}) collective-permute-start(bf16[384,384]{1,0:T(8,128)(2,1)S(1)} %constant_dynamic-slice_fusion), channel_id=1, source_target_pairs={{0,1},{1,0},{2,3},{3,2},{4,5},{5,4},{6,7},{7,6},{8,9},{9,8},{10,11... | collective-permute-start | bytes 884744 | tf_op jit(solution)/shard_map/ppermute | solution.py:483
  44.1 16.6 %collective-permute-start.19 = (bf16[256,1536]{1,0:T(8,128)(2,1)}, bf16[256,1536]{1,0:T(8,128)(2,1)S(1)}, u32[]{:S(2)}, u32[]{:S(2)}) collective-permute-start(bf16[256,1536]{1,0:T(8,128)(2,1)} %collective-permute-done.10.refs_12_.refs_20_), channel_id=1, source_target_pairs={{0,1},{1,0},{2,3},{3,2},{4,5},{5,4},{6,7},{7,6},{8,9},{9,8},{10,11... | collective-permute-start | bytes 2359304 | tf_op jit(solution)/shard_map/ppermute | solution.py:518
  44.1 7.5 %collective-permute-start.12 = (bf16[192,512]{1,0:T(8,128)(2,1)}, bf16[192,512]{1,0:T(8,128)(2,1)S(1)}, u32[]{:S(2)}, u32[]{:S(2)}) collective-permute-start(bf16[192,512]{1,0:T(8,128)(2,1)} %copy-done.35), channel_id=1, source_target_pairs={{0,2},{2,0},{4,6},{6,4},{8,10},{10,8},{12,14},{14,12},{1,3},{3,1},... | collective-permute-start | bytes 589832 | tf_op jit(solution)/shard_map/ppermute | solution.py:516
  45.7 9.1 %collective-permute-start.11 = (bf16[192,512]{1,0:T(8,128)(2,1)}, bf16[192,512]{1,0:T(8,128)(2,1)S(1)}, u32[]{:S(2)}, u32[]{:S(2)}) collective-permute-start(bf16[192,512]{1,0:T(8,128)(2,1)} %copy-done.35), channel_id=1, source_target_pairs={{0,4},{2,6},{4,8},{6,10},{8,12},{10,14},{12,0},{14,2},{1,5},{3,7},... | collective-permute-start | bytes 589832 | tf_op jit(solution)/shard_map/ppermute | solution.py:510
  58.6 20.4 %collective-permute-start.22 = (bf16[256,1536]{1,0:T(8,128)(2,1)}, bf16[256,1536]{1,0:T(8,128)(2,1)S(1)}, u32[]{:S(2)}, u32[]{:S(2)}) collective-permute-start(bf16[256,1536]{1,0:T(8,128)(2,1)} %collective-permute-done.21.refs_22_), channel_id=1, source_target_pairs={{0,1},{1,0},{2,3},{3,2},{4,5},{5,4},{6,7},{7,6},{8,9},{9,8},{10,11... | collective-permute-start | bytes 2359304 | tf_op jit(solution)/shard_map/ppermute | solution.py:518
  58.6 7.7 %collective-permute-start.18 = (bf16[192,512]{1,0:T(8,128)(2,1)S(1)}, bf16[192,512]{1,0:T(8,128)(2,1)S(1)}, u32[]{:S(2)}, u32[]{:S(2)}) collective-permute-start(bf16[192,512]{1,0:T(8,128)(2,1)S(1)} %collective-permute-done.13.refs_6_), channel_id=1, source_target_pairs={{0,2},{2,0},{4,6},{6,4},{8,10},{10,8},{12,14},{14,12},{1,3},{3,1},... | collective-permute-start | bytes 589832 | tf_op jit(solution)/shard_map/ppermute | solution.py:516
  59.8 19.2 %collective-permute-start.20 = (bf16[192,512]{1,0:T(8,128)(2,1)S(1)}, bf16[192,512]{1,0:T(8,128)(2,1)S(1)}, u32[]{:S(2)}, u32[]{:S(2)}) collective-permute-start(bf16[192,512]{1,0:T(8,128)(2,1)S(1)} %collective-permute-done.11.after_ref.refs_14_), channel_id=1, source_target_pairs={{0,2},{2,0},{4,6},{6,4},{8,10},{10,8},{12,14},{14,12},{1,3},{3,1},... | collective-permute-start | bytes 589832 | tf_op jit(solution)/shard_map/ppermute | solution.py:516
  97.6 12.4 %all-to-all-start.1 = ((bf16[8,16,256]{2,1,0:T(8,128)(2,1)}), bf16[8,16,256]{2,1,0:T(8,128)(2,1)S(1)}, u32[]{:S(2)}, u32[]{:S(2)}) async-start(bf16[8,16,256]{2,1,0:T(8,128)(2,1)} %get-tuple-element.30), calls=%async_computation.1 | async-start | bytes 131072 | tf_op jit(solution)/shard_map/all_to_all | solution.py:541
  (37 other events, 264.5 us)

commit v5 on v4

--- a/solution.py
+++ b/solution.py
@@ -11,13 +11,11 @@
 HD = 64
 EPSILON = 1e-06
 FLOOR = -1e30
-CHUNKS = (256, 256)
 QROWS = 8
 NORM_ROWS = 16
 LANES = 128
-UNIT_TILES = 2
 UNIT_ROWS = 16
-MLP_VMEM = 24 * 1024 * 1024
+MLP_VMEM = 32 * 1024 * 1024
 NORM_VMEM = 8 * 1024 * 1024
 SMALL_VMEM = 4 * 1024 * 1024
 
@@ -29,17 +27,23 @@
     return (centred * lax.rsqrt(variance + EPSILON) * gains).astype(jnp.bfloat16)
 
 
-def norm_kernel(flip, tiles_ref, gain_ref, *refs):
-    out_refs, (rows, hidden, in_sems, out_sems) = refs[:-4], refs[-4:]
+def in_hbm(*arrays):
+    return [pltpu.with_memory_space_constraint(x, pltpu.HBM) for x in arrays]
+
+
+def norm_kernel(flip, tiles_ref, gain_ref, out_ref, rows, hidden, in_sems, out_sems):
     core = lax.axis_index("sub")
-    half = len(out_refs)
+    half, length = rows.shape[:2]
     first = (1 - core if flip else core) * half
     copies = [
         pltpu.make_async_copy(tiles_ref.at[first + i], rows.at[i], in_sems.at[i])
         for i in range(half)
     ]
     stores = [
-        pltpu.make_async_copy(hidden.at[i], out_refs[i], out_sems.at[i]) for i in range(half)
+        pltpu.make_async_copy(
+            hidden.at[i], out_ref.at[pl.ds(i * length, length)], out_sems.at[i]
+        )
+        for i in range(half)
     ]
     for copy in copies:
         copy.start()
@@ -52,7 +56,7 @@
             hidden[i, here, :] = normed(rows[i, here, :].astype(jnp.float32), gain)
             return carry
 
-        lax.fori_loop(0, rows.shape[1] // NORM_ROWS, some_rows, 0, unroll=4)
+        lax.fori_loop(0, length // NORM_ROWS, some_rows, 0, unroll=4)
         stores[i].start()
     for store in stores:
         store.wait()
@@ -65,8 +69,8 @@
     return pl.pallas_call(
         functools.partial(norm_kernel, flip),
         in_specs=[hbm, pl.BlockSpec(memory_space=pltpu.VMEM)],
-        out_specs=[hbm] * half,
-        out_shape=[jax.ShapeDtypeStruct((length, width), jnp.bfloat16)] * half,
+        out_specs=hbm,
+        out_shape=pltpu.HBM((half * length, width), jnp.bfloat16),
         scratch_shapes=[
             pltpu.VMEM((half, length, width), jnp.bfloat16),
             pltpu.VMEM((half, length, width), jnp.bfloat16),
@@ -74,44 +78,59 @@
             pltpu.SemaphoreType.DMA((half,)),
         ],
         compiler_params=pltpu.CompilerParams(vmem_limit_bytes=NORM_VMEM),
-        cost_estimate=pl.CostEstimate(
-            flops=8 * half * length * width,
-            bytes_accessed=4 * half * length * width,
-            transcendentals=half * length,
-        ),
-    )(tiles, gain)
+        cost_estimate=pl.CostEstimate(flops=0, bytes_accessed=0, transcendentals=0),
+    )(*in_hbm(tiles), gain)
 
 
 def after(value, *others):
     return lax.optimization_barrier((value, *others))[0]
 
 
-def block_copies(blocks, weights, sems, ny):
-    n_dev = len(blocks)
-    me = lax.axis_index("dev")
-    nz = n_dev // ny
-    my_z = me // ny
-    my_y = me - my_z * ny
-    depth = blocks[0].shape[0]
-    copies = []
-    for k in range(n_dev):
-        step, flip = k // ny, k % ny
+class Layout:
+    def __init__(self, n_dev, ny, depth):
+        self.ny, self.nz, self.depth = ny, n_dev // ny, depth
+        self.pair = ny * depth
+        self.relative = self.pair % LANES == 0
+        self.early = self.nz // 2 * self.pair if self.relative else 0
+        self.width = n_dev * depth
+
+    def place(self):
+        me = lax.axis_index("dev")
+        my_z = me // self.ny
+        return my_z, me - my_z * self.ny
+
+    def source(self, step):
+        my_z, _ = self.place()
         z = my_z - step
-        z = jnp.where(z < 0, z + nz, z)
-        y = 1 - my_y if flip else my_y
-        start = pl.multiple_of((z * ny + y) * depth, depth)
-        copies.append(
-            pltpu.make_async_copy(blocks[k], weights.at[pl.ds(start, depth)], sems.at[k])
-        )
-    return copies
-
-
-def tile_copies(tile_refs, rows, sems):
-    length = tile_refs[0].shape[0]
-    return [
-        pltpu.make_async_copy(ref, rows.at[pl.ds(i * length, length)], sems.at[i])
-        for i, ref in enumerate(tile_refs)
-    ]
+        return jnp.where(z < 0, z + self.nz, z)
+
+    def block_copies(self, blocks, weights, sems):
+        _, my_y = self.place()
+        copies = []
+        for k, block in enumerate(blocks):
+            step, flip = k // self.ny, k % self.ny
+            y = 1 - my_y if flip else my_y
+            at = step if self.relative else self.source(step)
+            start = pl.multiple_of(at * self.pair + y * self.depth, self.depth)
+            copies.append(
+                pltpu.make_async_copy(block, weights.at[pl.ds(start, self.depth)], sems.at[k])
+            )
+        return copies
+
+    def row_copies(self, tiles_ref, rows, sems, steps):
+        if not self.relative:
+            return [pltpu.make_async_copy(tiles_ref, rows, sems.at[0])]
+        copies = []
+        for step in steps:
+            start = pl.multiple_of(self.source(step) * self.pair, LANES)
+            copies.append(
+                pltpu.make_async_copy(
+                    tiles_ref.at[:, pl.ds(start, self.pair)],
+                    rows.at[:, step * self.pair : (step + 1) * self.pair],
+                    sems.at[step],
+                )
+            )
+        return copies
 
 
 def gated_means(both, out_ref, at, length):
@@ -129,99 +148,151 @@
         )
 
 
-def run_units(units, products, length):
+def product(rows, weights, first, last):
+    return jnp.dot(
+        rows[:, first:last], weights[first:last, :], preferred_element_type=jnp.float32
+    )
+
+
+def early_kernel(layout, *refs):
+    steps = range(layout.nz // 2)
+    n_blocks = len(steps) * layout.ny
+    blocks, tile_refs = refs[:n_blocks], refs[n_blocks : n_blocks + 2]
+    out_ref, weights, rows, sums, weight_sems, row_sems, out_sems = refs[n_blocks + 2 :]
+    loads = layout.block_copies(blocks, weights, weight_sems)
+    row_loads = [
+        layout.row_copies(ref, rows.at[i], row_sems.at[i], steps)
+        for i, ref in enumerate(tile_refs)
+    ]
+    for copy in row_loads[0] + loads + row_loads[1]:
+        copy.start()
+    for copy in loads:
+        copy.wait()
+    stores = []
+    for i in range(2):
+        for copy in row_loads[i]:
+            copy.wait()
+        sums[i] = product(rows.at[i], weights, 0, layout.early)
+        stores.append(pltpu.make_async_copy(sums.at[i], out_ref.at[i], out_sems.at[i]))
+        stores[i].start()
+    for store in stores:
+        store.wait()
+
+
+def early_mlp(layout, blocks, tiles):
+    n_rows = tiles[0].shape[0]
+    cols = blocks[0].shape[1]
+    hbm = pl.BlockSpec(memory_space=pltpu.HBM)
+    return pl.pallas_call(
+        functools.partial(early_kernel, layout),
+        in_specs=[hbm] * (len(blocks) + 2),
+        out_specs=hbm,
+        out_shape=pltpu.HBM((2, n_rows, cols), jnp.float32),
+        scratch_shapes=[
+            pltpu.VMEM((layout.early, cols), jnp.bfloat16),
+            pltpu.VMEM((2, n_rows, layout.early), jnp.bfloat16),
+            pltpu.VMEM((2, n_rows, cols), jnp.float32),
+            pltpu.SemaphoreType.DMA((len(blocks),)),
+            pltpu.SemaphoreType.DMA((2, layout.nz)),
+            pltpu.SemaphoreType.DMA((2,)),
+        ],
+        compiler_params=pltpu.CompilerParams(vmem_limit_bytes=MLP_VMEM),
+        cost_estimate=pl.CostEstimate(flops=0, bytes_accessed=0, transcendentals=0),
+    )(*in_hbm(*blocks, *tiles))
+
+
+def middle_kernel(layout, length, *refs):
+    n_blocks = layout.nz * layout.ny
+    n_sums = 1 if layout.relative else 0
+    blocks, tile_refs = refs[:n_blocks], refs[n_blocks : n_blocks + 3]
+    sum_refs = refs[n_blocks + 3 : n_blocks + 3 + n_sums]
+    out_ref, weights, rows, sums, even, odd, weight_sems, row_sems, sum_sems = refs[
+        n_blocks + 3 + n_sums :
+    ]
+    early = layout.early
+    loads = layout.block_copies(blocks, weights, weight_sems)
+    late_blocks = early // layout.depth
+    steps = [range(early // layout.pair, layout.nz)] * 2 + [range(layout.nz)]
+    row_loads = [
+        layout.row_copies(ref, rows.at[i], row_sems.at[i], steps[i])
+        for i, ref in enumerate(tile_refs)
+    ]
+    sum_loads = [
+        pltpu.make_async_copy(ref.at[i], sums.at[i], sum_sems.at[i])
+        for ref in sum_refs
+        for i in range(2)
+    ]
+    for copy in loads[late_blocks:] + row_loads[0] + sum_loads[:1]:
+        copy.start()
+    for copy in row_loads[1] + sum_loads[1:] + row_loads[2] + loads[:late_blocks]:
+        copy.start()
+    waits = [
+        loads[late_blocks:] + row_loads[0] + sum_loads[:1],
+        row_loads[1] + sum_loads[1:],
+        row_loads[2] + loads[:late_blocks],
+    ]
     pending = None
-    for i, (waits, rows, weights, out_ref, at) in enumerate(units):
-        for copy in waits:
+    for i in range(3):
+        for copy in waits[i]:
             copy.wait()
-        both = products[i % 2]
-        both[...] = jnp.dot(rows[...], weights[...], preferred_element_type=jnp.float32)
+        both = (even, odd)[i % 2]
+        if i < 2 and n_sums:
+            both[...] = product(rows.at[i], weights, early, layout.width) + sums[i]
+        else:
+            both[...] = product(rows.at[i], weights, 0, layout.width)
         if pending is not None:
             gated_means(*pending, length)
-        pending = (both, out_ref, at)
+        pending = (both, out_ref, 2 * i)
     gated_means(*pending, length)
 
 
-def mlp_scratch(n_dev, chunks, n_tiles, length):
-    depth, both_cols = chunks[0][0].shape
-    width = n_dev * depth
-    unit = (UNIT_TILES * length, both_cols)
-    return [
-        pltpu.VMEM((len(chunks), width, both_cols), jnp.bfloat16),
-        pltpu.VMEM((n_tiles * length, width), jnp.bfloat16),
-        pltpu.VMEM(unit, jnp.float32),
-        pltpu.VMEM(unit, jnp.float32),
-        pltpu.SemaphoreType.DMA((len(chunks), n_dev)),
-        pltpu.SemaphoreType.DMA((n_tiles,)),
-    ]
-
-
-def mlp_cost(blocks, n_tiles, tiles):
-    both_cols = blocks[0].shape[1]
-    length, width = tiles[0].shape
-    return pl.CostEstimate(
-        flops=2 * n_tiles * length * width * both_cols,
-        bytes_accessed=2 * (n_tiles * length * width + width * both_cols),
-        transcendentals=n_tiles * length * both_cols // 2,
-    )
-
-
-def first_mlp_kernel(n_dev, ny, n_tiles, after_ref, *refs):
-    del after_ref
-    blocks, tile_refs = refs[:n_dev], refs[n_dev : n_dev + n_tiles]
-    out_ref, weights, rows, even, odd, weight_sems, row_sems = refs[n_dev + n_tiles :]
-    length = tile_refs[0].shape[0]
-    loads = block_copies(blocks, weights.at[0], weight_sems.at[0], ny)
-    row_loads = tile_copies(tile_refs, rows, row_sems)
-    for copy in loads + row_loads:
-        copy.start()
-    units = []
-    for i in range(0, n_tiles, UNIT_TILES):
-        here = slice(i * length, (i + UNIT_TILES) * length)
-        waits = row_loads[i : i + UNIT_TILES] + (loads if i == 0 else [])
-        units.append((waits, rows.at[here], weights.at[0], out_ref, i))
-    run_units(units, (even, odd), length)
-
-
-def first_mlp(after_this, blocks, tiles, ny):
-    n_dev, n_tiles = len(blocks), len(tiles)
+def middle_mlp(layout, blocks, tiles, sums, length):
+    n_rows, width = tiles[0].shape
+    cols = blocks[0].shape[1]
     hbm = pl.BlockSpec(memory_space=pltpu.HBM)
     return pl.pallas_call(
-        functools.partial(first_mlp_kernel, n_dev, ny, n_tiles),
-        in_specs=[hbm] * (1 + n_dev + n_tiles),
+        functools.partial(middle_kernel, layout, length),
+        in_specs=[hbm] * (len(blocks) + 3 + len(sums)),
         out_specs=pl.BlockSpec(memory_space=pltpu.VMEM),
-        out_shape=jax.ShapeDtypeStruct((n_tiles, blocks[0].shape[1] // 2), jnp.float32),
-        scratch_shapes=mlp_scratch(n_dev, [blocks], n_tiles, tiles[0].shape[0]),
+        out_shape=jax.ShapeDtypeStruct((3 * n_rows // length, cols // 2), jnp.float32),
+        scratch_shapes=[
+            pltpu.VMEM((width, cols), jnp.bfloat16),
+            pltpu.VMEM((3, n_rows, width), jnp.bfloat16),
+            pltpu.VMEM((2, n_rows, cols), jnp.float32),
+            pltpu.VMEM((n_rows, cols), jnp.float32),
+            pltpu.VMEM((n_rows, cols), jnp.float32),
+            pltpu.SemaphoreType.DMA((len(blocks),)),
+            pltpu.SemaphoreType.DMA((3, layout.nz)),
+            pltpu.SemaphoreType.DMA((2,)),
+        ],
         compiler_params=pltpu.CompilerParams(vmem_limit_bytes=MLP_VMEM),
-        cost_estimate=mlp_cost(blocks, n_tiles, tiles),
-    )(after_this, *blocks, *tiles)
-
-
-def last_mlp_kernel(n_dev, n_grp, n_sub, ny, slot_count, first_ref, *refs):
-    n_tiles = 2 * slot_count
-    half = slot_count // 2
-    blocks, tile_refs = refs[: 2 * n_dev], refs[2 * n_dev : 2 * n_dev + n_tiles]
-    out_ref, weights, rows, even, odd, weight_sems, row_sems, late, rest = refs[
-        2 * n_dev + n_tiles :
-    ]
-    length = tile_refs[0].shape[0]
-    loads = [
-        block_copies(blocks[c * n_dev : (c + 1) * n_dev], weights.at[c], weight_sems.at[c], ny)
-        for c in range(2)
-    ]
-    row_loads = tile_copies(tile_refs, rows, row_sems)
-    for copy in loads[1] + row_loads + loads[0]:
+        cost_estimate=pl.CostEstimate(
+            flops=4 * n_rows * width * cols,
+            bytes_accessed=2 * (3 * n_rows * width + width * cols) + 8 * n_rows * cols,
+            transcendentals=0,
+        ),
+    )(*in_hbm(*blocks[:-1]), blocks[-1], *in_hbm(*tiles, *sums))
+
+
+def last_kernel(layout, length, n_grp, n_sub, means_ref, *refs):
+    n_blocks = layout.nz * layout.ny
+    blocks, tiles_ref = refs[:n_blocks], refs[n_blocks]
+    out_ref, weights, rows, both, means, weight_sems, row_sems = refs[n_blocks + 1 :]
+    loads = layout.block_copies(blocks, weights, weight_sems)
+    row_loads = layout.row_copies(tiles_ref, rows, row_sems, range(layout.nz))
+    for copy in row_loads + loads:
         copy.start()
-    units = []
-    for i in range(0, n_tiles, UNIT_TILES):
-        here = slice(i * length, (i + UNIT_TILES) * length)
-        waits = row_loads[i : i + UNIT_TILES] + (loads[1] if i == 0 else [])
-        units.append((waits, rows.at[here], weights.at[1], rest, i))
-    units.append((loads[0], units[-1][1], weights.at[0], late, 0))
-    run_units(units, (even, odd), length)
+    for copy in row_loads + loads:
+        copy.wait()
+    n_rows = rows.shape[0]
+    for i in range(0, n_rows, length):
+        here = slice(i, i + length)
+        both[here, :] = product(rows.at[here], weights, 0, layout.width)
+    gated_means(both, means, 0, length)
 
     group, core = lax.axis_index("grp"), lax.axis_index("sub")
     low = core == 0
+    half = n_rows // length
 
     def packed(mine, others):
         rows = jnp.concatenate(
@@ -231,47 +302,43 @@
             [rows[:, k : k + LANES] for k in range(0, rows.shape[1], LANES)], axis=0
         )
 
-    def features(ref, at):
-        return jnp.concatenate([ref[at : at + 1, :], rest[at : at + 1, :]], axis=1)
-
-    own = [features(first_ref, i) for i in range(slot_count)]
-    own = packed(jnp.concatenate(own[:half], axis=0), jnp.concatenate(own[half:], axis=0))
-    at = slot_count
-    early = [features(first_ref, at), features(first_ref, at + 1)]
-    at += 2
-    last = [
-        jnp.concatenate([late[i : i + 1, :], rest[at + i : at + i + 1, :]], axis=1)
-        for i in range(2)
-    ]
-    pair = packed(
-        jnp.concatenate([early[0], last[0]], axis=0), jnp.concatenate([early[1], last[1]], axis=0)
-    )
+    before = means_ref[...]
+    own = packed(before[:half], before[half : 2 * half])
+    pair = packed(before[2 * half :], means[...])
     for g in range(n_grp):
         chosen = jnp.where(group == g, own, pair).astype(jnp.bfloat16)
         for s in range(n_sub):
             out_ref[g * n_sub + s] = chosen
 
 
-def last_mlp(first_means, chunks, tiles, slot_count, n_grp, n_sub, ny):
-    n_dev = len(chunks[0])
-    cols = sum(blocks[0].shape[1] // 2 for blocks in chunks)
+def last_mlp(layout, means, blocks, tiles, length, n_grp, n_sub):
+    n_rows, width = tiles.shape
+    cols = blocks[0].shape[1]
+    half = n_rows // length
     hbm = pl.BlockSpec(memory_space=pltpu.HBM)
     vmem = pl.BlockSpec(memory_space=pltpu.VMEM)
     return pl.pallas_call(
-        functools.partial(last_mlp_kernel, n_dev, n_grp, n_sub, ny, slot_count),
-        in_specs=[vmem] + [hbm] * (2 * n_dev + len(tiles)),
+        functools.partial(last_kernel, layout, length, n_grp, n_sub),
+        in_specs=[vmem] + [hbm] * (len(blocks) + 1),
         out_specs=vmem,
         out_shape=jax.ShapeDtypeStruct(
-            (n_grp * n_sub, slot_count * cols // LANES, LANES), jnp.bfloat16
+            (n_grp * n_sub, half * cols // LANES, LANES), jnp.bfloat16
         ),
         scratch_shapes=[
-            *mlp_scratch(n_dev, chunks, len(tiles), tiles[0].shape[0]),
-            pltpu.VMEM((UNIT_TILES, chunks[0][0].shape[1] // 2), jnp.float32),
-            pltpu.VMEM((len(tiles), chunks[1][0].shape[1] // 2), jnp.float32),
+            pltpu.VMEM((width, cols), jnp.bfloat16),
+            pltpu.VMEM((n_rows, width), jnp.bfloat16),
+            pltpu.VMEM((n_rows, cols), jnp.float32),
+            pltpu.VMEM((half, cols // 2), jnp.float32),
+            pltpu.SemaphoreType.DMA((len(blocks),)),
+            pltpu.SemaphoreType.DMA((layout.nz,)),
         ],
         compiler_params=pltpu.CompilerParams(vmem_limit_bytes=MLP_VMEM),
-        cost_estimate=mlp_cost(chunks[1], len(tiles) + UNIT_TILES, tiles),
-    )(first_means, *chunks[0], *chunks[1], *tiles)
+        cost_estimate=pl.CostEstimate(
+            flops=2 * n_rows * width * cols,
+            bytes_accessed=2 * (n_rows * width + width * cols),
+            transcendentals=0,
+        ),
+    )(means, *in_hbm(*blocks[:-1]), blocks[-1], tiles)
 
 
 def small_mod(value, rate):
@@ -458,22 +525,17 @@
     along_y = [(d, d ^ 1) for d in range(n_dev)]
 
     half_cols = hidden_cols // 2
-    base = (group % 2) * half_cols
-    own_blocks = []
-    for cols in CHUNKS:
-        own_blocks.append(
-            jnp.concatenate(
-                [
-                    lax.dynamic_slice_in_dim(w, base, cols, 1)
-                    for w in (gate_weight, up_weight)
-                ],
-                axis=1,
-            )
-        )
-        base = base + cols
-    first = norm_tiles(tiles, tile_gain, False)
+    block = jnp.concatenate(
+        [
+            lax.dynamic_slice_in_dim(w, (group % 2) * half_cols, half_cols, 1)
+            for w in (gate_weight, up_weight)
+        ],
+        axis=1,
+    )
+    layout = Layout(n_dev, ny, gate_weight.shape[0])
+    first = norm_tiles(tiles, after(tile_gain, block), False)
     second = norm_tiles(tiles, tile_gain, True)
-    pair_first = [lax.ppermute(rows, "grp", to_pair) for rows in first]
+    pair_first = lax.ppermute(first, "grp", to_pair)
 
     proj_far = lax.ppermute(embed_proj, "sub", to_sibling)
     wq_far = lax.ppermute(slide_wq, "sub", to_sibling)
@@ -493,34 +555,22 @@
         compiler_params=pltpu.CompilerParams(vmem_limit_bytes=SMALL_VMEM),
     )(counts, slide_of, rates)
 
-    own_blocks[1] = after(own_blocks[1], first[0])
-    beside = {
-        (1, 1): [second[0]],
-        (2, 0): [proj_far],
-        (2, 1): [wq_far, pair_first[0]],
-        (3, 0): [wk_far, wv_far],
-        (3, 1): [wo_far, many],
-    }
-    chunks = [[] for _ in own_blocks]
-    held = list(own_blocks)
-    last = None
+    beside = {1: [first, second], 2: [proj_far, wq_far], 3: [wk_far, wv_far, wo_far, many]}
+    blocks = []
+    sums = []
     for step in range(nz):
-        for c, blocks in enumerate(chunks):
-            if step:
-                arrived = lax.ppermute(held[c], "dev", along_z)
-                others = beside.get((step, c), [])
-                if last is not None:
-                    others = [last, *others]
-                held[c] = after(arrived, blocks[-1], *others)
-                last = held[c]
-            blocks += [held[c], lax.ppermute(held[c], "dev", along_y)]
-    pair_first[1] = after(pair_first[1], last)
-    pair_second = [lax.ppermute(rows, "sub", to_sibling) for rows in pair_first]
-
-    pieces = [rows for piece in zip(pair_first, pair_second) for rows in piece]
-    own_tiles = [*first, *second]
-    first_means = first_mlp(last, chunks[0], own_tiles + pieces[:2], ny)
-    parts = last_mlp(first_means, chunks, own_tiles + pieces, slot_count, n_grp, n_sub, ny)
+        if step:
+            block = lax.ppermute(block, "dev", along_z)
+            others = beside.get(step, [])
+            if layout.relative and step == nz - 1:
+                sums = [early_mlp(layout, blocks[: nz // 2 * ny], [first, second])]
+            block = after(block, blocks[-1], *others, *sums)
+        blocks += [block, lax.ppermute(block, "dev", along_y)]
+    pair_first = after(pair_first, block)
+    pair_second = lax.ppermute(pair_first, "sub", to_sibling)
+
+    means = middle_mlp(layout, blocks, [first, second, pair_first], sums, length)
+    parts = last_mlp(layout, means, blocks, pair_second, length, n_grp, n_sub)
     parts = lax.all_to_all(parts, ("grp", "sub"), split_axis=0, concat_axis=0, tiled=True)
 
     out_width = embed_proj.shape[1]

time: 114 us -> 101 us (0.89)
  starting transfers between devices: 25.5 us -> 17.1 us
  local copies, waits for them, and re-layouts: 16.3 us -> 12.3 us
  waiting for transfers between devices: 35 us -> 32.8 us
  Pallas kernels: 28.8 us -> 30.9 us
    ppermute x18 -> x9, starting transfers between devices: 18.9 us -> 11.3 us  [the longest x4 6.14 us: on_device(): blocks += [block, lax.ppermute(block, 'dev', along_y)]]
    unnamed x74 -> x54, local copies, waits for them, and re-layouts: 15.2 us -> 11.2 us
    pallas_call x2, Pallas kernels: 4.97 us -> 8.04 us  [norm_tiles(): pl.pallas_call(functools.partial(norm_kernel, flip), in_specs=[hbm, pl.Bl...]
    all_to_all x1, waiting for transfers between devices: 5.43 us -> 4 us  [on_device(): sent = lax.all_to_all(sent, 'dev', split_axis=0, concat_axis=0, tiled=True)]
    ppermute x18 -> x9, waiting for transfers between devices: 29.6 us -> 28.8 us  [the longest x3 18.8 us: on_device(): block = lax.ppermute(block, 'dev', along_z)]
    pallas_call x2 -> x3, Pallas kernels: 16.8 us -> 16.8 us  [the longest x1 7.7 us: middle_mlp(): pl.pallas_call(functools.partial(middle_kernel, layout, length), in_specs...]
  transfers between devices with their start and end apart: 24 -> 15, of which waited for: 9 -> 5; matrix products, arithmetic and copies ran while one was open for 1% -> 1% of each run, Pallas kernels for 12% -> 23%
where the time goes in v5:
time: 101 us; the launch traced here: 100 us
  waiting for transfers between devices  32.8 us (32%)
  Pallas kernels  30.9 us (31%)
  starting transfers between devices  17.1 us (17%)
  local copies, waits for them, and re-layouts  12.3 us (12%)
  blocking collectives  6.21 us (6%)
    ppermute x3, waiting for transfers between devices, on_device(): block = lax.ppermute(block, 'dev', along_z)  18.8 us
    unnamed x54, local copies, waits for them, and re-layouts  11.2 us
    ppermute x4, waiting for transfers between devices, on_device(): blocks += [block, lax.ppermute(block, 'dev', along_y)]  9.95 us
    pallas_call x2, Pallas kernels, norm_tiles(): pl.pallas_call(functools.partial(norm_kernel, flip), in_specs=[hbm, pl.Bl...  8.04 us
    pallas_call x1, Pallas kernels, middle_mlp(): pl.pallas_call(functools.partial(middle_kernel, layout, length), in_specs...  7.7 us
    all_to_all x1, blocking collectives, on_device(): lax.all_to_all(parts, ('grp', 'sub'), split_axis=0, concat_axis=0, tiled=...  6.21 us
    ppermute x4, starting transfers between devices, on_device(): blocks += [block, lax.ppermute(block, 'dev', along_y)]  6.14 us
    pallas_call x1, Pallas kernels, early_mlp(): pl.pallas_call(functools.partial(early_kernel, layout), in_specs=[hbm] *...  5.13 us
  transfers between devices with their start and end apart: 15, of which 5 were waited for; matrix products, arithmetic and copies ran while one was open for 1% of the time, Pallas kernels for 23%

profile of v5, /device:TPU:0, one launch (start us, length us, event | category | flops | bytes accessed | tf_op | source)
XLA Modules:
  0.0 100.3 jit_solution(16828067529186084807)
XLA Ops:
  2.3 4.1 %shard_map.140.refs_4_.refs_8_ = bf16[512,1536]{1,0:T(8,128)(2,1)} custom-call(bf16[4,256,1536]{2,1,0:T(8,128)(2,1)} %tiles_ref.3, f32[1536]{0:T(1024)S(1)} %copy-done.16), custom_call_target="tpu_custom_call" | custom-call | tf_op jit(solution)/shard_map/pallas_call | solution.py:69
  6.4 2.6 %collective-permute-start.12 = (bf16[512,1536]{1,0:T(8,128)(2,1)}, bf16[512,1536]{1,0:T(8,128)(2,1)}, u32[]{:S(2)}, u32[]{:S(2)}) collective-permute-start(bf16[512,1536]{1,0:T(8,128)(2,1)} %shard_map.140.refs_4_.refs_8_), channel_id=1, source_target_pairs={{0,16},{16,0},{1,17},{17,1},{2,18},{18,2},{3,19},{19,3},{4,20},{20... | collective-permute-start | bytes 4718600 | tf_op jit(solution)/shard_map/ppermute | solution.py:538
  9.0 1.6 %collective-permute-start.1 = (bf16[192,1024]{1,0:T(8,128)(2,1)S(1)}, bf16[192,1024]{1,0:T(8,128)(2,1)}, u32[]{:S(2)}, u32[]{:S(2)}) collective-permute-start(bf16[192,1024]{1,0:T(8,128)(2,1)S(1)} %pad_maximum_fusion.refs_0_), channel_id=1, source_target_pairs={{0,4},{2,6},{4,8},{6,10},{8,12},{10,14},{12,0},{14,2},{1,5},{3,7},... | collective-permute-start | bytes 1179656 | tf_op jit(solution)/shard_map/ppermute | solution.py:563
  10.6 1.5 %collective-permute-start = (bf16[192,1024]{1,0:T(8,128)(2,1)S(1)}, bf16[192,1024]{1,0:T(8,128)(2,1)S(1)}, u32[]{:S(2)}, u32[]{:S(2)}) collective-permute-start(bf16[192,1024]{1,0:T(8,128)(2,1)S(1)} %pad_maximum_fusion.refs_0_), channel_id=1, source_target_pairs={{0,2},{2,0},{4,6},{6,4},{8,10},{10,8},{12,14},{14,12},{1,3},{3,1},... | collective-permute-start | bytes 1179656 | tf_op jit(solution)/shard_map/ppermute | solution.py:568
  12.1 4.0 %shard_map.141.refs_5_.refs_9_ = bf16[512,1536]{1,0:T(8,128)(2,1)} custom-call(bf16[4,256,1536]{2,1,0:T(8,128)(2,1)} %tiles_ref.3, f32[1536]{0:T(1024)S(1)} %copy-done.16), custom_call_target="tpu_custom_call" | custom-call | tf_op jit(solution)/shard_map/pallas_call | solution.py:69
  16.1 6.1 %collective-permute-done.1.refs_2_ = bf16[192,1024]{1,0:T(8,128)(2,1)} collective-permute-done((bf16[192,1024]{1,0:T(8,128)(2,1)S(1)}, bf16[192,1024]{1,0:T(8,128)(2,1)}, u32[]{:S(2)}, u32[]{:S(2)}) %collective-permute-start.1) | collective-permute-done | bytes 393248 | tf_op jit(solution)/shard_map/ppermute | solution.py:563
  23.8 1.5 %collective-permute-start.2 = (bf16[192,1024]{1,0:T(8,128)(2,1)}, bf16[192,1024]{1,0:T(8,128)(2,1)}, u32[]{:S(2)}, u32[]{:S(2)}) collective-permute-start(bf16[192,1024]{1,0:T(8,128)(2,1)} %collective-permute-done.1.refs_2_), channel_id=1, source_target_pairs={{0,2},{2,0},{4,6},{6,4},{8,10},{10,8},{12,14},{14,12},{1,3},{3,1},... | collective-permute-start | bytes 1179656 | tf_op jit(solution)/shard_map/ppermute | solution.py:568
  25.5 10.0 %collective-permute-done.3.refs_4_ = bf16[192,1024]{1,0:T(8,128)(2,1)} collective-permute-done((bf16[192,1024]{1,0:T(8,128)(2,1)}, bf16[192,1024]{1,0:T(8,128)(2,1)}, u32[]{:S(2)}, u32[]{:S(2)}) %collective-permute-start.3) | collective-permute-done | bytes 393248 | tf_op jit(solution)/shard_map/ppermute | solution.py:563
  36.8 1.5 %collective-permute-start.6 = (bf16[192,1024]{1,0:T(8,128)(2,1)}, bf16[192,1024]{1,0:T(8,128)(2,1)S(1)}, u32[]{:S(2)}, u32[]{:S(2)}) collective-permute-start(bf16[192,1024]{1,0:T(8,128)(2,1)} %collective-permute-done.3.refs_4_), channel_id=1, source_target_pairs={{0,2},{2,0},{4,6},{6,4},{8,10},{10,8},{12,14},{14,12},{1,3},{3,1},... | collective-permute-start | bytes 1179656 | tf_op jit(solution)/shard_map/ppermute | solution.py:568
  39.6 5.1 %shard_map.143.refs_11_ = f32[2,512,1024]{2,1,0:T(8,128)} custom-call(bf16[192,1024]{1,0:T(8,128)(2,1)} %copy-done.23, bf16[192,1024]{1,0:T(8,128)(2,1)} %copy-done.24, bf16[192,1024]{1,0:T(8,128)(2,1)} %collective-permute-done.1.refs_2_, bf16[192,1024]{1,0:T(8,128)(2,1)} %collective-permute-done.2.refs_3_, bf16[512,1536]{1,0:T(8,128)(2,1)} %shard_map.140.refs_4_.refs_8_, ...), custom_call_target="tpu_custom_call" | custom-call | tf_op jit(solution)/shard_map/pallas_call | solution.py:186
  46.4 2.7 %collective-permute-done.7.refs_6_ = bf16[192,1024]{1,0:T(8,128)(2,1)S(1)} collective-permute-done((bf16[192,1024]{1,0:T(8,128)(2,1)}, bf16[192,1024]{1,0:T(8,128)(2,1)S(1)}, u32[]{:S(2)}, u32[]{:S(2)}) %collective-permute-start.7) | collective-permute-done | bytes 393248 | tf_op jit(solution)/shard_map/ppermute | solution.py:563
  49.2 1.6 %collective-permute-start.11 = (bf16[192,1024]{1,0:T(8,128)(2,1)S(1)}, bf16[192,1024]{1,0:T(8,128)(2,1)S(1)}, u32[]{:S(2)}, u32[]{:S(2)}) collective-permute-start(bf16[192,1024]{1,0:T(8,128)(2,1)S(1)} %collective-permute-done.7.refs_6_), channel_id=1, source_target_pairs={{0,2},{2,0},{4,6},{6,4},{8,10},{10,8},{12,14},{14,12},{1,3},{3,1},... | collective-permute-start | bytes 1179656 | tf_op jit(solution)/shard_map/ppermute | solution.py:568
  50.8 9.9 %collective-permute-done.11.refs_7_ = bf16[192,1024]{1,0:T(8,128)(2,1)S(1)} collective-permute-done((bf16[192,1024]{1,0:T(8,128)(2,1)S(1)}, bf16[192,1024]{1,0:T(8,128)(2,1)S(1)}, u32[]{:S(2)}, u32[]{:S(2)}) %collective-permute-start.11) | collective-permute-done | bytes 393248 | tf_op jit(solution)/shard_map/ppermute | solution.py:568
  60.8 7.7 %shard_map.144.means_ref = f32[6,512]{1,0:T(8,128)S(1)} custom-call(bf16[192,1024]{1,0:T(8,128)(2,1)} %copy-done.23, bf16[192,1024]{1,0:T(8,128)(2,1)} %copy-done.24, bf16[192,1024]{1,0:T(8,128)(2,1)} %collective-permute-done.1.refs_2_, bf16[192,1024]{1,0:T(8,128)(2,1)} %collective-permute-done.2.refs_3_, bf16[192,1024]{1,0:T(8,128)(2,1)} %collective-permute-done.3.refs_4_, ...), custom_call_target="tpu_custom_call" | custom-call | flops 3221225472 | bytes 12058624 | tf_op jit(solution)/shard_map/pallas_call | solution.py:253
  68.5 3.9 %shard_map.145 = bf16[4,16,128]{2,1,0:T(8,128)(2,1)S(1)} custom-call(f32[6,512]{1,0:T(8,128)S(1)} %shard_map.144.means_ref, bf16[192,1024]{1,0:T(8,128)(2,1)} %copy-done.23, bf16[192,1024]{1,0:T(8,128)(2,1)} %copy-done.24, bf16[192,1024]{1,0:T(8,128)(2,1)} %collective-permute-done.1.refs_2_, bf16[192,1024]{1,0:T(8,128)(2,1)} %collective-permute-done.2.refs_3_, ...), custom_call_target="tpu_custom_call" | custom-call | flops 1610612736 | bytes 4718592 | tf_op jit(solution)/shard_map/pallas_call | solution.py:320
  72.5 6.2 %all_to_all.10.parts_ref = bf16[4,16,128]{2,1,0:T(8,128)(2,1)S(1)} all-to-all(bf16[4,16,128]{2,1,0:T(8,128)(2,1)S(1)} %shard_map.145), channel_id=1, replica_groups=mesh['grp'=2,'dev'=8,'sub'=2] {'grp','sub'}, dimensions={0} | all-to-all | bytes 32768 | tf_op jit(solution)/shard_map/all_to_all | solution.py:574
  78.7 1.9 %shard_map.146 = (bf16[4,1024]{1,0:T(4,128)(2,1)}, f32[8,768]{1,0:T(8,128)S(1)}, bf16[8,16,256]{2,1,0:T(8,128)(2,1)}) custom-call(s32[8]{0:T(128)S(1)} %copy-done.19, bf16[4,16,128]{2,1,0:T(8,128)(2,1)S(1)} %all_to_all.10.parts_ref, f32[768]{0:T(1024)S(1)} %copy-done.17, bf16[1024,768]{1,0:T(8,128)(2,1)S(1)} %copy-done, ...), custom_call_target="tpu_custom_call" | custom-call | tf_op jit(solution)/shard_map/pallas_call | solution.py:580
  81.2 4.8 %all-to-all-start.1 = ((bf16[8,16,256]{2,1,0:T(8,128)(2,1)}), bf16[8,16,256]{2,1,0:T(8,128)(2,1)S(1)}, u32[]{:S(2)}, u32[]{:S(2)}) async-start(bf16[8,16,256]{2,1,0:T(8,128)(2,1)} %get-tuple-element.16), calls=%async_computation.1 | async-start | bytes 131072 | tf_op jit(solution)/shard_map/all_to_all | solution.py:591
  87.3 1.5 %shard_map.147.query_ref = bf16[96,768]{1,0:T(8,128)(2,1)S(1)} custom-call(f32[8,768]{1,0:T(8,128)S(1)} %copy-done.14, f32[768]{0:T(1024)S(1)} %copy-done.18, bf16[768,384]{1,0:T(8,128)(2,1)S(1)} %copy-done.2, bf16[768,384]{1,0:T(8,128)(2,1)} %collective-permute-done.5.wq_far_ref), custom_call_target="tpu_custom_call" | custom-call | tf_op jit(solution)/shard_map/pallas_call | solution.py:592
  88.8 4.0 %all-to-all-done.1.sent_ref = bf16[8,16,256]{2,1,0:T(8,128)(2,1)S(1)} async-done(((bf16[8,16,256]{2,1,0:T(8,128)(2,1)}), bf16[8,16,256]{2,1,0:T(8,128)(2,1)S(1)}, u32[]{:S(2)}, u32[]{:S(2)}) %all-to-all-start.1) | async-done | bytes 65568 | tf_op jit(solution)/shard_map/all_to_all | solution.py:591
  92.8 1.1 %copy-done.4 = bf16[768,384]{1,0:T(8,128)(2,1)S(1)} copy-done((bf16[768,384]{1,0:T(8,128)(2,1)S(1)}, bf16[768,384]{1,0:T(8,128)(2,1)}, u32[]{:S(2)}) %copy-start.4) | copy-done | bytes 589848
  93.9 1.1 %copy-done.6 = bf16[768,384]{1,0:T(8,128)(2,1)S(1)} copy-done((bf16[768,384]{1,0:T(8,128)(2,1)S(1)}, bf16[768,384]{1,0:T(8,128)(2,1)}, u32[]{:S(2)}) %copy-start.6) | copy-done | bytes 589848
  95.0 1.1 %copy-done.8 = bf16[768,384]{1,0:T(8,128)(2,1)S(1)} copy-done((bf16[768,384]{1,0:T(8,128)(2,1)S(1)}, bf16[768,384]{1,0:T(8,128)(2,1)}, u32[]{:S(2)}) %copy-start.8) | copy-done | bytes 589848
  98.2 2.1 %shard_map.148 = bf16[4,384]{1,0:T(4,128)(2,1)} custom-call(s32[8]{0:T(128)S(1)} %copy-done.20, bf16[8,16,256]{2,1,0:T(8,128)(2,1)S(1)} %all-to-all-done.1.sent_ref, f32[8,768]{1,0:T(8,128)S(1)} %copy-done.15, bf16[96,768]{1,0:T(8,128)(2,1)S(1)} %shard_map.147.query_ref, f32[96,32]{1,0:T(8,128)S(1)} %copy-done.12, bf16[768,384]{1,0:T(8,128)(2,1)S(1)} %copy-done.3, ...), custom_call_target="tpu_custom_call" | custom-call | tf_op jit(solution)/shard_map/pallas_call | solution.py:599
  (73 shorter events, 11.9 us)
Async XLA Ops:
  0.6 35.4 %collective-permute-start.4 = (bf16[1024,768]{1,0:T(8,128)(2,1)}, bf16[1024,768]{1,0:T(8,128)(2,1)S(1)}, u32[]{:S(2)}, u32[]{:S(2)}) collective-permute-start(bf16[1024,768]{1,0:T(8,128)(2,1)} %near_ref.1), channel_id=1, source_target_pairs={{0,1},{1,0},{2,3},{3,2},{4,5},{5,4},{6,7},{7,6},{8,9},{9,8},{10,11... | collective-permute-start | bytes 4718600 | tf_op jit(solution)/shard_map/ppermute | solution.py:540
  6.3 19.0 %copy-start.1 = (bf16[384,768]{1,0:T(8,128)(2,1)S(1)}, bf16[384,768]{1,0:T(8,128)(2,1)}, u32[]{:S(2)}) copy-start(bf16[384,768]{1,0:T(8,128)(2,1)} %wo_ref.1) | copy-start | bytes 1769476
  6.4 29.2 %copy-start.3 = (bf16[768,384]{1,0:T(8,128)(2,1)S(1)}, bf16[768,384]{1,0:T(8,128)(2,1)}, u32[]{:S(2)}) copy-start(bf16[768,384]{1,0:T(8,128)(2,1)} %wk_ref.1) | copy-start | bytes 1769476
  6.4 31.9 %copy-start.19 = (s32[8]{0:T(128)S(1)}, s32[8]{0:T(128)}, u32[]{:S(2)}) copy-start(s32[8]{0:T(128)} %counts_ref.5) | copy-start | bytes 100
  6.4 31.9 %copy-start.21 = (s32[8]{0:T(128)S(1)}, s32[8]{0:T(128)}, u32[]{:S(2)}) copy-start(s32[8]{0:T(128)} %slide_ref.1) | copy-start | bytes 100
  6.4 31.9 %copy-start.22 = (s32[12]{0:T(128)S(1)}, s32[12]{0:T(128)}, u32[]{:S(2)}) copy-start(s32[12]{0:T(128)} %rates_ref.1) | copy-start | bytes 148
  6.4 42.7 %collective-permute-start.12 = (bf16[512,1536]{1,0:T(8,128)(2,1)}, bf16[512,1536]{1,0:T(8,128)(2,1)}, u32[]{:S(2)}, u32[]{:S(2)}) collective-permute-start(bf16[512,1536]{1,0:T(8,128)(2,1)} %shard_map.140.refs_4_.refs_8_), channel_id=1, source_target_pairs={{0,16},{16,0},{1,17},{17,1},{2,18},{18,2},{3,19},{19,3},{4,20},{20... | collective-permute-start | bytes 4718600 | tf_op jit(solution)/shard_map/ppermute | solution.py:538
  9.0 13.2 %collective-permute-start.1 = (bf16[192,1024]{1,0:T(8,128)(2,1)S(1)}, bf16[192,1024]{1,0:T(8,128)(2,1)}, u32[]{:S(2)}, u32[]{:S(2)}) collective-permute-start(bf16[192,1024]{1,0:T(8,128)(2,1)S(1)} %pad_maximum_fusion.refs_0_), channel_id=1, source_target_pairs={{0,4},{2,6},{4,8},{6,10},{8,12},{10,14},{12,0},{14,2},{1,5},{3,7},... | collective-permute-start | bytes 1179656 | tf_op jit(solution)/shard_map/ppermute | solution.py:563
  10.6 11.6 %collective-permute-start = (bf16[192,1024]{1,0:T(8,128)(2,1)S(1)}, bf16[192,1024]{1,0:T(8,128)(2,1)S(1)}, u32[]{:S(2)}, u32[]{:S(2)}) collective-permute-start(bf16[192,1024]{1,0:T(8,128)(2,1)S(1)} %pad_maximum_fusion.refs_0_), channel_id=1, source_target_pairs={{0,2},{2,0},{4,6},{6,4},{8,10},{10,8},{12,14},{14,12},{1,3},{3,1},... | collective-permute-start | bytes 1179656 | tf_op jit(solution)/shard_map/ppermute | solution.py:568
  12.1 13.3 %collective-permute-start.5 = (bf16[768,384]{1,0:T(8,128)(2,1)S(1)}, bf16[768,384]{1,0:T(8,128)(2,1)}, u32[]{:S(2)}, u32[]{:S(2)}) collective-permute-start(bf16[768,384]{1,0:T(8,128)(2,1)S(1)} %copy-done.2), channel_id=1, source_target_pairs={{0,1},{1,0},{2,3},{3,2},{4,5},{5,4},{6,7},{7,6},{8,9},{9,8},{10,11... | collective-permute-start | bytes 1769480 | tf_op jit(solution)/shard_map/ppermute | solution.py:541
  22.9 12.6 %collective-permute-start.3 = (bf16[192,1024]{1,0:T(8,128)(2,1)}, bf16[192,1024]{1,0:T(8,128)(2,1)}, u32[]{:S(2)}, u32[]{:S(2)}) collective-permute-start(bf16[192,1024]{1,0:T(8,128)(2,1)} %collective-permute-done.1.refs_2_), channel_id=1, source_target_pairs={{0,4},{2,6},{4,8},{6,10},{8,12},{10,14},{12,0},{14,2},{1,5},{3,7},... | collective-permute-start | bytes 1179656 | tf_op jit(solution)/shard_map/ppermute | solution.py:563
  23.8 11.7 %collective-permute-start.2 = (bf16[192,1024]{1,0:T(8,128)(2,1)}, bf16[192,1024]{1,0:T(8,128)(2,1)}, u32[]{:S(2)}, u32[]{:S(2)}) collective-permute-start(bf16[192,1024]{1,0:T(8,128)(2,1)} %collective-permute-done.1.refs_2_), channel_id=1, source_target_pairs={{0,2},{2,0},{4,6},{6,4},{8,10},{10,8},{12,14},{14,12},{1,3},{3,1},... | collective-permute-start | bytes 1179656 | tf_op jit(solution)/shard_map/ppermute | solution.py:568
  25.4 10.6 %collective-permute-start.10 = (bf16[384,384]{1,0:T(8,128)(2,1)S(1)}, bf16[384,384]{1,0:T(8,128)(2,1)S(1)}, u32[]{:S(2)}, u32[]{:S(2)}) collective-permute-start(bf16[384,384]{1,0:T(8,128)(2,1)S(1)} %constant_dynamic-slice_fusion), channel_id=1, source_target_pairs={{0,1},{1,0},{2,3},{3,2},{4,5},{5,4},{6,7},{7,6},{8,9},{9,8},{10,11... | collective-permute-start | bytes 884744 | tf_op jit(solution)/shard_map/ppermute | solution.py:545
  35.5 9.2 %collective-permute-start.8 = (bf16[768,384]{1,0:T(8,128)(2,1)S(1)}, bf16[768,384]{1,0:T(8,128)(2,1)S(1)}, u32[]{:S(2)}, u32[]{:S(2)}) collective-permute-start(bf16[768,384]{1,0:T(8,128)(2,1)S(1)} %copy-done.3), channel_id=1, source_target_pairs={{0,1},{1,0},{2,3},{3,2},{4,5},{5,4},{6,7},{7,6},{8,9},{9,8},{10,11... | collective-permute-start | bytes 1769480 | tf_op jit(solution)/shard_map/ppermute | solution.py:542
  35.5 10.1 %collective-permute-start.9 = (bf16[768,384]{1,0:T(8,128)(2,1)}, bf16[768,384]{1,0:T(8,128)(2,1)S(1)}, u32[]{:S(2)}, u32[]{:S(2)}) collective-permute-start(bf16[768,384]{1,0:T(8,128)(2,1)} %wv_ref.1), channel_id=1, source_target_pairs={{0,1},{1,0},{2,3},{3,2},{4,5},{5,4},{6,7},{7,6},{8,9},{9,8},{10,11... | collective-permute-start | bytes 1769480 | tf_op jit(solution)/shard_map/ppermute | solution.py:543
  36.0 13.1 %collective-permute-start.7 = (bf16[192,1024]{1,0:T(8,128)(2,1)}, bf16[192,1024]{1,0:T(8,128)(2,1)S(1)}, u32[]{:S(2)}, u32[]{:S(2)}) collective-permute-start(bf16[192,1024]{1,0:T(8,128)(2,1)} %collective-permute-done.3.refs_4_), channel_id=1, source_target_pairs={{0,4},{2,6},{4,8},{6,10},{8,12},{10,14},{12,0},{14,2},{1,5},{3,7},... | collective-permute-start | bytes 1179656 | tf_op jit(solution)/shard_map/ppermute | solution.py:563
  36.8 12.4 %collective-permute-start.6 = (bf16[192,1024]{1,0:T(8,128)(2,1)}, bf16[192,1024]{1,0:T(8,128)(2,1)S(1)}, u32[]{:S(2)}, u32[]{:S(2)}) collective-permute-start(bf16[192,1024]{1,0:T(8,128)(2,1)} %collective-permute-done.3.refs_4_), channel_id=1, source_target_pairs={{0,2},{2,0},{4,6},{6,4},{8,10},{10,8},{12,14},{14,12},{1,3},{3,1},... | collective-permute-start | bytes 1179656 | tf_op jit(solution)/shard_map/ppermute | solution.py:568
  49.1 11.6 %copy-start.25 = (bf16[192,1024]{1,0:T(8,128)(2,1)}, bf16[192,1024]{1,0:T(8,128)(2,1)S(1)}, u32[]{:S(2)}) copy-start(bf16[192,1024]{1,0:T(8,128)(2,1)S(1)} %collective-permute-done.7.refs_6_) | copy-start | bytes 1179652
  49.1 11.6 %copy-start.26 = (bf16[192,1024]{1,0:T(8,128)(2,1)}, bf16[192,1024]{1,0:T(8,128)(2,1)S(1)}, u32[]{:S(2)}) copy-start(bf16[192,1024]{1,0:T(8,128)(2,1)S(1)} %collective-permute-done.6.refs_5_) | copy-start | bytes 1179652
  49.1 19.4 %collective-permute-start.13 = (bf16[512,1536]{1,0:T(8,128)(2,1)}, bf16[512,1536]{1,0:T(8,128)(2,1)S(1)}, u32[]{:S(2)}, u32[]{:S(2)}) collective-permute-start(bf16[512,1536]{1,0:T(8,128)(2,1)} %collective-permute-done.12.refs_10_), channel_id=1, source_target_pairs={{0,1},{1,0},{2,3},{3,2},{4,5},{5,4},{6,7},{7,6},{8,9},{9,8},{10,11... | collective-permute-start | bytes 4718600 | tf_op jit(solution)/shard_map/ppermute | solution.py:570
  49.2 11.5 %collective-permute-start.11 = (bf16[192,1024]{1,0:T(8,128)(2,1)S(1)}, bf16[192,1024]{1,0:T(8,128)(2,1)S(1)}, u32[]{:S(2)}, u32[]{:S(2)}) collective-permute-start(bf16[192,1024]{1,0:T(8,128)(2,1)S(1)} %collective-permute-done.7.refs_6_), channel_id=1, source_target_pairs={{0,2},{2,0},{4,6},{6,4},{8,10},{10,8},{12,14},{14,12},{1,3},{3,1},... | collective-permute-start | bytes 1179656 | tf_op jit(solution)/shard_map/ppermute | solution.py:568
  68.5 10.2 %copy-start = (bf16[1024,768]{1,0:T(8,128)(2,1)S(1)}, bf16[1024,768]{1,0:T(8,128)(2,1)}, u32[]{:S(2)}) copy-start(bf16[1024,768]{1,0:T(8,128)(2,1)} %near_ref.1) | copy-start | bytes 4718596
  81.2 11.7 %copy-start.10 = (bf16[384,384]{1,0:T(8,128)(2,1)S(1)}, bf16[384,384]{1,0:T(8,128)(2,1)}, u32[]{:S(2)}) copy-start(bf16[384,384]{1,0:T(8,128)(2,1)} %copy-done.9) | copy-start | bytes 884740
  81.2 11.7 %all-to-all-start.1 = ((bf16[8,16,256]{2,1,0:T(8,128)(2,1)}), bf16[8,16,256]{2,1,0:T(8,128)(2,1)S(1)}, u32[]{:S(2)}, u32[]{:S(2)}) async-start(bf16[8,16,256]{2,1,0:T(8,128)(2,1)} %get-tuple-element.16), calls=%async_computation.1 | async-start | bytes 131072 | tf_op jit(solution)/shard_map/all_to_all | solution.py:591
  (18 other events, 41.1 us)

commit v6 on v5

--- a/solution.py
+++ b/solution.py
@@ -15,6 +15,7 @@
 NORM_ROWS = 16
 LANES = 128
 UNIT_ROWS = 16
+ROW_TILE = 16
 MLP_VMEM = 32 * 1024 * 1024
 NORM_VMEM = 8 * 1024 * 1024
 SMALL_VMEM = 4 * 1024 * 1024
@@ -29,6 +30,10 @@
 
 def in_hbm(*arrays):
     return [pltpu.with_memory_space_constraint(x, pltpu.HBM) for x in arrays]
+
+
+def in_vmem(*arrays):
+    return [pltpu.with_memory_space_constraint(x, pltpu.VMEM) for x in arrays]
 
 
 def norm_kernel(flip, tiles_ref, gain_ref, out_ref, rows, hidden, in_sems, out_sems):
@@ -91,7 +96,10 @@
         self.ny, self.nz, self.depth = ny, n_dev // ny, depth
         self.pair = ny * depth
         self.relative = self.pair % LANES == 0
-        self.early = self.nz // 2 * self.pair if self.relative else 0
+        self.early_steps = self.nz - 1
+        self.early = self.early_steps * self.pair if self.relative else 0
+        cut = max(ROW_TILE, depth // 2 // ROW_TILE * ROW_TILE)
+        self.parts = [slice(0, cut), slice(cut, depth)]
         self.width = n_dev * depth
 
     def place(self):
@@ -107,14 +115,15 @@
     def block_copies(self, blocks, weights, sems):
         _, my_y = self.place()
         copies = []
+        n_parts = len(self.parts)
         for k, block in enumerate(blocks):
-            step, flip = k // self.ny, k % self.ny
+            step, flip, part = k // n_parts // self.ny, k // n_parts % self.ny, k % n_parts
             y = 1 - my_y if flip else my_y
             at = step if self.relative else self.source(step)
-            start = pl.multiple_of(at * self.pair + y * self.depth, self.depth)
-            copies.append(
-                pltpu.make_async_copy(block, weights.at[pl.ds(start, self.depth)], sems.at[k])
-            )
+            here = self.parts[part]
+            start = pl.multiple_of(at * self.pair + y * self.depth + here.start, ROW_TILE)
+            place = weights.at[pl.ds(start, here.stop - here.start)]
+            copies.append(pltpu.make_async_copy(block, place, sems.at[k]))
         return copies
 
     def row_copies(self, tiles_ref, rows, sems, steps):
@@ -155,8 +164,8 @@
 
 
 def early_kernel(layout, *refs):
-    steps = range(layout.nz // 2)
-    n_blocks = len(steps) * layout.ny
+    steps = range(layout.early_steps)
+    n_blocks = len(steps) * layout.ny * len(layout.parts)
     blocks, tile_refs = refs[:n_blocks], refs[n_blocks : n_blocks + 2]
     out_ref, weights, rows, sums, weight_sems, row_sems, out_sems = refs[n_blocks + 2 :]
     loads = layout.block_copies(blocks, weights, weight_sems)
@@ -197,12 +206,16 @@
             pltpu.SemaphoreType.DMA((2,)),
         ],
         compiler_params=pltpu.CompilerParams(vmem_limit_bytes=MLP_VMEM),
-        cost_estimate=pl.CostEstimate(flops=0, bytes_accessed=0, transcendentals=0),
+        cost_estimate=pl.CostEstimate(
+            flops=4 * n_rows * layout.early * cols,
+            bytes_accessed=2 * layout.early * (cols + 2 * n_rows) + 8 * n_rows * cols,
+            transcendentals=0,
+        ),
     )(*in_hbm(*blocks, *tiles))
 
 
 def middle_kernel(layout, length, *refs):
-    n_blocks = layout.nz * layout.ny
+    n_blocks = layout.nz * layout.ny * len(layout.parts)
     n_sums = 1 if layout.relative else 0
     blocks, tile_refs = refs[:n_blocks], refs[n_blocks : n_blocks + 3]
     sum_refs = refs[n_blocks + 3 : n_blocks + 3 + n_sums]
@@ -211,7 +224,7 @@
     ]
     early = layout.early
     loads = layout.block_copies(blocks, weights, weight_sems)
-    late_blocks = early // layout.depth
+    late_blocks = early // layout.depth * len(layout.parts)
     steps = [range(early // layout.pair, layout.nz)] * 2 + [range(layout.nz)]
     row_loads = [
         layout.row_copies(ref, rows.at[i], row_sems.at[i], steps[i])
@@ -271,11 +284,11 @@
             bytes_accessed=2 * (3 * n_rows * width + width * cols) + 8 * n_rows * cols,
             transcendentals=0,
         ),
-    )(*in_hbm(*blocks[:-1]), blocks[-1], *in_hbm(*tiles, *sums))
+    )(*in_hbm(*blocks[:-2]), *blocks[-2:], *in_hbm(*tiles, *sums))
 
 
 def last_kernel(layout, length, n_grp, n_sub, means_ref, *refs):
-    n_blocks = layout.nz * layout.ny
+    n_blocks = layout.nz * layout.ny * len(layout.parts)
     blocks, tiles_ref = refs[:n_blocks], refs[n_blocks]
     out_ref, weights, rows, both, means, weight_sems, row_sems = refs[n_blocks + 1 :]
     loads = layout.block_copies(blocks, weights, weight_sems)
@@ -338,7 +351,7 @@
             bytes_accessed=2 * (n_rows * width + width * cols),
             transcendentals=0,
         ),
-    )(means, *in_hbm(*blocks[:-1]), blocks[-1], tiles)
+    )(means, *in_hbm(*blocks[:-2]), *blocks[-2:], tiles)
 
 
 def small_mod(value, rate):
@@ -436,11 +449,23 @@
     )
 
 
-def query_kernel(heads, mixed_ref, gain_ref, wq_ref, wq_far_ref, out_ref):
+def query_kernel(heads, mixed_ref, gain_ref, *refs):
+    n_in = (len(refs) - 1) // 2
+    weights, (out_ref, *kept), (wq, sems) = refs[:n_in], refs[n_in:-2], refs[-2:]
+    copies = [
+        pltpu.make_async_copy(weight, place, sems.at[k])
+        for k, (weight, place) in enumerate(zip(weights, [wq.at[0], wq.at[1], *kept]))
+    ]
+    for copy in copies:
+        copy.start()
     hidden = normed(mixed_ref[...], gain_ref[...].reshape(1, -1))
-    query = project(hidden, wq_ref, wq_far_ref)
+    for copy in copies[:2]:
+        copy.wait()
+    query = project(hidden, wq.at[0], wq.at[1])
     spread = jnp.concatenate([query] * heads, axis=0)
     out_ref[...] = jnp.where(heads_of(spread.shape), spread, 0.0).astype(jnp.bfloat16)
+    for copy in copies[2:]:
+        copy.wait()
 
 
 def slide_kernel(
@@ -449,13 +474,13 @@
     sent_ref,
     mixed_ref,
     query_ref,
-    many_ref,
     wk_ref,
     wk_far_ref,
     wv_ref,
     wv_far_ref,
     wo_ref,
     wo_far_ref,
+    many_ref,
     out_ref,
     rows,
 ):
@@ -525,15 +550,18 @@
     along_y = [(d, d ^ 1) for d in range(n_dev)]
 
     half_cols = hidden_cols // 2
-    block = jnp.concatenate(
-        [
-            lax.dynamic_slice_in_dim(w, (group % 2) * half_cols, half_cols, 1)
-            for w in (gate_weight, up_weight)
-        ],
-        axis=1,
-    )
     layout = Layout(n_dev, ny, gate_weight.shape[0])
-    first = norm_tiles(tiles, after(tile_gain, block), False)
+    held = [
+        jnp.concatenate(
+            [
+                lax.dynamic_slice_in_dim(w[part], (group % 2) * half_cols, half_cols, 1)
+                for w in (gate_weight, up_weight)
+            ],
+            axis=1,
+        )
+        for part in layout.parts
+    ]
+    first = norm_tiles(tiles, tile_gain, False)
     second = norm_tiles(tiles, tile_gain, True)
     pair_first = lax.ppermute(first, "grp", to_pair)
 
@@ -555,18 +583,26 @@
         compiler_params=pltpu.CompilerParams(vmem_limit_bytes=SMALL_VMEM),
     )(counts, slide_of, rates)
 
-    beside = {1: [first, second], 2: [proj_far, wq_far], 3: [wk_far, wv_far, wo_far, many]}
-    blocks = []
+    held[1] = after(held[1], first, proj_far, wq_far, many)
+    steps = []
+    last = None
+    for step in range(nz):
+        sent = []
+        for part in range(len(held)):
+            if step:
+                arrived = lax.ppermute(held[part], "dev", along_z)
+                others = [steps[-1][len(held) + part]]
+                if last is not None:
+                    others.append(last)
+                held[part] = last = after(arrived, *others)
+            sent.append(lax.ppermute(held[part], "dev", along_y))
+        steps.append([*held, *sent])
+    blocks = [block for step in steps for block in step]
     sums = []
-    for step in range(nz):
-        if step:
-            block = lax.ppermute(block, "dev", along_z)
-            others = beside.get(step, [])
-            if layout.relative and step == nz - 1:
-                sums = [early_mlp(layout, blocks[: nz // 2 * ny], [first, second])]
-            block = after(block, blocks[-1], *others, *sums)
-        blocks += [block, lax.ppermute(block, "dev", along_y)]
-    pair_first = after(pair_first, block)
+    if layout.relative:
+        early_blocks = blocks[: layout.early_steps * len(steps[0])]
+        sums = [early_mlp(layout, early_blocks, [after(first, last, wk_far, wv_far, wo_far), second])]
+    pair_first = after(pair_first, *steps[-1][-2:], *sums)
     pair_second = lax.ppermute(pair_first, "sub", to_sibling)
 
     means = middle_mlp(layout, blocks, [first, second, pair_first], sums, length)
@@ -583,19 +619,28 @@
         out_specs=(vmem, vmem, vmem),
         out_shape=(
             jax.ShapeDtypeStruct((slot_count, hidden_cols), jnp.bfloat16),
-            jax.ShapeDtypeStruct((QROWS, out_width), jnp.float32),
-            jax.ShapeDtypeStruct((n_dev, sent_rows, sent_cols), jnp.bfloat16),
+            pltpu.VMEM((QROWS, out_width), jnp.float32),
+            pltpu.VMEM((n_dev, sent_rows, sent_cols), jnp.bfloat16),
         ),
         compiler_params=small,
-    )(counts, parts, slide_gain, embed_proj, proj_far)
+    )(counts, *in_vmem(parts), slide_gain, embed_proj, proj_far)
     sent = lax.all_to_all(sent, "dev", split_axis=0, concat_axis=0, tiled=True)
-    query = pl.pallas_call(
+    hbm = pl.BlockSpec(memory_space=pltpu.HBM)
+    weights = [slide_wk, wk_far, slide_wv, wv_far, slide_wo, wo_far, many]
+    query, *weights = pl.pallas_call(
         functools.partial(query_kernel, heads),
-        in_specs=[vmem] * 4,
-        out_specs=vmem,
-        out_shape=jax.ShapeDtypeStruct((heads * QROWS, out_width), jnp.bfloat16),
+        in_specs=[vmem] * 2 + [hbm] * (2 + len(weights)),
+        out_specs=[vmem] * (1 + len(weights)),
+        out_shape=[
+            pltpu.VMEM((heads * QROWS, out_width), jnp.bfloat16),
+            *[pltpu.VMEM(x.shape, x.dtype) for x in weights],
+        ],
+        scratch_shapes=[
+            pltpu.VMEM((2, *slide_wq.shape), jnp.bfloat16),
+            pltpu.SemaphoreType.DMA((2 + len(weights),)),
+        ],
         compiler_params=small,
-    )(mixed, slide_gain, slide_wq, wq_far)
+    )(*in_vmem(mixed), slide_gain, *in_hbm(slide_wq, wq_far, *weights))
     slide_out = pl.pallas_call(
         functools.partial(slide_kernel, heads),
         in_specs=[smem] + [vmem] * 10,
@@ -603,7 +648,7 @@
         out_shape=jax.ShapeDtypeStruct((slot_count, out_cols), jnp.bfloat16),
         scratch_shapes=[pltpu.VMEM((n_dev * slot_count, out_width), jnp.float32)],
         compiler_params=small,
-    )(counts, sent, mixed, query, many, slide_wk, wk_far, slide_wv, wv_far, slide_wo, wo_far)
+    )(counts, *in_vmem(sent, mixed, query, *weights))
     return (tile_embed, slide_out)
 
 

time: 101 us -> 91.2 us (0.903)
  waiting for transfers between devices: 32.8 us -> 22.2 us
  local copies, waits for them, and re-layouts: 12.3 us -> 2.17 us
  starting transfers between devices: 17.1 us -> 25.8 us
  Pallas kernels: 30.9 us -> 33.5 us
    ppermute x7 -> x14, waiting for transfers between devices: 28.8 us -> 17.6 us  [the longest x6 10.8 us: on_device(): arrived = lax.ppermute(held[part], 'dev', along_z)]
    ppermute x7 -> x14, starting transfers between devices: 8.63 us -> 18.8 us  [the longest x8 10.8 us: on_device(): sent.append(lax.ppermute(held[part], 'dev', along_y))]
    unnamed x54 -> x44, local copies, waits for them, and re-layouts: 11.2 us -> 2.05 us
    pallas_call x1, Pallas kernels: 5.13 us -> 7.03 us  [early_mlp(): pl.pallas_call(functools.partial(early_kernel, layout), in_specs=[hbm] *...]
    all_to_all x1, starting transfers between devices: 4.75 us -> 3.35 us  [on_device(): sent = lax.all_to_all(sent, 'dev', split_axis=0, concat_axis=0, tiled=True)]
    dynamic_slice x1 -> x2, local copies, waits for them, and re-layouts: 1.05 us -> 0.04 us  [on_device(): lax.dynamic_slice_in_dim(w[part], group % 2 * half_cols, half_cols, 1)]
  transfers between devices with their start and end apart: 15 -> 22, of which waited for: 5 -> 10; matrix products, arithmetic and copies ran while one was open for 1% -> 0% of each run, Pallas kernels for 23% -> 28%
where the time goes in v6:
time: 91.2 us; the launch traced here: 90.9 us
  Pallas kernels  33.5 us (37%)
  starting transfers between devices  25.8 us (28%)
  waiting for transfers between devices  22.2 us (24%)
  blocking collectives  6.21 us (7%)
  local copies, waits for them, and re-layouts  2.17 us (2%)
  between operations  0.97 us (1%)
    ppermute x6, waiting for transfers between devices, on_device(): arrived = lax.ppermute(held[part], 'dev', along_z)  10.8 us
    ppermute x8, starting transfers between devices, on_device(): sent.append(lax.ppermute(held[part], 'dev', along_y))  10.8 us
    ppermute x6, starting transfers between devices, on_device(): arrived = lax.ppermute(held[part], 'dev', along_z)  7.99 us
    pallas_call x2, Pallas kernels, norm_tiles(): pl.pallas_call(functools.partial(norm_kernel, flip), in_specs=[hbm, pl.Bl...  7.89 us
    pallas_call x1, Pallas kernels, middle_mlp(): pl.pallas_call(functools.partial(middle_kernel, layout, length), in_specs...  7.55 us
    pallas_call x1, Pallas kernels, early_mlp(): pl.pallas_call(functools.partial(early_kernel, layout), in_specs=[hbm] *...  7.03 us
    ppermute x8, waiting for transfers between devices, on_device(): sent.append(lax.ppermute(held[part], 'dev', along_y))  6.82 us
    all_to_all x1, blocking collectives, on_device(): lax.all_to_all(parts, ('grp', 'sub'), split_axis=0, concat_axis=0, tiled=...  6.21 us
  transfers between devices with their start and end apart: 22, of which 10 were waited for; matrix products, arithmetic and copies ran while one was open for 0% of the time, Pallas kernels for 28%

profile of v6, /device:TPU:0, one launch (start us, length us, event | category | flops | bytes accessed | tf_op | source)
XLA Modules:
  0.0 90.9 jit_solution(15992618436560018131)
XLA Ops:
  1.9 4.0 %shard_map.140.refs_12_.refs_16_ = bf16[512,1536]{1,0:T(8,128)(2,1)} custom-call(bf16[4,256,1536]{2,1,0:T(8,128)(2,1)} %tiles_ref.3, f32[1536]{0:T(1024)S(1)} %copy-done.2), custom_call_target="tpu_custom_call" | custom-call | tf_op jit(solution)/shard_map/pallas_call | solution.py:74
  5.9 3.0 %collective-permute-start.16 = (bf16[512,1536]{1,0:T(8,128)(2,1)}, bf16[512,1536]{1,0:T(8,128)(2,1)}, u32[]{:S(2)}, u32[]{:S(2)}) collective-permute-start(bf16[512,1536]{1,0:T(8,128)(2,1)} %shard_map.140.refs_12_.refs_16_), channel_id=1, source_target_pairs={{0,16},{16,0},{1,17},{17,1},{2,18},{18,2},{3,19},{19,3},{4,20},{20... | collective-permute-start | bytes 4718600 | tf_op jit(solution)/shard_map/ppermute | solution.py:566
  9.1 1.6 %collective-permute-start.4 = (bf16[96,1024]{1,0:T(8,128)(2,1)S(1)}, bf16[96,1024]{1,0:T(8,128)(2,1)S(1)}, u32[]{:S(2)}, u32[]{:S(2)}) collective-permute-start(bf16[96,1024]{1,0:T(8,128)(2,1)S(1)} %pad_maximum_fusion.refs_0_), channel_id=1, source_target_pairs={{0,4},{2,6},{4,8},{6,10},{8,12},{10,14},{12,0},{14,2},{1,5},{3,7},... | collective-permute-start | bytes 589832 | tf_op jit(solution)/shard_map/ppermute | solution.py:593
  10.7 1.5 %collective-permute-start.2 = (bf16[96,1024]{1,0:T(8,128)(2,1)S(1)}, bf16[96,1024]{1,0:T(8,128)(2,1)S(1)}, u32[]{:S(2)}, u32[]{:S(2)}) collective-permute-start(bf16[96,1024]{1,0:T(8,128)(2,1)S(1)} %pad_maximum_fusion.refs_0_), channel_id=1, source_target_pairs={{0,2},{2,0},{4,6},{6,4},{8,10},{10,8},{12,14},{14,12},{1,3},{3,1},... | collective-permute-start | bytes 589832 | tf_op jit(solution)/shard_map/ppermute | solution.py:598
  13.6 1.6 %collective-permute-start.5 = (bf16[96,1024]{1,0:T(8,128)(2,1)S(1)}, bf16[96,1024]{1,0:T(8,128)(2,1)S(1)}, u32[]{:S(2)}, u32[]{:S(2)}) collective-permute-start(bf16[96,1024]{1,0:T(8,128)(2,1)S(1)} %pad_maximum_fusion.1.refs_1_), channel_id=1, source_target_pairs={{0,4},{2,6},{4,8},{6,10},{8,12},{10,14},{12,0},{14,2},{1,5},{3,7},... | collective-permute-start | bytes 589832 | tf_op jit(solution)/shard_map/ppermute | solution.py:593
  15.7 2.2 %collective-permute-done.4.refs_4_ = bf16[96,1024]{1,0:T(8,128)(2,1)S(1)} collective-permute-done((bf16[96,1024]{1,0:T(8,128)(2,1)S(1)}, bf16[96,1024]{1,0:T(8,128)(2,1)S(1)}, u32[]{:S(2)}, u32[]{:S(2)}) %collective-permute-start.4) | collective-permute-done | bytes 196640 | tf_op jit(solution)/shard_map/ppermute | solution.py:593
  18.9 2.5 %collective-permute-start.6 = (bf16[96,1024]{1,0:T(8,128)(2,1)S(1)}, bf16[96,1024]{1,0:T(8,128)(2,1)S(1)}, u32[]{:S(2)}, u32[]{:S(2)}) collective-permute-start(bf16[96,1024]{1,0:T(8,128)(2,1)S(1)} %collective-permute-done.4.refs_4_), channel_id=1, source_target_pairs={{0,2},{2,0},{4,6},{6,4},{8,10},{10,8},{12,14},{14,12},{1,3},{3,1},... | collective-permute-start | bytes 589832 | tf_op jit(solution)/shard_map/ppermute | solution.py:598
  22.9 1.6 %collective-permute-start.9 = (bf16[96,1024]{1,0:T(8,128)(2,1)S(1)}, bf16[96,1024]{1,0:T(8,128)(2,1)}, u32[]{:S(2)}, u32[]{:S(2)}) collective-permute-start(bf16[96,1024]{1,0:T(8,128)(2,1)S(1)} %collective-permute-done.5.refs_5_), channel_id=1, source_target_pairs={{0,4},{2,6},{4,8},{6,10},{8,12},{10,14},{12,0},{14,2},{1,5},{3,7},... | collective-permute-start | bytes 589832 | tf_op jit(solution)/shard_map/ppermute | solution.py:593
  25.6 1.6 %collective-permute-done.8.refs_8_ = bf16[96,1024]{1,0:T(8,128)(2,1)} collective-permute-done((bf16[96,1024]{1,0:T(8,128)(2,1)S(1)}, bf16[96,1024]{1,0:T(8,128)(2,1)}, u32[]{:S(2)}, u32[]{:S(2)}) %collective-permute-start.8) | collective-permute-done | bytes 196640 | tf_op jit(solution)/shard_map/ppermute | solution.py:593
  27.2 2.0 %collective-permute-start.12 = (bf16[96,1024]{1,0:T(8,128)(2,1)}, bf16[96,1024]{1,0:T(8,128)(2,1)}, u32[]{:S(2)}, u32[]{:S(2)}) collective-permute-start(bf16[96,1024]{1,0:T(8,128)(2,1)} %collective-permute-done.8.refs_8_), channel_id=1, source_target_pairs={{0,4},{2,6},{4,8},{6,10},{8,12},{10,14},{12,0},{14,2},{1,5},{3,7},... | collective-permute-start | bytes 589832 | tf_op jit(solution)/shard_map/ppermute | solution.py:593
  29.2 2.3 %collective-permute-done.9.refs_9_ = bf16[96,1024]{1,0:T(8,128)(2,1)} collective-permute-done((bf16[96,1024]{1,0:T(8,128)(2,1)S(1)}, bf16[96,1024]{1,0:T(8,128)(2,1)}, u32[]{:S(2)}, u32[]{:S(2)}) %collective-permute-start.9) | collective-permute-done | bytes 196640 | tf_op jit(solution)/shard_map/ppermute | solution.py:593
  32.2 2.3 %collective-permute-start.10 = (bf16[96,1024]{1,0:T(8,128)(2,1)}, bf16[96,1024]{1,0:T(8,128)(2,1)}, u32[]{:S(2)}, u32[]{:S(2)}) collective-permute-start(bf16[96,1024]{1,0:T(8,128)(2,1)} %collective-permute-done.8.refs_8_), channel_id=1, source_target_pairs={{0,2},{2,0},{4,6},{6,4},{8,10},{10,8},{12,14},{14,12},{1,3},{3,1},... | collective-permute-start | bytes 589832 | tf_op jit(solution)/shard_map/ppermute | solution.py:598
  35.2 5.2 %collective-permute-done.10.refs_10_ = bf16[96,1024]{1,0:T(8,128)(2,1)} collective-permute-done((bf16[96,1024]{1,0:T(8,128)(2,1)}, bf16[96,1024]{1,0:T(8,128)(2,1)}, u32[]{:S(2)}, u32[]{:S(2)}) %collective-permute-start.10) | collective-permute-done | bytes 196640 | tf_op jit(solution)/shard_map/ppermute | solution.py:598
  40.4 3.2 %collective-permute-done.13.refs_13_ = bf16[96,1024]{1,0:T(8,128)(2,1)S(1)} collective-permute-done((bf16[96,1024]{1,0:T(8,128)(2,1)}, bf16[96,1024]{1,0:T(8,128)(2,1)S(1)}, u32[]{:S(2)}, u32[]{:S(2)}) %collective-permute-start.13) | collective-permute-done | bytes 196640 | tf_op jit(solution)/shard_map/ppermute | solution.py:593
  44.3 3.9 %shard_map.142.refs_13_.refs_17_ = bf16[512,1536]{1,0:T(8,128)(2,1)} custom-call(bf16[4,256,1536]{2,1,0:T(8,128)(2,1)} %tiles_ref.3, f32[1536]{0:T(1024)S(1)} %copy-done.3), custom_call_target="tpu_custom_call" | custom-call | tf_op jit(solution)/shard_map/pallas_call | solution.py:74
  51.6 7.0 %shard_map.143.refs_19_ = f32[2,512,1024]{2,1,0:T(8,128)} custom-call(bf16[96,1024]{1,0:T(8,128)(2,1)} %copy-done.8, bf16[96,1024]{1,0:T(8,128)(2,1)} %copy-done.9, bf16[96,1024]{1,0:T(8,128)(2,1)} %copy-done.12, bf16[96,1024]{1,0:T(8,128)(2,1)} %copy-done.14, bf16[96,1024]{1,0:T(8,128)(2,1)} %copy-done.11, bf16[96,1024]{1,0:T(8,128)(2,1)} %copy-done.13, ...), custom_call_target="tpu_custom_call" | custom-call | flops 2415919104 | bytes 8912896 | tf_op jit(solution)/shard_map/pallas_call | solution.py:195
  58.8 7.6 %shard_map.144.means_ref = f32[6,512]{1,0:T(8,128)S(1)} custom-call(bf16[96,1024]{1,0:T(8,128)(2,1)} %copy-done.8, bf16[96,1024]{1,0:T(8,128)(2,1)} %copy-done.9, bf16[96,1024]{1,0:T(8,128)(2,1)} %copy-done.12, bf16[96,1024]{1,0:T(8,128)(2,1)} %copy-done.14, bf16[96,1024]{1,0:T(8,128)(2,1)} %copy-done.11, bf16[96,1024]{1,0:T(8,128)(2,1)} %copy-done.13, ...), custom_call_target="tpu_custom_call" | custom-call | flops 3221225472 | bytes 12058624 | tf_op jit(solution)/shard_map/pallas_call | solution.py:266
  66.4 4.1 %shard_map.145 = bf16[4,16,128]{2,1,0:T(8,128)(2,1)S(1)} custom-call(f32[6,512]{1,0:T(8,128)S(1)} %shard_map.144.means_ref, bf16[96,1024]{1,0:T(8,128)(2,1)} %copy-done.8, bf16[96,1024]{1,0:T(8,128)(2,1)} %copy-done.9, bf16[96,1024]{1,0:T(8,128)(2,1)} %copy-done.12, bf16[96,1024]{1,0:T(8,128)(2,1)} %copy-done.14, bf16[96,1024]{1,0:T(8,128)(2,1)} %copy-done.11, ...), custom_call_target="tpu_custom_call" | custom-call | flops 1610612736 | bytes 4718592 | tf_op jit(solution)/shard_map/pallas_call | solution.py:333
  70.5 6.2 %all_to_all.10.parts_ref = bf16[4,16,128]{2,1,0:T(8,128)(2,1)S(1)} all-to-all(bf16[4,16,128]{2,1,0:T(8,128)(2,1)S(1)} %shard_map.145), channel_id=1, replica_groups=mesh['grp'=2,'dev'=8,'sub'=2] {'grp','sub'}, dimensions={0} | all-to-all | bytes 32768 | tf_op jit(solution)/shard_map/all_to_all | solution.py:610
  76.7 1.9 %shard_map.146 = (bf16[4,1024]{1,0:T(4,128)(2,1)}, f32[8,768]{1,0:T(8,128)S(1)}, bf16[8,16,256]{2,1,0:T(8,128)(2,1)}) custom-call(s32[8]{0:T(128)S(1)} %copy-done.5, bf16[4,16,128]{2,1,0:T(8,128)(2,1)S(1)} %all_to_all.10.parts_ref, f32[768]{0:T(1024)S(1)} %copy-done.4, bf16[1024,768]{1,0:T(8,128)(2,1)S(1)} %copy-done, ...), custom_call_target="tpu_custom_call" | custom-call | tf_op jit(solution)/shard_map/pallas_call | solution.py:616
  78.6 3.3 %all-to-all-start.1 = ((bf16[8,16,256]{2,1,0:T(8,128)(2,1)}), bf16[8,16,256]{2,1,0:T(8,128)(2,1)S(1)}, u32[]{:S(2)}, u32[]{:S(2)}) async-start(bf16[8,16,256]{2,1,0:T(8,128)(2,1)} %get-tuple-element.32), calls=%async_computation.1 | async-start | bytes 131072 | tf_op jit(solution)/shard_map/all_to_all | solution.py:627
  81.9 2.3 %shard_map.147 = (bf16[96,768]{1,0:T(8,128)(2,1)S(1)}, bf16[768,384]{1,0:T(8,128)(2,1)S(1)}, bf16[768,384]{1,0:T(8,128)(2,1)S(1)}, bf16[768,384]{1,0:T(8,128)(2,...) custom-call(f32[8,768]{1,0:T(8,128)S(1)} %get-tuple-element.33.mixed, ...), custom_call_target="tpu_custom_call" | custom-call | tf_op jit(solution)/shard_map/pallas_call | solution.py:630
  84.2 4.5 %all-to-all-done.1.sent_ref = bf16[8,16,256]{2,1,0:T(8,128)(2,1)S(1)} async-done(((bf16[8,16,256]{2,1,0:T(8,128)(2,1)}), bf16[8,16,256]{2,1,0:T(8,128)(2,1)S(1)}, u32[]{:S(2)}, u32[]{:S(2)}) %all-to-all-start.1) | async-done | bytes 65568 | tf_op jit(solution)/shard_map/all_to_all | solution.py:627
  88.8 2.1 %shard_map.148 = bf16[4,384]{1,0:T(4,128)(2,1)} custom-call(s32[8]{0:T(128)S(1)} %copy-done.5, bf16[8,16,256]{2,1,0:T(8,128)(2,1)S(1)} %all-to-all-done.1.sent_ref, f32[8,768]{1,0:T(8,128)S(1)} %get-tuple-element.33.mixed_ref, bf16[96,768]{1,0:T(8,128)(2,1)S(1)} %get-tuple-element.34.query_ref, bf16[768,384]{1,0:T(8,128)(2,1)S(1)} %get-tuple-element.35.wk_ref, ...), custom_call_target="tpu_custom_call" | custom-call | tf_op jit(solution)/shard_map/pallas_call | solution.py:644
  (81 shorter events, 12.4 us)
Async XLA Ops:
  0.6 13.0 %collective-permute-start = (bf16[1024,768]{1,0:T(8,128)(2,1)}, bf16[1024,768]{1,0:T(8,128)(2,1)S(1)}, u32[]{:S(2)}, u32[]{:S(2)}) collective-permute-start(bf16[1024,768]{1,0:T(8,128)(2,1)} %near_ref.1), channel_id=1, source_target_pairs={{0,1},{1,0},{2,3},{3,2},{4,5},{5,4},{6,7},{7,6},{8,9},{9,8},{10,11... | collective-permute-start | bytes 4718600 | tf_op jit(solution)/shard_map/ppermute | solution.py:568
  1.1 12.5 %collective-permute-start.1 = (bf16[768,384]{1,0:T(8,128)(2,1)}, bf16[768,384]{1,0:T(8,128)(2,1)}, u32[]{:S(2)}, u32[]{:S(2)}) collective-permute-start(bf16[768,384]{1,0:T(8,128)(2,1)} %refs_0_.1), channel_id=1, source_target_pairs={{0,1},{1,0},{2,3},{3,2},{4,5},{5,4},{6,7},{7,6},{8,9},{9,8},{10,11... | collective-permute-start | bytes 1769480 | tf_op jit(solution)/shard_map/ppermute | solution.py:569
  5.9 52.8 %collective-permute-start.16 = (bf16[512,1536]{1,0:T(8,128)(2,1)}, bf16[512,1536]{1,0:T(8,128)(2,1)}, u32[]{:S(2)}, u32[]{:S(2)}) collective-permute-start(bf16[512,1536]{1,0:T(8,128)(2,1)} %shard_map.140.refs_12_.refs_16_), channel_id=1, source_target_pairs={{0,16},{16,0},{1,17},{17,1},{2,18},{18,2},{3,19},{19,3},{4,20},{20... | collective-permute-start | bytes 4718600 | tf_op jit(solution)/shard_map/ppermute | solution.py:566
  9.1 39.2 %copy-start.8 = (bf16[96,1024]{1,0:T(8,128)(2,1)}, bf16[96,1024]{1,0:T(8,128)(2,1)S(1)}, u32[]{:S(2)}) copy-start(bf16[96,1024]{1,0:T(8,128)(2,1)S(1)} %pad_maximum_fusion.refs_0_) | copy-start | bytes 589828
  9.1 8.8 %collective-permute-start.4 = (bf16[96,1024]{1,0:T(8,128)(2,1)S(1)}, bf16[96,1024]{1,0:T(8,128)(2,1)S(1)}, u32[]{:S(2)}, u32[]{:S(2)}) collective-permute-start(bf16[96,1024]{1,0:T(8,128)(2,1)S(1)} %pad_maximum_fusion.refs_0_), channel_id=1, source_target_pairs={{0,4},{2,6},{4,8},{6,10},{8,12},{10,14},{12,0},{14,2},{1,5},{3,7},... | collective-permute-start | bytes 589832 | tf_op jit(solution)/shard_map/ppermute | solution.py:593
  10.7 7.2 %collective-permute-start.2 = (bf16[96,1024]{1,0:T(8,128)(2,1)S(1)}, bf16[96,1024]{1,0:T(8,128)(2,1)S(1)}, u32[]{:S(2)}, u32[]{:S(2)}) collective-permute-start(bf16[96,1024]{1,0:T(8,128)(2,1)S(1)} %pad_maximum_fusion.refs_0_), channel_id=1, source_target_pairs={{0,2},{2,0},{4,6},{6,4},{8,10},{10,8},{12,14},{14,12},{1,3},{3,1},... | collective-permute-start | bytes 589832 | tf_op jit(solution)/shard_map/ppermute | solution.py:598
  12.3 39.3 %copy-start.9 = (bf16[96,1024]{1,0:T(8,128)(2,1)}, bf16[96,1024]{1,0:T(8,128)(2,1)S(1)}, u32[]{:S(2)}) copy-start(bf16[96,1024]{1,0:T(8,128)(2,1)S(1)} %pad_maximum_fusion.1.refs_1_) | copy-start | bytes 589828
  13.6 8.9 %collective-permute-start.5 = (bf16[96,1024]{1,0:T(8,128)(2,1)S(1)}, bf16[96,1024]{1,0:T(8,128)(2,1)S(1)}, u32[]{:S(2)}, u32[]{:S(2)}) collective-permute-start(bf16[96,1024]{1,0:T(8,128)(2,1)S(1)} %pad_maximum_fusion.1.refs_1_), channel_id=1, source_target_pairs={{0,4},{2,6},{4,8},{6,10},{8,12},{10,14},{12,0},{14,2},{1,5},{3,7},... | collective-permute-start | bytes 589832 | tf_op jit(solution)/shard_map/ppermute | solution.py:593
  15.2 7.7 %collective-permute-start.3 = (bf16[96,1024]{1,0:T(8,128)(2,1)S(1)}, bf16[96,1024]{1,0:T(8,128)(2,1)S(1)}, u32[]{:S(2)}, u32[]{:S(2)}) collective-permute-start(bf16[96,1024]{1,0:T(8,128)(2,1)S(1)} %pad_maximum_fusion.1.refs_1_), channel_id=1, source_target_pairs={{0,2},{2,0},{4,6},{6,4},{8,10},{10,8},{12,14},{14,12},{1,3},{3,1},... | collective-permute-start | bytes 589832 | tf_op jit(solution)/shard_map/ppermute | solution.py:598
  17.9 9.3 %collective-permute-start.8 = (bf16[96,1024]{1,0:T(8,128)(2,1)S(1)}, bf16[96,1024]{1,0:T(8,128)(2,1)}, u32[]{:S(2)}, u32[]{:S(2)}) collective-permute-start(bf16[96,1024]{1,0:T(8,128)(2,1)S(1)} %collective-permute-done.4.refs_4_), channel_id=1, source_target_pairs={{0,4},{2,6},{4,8},{6,10},{8,12},{10,14},{12,0},{14,2},{1,5},{3,7},... | collective-permute-start | bytes 589832 | tf_op jit(solution)/shard_map/ppermute | solution.py:593
  18.9 8.3 %collective-permute-start.6 = (bf16[96,1024]{1,0:T(8,128)(2,1)S(1)}, bf16[96,1024]{1,0:T(8,128)(2,1)S(1)}, u32[]{:S(2)}, u32[]{:S(2)}) collective-permute-start(bf16[96,1024]{1,0:T(8,128)(2,1)S(1)} %collective-permute-done.4.refs_4_), channel_id=1, source_target_pairs={{0,2},{2,0},{4,6},{6,4},{8,10},{10,8},{12,14},{14,12},{1,3},{3,1},... | collective-permute-start | bytes 589832 | tf_op jit(solution)/shard_map/ppermute | solution.py:598
  22.9 8.6 %collective-permute-start.9 = (bf16[96,1024]{1,0:T(8,128)(2,1)S(1)}, bf16[96,1024]{1,0:T(8,128)(2,1)}, u32[]{:S(2)}, u32[]{:S(2)}) collective-permute-start(bf16[96,1024]{1,0:T(8,128)(2,1)S(1)} %collective-permute-done.5.refs_5_), channel_id=1, source_target_pairs={{0,4},{2,6},{4,8},{6,10},{8,12},{10,14},{12,0},{14,2},{1,5},{3,7},... | collective-permute-start | bytes 589832 | tf_op jit(solution)/shard_map/ppermute | solution.py:593
  24.4 7.0 %collective-permute-start.7 = (bf16[96,1024]{1,0:T(8,128)(2,1)S(1)}, bf16[96,1024]{1,0:T(8,128)(2,1)S(1)}, u32[]{:S(2)}, u32[]{:S(2)}) collective-permute-start(bf16[96,1024]{1,0:T(8,128)(2,1)S(1)} %collective-permute-done.5.refs_5_), channel_id=1, source_target_pairs={{0,2},{2,0},{4,6},{6,4},{8,10},{10,8},{12,14},{14,12},{1,3},{3,1},... | collective-permute-start | bytes 589832 | tf_op jit(solution)/shard_map/ppermute | solution.py:598
  27.2 7.8 %collective-permute-start.12 = (bf16[96,1024]{1,0:T(8,128)(2,1)}, bf16[96,1024]{1,0:T(8,128)(2,1)}, u32[]{:S(2)}, u32[]{:S(2)}) collective-permute-start(bf16[96,1024]{1,0:T(8,128)(2,1)} %collective-permute-done.8.refs_8_), channel_id=1, source_target_pairs={{0,4},{2,6},{4,8},{6,10},{8,12},{10,14},{12,0},{14,2},{1,5},{3,7},... | collective-permute-start | bytes 589832 | tf_op jit(solution)/shard_map/ppermute | solution.py:593
  29.2 22.4 %collective-permute-start.17 = (bf16[768,384]{1,0:T(8,128)(2,1)}, bf16[768,384]{1,0:T(8,128)(2,1)}, u32[]{:S(2)}, u32[]{:S(2)}) collective-permute-start(bf16[768,384]{1,0:T(8,128)(2,1)} %refs_2_.1), channel_id=1, source_target_pairs={{0,1},{1,0},{2,3},{3,2},{4,5},{5,4},{6,7},{7,6},{8,9},{9,8},{10,11... | collective-permute-start | bytes 1769480 | tf_op jit(solution)/shard_map/ppermute | solution.py:570
  31.5 20.1 %collective-permute-start.18 = (bf16[768,384]{1,0:T(8,128)(2,1)}, bf16[768,384]{1,0:T(8,128)(2,1)}, u32[]{:S(2)}, u32[]{:S(2)}) collective-permute-start(bf16[768,384]{1,0:T(8,128)(2,1)} %refs_4_.1), channel_id=1, source_target_pairs={{0,1},{1,0},{2,3},{3,2},{4,5},{5,4},{6,7},{7,6},{8,9},{9,8},{10,11... | collective-permute-start | bytes 1769480 | tf_op jit(solution)/shard_map/ppermute | solution.py:571
  32.2 8.2 %collective-permute-start.10 = (bf16[96,1024]{1,0:T(8,128)(2,1)}, bf16[96,1024]{1,0:T(8,128)(2,1)}, u32[]{:S(2)}, u32[]{:S(2)}) collective-permute-start(bf16[96,1024]{1,0:T(8,128)(2,1)} %collective-permute-done.8.refs_8_), channel_id=1, source_target_pairs={{0,2},{2,0},{4,6},{6,4},{8,10},{10,8},{12,14},{14,12},{1,3},{3,1},... | collective-permute-start | bytes 589832 | tf_op jit(solution)/shard_map/ppermute | solution.py:598
  34.9 8.6 %collective-permute-start.13 = (bf16[96,1024]{1,0:T(8,128)(2,1)}, bf16[96,1024]{1,0:T(8,128)(2,1)S(1)}, u32[]{:S(2)}, u32[]{:S(2)}) collective-permute-start(bf16[96,1024]{1,0:T(8,128)(2,1)} %collective-permute-done.9.refs_9_), channel_id=1, source_target_pairs={{0,4},{2,6},{4,8},{6,10},{8,12},{10,14},{12,0},{14,2},{1,5},{3,7},... | collective-permute-start | bytes 589832 | tf_op jit(solution)/shard_map/ppermute | solution.py:593
  40.4 9.8 %collective-permute-start.19 = (bf16[384,384]{1,0:T(8,128)(2,1)S(1)}, bf16[384,384]{1,0:T(8,128)(2,1)S(1)}, u32[]{:S(2)}, u32[]{:S(2)}) collective-permute-start(bf16[384,384]{1,0:T(8,128)(2,1)S(1)} %constant_dynamic-slice_fusion), channel_id=1, source_target_pairs={{0,1},{1,0},{2,3},{3,2},{4,5},{5,4},{6,7},{7,6},{8,9},{9,8},{10,11... | collective-permute-start | bytes 884744 | tf_op jit(solution)/shard_map/ppermute | solution.py:573
  43.6 5.9 %collective-permute-start.11 = (bf16[96,1024]{1,0:T(8,128)(2,1)}, bf16[96,1024]{1,0:T(8,128)(2,1)S(1)}, u32[]{:S(2)}, u32[]{:S(2)}) collective-permute-start(bf16[96,1024]{1,0:T(8,128)(2,1)} %collective-permute-done.9.refs_9_), channel_id=1, source_target_pairs={{0,2},{2,0},{4,6},{6,4},{8,10},{10,8},{12,14},{14,12},{1,3},{3,1},... | collective-permute-start | bytes 589832 | tf_op jit(solution)/shard_map/ppermute | solution.py:598
  49.5 9.2 %collective-permute-start.14 = (bf16[96,1024]{1,0:T(8,128)(2,1)}, bf16[96,1024]{1,0:T(8,128)(2,1)S(1)}, u32[]{:S(2)}, u32[]{:S(2)}) collective-permute-start(bf16[96,1024]{1,0:T(8,128)(2,1)} %collective-permute-done.12.refs_12_), channel_id=1, source_target_pairs={{0,2},{2,0},{4,6},{6,4},{8,10},{10,8},{12,14},{14,12},{1,3},{3,1},... | collective-permute-start | bytes 589832 | tf_op jit(solution)/shard_map/ppermute | solution.py:598
  50.2 8.5 %collective-permute-start.15 = (bf16[96,1024]{1,0:T(8,128)(2,1)S(1)}, bf16[96,1024]{1,0:T(8,128)(2,1)S(1)}, u32[]{:S(2)}, u32[]{:S(2)}) collective-permute-start(bf16[96,1024]{1,0:T(8,128)(2,1)S(1)} %collective-permute-done.13.refs_13_), channel_id=1, source_target_pairs={{0,2},{2,0},{4,6},{6,4},{8,10},{10,8},{12,14},{14,12},{1,3},{3,1},... | collective-permute-start | bytes 589832 | tf_op jit(solution)/shard_map/ppermute | solution.py:598
  58.7 7.7 %collective-permute-start.20 = (bf16[512,1536]{1,0:T(8,128)(2,1)}, bf16[512,1536]{1,0:T(8,128)(2,1)S(1)}, u32[]{:S(2)}, u32[]{:S(2)}) collective-permute-start(bf16[512,1536]{1,0:T(8,128)(2,1)} %collective-permute-done.16.refs_18_), channel_id=1, source_target_pairs={{0,1},{1,0},{2,3},{3,2},{4,5},{5,4},{6,7},{7,6},{8,9},{9,8},{10,11... | collective-permute-start | bytes 4718600 | tf_op jit(solution)/shard_map/ppermute | solution.py:606
  78.6 10.2 %all-to-all-start.1 = ((bf16[8,16,256]{2,1,0:T(8,128)(2,1)}), bf16[8,16,256]{2,1,0:T(8,128)(2,1)S(1)}, u32[]{:S(2)}, u32[]{:S(2)}) async-start(bf16[8,16,256]{2,1,0:T(8,128)(2,1)} %get-tuple-element.32), calls=%async_computation.1 | async-start | bytes 131072 | tf_op jit(solution)/shard_map/all_to_all | solution.py:627
  (20 other events, 225.1 us)

commit v7 on v6

--- a/solution.py
+++ b/solution.py
@@ -36,10 +36,10 @@
     return [pltpu.with_memory_space_constraint(x, pltpu.VMEM) for x in arrays]
 
 
-def norm_kernel(flip, tiles_ref, gain_ref, out_ref, rows, hidden, in_sems, out_sems):
+def norm_kernel(tiles_ref, gain_ref, out_ref, rows, hidden, in_sems, out_sems):
     core = lax.axis_index("sub")
     half, length = rows.shape[:2]
-    first = (1 - core if flip else core) * half
+    first = core * half
     copies = [
         pltpu.make_async_copy(tiles_ref.at[first + i], rows.at[i], in_sems.at[i])
         for i in range(half)
@@ -67,12 +67,12 @@
         store.wait()
 
 
-def norm_tiles(tiles, gain, flip):
+def norm_tiles(tiles, gain):
     slot_count, length, width = tiles.shape
     half = slot_count // 2
     hbm = pl.BlockSpec(memory_space=pltpu.HBM)
     return pl.pallas_call(
-        functools.partial(norm_kernel, flip),
+        norm_kernel,
         in_specs=[hbm, pl.BlockSpec(memory_space=pltpu.VMEM)],
         out_specs=hbm,
         out_shape=pltpu.HBM((half * length, width), jnp.bfloat16),
@@ -561,8 +561,8 @@
         )
         for part in layout.parts
     ]
-    first = norm_tiles(tiles, tile_gain, False)
-    second = norm_tiles(tiles, tile_gain, True)
+    first = norm_tiles(tiles, tile_gain)
+    second = lax.ppermute(first, "sub", to_sibling)
     pair_first = lax.ppermute(first, "grp", to_pair)
 
     proj_far = lax.ppermute(embed_proj, "sub", to_sibling)
@@ -583,7 +583,7 @@
         compiler_params=pltpu.CompilerParams(vmem_limit_bytes=SMALL_VMEM),
     )(counts, slide_of, rates)
 
-    held[1] = after(held[1], first, proj_far, wq_far, many)
+    held[1] = after(held[1], first, proj_far, wq_far)
     steps = []
     last = None
     for step in range(nz):
@@ -592,6 +592,8 @@
             if step:
                 arrived = lax.ppermute(held[part], "dev", along_z)
                 others = [steps[-1][len(held) + part]]
+                if (step, part) == (1, 1):
+                    others += [second, many]
                 if last is not None:
                     others.append(last)
                 held[part] = last = after(arrived, *others)
@@ -601,11 +603,12 @@
     sums = []
     if layout.relative:
         early_blocks = blocks[: layout.early_steps * len(steps[0])]
-        sums = [early_mlp(layout, early_blocks, [after(first, last, wk_far, wv_far, wo_far), second])]
+        sums = [early_mlp(layout, early_blocks, [after(first, last), second])]
     pair_first = after(pair_first, *steps[-1][-2:], *sums)
     pair_second = lax.ppermute(pair_first, "sub", to_sibling)
 
     means = middle_mlp(layout, blocks, [first, second, pair_first], sums, length)
+    means = after(means, wk_far, wv_far, wo_far)
     parts = last_mlp(layout, means, blocks, pair_second, length, n_grp, n_sub)
     parts = lax.all_to_all(parts, ("grp", "sub"), split_axis=0, concat_axis=0, tiled=True)
 

time: 91.2 us -> 88.6 us (0.971)
  Pallas kernels: 33.5 us -> 30.3 us
  local copies, waits for them, and re-layouts: 2.17 us -> 4.28 us
  starting transfers between devices: 25.8 us -> 24.4 us
    pallas_call x2 -> x1, Pallas kernels: 7.89 us -> 3.94 us  [norm_tiles(): pl.pallas_call(norm_kernel, in_specs=[hbm, pl.BlockSpec(memory_space=pltp...]
    ppermute x6, starting transfers between devices: 7.99 us -> 4.79 us  [on_device(): arrived = lax.ppermute(held[part], 'dev', along_z)]
    slice x2, local copies, waits for them, and re-layouts: 0.06 us -> 1.84 us  [on_device(): w[part]]
    ppermute x8, waiting for transfers between devices: 6.82 us -> 5.42 us  [on_device(): sent.append(lax.ppermute(held[part], 'dev', along_y))]
    ppermute x6, waiting for transfers between devices: 10.8 us -> 11.9 us  [on_device(): arrived = lax.ppermute(held[part], 'dev', along_z)]
    dynamic_slice x1, local copies, waits for them, and re-layouts: 0.03 us -> 0.99 us  [on_device(): lax.dynamic_slice_in_dim(slide_wo, (1 - core) * out_cols, out_cols, 1)]
    unnamed x44 -> x54, local copies, waits for them, and re-layouts: 2.05 us -> 1.41 us
  transfers between devices with their start and end apart: 22 -> 23, of which waited for: 10 -> 9; matrix products, arithmetic and copies ran while one was open for 0% -> 3% of each run, Pallas kernels for 28% -> 24%
where the time goes in v7:
time: 88.6 us; the launch traced here: 88.2 us
  Pallas kernels  30.3 us (34%)
  starting transfers between devices  24.4 us (28%)
  waiting for transfers between devices  21.9 us (25%)
  blocking collectives  6.21 us (7%)
  local copies, waits for them, and re-layouts  4.28 us (5%)
  between operations  1.01 us (1%)
    ppermute x6, waiting for transfers between devices, on_device(): arrived = lax.ppermute(held[part], 'dev', along_z)  11.9 us
    ppermute x8, starting transfers between devices, on_device(): sent.append(lax.ppermute(held[part], 'dev', along_y))  11.5 us
    pallas_call x1, Pallas kernels, middle_mlp(): pl.pallas_call(functools.partial(middle_kernel, layout, length), in_specs...  7.49 us
    pallas_call x1, Pallas kernels, early_mlp(): pl.pallas_call(functools.partial(early_kernel, layout), in_specs=[hbm] *...  7.05 us
    all_to_all x1, blocking collectives, on_device(): lax.all_to_all(parts, ('grp', 'sub'), split_axis=0, concat_axis=0, tiled=...  6.21 us
    ppermute x8, waiting for transfers between devices, on_device(): sent.append(lax.ppermute(held[part], 'dev', along_y))  5.42 us
    pallas_call x1, Pallas kernels, last_mlp(): pl.pallas_call(functools.partial(last_kernel, layout, length, n_grp, n_su...  4.91 us
    ppermute x6, starting transfers between devices, on_device(): arrived = lax.ppermute(held[part], 'dev', along_z)  4.79 us
  transfers between devices with their start and end apart: 23, of which 9 were waited for; matrix products, arithmetic and copies ran while one was open for 3% of the time, Pallas kernels for 24%

profile of v7, /device:TPU:0, one launch (start us, length us, event | category | flops | bytes accessed | tf_op | source)
XLA Modules:
  0.0 88.2 jit_solution(15464677265137183991)
XLA Ops:
  1.8 3.9 %shard_map.140.refs_12_.refs_16_ = bf16[512,1536]{1,0:T(8,128)(2,1)} custom-call(bf16[4,256,1536]{2,1,0:T(8,128)(2,1)} %tiles_ref.1, f32[1536]{0:T(1024)S(1)} %copy-done.3), custom_call_target="tpu_custom_call" | custom-call | tf_op jit(solution)/shard_map/pallas_call | solution.py:74
  6.0 2.9 %collective-permute-start.17 = (bf16[512,1536]{1,0:T(8,128)(2,1)}, bf16[512,1536]{1,0:T(8,128)(2,1)}, u32[]{:S(2)}, u32[]{:S(2)}) collective-permute-start(bf16[512,1536]{1,0:T(8,128)(2,1)} %shard_map.140.refs_12_.refs_16_), channel_id=1, source_target_pairs={{0,16},{16,0},{1,17},{17,1},{2,18},{18,2},{3,19},{19,3},{4,20},{20... | collective-permute-start | bytes 4718600 | tf_op jit(solution)/shard_map/ppermute | solution.py:566
  10.8 1.6 %collective-permute-start.2 = (bf16[96,1024]{1,0:T(8,128)(2,1)S(1)}, bf16[96,1024]{1,0:T(8,128)(2,1)S(1)}, u32[]{:S(2)}, u32[]{:S(2)}) collective-permute-start(bf16[96,1024]{1,0:T(8,128)(2,1)S(1)} %pad_maximum_fusion.refs_0_), channel_id=1, source_target_pairs={{0,2},{2,0},{4,6},{6,4},{8,10},{10,8},{12,14},{14,12},{1,3},{3,1},... | collective-permute-start | bytes 589832 | tf_op jit(solution)/shard_map/ppermute | solution.py:600
  12.4 1.6 %collective-permute-start.4 = (bf16[96,1024]{1,0:T(8,128)(2,1)S(1)}, bf16[96,1024]{1,0:T(8,128)(2,1)S(1)}, u32[]{:S(2)}, u32[]{:S(2)}) collective-permute-start(bf16[96,1024]{1,0:T(8,128)(2,1)S(1)} %pad_maximum_fusion.refs_0_), channel_id=1, source_target_pairs={{0,4},{2,6},{4,8},{6,10},{8,12},{10,14},{12,0},{14,2},{1,5},{3,7},... | collective-permute-start | bytes 589832 | tf_op jit(solution)/shard_map/ppermute | solution.py:593
  14.8 3.7 %collective-permute-done.2.refs_2_ = bf16[96,1024]{1,0:T(8,128)(2,1)S(1)} collective-permute-done((bf16[96,1024]{1,0:T(8,128)(2,1)S(1)}, bf16[96,1024]{1,0:T(8,128)(2,1)S(1)}, u32[]{:S(2)}, u32[]{:S(2)}) %collective-permute-start.2) | collective-permute-done | bytes 196640 | tf_op jit(solution)/shard_map/ppermute | solution.py:600
  18.6 1.6 %collective-permute-start.5 = (bf16[96,1024]{1,0:T(8,128)(2,1)S(1)}, bf16[96,1024]{1,0:T(8,128)(2,1)S(1)}, u32[]{:S(2)}, u32[]{:S(2)}) collective-permute-start(bf16[96,1024]{1,0:T(8,128)(2,1)S(1)} %pad_maximum_fusion.1.refs_1_), channel_id=1, source_target_pairs={{0,4},{2,6},{4,8},{6,10},{8,12},{10,14},{12,0},{14,2},{1,5},{3,7},... | collective-permute-start | bytes 589832 | tf_op jit(solution)/shard_map/ppermute | solution.py:593
  21.5 1.5 %collective-permute-start.7 = (bf16[96,1024]{1,0:T(8,128)(2,1)S(1)}, bf16[96,1024]{1,0:T(8,128)(2,1)S(1)}, u32[]{:S(2)}, u32[]{:S(2)}) collective-permute-start(bf16[96,1024]{1,0:T(8,128)(2,1)S(1)} %collective-permute-done.4.refs_4_), channel_id=1, source_target_pairs={{0,2},{2,0},{4,6},{6,4},{8,10},{10,8},{12,14},{14,12},{1,3},{3,1},... | collective-permute-start | bytes 589832 | tf_op jit(solution)/shard_map/ppermute | solution.py:600
  23.0 1.6 %collective-permute-start.9 = (bf16[96,1024]{1,0:T(8,128)(2,1)S(1)}, bf16[96,1024]{1,0:T(8,128)(2,1)S(1)}, u32[]{:S(2)}, u32[]{:S(2)}) collective-permute-start(bf16[96,1024]{1,0:T(8,128)(2,1)S(1)} %collective-permute-done.4.refs_4_), channel_id=1, source_target_pairs={{0,4},{2,6},{4,8},{6,10},{8,12},{10,14},{12,0},{14,2},{1,5},{3,7},... | collective-permute-start | bytes 589832 | tf_op jit(solution)/shard_map/ppermute | solution.py:593
  24.6 2.4 %collective-permute-done.5.refs_5_ = bf16[96,1024]{1,0:T(8,128)(2,1)S(1)} collective-permute-done((bf16[96,1024]{1,0:T(8,128)(2,1)S(1)}, bf16[96,1024]{1,0:T(8,128)(2,1)S(1)}, u32[]{:S(2)}, u32[]{:S(2)}) %collective-permute-start.5) | collective-permute-done | bytes 196640 | tf_op jit(solution)/shard_map/ppermute | solution.py:593
  27.0 2.3 %collective-permute-start.8 = (bf16[96,1024]{1,0:T(8,128)(2,1)S(1)}, bf16[96,1024]{1,0:T(8,128)(2,1)S(1)}, u32[]{:S(2)}, u32[]{:S(2)}) collective-permute-start(bf16[96,1024]{1,0:T(8,128)(2,1)S(1)} %collective-permute-done.5.refs_5_), channel_id=1, source_target_pairs={{0,2},{2,0},{4,6},{6,4},{8,10},{10,8},{12,14},{14,12},{1,3},{3,1},... | collective-permute-start | bytes 589832 | tf_op jit(solution)/shard_map/ppermute | solution.py:600
  29.4 2.7 %collective-permute-done.9.refs_8_ = bf16[96,1024]{1,0:T(8,128)(2,1)S(1)} collective-permute-done((bf16[96,1024]{1,0:T(8,128)(2,1)S(1)}, bf16[96,1024]{1,0:T(8,128)(2,1)S(1)}, u32[]{:S(2)}, u32[]{:S(2)}) %collective-permute-start.9) | collective-permute-done | bytes 196640 | tf_op jit(solution)/shard_map/ppermute | solution.py:593
  33.6 1.6 %collective-permute-done.10.refs_9_ = bf16[96,1024]{1,0:T(8,128)(2,1)S(1)} collective-permute-done((bf16[96,1024]{1,0:T(8,128)(2,1)S(1)}, bf16[96,1024]{1,0:T(8,128)(2,1)S(1)}, u32[]{:S(2)}, u32[]{:S(2)}) %collective-permute-start.10) | collective-permute-done | bytes 196640 | tf_op jit(solution)/shard_map/ppermute | solution.py:593
  35.1 2.8 %collective-permute-start.12 = (bf16[96,1024]{1,0:T(8,128)(2,1)S(1)}, bf16[96,1024]{1,0:T(8,128)(2,1)S(1)}, u32[]{:S(2)}, u32[]{:S(2)}) collective-permute-start(bf16[96,1024]{1,0:T(8,128)(2,1)S(1)} %collective-permute-done.10.refs_9_), channel_id=1, source_target_pairs={{0,2},{2,0},{4,6},{6,4},{8,10},{10,8},{12,14},{14,12},{1,3},{3,1},... | collective-permute-start | bytes 589832 | tf_op jit(solution)/shard_map/ppermute | solution.py:600
  39.2 3.5 %collective-permute-done.13.refs_12_ = bf16[96,1024]{1,0:T(8,128)(2,1)S(1)} collective-permute-done((bf16[96,1024]{1,0:T(8,128)(2,1)S(1)}, bf16[96,1024]{1,0:T(8,128)(2,1)S(1)}, u32[]{:S(2)}, u32[]{:S(2)}) %collective-permute-start.13) | collective-permute-done | bytes 196640 | tf_op jit(solution)/shard_map/ppermute | solution.py:593
  43.7 1.6 %collective-permute-done.14.refs_13_ = bf16[96,1024]{1,0:T(8,128)(2,1)S(1)} collective-permute-done((bf16[96,1024]{1,0:T(8,128)(2,1)S(1)}, bf16[96,1024]{1,0:T(8,128)(2,1)S(1)}, u32[]{:S(2)}, u32[]{:S(2)}) %collective-permute-start.14) | collective-permute-done | bytes 196640 | tf_op jit(solution)/shard_map/ppermute | solution.py:593
  45.9 7.1 %shard_map.142.refs_19_ = f32[2,512,1024]{2,1,0:T(8,128)} custom-call(bf16[96,1024]{1,0:T(8,128)(2,1)} %copy-done.8, bf16[96,1024]{1,0:T(8,128)(2,1)} %copy-done.9, bf16[96,1024]{1,0:T(8,128)(2,1)} %copy-done.10, bf16[96,1024]{1,0:T(8,128)(2,1)} %copy-done.12, bf16[96,1024]{1,0:T(8,128)(2,1)} %copy-done.11, bf16[96,1024]{1,0:T(8,128)(2,1)} %copy-done.13, ...), custom_call_target="tpu_custom_call" | custom-call | flops 2415919104 | bytes 8912896 | tf_op jit(solution)/shard_map/pallas_call | solution.py:195
  55.2 7.5 %shard_map.143.means_ref = f32[6,512]{1,0:T(8,128)S(1)} custom-call(bf16[96,1024]{1,0:T(8,128)(2,1)} %copy-done.8, bf16[96,1024]{1,0:T(8,128)(2,1)} %copy-done.9, bf16[96,1024]{1,0:T(8,128)(2,1)} %copy-done.10, bf16[96,1024]{1,0:T(8,128)(2,1)} %copy-done.12, bf16[96,1024]{1,0:T(8,128)(2,1)} %copy-done.11, bf16[96,1024]{1,0:T(8,128)(2,1)} %copy-done.13, ...), custom_call_target="tpu_custom_call" | custom-call | flops 3221225472 | bytes 12058624 | tf_op jit(solution)/shard_map/pallas_call | solution.py:266
  62.8 4.9 %shard_map.144 = bf16[4,16,128]{2,1,0:T(8,128)(2,1)S(1)} custom-call(f32[6,512]{1,0:T(8,128)S(1)} %shard_map.143.means_ref, bf16[96,1024]{1,0:T(8,128)(2,1)} %copy-done.8, bf16[96,1024]{1,0:T(8,128)(2,1)} %copy-done.9, bf16[96,1024]{1,0:T(8,128)(2,1)} %copy-done.10, bf16[96,1024]{1,0:T(8,128)(2,1)} %copy-done.12, bf16[96,1024]{1,0:T(8,128)(2,1)} %copy-done.11, ...), custom_call_target="tpu_custom_call" | custom-call | flops 1610612736 | bytes 4718592 | tf_op jit(solution)/shard_map/pallas_call | solution.py:333
  67.7 6.2 %all_to_all.10.parts_ref = bf16[4,16,128]{2,1,0:T(8,128)(2,1)S(1)} all-to-all(bf16[4,16,128]{2,1,0:T(8,128)(2,1)S(1)} %shard_map.144), channel_id=1, replica_groups=mesh['grp'=2,'dev'=8,'sub'=2] {'grp','sub'}, dimensions={0} | all-to-all | bytes 32768 | tf_op jit(solution)/shard_map/all_to_all | solution.py:613
  73.9 1.9 %shard_map.145 = (bf16[4,1024]{1,0:T(4,128)(2,1)}, f32[8,768]{1,0:T(8,128)S(1)}, bf16[8,16,256]{2,1,0:T(8,128)(2,1)}) custom-call(s32[8]{0:T(128)S(1)} %copy-done.4, bf16[4,16,128]{2,1,0:T(8,128)(2,1)S(1)} %all_to_all.10.parts_ref, f32[768]{0:T(1024)S(1)} %copy-done.2, bf16[1024,768]{1,0:T(8,128)(2,1)S(1)} %copy-done, ...), custom_call_target="tpu_custom_call" | custom-call | tf_op jit(solution)/shard_map/pallas_call | solution.py:619
  75.8 3.4 %all-to-all-start.1 = ((bf16[8,16,256]{2,1,0:T(8,128)(2,1)}), bf16[8,16,256]{2,1,0:T(8,128)(2,1)S(1)}, u32[]{:S(2)}, u32[]{:S(2)}) async-start(bf16[8,16,256]{2,1,0:T(8,128)(2,1)} %get-tuple-element.34), calls=%async_computation.1 | async-start | bytes 131072 | tf_op jit(solution)/shard_map/all_to_all | solution.py:630
  79.2 2.3 %shard_map.146 = (bf16[96,768]{1,0:T(8,128)(2,1)S(1)}, bf16[768,384]{1,0:T(8,128)(2,1)S(1)}, bf16[768,384]{1,0:T(8,128)(2,1)S(1)}, bf16[768,384]{1,0:T(8,128)(2,...) custom-call(f32[8,768]{1,0:T(8,128)S(1)} %get-tuple-element.35.mixed, ...), custom_call_target="tpu_custom_call" | custom-call | tf_op jit(solution)/shard_map/pallas_call | solution.py:633
  81.5 4.6 %all-to-all-done.1.sent_ref = bf16[8,16,256]{2,1,0:T(8,128)(2,1)S(1)} async-done(((bf16[8,16,256]{2,1,0:T(8,128)(2,1)}), bf16[8,16,256]{2,1,0:T(8,128)(2,1)S(1)}, u32[]{:S(2)}, u32[]{:S(2)}) %all-to-all-start.1) | async-done | bytes 65568 | tf_op jit(solution)/shard_map/all_to_all | solution.py:630
  86.1 2.1 %shard_map.147 = bf16[4,384]{1,0:T(4,128)(2,1)} custom-call(s32[8]{0:T(128)S(1)} %copy-done.4, bf16[8,16,256]{2,1,0:T(8,128)(2,1)S(1)} %all-to-all-done.1.sent_ref, f32[8,768]{1,0:T(8,128)S(1)} %get-tuple-element.35.mixed_ref, bf16[96,768]{1,0:T(8,128)(2,1)S(1)} %get-tuple-element.36.query_ref, bf16[768,384]{1,0:T(8,128)(2,1)S(1)} %get-tuple-element.37.wk_ref, ...), custom_call_target="tpu_custom_call" | custom-call | tf_op jit(solution)/shard_map/pallas_call | solution.py:647
  (92 shorter events, 11.8 us)
Async XLA Ops:
  0.6 13.5 %collective-permute-start = (bf16[1024,768]{1,0:T(8,128)(2,1)}, bf16[1024,768]{1,0:T(8,128)(2,1)S(1)}, u32[]{:S(2)}, u32[]{:S(2)}) collective-permute-start(bf16[1024,768]{1,0:T(8,128)(2,1)} %near_ref.1), channel_id=1, source_target_pairs={{0,1},{1,0},{2,3},{3,2},{4,5},{5,4},{6,7},{7,6},{8,9},{9,8},{10,11... | collective-permute-start | bytes 4718600 | tf_op jit(solution)/shard_map/ppermute | solution.py:568
  5.8 17.2 %collective-permute-start.6 = (bf16[512,1536]{1,0:T(8,128)(2,1)}, bf16[512,1536]{1,0:T(8,128)(2,1)S(1)}, u32[]{:S(2)}, u32[]{:S(2)}) collective-permute-start(bf16[512,1536]{1,0:T(8,128)(2,1)} %shard_map.140.refs_12_.refs_16_), channel_id=1, source_target_pairs={{0,1},{1,0},{2,3},{3,2},{4,5},{5,4},{6,7},{7,6},{8,9},{9,8},{10,11... | collective-permute-start | bytes 4718600 | tf_op jit(solution)/shard_map/ppermute | solution.py:565
  6.0 47.0 %collective-permute-start.17 = (bf16[512,1536]{1,0:T(8,128)(2,1)}, bf16[512,1536]{1,0:T(8,128)(2,1)}, u32[]{:S(2)}, u32[]{:S(2)}) collective-permute-start(bf16[512,1536]{1,0:T(8,128)(2,1)} %shard_map.140.refs_12_.refs_16_), channel_id=1, source_target_pairs={{0,16},{16,0},{1,17},{17,1},{2,18},{18,2},{3,19},{19,3},{4,20},{20... | collective-permute-start | bytes 4718600 | tf_op jit(solution)/shard_map/ppermute | solution.py:566
  8.9 3.5 %collective-permute-start.1 = (bf16[768,384]{1,0:T(8,128)(2,1)}, bf16[768,384]{1,0:T(8,128)(2,1)}, u32[]{:S(2)}, u32[]{:S(2)}) collective-permute-start(bf16[768,384]{1,0:T(8,128)(2,1)} %refs_0_.1), channel_id=1, source_target_pairs={{0,1},{1,0},{2,3},{3,2},{4,5},{5,4},{6,7},{7,6},{8,9},{9,8},{10,11... | collective-permute-start | bytes 1769480 | tf_op jit(solution)/shard_map/ppermute | solution.py:569
  10.8 35.0 %copy-start.8 = (bf16[96,1024]{1,0:T(8,128)(2,1)}, bf16[96,1024]{1,0:T(8,128)(2,1)S(1)}, u32[]{:S(2)}) copy-start(bf16[96,1024]{1,0:T(8,128)(2,1)S(1)} %pad_maximum_fusion.refs_0_) | copy-start | bytes 589828
  10.8 7.8 %collective-permute-start.2 = (bf16[96,1024]{1,0:T(8,128)(2,1)S(1)}, bf16[96,1024]{1,0:T(8,128)(2,1)S(1)}, u32[]{:S(2)}, u32[]{:S(2)}) collective-permute-start(bf16[96,1024]{1,0:T(8,128)(2,1)S(1)} %pad_maximum_fusion.refs_0_), channel_id=1, source_target_pairs={{0,2},{2,0},{4,6},{6,4},{8,10},{10,8},{12,14},{14,12},{1,3},{3,1},... | collective-permute-start | bytes 589832 | tf_op jit(solution)/shard_map/ppermute | solution.py:600
  12.4 9.0 %collective-permute-start.4 = (bf16[96,1024]{1,0:T(8,128)(2,1)S(1)}, bf16[96,1024]{1,0:T(8,128)(2,1)S(1)}, u32[]{:S(2)}, u32[]{:S(2)}) collective-permute-start(bf16[96,1024]{1,0:T(8,128)(2,1)S(1)} %pad_maximum_fusion.refs_0_), channel_id=1, source_target_pairs={{0,4},{2,6},{4,8},{6,10},{8,12},{10,14},{12,0},{14,2},{1,5},{3,7},... | collective-permute-start | bytes 589832 | tf_op jit(solution)/shard_map/ppermute | solution.py:593
  14.1 10.5 %collective-permute-start.3 = (bf16[96,1024]{1,0:T(8,128)(2,1)S(1)}, bf16[96,1024]{1,0:T(8,128)(2,1)S(1)}, u32[]{:S(2)}, u32[]{:S(2)}) collective-permute-start(bf16[96,1024]{1,0:T(8,128)(2,1)S(1)} %pad_maximum_fusion.1.refs_1_), channel_id=1, source_target_pairs={{0,2},{2,0},{4,6},{6,4},{8,10},{10,8},{12,14},{14,12},{1,3},{3,1},... | collective-permute-start | bytes 589832 | tf_op jit(solution)/shard_map/ppermute | solution.py:600
  18.6 8.5 %collective-permute-start.5 = (bf16[96,1024]{1,0:T(8,128)(2,1)S(1)}, bf16[96,1024]{1,0:T(8,128)(2,1)S(1)}, u32[]{:S(2)}, u32[]{:S(2)}) collective-permute-start(bf16[96,1024]{1,0:T(8,128)(2,1)S(1)} %pad_maximum_fusion.1.refs_1_), channel_id=1, source_target_pairs={{0,4},{2,6},{4,8},{6,10},{8,12},{10,14},{12,0},{14,2},{1,5},{3,7},... | collective-permute-start | bytes 589832 | tf_op jit(solution)/shard_map/ppermute | solution.py:593
  21.5 7.9 %collective-permute-start.7 = (bf16[96,1024]{1,0:T(8,128)(2,1)S(1)}, bf16[96,1024]{1,0:T(8,128)(2,1)S(1)}, u32[]{:S(2)}, u32[]{:S(2)}) collective-permute-start(bf16[96,1024]{1,0:T(8,128)(2,1)S(1)} %collective-permute-done.4.refs_4_), channel_id=1, source_target_pairs={{0,2},{2,0},{4,6},{6,4},{8,10},{10,8},{12,14},{14,12},{1,3},{3,1},... | collective-permute-start | bytes 589832 | tf_op jit(solution)/shard_map/ppermute | solution.py:600
  23.0 9.1 %collective-permute-start.9 = (bf16[96,1024]{1,0:T(8,128)(2,1)S(1)}, bf16[96,1024]{1,0:T(8,128)(2,1)S(1)}, u32[]{:S(2)}, u32[]{:S(2)}) collective-permute-start(bf16[96,1024]{1,0:T(8,128)(2,1)S(1)} %collective-permute-done.4.refs_4_), channel_id=1, source_target_pairs={{0,4},{2,6},{4,8},{6,10},{8,12},{10,14},{12,0},{14,2},{1,5},{3,7},... | collective-permute-start | bytes 589832 | tf_op jit(solution)/shard_map/ppermute | solution.py:593
  27.0 8.1 %collective-permute-start.10 = (bf16[96,1024]{1,0:T(8,128)(2,1)S(1)}, bf16[96,1024]{1,0:T(8,128)(2,1)S(1)}, u32[]{:S(2)}, u32[]{:S(2)}) collective-permute-start(bf16[96,1024]{1,0:T(8,128)(2,1)S(1)} %collective-permute-done.5.refs_5_), channel_id=1, source_target_pairs={{0,4},{2,6},{4,8},{6,10},{8,12},{10,14},{12,0},{14,2},{1,5},{3,7},... | collective-permute-start | bytes 589832 | tf_op jit(solution)/shard_map/ppermute | solution.py:593
  27.0 8.1 %collective-permute-start.8 = (bf16[96,1024]{1,0:T(8,128)(2,1)S(1)}, bf16[96,1024]{1,0:T(8,128)(2,1)S(1)}, u32[]{:S(2)}, u32[]{:S(2)}) collective-permute-start(bf16[96,1024]{1,0:T(8,128)(2,1)S(1)} %collective-permute-done.5.refs_5_), channel_id=1, source_target_pairs={{0,2},{2,0},{4,6},{6,4},{8,10},{10,8},{12,14},{14,12},{1,3},{3,1},... | collective-permute-start | bytes 589832 | tf_op jit(solution)/shard_map/ppermute | solution.py:600
  32.1 7.1 %collective-permute-start.11 = (bf16[96,1024]{1,0:T(8,128)(2,1)S(1)}, bf16[96,1024]{1,0:T(8,128)(2,1)S(1)}, u32[]{:S(2)}, u32[]{:S(2)}) collective-permute-start(bf16[96,1024]{1,0:T(8,128)(2,1)S(1)} %collective-permute-done.9.refs_8_), channel_id=1, source_target_pairs={{0,2},{2,0},{4,6},{6,4},{8,10},{10,8},{12,14},{14,12},{1,3},{3,1},... | collective-permute-start | bytes 589832 | tf_op jit(solution)/shard_map/ppermute | solution.py:600
  33.6 9.2 %collective-permute-start.13 = (bf16[96,1024]{1,0:T(8,128)(2,1)S(1)}, bf16[96,1024]{1,0:T(8,128)(2,1)S(1)}, u32[]{:S(2)}, u32[]{:S(2)}) collective-permute-start(bf16[96,1024]{1,0:T(8,128)(2,1)S(1)} %collective-permute-done.9.refs_8_), channel_id=1, source_target_pairs={{0,4},{2,6},{4,8},{6,10},{8,12},{10,14},{12,0},{14,2},{1,5},{3,7},... | collective-permute-start | bytes 589832 | tf_op jit(solution)/shard_map/ppermute | solution.py:593
  35.1 8.6 %collective-permute-start.12 = (bf16[96,1024]{1,0:T(8,128)(2,1)S(1)}, bf16[96,1024]{1,0:T(8,128)(2,1)S(1)}, u32[]{:S(2)}, u32[]{:S(2)}) collective-permute-start(bf16[96,1024]{1,0:T(8,128)(2,1)S(1)} %collective-permute-done.10.refs_9_), channel_id=1, source_target_pairs={{0,2},{2,0},{4,6},{6,4},{8,10},{10,8},{12,14},{14,12},{1,3},{3,1},... | collective-permute-start | bytes 589832 | tf_op jit(solution)/shard_map/ppermute | solution.py:600
  37.9 7.5 %collective-permute-start.14 = (bf16[96,1024]{1,0:T(8,128)(2,1)S(1)}, bf16[96,1024]{1,0:T(8,128)(2,1)S(1)}, u32[]{:S(2)}, u32[]{:S(2)}) collective-permute-start(bf16[96,1024]{1,0:T(8,128)(2,1)S(1)} %collective-permute-done.10.refs_9_), channel_id=1, source_target_pairs={{0,4},{2,6},{4,8},{6,10},{8,12},{10,14},{12,0},{14,2},{1,5},{3,7},... | collective-permute-start | bytes 589832 | tf_op jit(solution)/shard_map/ppermute | solution.py:593
  42.7 10.2 %collective-permute-start.15 = (bf16[96,1024]{1,0:T(8,128)(2,1)S(1)}, bf16[96,1024]{1,0:T(8,128)(2,1)S(1)}, u32[]{:S(2)}, u32[]{:S(2)}) collective-permute-start(bf16[96,1024]{1,0:T(8,128)(2,1)S(1)} %collective-permute-done.13.refs_12_), channel_id=1, source_target_pairs={{0,2},{2,0},{4,6},{6,4},{8,10},{10,8},{12,14},{14,12},{1,3},{3,1},... | collective-permute-start | bytes 589832 | tf_op jit(solution)/shard_map/ppermute | solution.py:600
  45.4 7.6 %collective-permute-start.16 = (bf16[96,1024]{1,0:T(8,128)(2,1)S(1)}, bf16[96,1024]{1,0:T(8,128)(2,1)S(1)}, u32[]{:S(2)}, u32[]{:S(2)}) collective-permute-start(bf16[96,1024]{1,0:T(8,128)(2,1)S(1)} %collective-permute-done.14.refs_13_), channel_id=1, source_target_pairs={{0,2},{2,0},{4,6},{6,4},{8,10},{10,8},{12,14},{14,12},{1,3},{3,1},... | collective-permute-start | bytes 589832 | tf_op jit(solution)/shard_map/ppermute | solution.py:600
  53.0 9.7 %collective-permute-start.21 = (bf16[512,1536]{1,0:T(8,128)(2,1)}, bf16[512,1536]{1,0:T(8,128)(2,1)}, u32[]{:S(2)}, u32[]{:S(2)}) collective-permute-start(bf16[512,1536]{1,0:T(8,128)(2,1)} %collective-permute-done.17.refs_18_), channel_id=1, source_target_pairs={{0,1},{1,0},{2,3},{3,2},{4,5},{5,4},{6,7},{7,6},{8,9},{9,8},{10,11... | collective-permute-start | bytes 4718600 | tf_op jit(solution)/shard_map/ppermute | solution.py:608
  53.1 9.6 %collective-permute-start.18 = (bf16[768,384]{1,0:T(8,128)(2,1)}, bf16[768,384]{1,0:T(8,128)(2,1)S(1)}, u32[]{:S(2)}, u32[]{:S(2)}) collective-permute-start(bf16[768,384]{1,0:T(8,128)(2,1)} %refs_2_.1), channel_id=1, source_target_pairs={{0,1},{1,0},{2,3},{3,2},{4,5},{5,4},{6,7},{7,6},{8,9},{9,8},{10,11... | collective-permute-start | bytes 1769480 | tf_op jit(solution)/shard_map/ppermute | solution.py:570
  53.6 9.1 %collective-permute-start.19 = (bf16[768,384]{1,0:T(8,128)(2,1)}, bf16[768,384]{1,0:T(8,128)(2,1)S(1)}, u32[]{:S(2)}, u32[]{:S(2)}) collective-permute-start(bf16[768,384]{1,0:T(8,128)(2,1)} %refs_4_.1), channel_id=1, source_target_pairs={{0,1},{1,0},{2,3},{3,2},{4,5},{5,4},{6,7},{7,6},{8,9},{9,8},{10,11... | collective-permute-start | bytes 1769480 | tf_op jit(solution)/shard_map/ppermute | solution.py:571
  54.7 8.0 %collective-permute-start.20 = (bf16[384,384]{1,0:T(8,128)(2,1)S(1)}, bf16[384,384]{1,0:T(8,128)(2,1)S(1)}, u32[]{:S(2)}, u32[]{:S(2)}) collective-permute-start(bf16[384,384]{1,0:T(8,128)(2,1)S(1)} %constant_dynamic-slice_fusion), channel_id=1, source_target_pairs={{0,1},{1,0},{2,3},{3,2},{4,5},{5,4},{6,7},{7,6},{8,9},{9,8},{10,11... | collective-permute-start | bytes 884744 | tf_op jit(solution)/shard_map/ppermute | solution.py:573
  75.8 10.3 %all-to-all-start.1 = ((bf16[8,16,256]{2,1,0:T(8,128)(2,1)}), bf16[8,16,256]{2,1,0:T(8,128)(2,1)S(1)}, u32[]{:S(2)}, u32[]{:S(2)}) async-start(bf16[8,16,256]{2,1,0:T(8,128)(2,1)} %get-tuple-element.34), calls=%async_computation.1 | async-start | bytes 131072 | tf_op jit(solution)/shard_map/all_to_all | solution.py:630
  (26 other events, 309.6 us)

commit v8 on v7

--- a/solution.py
+++ b/solution.py
@@ -13,10 +13,12 @@
 FLOOR = -1e30
 QROWS = 8
 NORM_ROWS = 16
+NORM_PIECE = 128
 LANES = 128
 UNIT_ROWS = 16
 ROW_TILE = 16
-MLP_VMEM = 32 * 1024 * 1024
+MXU = 256
+MLP_VMEM = 24 * 1024 * 1024
 NORM_VMEM = 8 * 1024 * 1024
 SMALL_VMEM = 4 * 1024 * 1024
 
@@ -36,55 +38,77 @@
     return [pltpu.with_memory_space_constraint(x, pltpu.VMEM) for x in arrays]
 
 
-def norm_kernel(tiles_ref, gain_ref, out_ref, rows, hidden, in_sems, out_sems):
+def start_kernel(parts, tiles_ref, gain_ref, gate_ref, up_ref, *refs):
+    out_ref, *block_refs = refs[: 1 + len(parts)]
+    rows, hidden, gain, in_sems, out_sems, block_sems, gain_sem = refs[1 + len(parts) :]
     core = lax.axis_index("sub")
-    half, length = rows.shape[:2]
-    first = core * half
-    copies = [
-        pltpu.make_async_copy(tiles_ref.at[first + i], rows.at[i], in_sems.at[i])
-        for i in range(half)
-    ]
-    stores = [
-        pltpu.make_async_copy(
-            hidden.at[i], out_ref.at[pl.ds(i * length, length)], out_sems.at[i]
-        )
-        for i in range(half)
-    ]
-    for copy in copies:
-        copy.start()
-    gain = gain_ref[...].reshape(1, -1)
-    for i in range(half):
+    half, length = tiles_ref.shape[0] // 2, tiles_ref.shape[1]
+    half_cols = gate_ref.shape[1] // 2
+    n_pieces = rows.shape[0] // NORM_PIECE
+    gain_copy = pltpu.make_async_copy(gain_ref, gain, gain_sem)
+    gain_copy.start()
+    copies, stores = [], []
+    for i in range(n_pieces):
+        here = pl.ds(i * NORM_PIECE, NORM_PIECE)
+        tile, first = divmod(i * NORM_PIECE, length)
+        source = tiles_ref.at[core * half + tile, pl.ds(first, NORM_PIECE)]
+        copies.append(pltpu.make_async_copy(source, rows.at[here], in_sems.at[i]))
+        stores.append(pltpu.make_async_copy(hidden.at[here], out_ref.at[here], out_sems.at[i]))
+        copies[-1].start()
+    packs = []
+    columns = pl.ds(pl.multiple_of(lax.rem(lax.axis_index("grp"), 2) * half_cols, LANES), half_cols)
+    for k, (part, block_ref) in enumerate(zip(parts, block_refs)):
+        for i, ref in enumerate((gate_ref, up_ref)):
+            packs.append(
+                pltpu.make_async_copy(
+                    ref.at[part, columns],
+                    block_ref.at[:, i * half_cols : (i + 1) * half_cols],
+                    block_sems.at[k, i],
+                )
+            )
+            packs[-1].start()
+    gain_copy.wait()
+    gains = gain[...].reshape(1, -1)
+    for i in range(n_pieces):
         copies[i].wait()
 
         def some_rows(j, carry):
-            here = pl.ds(pl.multiple_of(j * NORM_ROWS, NORM_ROWS), NORM_ROWS)
-            hidden[i, here, :] = normed(rows[i, here, :].astype(jnp.float32), gain)
+            start = pl.multiple_of(i * NORM_PIECE + j * NORM_ROWS, NORM_ROWS)
+            here = pl.ds(start, NORM_ROWS)
+            hidden[here, :] = normed(rows[here, :].astype(jnp.float32), gains)
             return carry
 
-        lax.fori_loop(0, length // NORM_ROWS, some_rows, 0, unroll=4)
+        lax.fori_loop(0, NORM_PIECE // NORM_ROWS, some_rows, 0, unroll=True)
         stores[i].start()
-    for store in stores:
-        store.wait()
-
-
-def norm_tiles(tiles, gain):
+    for copy in packs + stores:
+        copy.wait()
+
+
+def start_work(tiles, gain, gate_weight, up_weight, parts):
     slot_count, length, width = tiles.shape
-    half = slot_count // 2
+    n_rows = slot_count // 2 * length
     hbm = pl.BlockSpec(memory_space=pltpu.HBM)
+    cols = gate_weight.shape[1]
     return pl.pallas_call(
-        norm_kernel,
-        in_specs=[hbm, pl.BlockSpec(memory_space=pltpu.VMEM)],
-        out_specs=hbm,
-        out_shape=pltpu.HBM((half * length, width), jnp.bfloat16),
+        functools.partial(start_kernel, parts),
+        in_specs=[hbm] * 4,
+        out_specs=[hbm] * (1 + len(parts)),
+        out_shape=[
+            pltpu.HBM((n_rows, width), jnp.bfloat16),
+            *[pltpu.HBM((part.stop - part.start, cols), jnp.bfloat16) for part in parts],
+        ],
         scratch_shapes=[
-            pltpu.VMEM((half, length, width), jnp.bfloat16),
-            pltpu.VMEM((half, length, width), jnp.bfloat16),
-            pltpu.SemaphoreType.DMA((half,)),
-            pltpu.SemaphoreType.DMA((half,)),
+            pltpu.VMEM((n_rows, width), jnp.bfloat16),
+            pltpu.VMEM((n_rows, width), jnp.bfloat16),
+            pltpu.VMEM((width,), jnp.float32),
+            pltpu.SemaphoreType.DMA((n_rows // NORM_PIECE,)),
+            pltpu.SemaphoreType.DMA((n_rows // NORM_PIECE,)),
+            pltpu.SemaphoreType.DMA((len(parts), 2)),
+            pltpu.SemaphoreType.DMA(()),
         ],
         compiler_params=pltpu.CompilerParams(vmem_limit_bytes=NORM_VMEM),
         cost_estimate=pl.CostEstimate(flops=0, bytes_accessed=0, transcendentals=0),
-    )(*in_hbm(tiles), gain)
+    )(*in_hbm(tiles, gain, gate_weight, up_weight))
 
 
 def after(value, *others):
@@ -97,7 +121,7 @@
         self.pair = ny * depth
         self.relative = self.pair % LANES == 0
         self.early_steps = self.nz - 1
-        self.early = self.early_steps * self.pair if self.relative else 0
+        self.early = self.early_steps * self.pair // MXU * MXU if self.relative else 0
         cut = max(ROW_TILE, depth // 2 // ROW_TILE * ROW_TILE)
         self.parts = [slice(0, cut), slice(cut, depth)]
         self.width = n_dev * depth
@@ -112,12 +136,13 @@
         z = my_z - step
         return jnp.where(z < 0, z + self.nz, z)
 
-    def block_copies(self, blocks, weights, sems):
+    def block_copies(self, blocks, weights, sems, end=None):
         _, my_y = self.place()
         copies = []
         n_parts = len(self.parts)
+        first = 0 if end is None else end - len(blocks) // n_parts // self.ny
         for k, block in enumerate(blocks):
-            step, flip, part = k // n_parts // self.ny, k // n_parts % self.ny, k % n_parts
+            step, flip, part = first + k // n_parts // self.ny, k // n_parts % self.ny, k % n_parts
             y = 1 - my_y if flip else my_y
             at = step if self.relative else self.source(step)
             here = self.parts[part]
@@ -167,7 +192,7 @@
     steps = range(layout.early_steps)
     n_blocks = len(steps) * layout.ny * len(layout.parts)
     blocks, tile_refs = refs[:n_blocks], refs[n_blocks : n_blocks + 2]
-    out_ref, weights, rows, sums, weight_sems, row_sems, out_sems = refs[n_blocks + 2 :]
+    out_ref, weights, rows, weight_sems, row_sems = refs[n_blocks + 2 :]
     loads = layout.block_copies(blocks, weights, weight_sems)
     row_loads = [
         layout.row_copies(ref, rows.at[i], row_sems.at[i], steps)
@@ -177,33 +202,29 @@
         copy.start()
     for copy in loads:
         copy.wait()
-    stores = []
     for i in range(2):
         for copy in row_loads[i]:
             copy.wait()
-        sums[i] = product(rows.at[i], weights, 0, layout.early)
-        stores.append(pltpu.make_async_copy(sums.at[i], out_ref.at[i], out_sems.at[i]))
-        stores[i].start()
-    for store in stores:
-        store.wait()
+        out_ref[i] = product(rows.at[i], weights, 0, layout.early)
 
 
 def early_mlp(layout, blocks, tiles):
     n_rows = tiles[0].shape[0]
     cols = blocks[0].shape[1]
     hbm = pl.BlockSpec(memory_space=pltpu.HBM)
+    vmem = pl.BlockSpec(memory_space=pltpu.VMEM)
     return pl.pallas_call(
         functools.partial(early_kernel, layout),
         in_specs=[hbm] * (len(blocks) + 2),
-        out_specs=hbm,
-        out_shape=pltpu.HBM((2, n_rows, cols), jnp.float32),
+        out_specs=(vmem, vmem),
+        out_shape=(
+            pltpu.VMEM((2, n_rows, cols), jnp.float32),
+            pltpu.VMEM((layout.width, cols), jnp.bfloat16),
+        ),
         scratch_shapes=[
-            pltpu.VMEM((layout.early, cols), jnp.bfloat16),
-            pltpu.VMEM((2, n_rows, layout.early), jnp.bfloat16),
-            pltpu.VMEM((2, n_rows, cols), jnp.float32),
+            pltpu.VMEM((2, n_rows, layout.early_steps * layout.pair), jnp.bfloat16),
             pltpu.SemaphoreType.DMA((len(blocks),)),
             pltpu.SemaphoreType.DMA((2, layout.nz)),
-            pltpu.SemaphoreType.DMA((2,)),
         ],
         compiler_params=pltpu.CompilerParams(vmem_limit_bytes=MLP_VMEM),
         cost_estimate=pl.CostEstimate(
@@ -214,43 +235,28 @@
     )(*in_hbm(*blocks, *tiles))
 
 
-def middle_kernel(layout, length, *refs):
-    n_blocks = layout.nz * layout.ny * len(layout.parts)
-    n_sums = 1 if layout.relative else 0
+def middle_kernel(layout, length, n_blocks, *refs):
     blocks, tile_refs = refs[:n_blocks], refs[n_blocks : n_blocks + 3]
-    sum_refs = refs[n_blocks + 3 : n_blocks + 3 + n_sums]
-    out_ref, weights, rows, sums, even, odd, weight_sems, row_sems, sum_sems = refs[
-        n_blocks + 3 + n_sums :
-    ]
+    early_refs = refs[n_blocks + 3 : -7]
+    out_ref, weights, rows, even, odd, weight_sems, row_sems = refs[-7:]
     early = layout.early
-    loads = layout.block_copies(blocks, weights, weight_sems)
-    late_blocks = early // layout.depth * len(layout.parts)
+    loads = layout.block_copies(blocks, weights, weight_sems, layout.nz)
     steps = [range(early // layout.pair, layout.nz)] * 2 + [range(layout.nz)]
     row_loads = [
         layout.row_copies(ref, rows.at[i], row_sems.at[i], steps[i])
         for i, ref in enumerate(tile_refs)
     ]
-    sum_loads = [
-        pltpu.make_async_copy(ref.at[i], sums.at[i], sum_sems.at[i])
-        for ref in sum_refs
-        for i in range(2)
-    ]
-    for copy in loads[late_blocks:] + row_loads[0] + sum_loads[:1]:
-        copy.start()
-    for copy in row_loads[1] + sum_loads[1:] + row_loads[2] + loads[:late_blocks]:
-        copy.start()
-    waits = [
-        loads[late_blocks:] + row_loads[0] + sum_loads[:1],
-        row_loads[1] + sum_loads[1:],
-        row_loads[2] + loads[:late_blocks],
-    ]
+    waits = [row_loads[0] + loads, row_loads[1], row_loads[2]]
+    for copies in waits:
+        for copy in copies:
+            copy.start()
     pending = None
     for i in range(3):
         for copy in waits[i]:
             copy.wait()
         both = (even, odd)[i % 2]
-        if i < 2 and n_sums:
-            both[...] = product(rows.at[i], weights, early, layout.width) + sums[i]
+        if i < 2 and early:
+            both[...] = product(rows.at[i], weights, early, layout.width) + early_refs[0][i]
         else:
             both[...] = product(rows.at[i], weights, 0, layout.width)
         if pending is not None:
@@ -259,53 +265,55 @@
     gated_means(*pending, length)
 
 
-def middle_mlp(layout, blocks, tiles, sums, length):
+def middle_mlp(layout, blocks, tiles, early, length):
     n_rows, width = tiles[0].shape
     cols = blocks[0].shape[1]
     hbm = pl.BlockSpec(memory_space=pltpu.HBM)
+    vmem = pl.BlockSpec(memory_space=pltpu.VMEM)
     return pl.pallas_call(
-        functools.partial(middle_kernel, layout, length),
-        in_specs=[hbm] * (len(blocks) + 3 + len(sums)),
-        out_specs=pl.BlockSpec(memory_space=pltpu.VMEM),
-        out_shape=jax.ShapeDtypeStruct((3 * n_rows // length, cols // 2), jnp.float32),
+        functools.partial(middle_kernel, layout, length, len(blocks)),
+        in_specs=[hbm] * (len(blocks) + 3) + [vmem] * len(early),
+        out_specs=(vmem, vmem),
+        out_shape=(
+            pltpu.VMEM((3 * n_rows // length, cols // 2), jnp.float32),
+            pltpu.VMEM((width, cols), jnp.bfloat16),
+        ),
+        input_output_aliases={len(blocks) + 4: 1} if early else {},
         scratch_shapes=[
-            pltpu.VMEM((width, cols), jnp.bfloat16),
             pltpu.VMEM((3, n_rows, width), jnp.bfloat16),
-            pltpu.VMEM((2, n_rows, cols), jnp.float32),
             pltpu.VMEM((n_rows, cols), jnp.float32),
             pltpu.VMEM((n_rows, cols), jnp.float32),
             pltpu.SemaphoreType.DMA((len(blocks),)),
             pltpu.SemaphoreType.DMA((3, layout.nz)),
-            pltpu.SemaphoreType.DMA((2,)),
         ],
         compiler_params=pltpu.CompilerParams(vmem_limit_bytes=MLP_VMEM),
         cost_estimate=pl.CostEstimate(
             flops=4 * n_rows * width * cols,
-            bytes_accessed=2 * (3 * n_rows * width + width * cols) + 8 * n_rows * cols,
+            bytes_accessed=2 * (3 * n_rows * width + width * cols),
             transcendentals=0,
         ),
-    )(*in_hbm(*blocks[:-2]), *blocks[-2:], *in_hbm(*tiles, *sums))
-
-
-def last_kernel(layout, length, n_grp, n_sub, means_ref, *refs):
-    n_blocks = layout.nz * layout.ny * len(layout.parts)
-    blocks, tiles_ref = refs[:n_blocks], refs[n_blocks]
-    out_ref, weights, rows, both, means, weight_sems, row_sems = refs[n_blocks + 1 :]
-    loads = layout.block_copies(blocks, weights, weight_sems)
+    )(*blocks, *in_hbm(*tiles), *in_vmem(*early))
+
+
+def last_kernel(
+    layout, length, n_grp, n_sub, means_ref, weights, tiles_ref, out_ref, rows, both, means, row_sems
+):
     row_loads = layout.row_copies(tiles_ref, rows, row_sems, range(layout.nz))
-    for copy in row_loads + loads:
+    for copy in row_loads:
         copy.start()
-    for copy in row_loads + loads:
+    for copy in row_loads:
         copy.wait()
     n_rows = rows.shape[0]
-    for i in range(0, n_rows, length):
-        here = slice(i, i + length)
-        both[here, :] = product(rows.at[here], weights, 0, layout.width)
-    gated_means(both, means, 0, length)
+    half = n_rows // length
+    for i in range(half):
+        here = slice(i * length, (i + 1) * length)
+        both[i][...] = product(rows.at[here], weights, 0, layout.width)
+        if i:
+            gated_means(both[i - 1], means, i - 1, length)
+    gated_means(both[half - 1], means, half - 1, length)
 
     group, core = lax.axis_index("grp"), lax.axis_index("sub")
     low = core == 0
-    half = n_rows // length
 
     def packed(mine, others):
         rows = jnp.concatenate(
@@ -324,25 +332,23 @@
             out_ref[g * n_sub + s] = chosen
 
 
-def last_mlp(layout, means, blocks, tiles, length, n_grp, n_sub):
+def last_mlp(layout, means, weights, tiles, length, n_grp, n_sub):
     n_rows, width = tiles.shape
-    cols = blocks[0].shape[1]
+    cols = weights.shape[1]
     half = n_rows // length
-    hbm = pl.BlockSpec(memory_space=pltpu.HBM)
+    any_spec = pl.BlockSpec(memory_space=pl.ANY)
     vmem = pl.BlockSpec(memory_space=pltpu.VMEM)
     return pl.pallas_call(
         functools.partial(last_kernel, layout, length, n_grp, n_sub),
-        in_specs=[vmem] + [hbm] * (len(blocks) + 1),
+        in_specs=[vmem, vmem, any_spec],
         out_specs=vmem,
         out_shape=jax.ShapeDtypeStruct(
             (n_grp * n_sub, half * cols // LANES, LANES), jnp.bfloat16
         ),
         scratch_shapes=[
-            pltpu.VMEM((width, cols), jnp.bfloat16),
             pltpu.VMEM((n_rows, width), jnp.bfloat16),
-            pltpu.VMEM((n_rows, cols), jnp.float32),
+            [pltpu.VMEM((length, cols), jnp.float32) for _ in range(half)],
             pltpu.VMEM((half, cols // 2), jnp.float32),
-            pltpu.SemaphoreType.DMA((len(blocks),)),
             pltpu.SemaphoreType.DMA((layout.nz,)),
         ],
         compiler_params=pltpu.CompilerParams(vmem_limit_bytes=MLP_VMEM),
@@ -351,7 +357,7 @@
             bytes_accessed=2 * (n_rows * width + width * cols),
             transcendentals=0,
         ),
-    )(means, *in_hbm(*blocks[:-2]), *blocks[-2:], tiles)
+    )(*in_vmem(means, weights), tiles)
 
 
 def small_mod(value, rate):
@@ -542,26 +548,15 @@
     ny = 2
     nz = n_dev // ny
     heads = slide_wq.shape[1] * n_sub // HD
-    group, core = lax.axis_index("grp"), lax.axis_index("sub")
+    core = lax.axis_index("sub")
 
     to_pair = [(g, g ^ 1) for g in range(n_grp)]
     to_sibling = [(s, s ^ 1) for s in range(n_sub)]
     along_z = [(d, (d + ny) % n_dev) for d in range(n_dev)]
     along_y = [(d, d ^ 1) for d in range(n_dev)]
 
-    half_cols = hidden_cols // 2
     layout = Layout(n_dev, ny, gate_weight.shape[0])
-    held = [
-        jnp.concatenate(
-            [
-                lax.dynamic_slice_in_dim(w[part], (group % 2) * half_cols, half_cols, 1)
-                for w in (gate_weight, up_weight)
-            ],
-            axis=1,
-        )
-        for part in layout.parts
-    ]
-    first = norm_tiles(tiles, tile_gain)
+    first, *held = start_work(tiles, tile_gain, gate_weight, up_weight, layout.parts)
     second = lax.ppermute(first, "sub", to_sibling)
     pair_first = lax.ppermute(first, "grp", to_pair)
 
@@ -570,9 +565,8 @@
     wk_far = lax.ppermute(slide_wk, "sub", to_sibling)
     wv_far = lax.ppermute(slide_wv, "sub", to_sibling)
     out_cols = slide_wo.shape[1] // n_sub
-    wo_far = lax.ppermute(
-        lax.dynamic_slice_in_dim(slide_wo, (1 - core) * out_cols, out_cols, 1), "sub", to_sibling
-    )
+    wo_part = lax.dynamic_slice_in_dim(slide_wo, (1 - core) * out_cols, out_cols, 1)
+    wo_far = lax.ppermute(wo_part, "sub", to_sibling)
     smem = pl.BlockSpec(memory_space=pltpu.SMEM)
     vmem = pl.BlockSpec(memory_space=pltpu.VMEM)
     many = pl.pallas_call(
@@ -583,7 +577,7 @@
         compiler_params=pltpu.CompilerParams(vmem_limit_bytes=SMALL_VMEM),
     )(counts, slide_of, rates)
 
-    held[1] = after(held[1], first, proj_far, wq_far)
+    held[1] = after(held[1], proj_far, wq_far)
     steps = []
     last = None
     for step in range(nz):
@@ -593,23 +587,24 @@
                 arrived = lax.ppermute(held[part], "dev", along_z)
                 others = [steps[-1][len(held) + part]]
                 if (step, part) == (1, 1):
-                    others += [second, many]
+                    others += [second]
+                if (step, part) == (nz - 1, 0):
+                    others += [many, wo_part]
                 if last is not None:
                     others.append(last)
                 held[part] = last = after(arrived, *others)
             sent.append(lax.ppermute(held[part], "dev", along_y))
         steps.append([*held, *sent])
     blocks = [block for step in steps for block in step]
-    sums = []
+    early = []
     if layout.relative:
-        early_blocks = blocks[: layout.early_steps * len(steps[0])]
-        sums = [early_mlp(layout, early_blocks, [after(first, last), second])]
-    pair_first = after(pair_first, *steps[-1][-2:], *sums)
+        n_early = layout.early_steps * len(steps[0])
+        early = early_mlp(layout, blocks[:n_early], [after(first, last), second])
+        blocks = blocks[n_early:]
+    pair_first = after(pair_first, *steps[-1][-2:], *early)
     pair_second = lax.ppermute(pair_first, "sub", to_sibling)
-
-    means = middle_mlp(layout, blocks, [first, second, pair_first], sums, length)
-    means = after(means, wk_far, wv_far, wo_far)
-    parts = last_mlp(layout, means, blocks, pair_second, length, n_grp, n_sub)
+    means, weights = middle_mlp(layout, blocks, [first, second, pair_first], early, length)
+    parts = last_mlp(layout, means, weights, pair_second, length, n_grp, n_sub)
     parts = lax.all_to_all(parts, ("grp", "sub"), split_axis=0, concat_axis=0, tiled=True)
 
     out_width = embed_proj.shape[1]

time: 88.6 us -> 89.3 us (level)
  local copies, waits for them, and re-layouts: 4.28 us -> 1.43 us
  starting transfers between devices: 24.4 us -> 26.8 us
  Pallas kernels: 30.3 us -> 32.6 us
    pallas_call x2, Pallas kernels: 11.4 us -> 18.5 us  [the longest x1 13.1 us: start_work(): pl.pallas_call(functools.partial(start_kernel, parts), in_specs=[hbm] * 4...]
    pallas_call x1, Pallas kernels: 4.91 us -> 2.07 us  [last_mlp(): pl.pallas_call(functools.partial(last_kernel, layout, length, n_grp, n_su...]
    ppermute x8, waiting for transfers between devices: 5.42 us -> 2.71 us  [on_device(): sent.append(lax.ppermute(held[part], 'dev', along_y))]
    pallas_call x1, Pallas kernels: 7.05 us -> 5.11 us  [early_mlp(): pl.pallas_call(functools.partial(early_kernel, layout), in_specs=[hbm] *...]
    slice x2 -> x0, local copies, waits for them, and re-layouts: 1.84 us -> none  [on_device(): w[part]]
    all_to_all x1, starting transfers between devices: 3.43 us -> 5.16 us  [on_device(): sent = lax.all_to_all(sent, 'dev', split_axis=0, concat_axis=0, tiled=True)]
    ppermute x6, waiting for transfers between devices: 11.9 us -> 13.3 us  [on_device(): arrived = lax.ppermute(held[part], 'dev', along_z)]
  transfers between devices with their start and end apart: 23 -> 23, of which waited for: 9 -> 11; matrix products, arithmetic and copies ran while one was open for 3% -> 1% of each run, Pallas kernels for 24% -> 34%
where the time goes in v8:
time: 89.3 us; the launch traced here: 89 us
  Pallas kernels  32.6 us (37%)
  starting transfers between devices  26.8 us (30%)
  waiting for transfers between devices  21.1 us (24%)
  blocking collectives  6.21 us (7%)
  local copies, waits for them, and re-layouts  1.43 us (2%)
    ppermute x6, waiting for transfers between devices, on_device(): arrived = lax.ppermute(held[part], 'dev', along_z)  13.3 us
    pallas_call x1, Pallas kernels, start_work(): pl.pallas_call(functools.partial(start_kernel, parts), in_specs=[hbm] * 4...  13.1 us
    ppermute x8, starting transfers between devices, on_device(): sent.append(lax.ppermute(held[part], 'dev', along_y))  12.1 us
    all_to_all x1, blocking collectives, on_device(): lax.all_to_all(parts, ('grp', 'sub'), split_axis=0, concat_axis=0, tiled=...  6.21 us
    pallas_call x1, Pallas kernels, middle_mlp(): pl.pallas_call(functools.partial(middle_kernel, layout, length, len(block...  5.4 us
    all_to_all x1, starting transfers between devices, on_device(): sent = lax.all_to_all(sent, 'dev', split_axis=0, concat_axis=0, tiled=True)  5.16 us
    pallas_call x1, Pallas kernels, early_mlp(): pl.pallas_call(functools.partial(early_kernel, layout), in_specs=[hbm] *...  5.11 us
    ppermute x6, starting transfers between devices, on_device(): arrived = lax.ppermute(held[part], 'dev', along_z)  4.85 us
  transfers between devices with their start and end apart: 23, of which 11 were waited for; matrix products, arithmetic and copies ran while one was open for 1% of the time, Pallas kernels for 34%

profile of v8, /device:TPU:0, one launch (start us, length us, event | category | flops | bytes accessed | tf_op | source)
XLA Modules:
  0.0 89.0 jit_solution(4470283468851515858)
XLA Ops:
  1.2 13.1 %shard_map.140 = (bf16[512,1536]{1,0:T(8,128)(2,1)}, bf16[96,1024]{1,0:T(8,128)(2,1)}, bf16[96,1024]{1,0:T(8,128)(2,1)}) custom-call(bf16[4,256,1536]{2,1,0:T(8,128)(2,1)} %tiles_ref.1, f32[1536]{0:T(1024)} %gain_ref.3, bf16[192,1024]{1,0:T(8,128)(2,1)} %gate_ref.1, bf16[192,1024]{1,0:T(8,128)(2,1)} %up_ref.1), custom_call_target="tpu_custom_call" | custom-call | tf_op jit(solution)/shard_map/pallas_call | solution.py:92
  14.5 2.9 %collective-permute-start.17 = (bf16[512,1536]{1,0:T(8,128)(2,1)}, bf16[512,1536]{1,0:T(8,128)(2,1)}, u32[]{:S(2)}, u32[]{:S(2)}) collective-permute-start(bf16[512,1536]{1,0:T(8,128)(2,1)} %get-tuple-element.39.refs_12_.refs_4_), channel_id=1, source_target_pairs={{0,16},{16,0},{1,17},{17,1},{2,18},{18,2},{3,19},{19,3},{4,20},{20... | collective-permute-start | bytes 4718600 | tf_op jit(solution)/shard_map/ppermute | solution.py:561
  17.4 1.5 %collective-permute-start.1 = (bf16[96,1024]{1,0:T(8,128)(2,1)}, bf16[96,1024]{1,0:T(8,128)(2,1)S(1)}, u32[]{:S(2)}, u32[]{:S(2)}) collective-permute-start(bf16[96,1024]{1,0:T(8,128)(2,1)} %get-tuple-element.29.refs_0_), channel_id=1, source_target_pairs={{0,2},{2,0},{4,6},{6,4},{8,10},{10,8},{12,14},{14,12},{1,3},{3,1},... | collective-permute-start | bytes 589832 | tf_op jit(solution)/shard_map/ppermute | solution.py:596
  19.4 2.0 %collective-permute-start = (bf16[96,1024]{1,0:T(8,128)(2,1)}, bf16[96,1024]{1,0:T(8,128)(2,1)S(1)}, u32[]{:S(2)}, u32[]{:S(2)}) collective-permute-start(bf16[96,1024]{1,0:T(8,128)(2,1)} %get-tuple-element.29.refs_0_), channel_id=1, source_target_pairs={{0,4},{2,6},{4,8},{6,10},{8,12},{10,14},{12,0},{14,2},{1,5},{3,7},... | collective-permute-start | bytes 589832 | tf_op jit(solution)/shard_map/ppermute | solution.py:587
  22.9 2.4 %collective-permute-done.1.refs_2_ = bf16[96,1024]{1,0:T(8,128)(2,1)S(1)} collective-permute-done((bf16[96,1024]{1,0:T(8,128)(2,1)}, bf16[96,1024]{1,0:T(8,128)(2,1)S(1)}, u32[]{:S(2)}, u32[]{:S(2)}) %collective-permute-start.1) | collective-permute-done | bytes 196640 | tf_op jit(solution)/shard_map/ppermute | solution.py:596
  25.3 1.6 %collective-permute-start.6 = (bf16[96,1024]{1,0:T(8,128)(2,1)}, bf16[96,1024]{1,0:T(8,128)(2,1)S(1)}, u32[]{:S(2)}, u32[]{:S(2)}) collective-permute-start(bf16[96,1024]{1,0:T(8,128)(2,1)} %get-tuple-element.32.refs_1_), channel_id=1, source_target_pairs={{0,4},{2,6},{4,8},{6,10},{8,12},{10,14},{12,0},{14,2},{1,5},{3,7},... | collective-permute-start | bytes 589832 | tf_op jit(solution)/shard_map/ppermute | solution.py:587
  26.9 2.1 %collective-permute-done.refs_4_ = bf16[96,1024]{1,0:T(8,128)(2,1)S(1)} collective-permute-done((bf16[96,1024]{1,0:T(8,128)(2,1)}, bf16[96,1024]{1,0:T(8,128)(2,1)S(1)}, u32[]{:S(2)}, u32[]{:S(2)}) %collective-permute-start) | collective-permute-done | bytes 196640 | tf_op jit(solution)/shard_map/ppermute | solution.py:587
  30.6 3.0 %collective-permute-done.6.refs_5_ = bf16[96,1024]{1,0:T(8,128)(2,1)S(1)} collective-permute-done((bf16[96,1024]{1,0:T(8,128)(2,1)}, bf16[96,1024]{1,0:T(8,128)(2,1)S(1)}, u32[]{:S(2)}, u32[]{:S(2)}) %collective-permute-start.6) | collective-permute-done | bytes 196640 | tf_op jit(solution)/shard_map/ppermute | solution.py:587
  33.7 1.6 %collective-permute-start.12 = (bf16[96,1024]{1,0:T(8,128)(2,1)S(1)}, bf16[96,1024]{1,0:T(8,128)(2,1)S(1)}, u32[]{:S(2)}, u32[]{:S(2)}) collective-permute-start(bf16[96,1024]{1,0:T(8,128)(2,1)S(1)} %collective-permute-done.6.refs_5_), channel_id=1, source_target_pairs={{0,2},{2,0},{4,6},{6,4},{8,10},{10,8},{12,14},{14,12},{1,3},{3,1},... | collective-permute-start | bytes 589832 | tf_op jit(solution)/shard_map/ppermute | solution.py:596
  36.4 2.8 %collective-permute-done.2.refs_8_ = bf16[96,1024]{1,0:T(8,128)(2,1)} collective-permute-done((bf16[96,1024]{1,0:T(8,128)(2,1)S(1)}, bf16[96,1024]{1,0:T(8,128)(2,1)}, u32[]{:S(2)}, u32[]{:S(2)}) %collective-permute-start.2) | collective-permute-done | bytes 196640 | tf_op jit(solution)/shard_map/ppermute | solution.py:587
  40.6 2.4 %collective-permute-done.11.refs_9_ = bf16[96,1024]{1,0:T(8,128)(2,1)} collective-permute-done((bf16[96,1024]{1,0:T(8,128)(2,1)S(1)}, bf16[96,1024]{1,0:T(8,128)(2,1)}, u32[]{:S(2)}, u32[]{:S(2)}) %collective-permute-start.11) | collective-permute-done | bytes 196640 | tf_op jit(solution)/shard_map/ppermute | solution.py:587
  43.1 1.7 %collective-permute-start.14 = (bf16[96,1024]{1,0:T(8,128)(2,1)}, bf16[96,1024]{1,0:T(8,128)(2,1)}, u32[]{:S(2)}, u32[]{:S(2)}) collective-permute-start(bf16[96,1024]{1,0:T(8,128)(2,1)} %collective-permute-done.11.refs_9_), channel_id=1, source_target_pairs={{0,2},{2,0},{4,6},{6,4},{8,10},{10,8},{12,14},{14,12},{1,3},{3,1},... | collective-permute-start | bytes 589832 | tf_op jit(solution)/shard_map/ppermute | solution.py:596
  47.0 2.4 %collective-permute-done.9.refs_0_ = bf16[96,1024]{1,0:T(8,128)(2,1)S(1)} collective-permute-done((bf16[96,1024]{1,0:T(8,128)(2,1)}, bf16[96,1024]{1,0:T(8,128)(2,1)S(1)}, u32[]{:S(2)}, u32[]{:S(2)}) %collective-permute-start.9) | collective-permute-done | bytes 196640 | tf_op jit(solution)/shard_map/ppermute | solution.py:587
  49.4 1.5 %collective-permute-start.15 = (bf16[96,1024]{1,0:T(8,128)(2,1)S(1)}, bf16[96,1024]{1,0:T(8,128)(2,1)S(1)}, u32[]{:S(2)}, u32[]{:S(2)}) collective-permute-start(bf16[96,1024]{1,0:T(8,128)(2,1)S(1)} %collective-permute-done.9.refs_0_), channel_id=1, source_target_pairs={{0,2},{2,0},{4,6},{6,4},{8,10},{10,8},{12,14},{14,12},{1,3},{3,1},... | collective-permute-start | bytes 589832 | tf_op jit(solution)/shard_map/ppermute | solution.py:596
  51.5 1.5 %collective-permute-start.16 = (bf16[96,1024]{1,0:T(8,128)(2,1)S(1)}, bf16[96,1024]{1,0:T(8,128)(2,1)S(1)}, u32[]{:S(2)}, u32[]{:S(2)}) collective-permute-start(bf16[96,1024]{1,0:T(8,128)(2,1)S(1)} %collective-permute-done.13.refs_1_), channel_id=1, source_target_pairs={{0,2},{2,0},{4,6},{6,4},{8,10},{10,8},{12,14},{14,12},{1,3},{3,1},... | collective-permute-start | bytes 589832 | tf_op jit(solution)/shard_map/ppermute | solution.py:596
  53.0 5.1 %shard_map.142 = (f32[2,512,1024]{2,1,0:T(8,128)S(1)}, bf16[1536,1024]{1,0:T(8,128)(2,1)S(1)}) custom-call(bf16[96,1024]{1,0:T(8,128)(2,1)} %get-tuple-element.29.refs_0_, bf16[96,1024]{1,0:T(8,128)(2,1)} %get-tuple-element.32.refs_1_, bf16[96,1024]{1,0:T(8,128)(2,1)} %copy-done.12, bf16[96,1024]{1,0:T(8,128)(2,1)} %copy-done.14, ...), custom_call_target="tpu_custom_call" | custom-call | flops 2147483648 | bytes 8388608 | tf_op jit(solution)/shard_map/pallas_call | solution.py:216
  59.3 5.4 %shard_map.143 = (f32[6,512]{1,0:T(8,128)S(1)}, bf16[1536,1024]{1,0:T(8,128)(2,1)S(1)}) custom-call(bf16[96,1024]{1,0:T(8,128)(2,1)S(1)} %collective-permute-done.9.refs_0_, bf16[96,1024]{1,0:T(8,128)(2,1)S(1)} %collective-permute-done.13.refs_1_, bf16[96,1024]{1,0:T(8,128)(2,1)S(1)} %collective-permute-done.15.refs_2_, ...), custom_call_target="tpu_custom_call", output_to_operand_aliasing={{1}: (8, {})} | custom-call | flops 3221225472 | bytes 7864320 | tf_op jit(solution)/shard_map/pallas_call | solution.py:273
  64.7 2.1 %shard_map.144 = bf16[4,16,128]{2,1,0:T(8,128)(2,1)S(1)} custom-call(f32[6,512]{1,0:T(8,128)S(1)} %get-tuple-element.43.means_ref, bf16[1536,1024]{1,0:T(8,128)(2,1)S(1)} %get-tuple-element.44.weights, bf16[512,1536]{1,0:T(8,128)(2,1)S(1)} %collective-permute-done.18.tiles_ref), custom_call_target="tpu_custom_call" | custom-call | flops 1610612736 | bytes 4718592 | tf_op jit(solution)/shard_map/pallas_call | solution.py:341
  66.8 6.2 %all_to_all.10.parts_ref = bf16[4,16,128]{2,1,0:T(8,128)(2,1)S(1)} all-to-all(bf16[4,16,128]{2,1,0:T(8,128)(2,1)S(1)} %shard_map.144), channel_id=1, replica_groups=mesh['grp'=2,'dev'=8,'sub'=2] {'grp','sub'}, dimensions={0} | all-to-all | bytes 32768 | tf_op jit(solution)/shard_map/all_to_all | solution.py:608
  73.0 1.9 %shard_map.145 = (bf16[4,1024]{1,0:T(4,128)(2,1)}, f32[8,768]{1,0:T(8,128)S(1)}, bf16[8,16,256]{2,1,0:T(8,128)(2,1)}) custom-call(s32[8]{0:T(128)S(1)} %copy-done.3, bf16[4,16,128]{2,1,0:T(8,128)(2,1)S(1)} %all_to_all.10.parts_ref, f32[768]{0:T(1024)S(1)} %copy-done.2, bf16[1024,768]{1,0:T(8,128)(2,1)S(1)} %copy-done, ...), custom_call_target="tpu_custom_call" | custom-call | tf_op jit(solution)/shard_map/pallas_call | solution.py:614
  74.9 5.2 %all-to-all-start.1 = ((bf16[8,16,256]{2,1,0:T(8,128)(2,1)}), bf16[8,16,256]{2,1,0:T(8,128)(2,1)S(1)}, u32[]{:S(2)}, u32[]{:S(2)}) async-start(bf16[8,16,256]{2,1,0:T(8,128)(2,1)} %get-tuple-element.46), calls=%async_computation.1 | async-start | bytes 131072 | tf_op jit(solution)/shard_map/all_to_all | solution.py:625
  80.0 2.3 %shard_map.146 = (bf16[96,768]{1,0:T(8,128)(2,1)S(1)}, bf16[768,384]{1,0:T(8,128)(2,1)S(1)}, bf16[768,384]{1,0:T(8,128)(2,1)S(1)}, bf16[768,384]{1,0:T(8,128)(2,...) custom-call(f32[8,768]{1,0:T(8,128)S(1)} %get-tuple-element.47.mixed, ...), custom_call_target="tpu_custom_call" | custom-call | tf_op jit(solution)/shard_map/pallas_call | solution.py:628
  82.3 4.6 %all-to-all-done.1.sent_ref = bf16[8,16,256]{2,1,0:T(8,128)(2,1)S(1)} async-done(((bf16[8,16,256]{2,1,0:T(8,128)(2,1)}), bf16[8,16,256]{2,1,0:T(8,128)(2,1)S(1)}, u32[]{:S(2)}, u32[]{:S(2)}) %all-to-all-start.1) | async-done | bytes 65568 | tf_op jit(solution)/shard_map/all_to_all | solution.py:625
  86.9 2.1 %shard_map.147 = bf16[4,384]{1,0:T(4,128)(2,1)} custom-call(s32[8]{0:T(128)S(1)} %copy-done.3, bf16[8,16,256]{2,1,0:T(8,128)(2,1)S(1)} %all-to-all-done.1.sent_ref, f32[8,768]{1,0:T(8,128)S(1)} %get-tuple-element.47.mixed_ref, bf16[96,768]{1,0:T(8,128)(2,1)S(1)} %get-tuple-element.48.query_ref, bf16[768,384]{1,0:T(8,128)(2,1)S(1)} %get-tuple-element.49.wk_ref, ...), custom_call_target="tpu_custom_call" | custom-call | tf_op jit(solution)/shard_map/pallas_call | solution.py:642
  (68 shorter events, 10.8 us)
Async XLA Ops:
  0.7 45.5 %copy-start.7 = (bf16[384,768]{1,0:T(8,128)(2,1)S(1)}, bf16[384,768]{1,0:T(8,128)(2,1)}, u32[]{:S(2)}) copy-start(bf16[384,768]{1,0:T(8,128)(2,1)} %refs_6_.1) | copy-start | bytes 1769476
  0.7 20.7 %collective-permute-start.4 = (bf16[1024,768]{1,0:T(8,128)(2,1)}, bf16[1024,768]{1,0:T(8,128)(2,1)S(1)}, u32[]{:S(2)}, u32[]{:S(2)}) collective-permute-start(bf16[1024,768]{1,0:T(8,128)(2,1)} %near_ref.1), channel_id=1, source_target_pairs={{0,1},{1,0},{2,3},{3,2},{4,5},{5,4},{6,7},{7,6},{8,9},{9,8},{10,11... | collective-permute-start | bytes 4718600 | tf_op jit(solution)/shard_map/ppermute | solution.py:563
  14.3 16.2 %collective-permute-start.8 = (bf16[512,1536]{1,0:T(8,128)(2,1)}, bf16[512,1536]{1,0:T(8,128)(2,1)S(1)}, u32[]{:S(2)}, u32[]{:S(2)}) collective-permute-start(bf16[512,1536]{1,0:T(8,128)(2,1)} %get-tuple-element.39.refs_12_.refs_4_), channel_id=1, source_target_pairs={{0,1},{1,0},{2,3},{3,2},{4,5},{5,4},{6,7},{7,6},{8,9},{9,8},{10,11... | collective-permute-start | bytes 4718600 | tf_op jit(solution)/shard_map/ppermute | solution.py:560
  14.5 43.7 %collective-permute-start.17 = (bf16[512,1536]{1,0:T(8,128)(2,1)}, bf16[512,1536]{1,0:T(8,128)(2,1)}, u32[]{:S(2)}, u32[]{:S(2)}) collective-permute-start(bf16[512,1536]{1,0:T(8,128)(2,1)} %get-tuple-element.39.refs_12_.refs_4_), channel_id=1, source_target_pairs={{0,16},{16,0},{1,17},{17,1},{2,18},{18,2},{3,19},{19,3},{4,20},{20... | collective-permute-start | bytes 4718600 | tf_op jit(solution)/shard_map/ppermute | solution.py:561
  17.4 2.0 %collective-permute-start.5 = (bf16[768,384]{1,0:T(8,128)(2,1)S(1)}, bf16[768,384]{1,0:T(8,128)(2,1)S(1)}, u32[]{:S(2)}, u32[]{:S(2)}) collective-permute-start(bf16[768,384]{1,0:T(8,128)(2,1)S(1)} %copy-done.8), channel_id=1, source_target_pairs={{0,1},{1,0},{2,3},{3,2},{4,5},{5,4},{6,7},{7,6},{8,9},{9,8},{10,11... | collective-permute-start | bytes 1769480 | tf_op jit(solution)/shard_map/ppermute | solution.py:564
  17.4 7.9 %collective-permute-start.1 = (bf16[96,1024]{1,0:T(8,128)(2,1)}, bf16[96,1024]{1,0:T(8,128)(2,1)S(1)}, u32[]{:S(2)}, u32[]{:S(2)}) collective-permute-start(bf16[96,1024]{1,0:T(8,128)(2,1)} %get-tuple-element.29.refs_0_), channel_id=1, source_target_pairs={{0,2},{2,0},{4,6},{6,4},{8,10},{10,8},{12,14},{14,12},{1,3},{3,1},... | collective-permute-start | bytes 589832 | tf_op jit(solution)/shard_map/ppermute | solution.py:596
  19.4 9.6 %collective-permute-start = (bf16[96,1024]{1,0:T(8,128)(2,1)}, bf16[96,1024]{1,0:T(8,128)(2,1)S(1)}, u32[]{:S(2)}, u32[]{:S(2)}) collective-permute-start(bf16[96,1024]{1,0:T(8,128)(2,1)} %get-tuple-element.29.refs_0_), channel_id=1, source_target_pairs={{0,4},{2,6},{4,8},{6,10},{8,12},{10,14},{12,0},{14,2},{1,5},{3,7},... | collective-permute-start | bytes 589832 | tf_op jit(solution)/shard_map/ppermute | solution.py:587
  21.4 9.2 %collective-permute-start.7 = (bf16[96,1024]{1,0:T(8,128)(2,1)}, bf16[96,1024]{1,0:T(8,128)(2,1)S(1)}, u32[]{:S(2)}, u32[]{:S(2)}) collective-permute-start(bf16[96,1024]{1,0:T(8,128)(2,1)} %get-tuple-element.32.refs_1_), channel_id=1, source_target_pairs={{0,2},{2,0},{4,6},{6,4},{8,10},{10,8},{12,14},{14,12},{1,3},{3,1},... | collective-permute-start | bytes 589832 | tf_op jit(solution)/shard_map/ppermute | solution.py:596
  25.3 8.3 %collective-permute-start.6 = (bf16[96,1024]{1,0:T(8,128)(2,1)}, bf16[96,1024]{1,0:T(8,128)(2,1)S(1)}, u32[]{:S(2)}, u32[]{:S(2)}) collective-permute-start(bf16[96,1024]{1,0:T(8,128)(2,1)} %get-tuple-element.32.refs_1_), channel_id=1, source_target_pairs={{0,4},{2,6},{4,8},{6,10},{8,12},{10,14},{12,0},{14,2},{1,5},{3,7},... | collective-permute-start | bytes 589832 | tf_op jit(solution)/shard_map/ppermute | solution.py:587
  29.1 7.4 %collective-permute-start.3 = (bf16[96,1024]{1,0:T(8,128)(2,1)S(1)}, bf16[96,1024]{1,0:T(8,128)(2,1)S(1)}, u32[]{:S(2)}, u32[]{:S(2)}) collective-permute-start(bf16[96,1024]{1,0:T(8,128)(2,1)S(1)} %collective-permute-done.refs_4_), channel_id=1, source_target_pairs={{0,2},{2,0},{4,6},{6,4},{8,10},{10,8},{12,14},{14,12},{1,3},{3,1},... | collective-permute-start | bytes 589832 | tf_op jit(solution)/shard_map/ppermute | solution.py:596
  30.6 8.6 %collective-permute-start.2 = (bf16[96,1024]{1,0:T(8,128)(2,1)S(1)}, bf16[96,1024]{1,0:T(8,128)(2,1)}, u32[]{:S(2)}, u32[]{:S(2)}) collective-permute-start(bf16[96,1024]{1,0:T(8,128)(2,1)S(1)} %collective-permute-done.refs_4_), channel_id=1, source_target_pairs={{0,4},{2,6},{4,8},{6,10},{8,12},{10,14},{12,0},{14,2},{1,5},{3,7},... | collective-permute-start | bytes 589832 | tf_op jit(solution)/shard_map/ppermute | solution.py:587
  33.7 6.9 %collective-permute-start.12 = (bf16[96,1024]{1,0:T(8,128)(2,1)S(1)}, bf16[96,1024]{1,0:T(8,128)(2,1)S(1)}, u32[]{:S(2)}, u32[]{:S(2)}) collective-permute-start(bf16[96,1024]{1,0:T(8,128)(2,1)S(1)} %collective-permute-done.6.refs_5_), channel_id=1, source_target_pairs={{0,2},{2,0},{4,6},{6,4},{8,10},{10,8},{12,14},{14,12},{1,3},{3,1},... | collective-permute-start | bytes 589832 | tf_op jit(solution)/shard_map/ppermute | solution.py:596
  35.3 7.7 %collective-permute-start.11 = (bf16[96,1024]{1,0:T(8,128)(2,1)S(1)}, bf16[96,1024]{1,0:T(8,128)(2,1)}, u32[]{:S(2)}, u32[]{:S(2)}) collective-permute-start(bf16[96,1024]{1,0:T(8,128)(2,1)S(1)} %collective-permute-done.6.refs_5_), channel_id=1, source_target_pairs={{0,4},{2,6},{4,8},{6,10},{8,12},{10,14},{12,0},{14,2},{1,5},{3,7},... | collective-permute-start | bytes 589832 | tf_op jit(solution)/shard_map/ppermute | solution.py:587
  39.2 7.8 %collective-permute-start.10 = (bf16[96,1024]{1,0:T(8,128)(2,1)}, bf16[96,1024]{1,0:T(8,128)(2,1)}, u32[]{:S(2)}, u32[]{:S(2)}) collective-permute-start(bf16[96,1024]{1,0:T(8,128)(2,1)} %collective-permute-done.2.refs_8_), channel_id=1, source_target_pairs={{0,2},{2,0},{4,6},{6,4},{8,10},{10,8},{12,14},{14,12},{1,3},{3,1},... | collective-permute-start | bytes 589832 | tf_op jit(solution)/shard_map/ppermute | solution.py:596
  40.4 9.0 %collective-permute-start.9 = (bf16[96,1024]{1,0:T(8,128)(2,1)}, bf16[96,1024]{1,0:T(8,128)(2,1)S(1)}, u32[]{:S(2)}, u32[]{:S(2)}) collective-permute-start(bf16[96,1024]{1,0:T(8,128)(2,1)} %collective-permute-done.2.refs_8_), channel_id=1, source_target_pairs={{0,4},{2,6},{4,8},{6,10},{8,12},{10,14},{12,0},{14,2},{1,5},{3,7},... | collective-permute-start | bytes 589832 | tf_op jit(solution)/shard_map/ppermute | solution.py:587
  43.0 8.5 %collective-permute-start.13 = (bf16[96,1024]{1,0:T(8,128)(2,1)}, bf16[96,1024]{1,0:T(8,128)(2,1)S(1)}, u32[]{:S(2)}, u32[]{:S(2)}) collective-permute-start(bf16[96,1024]{1,0:T(8,128)(2,1)} %collective-permute-done.11.refs_9_), channel_id=1, source_target_pairs={{0,4},{2,6},{4,8},{6,10},{8,12},{10,14},{12,0},{14,2},{1,5},{3,7},... | collective-permute-start | bytes 589832 | tf_op jit(solution)/shard_map/ppermute | solution.py:587
  43.1 8.4 %collective-permute-start.14 = (bf16[96,1024]{1,0:T(8,128)(2,1)}, bf16[96,1024]{1,0:T(8,128)(2,1)}, u32[]{:S(2)}, u32[]{:S(2)}) collective-permute-start(bf16[96,1024]{1,0:T(8,128)(2,1)} %collective-permute-done.11.refs_9_), channel_id=1, source_target_pairs={{0,2},{2,0},{4,6},{6,4},{8,10},{10,8},{12,14},{14,12},{1,3},{3,1},... | collective-permute-start | bytes 589832 | tf_op jit(solution)/shard_map/ppermute | solution.py:596
  49.4 8.8 %collective-permute-start.15 = (bf16[96,1024]{1,0:T(8,128)(2,1)S(1)}, bf16[96,1024]{1,0:T(8,128)(2,1)S(1)}, u32[]{:S(2)}, u32[]{:S(2)}) collective-permute-start(bf16[96,1024]{1,0:T(8,128)(2,1)S(1)} %collective-permute-done.9.refs_0_), channel_id=1, source_target_pairs={{0,2},{2,0},{4,6},{6,4},{8,10},{10,8},{12,14},{14,12},{1,3},{3,1},... | collective-permute-start | bytes 589832 | tf_op jit(solution)/shard_map/ppermute | solution.py:596
  51.5 6.7 %collective-permute-start.16 = (bf16[96,1024]{1,0:T(8,128)(2,1)S(1)}, bf16[96,1024]{1,0:T(8,128)(2,1)S(1)}, u32[]{:S(2)}, u32[]{:S(2)}) collective-permute-start(bf16[96,1024]{1,0:T(8,128)(2,1)S(1)} %collective-permute-done.13.refs_1_), channel_id=1, source_target_pairs={{0,2},{2,0},{4,6},{6,4},{8,10},{10,8},{12,14},{14,12},{1,3},{3,1},... | collective-permute-start | bytes 589832 | tf_op jit(solution)/shard_map/ppermute | solution.py:596
  58.2 6.5 %collective-permute-start.18 = (bf16[512,1536]{1,0:T(8,128)(2,1)}, bf16[512,1536]{1,0:T(8,128)(2,1)S(1)}, u32[]{:S(2)}, u32[]{:S(2)}) collective-permute-start(bf16[512,1536]{1,0:T(8,128)(2,1)} %collective-permute-done.17.refs_6_), channel_id=1, source_target_pairs={{0,1},{1,0},{2,3},{3,2},{4,5},{5,4},{6,7},{7,6},{8,9},{9,8},{10,11... | collective-permute-start | bytes 4718600 | tf_op jit(solution)/shard_map/ppermute | solution.py:605
  58.3 21.8 %collective-permute-start.19 = (bf16[768,384]{1,0:T(8,128)(2,1)S(1)}, bf16[768,384]{1,0:T(8,128)(2,1)}, u32[]{:S(2)}, u32[]{:S(2)}) collective-permute-start(bf16[768,384]{1,0:T(8,128)(2,1)S(1)} %copy-done.9), channel_id=1, source_target_pairs={{0,1},{1,0},{2,3},{3,2},{4,5},{5,4},{6,7},{7,6},{8,9},{9,8},{10,11... | collective-permute-start | bytes 1769480 | tf_op jit(solution)/shard_map/ppermute | solution.py:565
  58.8 21.3 %collective-permute-start.20 = (bf16[768,384]{1,0:T(8,128)(2,1)S(1)}, bf16[768,384]{1,0:T(8,128)(2,1)}, u32[]{:S(2)}, u32[]{:S(2)}) collective-permute-start(bf16[768,384]{1,0:T(8,128)(2,1)S(1)} %copy-done.10), channel_id=1, source_target_pairs={{0,1},{1,0},{2,3},{3,2},{4,5},{5,4},{6,7},{7,6},{8,9},{9,8},{10,11... | collective-permute-start | bytes 1769480 | tf_op jit(solution)/shard_map/ppermute | solution.py:566
  58.8 21.2 %collective-permute-start.21 = (bf16[384,384]{1,0:T(8,128)(2,1)}, bf16[384,384]{1,0:T(8,128)(2,1)}, u32[]{:S(2)}, u32[]{:S(2)}) collective-permute-start(bf16[384,384]{1,0:T(8,128)(2,1)} %constant_dynamic-slice_fusion), channel_id=1, source_target_pairs={{0,1},{1,0},{2,3},{3,2},{4,5},{5,4},{6,7},{7,6},{8,9},{9,8},{10,11... | collective-permute-start | bytes 884744 | tf_op jit(solution)/shard_map/ppermute | solution.py:569
  74.9 12.1 %all-to-all-start.1 = ((bf16[8,16,256]{2,1,0:T(8,128)(2,1)}), bf16[8,16,256]{2,1,0:T(8,128)(2,1)S(1)}, u32[]{:S(2)}, u32[]{:S(2)}) async-start(bf16[8,16,256]{2,1,0:T(8,128)(2,1)} %get-tuple-element.46), calls=%async_computation.1 | async-start | bytes 131072 | tf_op jit(solution)/shard_map/all_to_all | solution.py:625
  (17 other events, 296.9 us)

commit v9 on v8

--- a/solution.py
+++ b/solution.py
@@ -13,7 +13,6 @@
 FLOOR = -1e30
 QROWS = 8
 NORM_ROWS = 16
-NORM_PIECE = 128
 LANES = 128
 UNIT_ROWS = 16
 ROW_TILE = 16
@@ -38,77 +37,87 @@
     return [pltpu.with_memory_space_constraint(x, pltpu.VMEM) for x in arrays]
 
 
-def start_kernel(parts, tiles_ref, gain_ref, gate_ref, up_ref, *refs):
-    out_ref, *block_refs = refs[: 1 + len(parts)]
-    rows, hidden, gain, in_sems, out_sems, block_sems, gain_sem = refs[1 + len(parts) :]
+def start_kernel(parts, *refs):
+    tiles_ref, gain_ref, gate_ref, up_ref, *slide_refs = refs[:8]
+    out_ref, pack_ref, *block_refs = refs[8 : 10 + len(parts)]
+    rows, hidden, gain, in_sems, out_sems, block_sems, slide_sems, gain_sem = refs[10 + len(parts) :]
     core = lax.axis_index("sub")
-    half, length = tiles_ref.shape[0] // 2, tiles_ref.shape[1]
+    half, length = rows.shape[:2]
     half_cols = gate_ref.shape[1] // 2
-    n_pieces = rows.shape[0] // NORM_PIECE
     gain_copy = pltpu.make_async_copy(gain_ref, gain, gain_sem)
-    gain_copy.start()
-    copies, stores = [], []
-    for i in range(n_pieces):
-        here = pl.ds(i * NORM_PIECE, NORM_PIECE)
-        tile, first = divmod(i * NORM_PIECE, length)
-        source = tiles_ref.at[core * half + tile, pl.ds(first, NORM_PIECE)]
-        copies.append(pltpu.make_async_copy(source, rows.at[here], in_sems.at[i]))
-        stores.append(pltpu.make_async_copy(hidden.at[here], out_ref.at[here], out_sems.at[i]))
-        copies[-1].start()
+    copies = [
+        pltpu.make_async_copy(tiles_ref.at[core * half + i], rows.at[i], in_sems.at[i])
+        for i in range(half)
+    ]
+    stores = [
+        pltpu.make_async_copy(
+            hidden.at[i], out_ref.at[pl.ds(i * length, length)], out_sems.at[i]
+        )
+        for i in range(half)
+    ]
     packs = []
     columns = pl.ds(pl.multiple_of(lax.rem(lax.axis_index("grp"), 2) * half_cols, LANES), half_cols)
     for k, (part, block_ref) in enumerate(zip(parts, block_refs)):
         for i, ref in enumerate((gate_ref, up_ref)):
+            place = block_ref.at[:, i * half_cols : (i + 1) * half_cols]
             packs.append(
-                pltpu.make_async_copy(
-                    ref.at[part, columns],
-                    block_ref.at[:, i * half_cols : (i + 1) * half_cols],
-                    block_sems.at[k, i],
-                )
+                pltpu.make_async_copy(ref.at[part, columns], place, block_sems.at[k, i])
             )
-            packs[-1].start()
+    cols = pack_ref.shape[1]
+    others = pl.ds(pl.multiple_of((1 - core) * cols, LANES), cols)
+    at = 0
+    for k, ref in enumerate(slide_refs):
+        place = pack_ref.at[at : at + ref.shape[0]]
+        source = ref if ref.shape[1] == cols else ref.at[:, others]
+        packs.append(pltpu.make_async_copy(source, place, slide_sems.at[k]))
+        at += ref.shape[0]
+    for copy in [gain_copy] + copies + packs:
+        copy.start()
     gain_copy.wait()
     gains = gain[...].reshape(1, -1)
-    for i in range(n_pieces):
+    for i in range(half):
         copies[i].wait()
 
         def some_rows(j, carry):
-            start = pl.multiple_of(i * NORM_PIECE + j * NORM_ROWS, NORM_ROWS)
-            here = pl.ds(start, NORM_ROWS)
-            hidden[here, :] = normed(rows[here, :].astype(jnp.float32), gains)
+            here = pl.ds(pl.multiple_of(j * NORM_ROWS, NORM_ROWS), NORM_ROWS)
+            hidden[i, here, :] = normed(rows[i, here, :].astype(jnp.float32), gains)
             return carry
 
-        lax.fori_loop(0, NORM_PIECE // NORM_ROWS, some_rows, 0, unroll=True)
+        lax.fori_loop(0, length // NORM_ROWS, some_rows, 0, unroll=4)
         stores[i].start()
     for copy in packs + stores:
         copy.wait()
 
 
-def start_work(tiles, gain, gate_weight, up_weight, parts):
+def start_work(tiles, gain, gate_weight, up_weight, slide_weights, parts):
     slot_count, length, width = tiles.shape
-    n_rows = slot_count // 2 * length
+    half = slot_count // 2
     hbm = pl.BlockSpec(memory_space=pltpu.HBM)
+    vmem = pl.BlockSpec(memory_space=pltpu.VMEM)
     cols = gate_weight.shape[1]
+    pack = (sum(w.shape[0] for w in slide_weights), slide_weights[0].shape[1])
     return pl.pallas_call(
         functools.partial(start_kernel, parts),
-        in_specs=[hbm] * 4,
-        out_specs=[hbm] * (1 + len(parts)),
+        in_specs=[hbm] * (4 + len(slide_weights)),
+        out_specs=[hbm] + [vmem] * (1 + len(parts)),
         out_shape=[
-            pltpu.HBM((n_rows, width), jnp.bfloat16),
-            *[pltpu.HBM((part.stop - part.start, cols), jnp.bfloat16) for part in parts],
+            pltpu.HBM((half * length, width), jnp.bfloat16),
+            pltpu.VMEM(pack, jnp.bfloat16),
+            *[pltpu.VMEM((part.stop - part.start, cols), jnp.bfloat16) for part in parts],
         ],
         scratch_shapes=[
-            pltpu.VMEM((n_rows, width), jnp.bfloat16),
-            pltpu.VMEM((n_rows, width), jnp.bfloat16),
+            pltpu.VMEM((half, length, width), jnp.bfloat16),
+            pltpu.VMEM((half, length, width), jnp.bfloat16),
             pltpu.VMEM((width,), jnp.float32),
-            pltpu.SemaphoreType.DMA((n_rows // NORM_PIECE,)),
-            pltpu.SemaphoreType.DMA((n_rows // NORM_PIECE,)),
+            pltpu.SemaphoreType.DMA((half,)),
+            pltpu.SemaphoreType.DMA((half,)),
             pltpu.SemaphoreType.DMA((len(parts), 2)),
+            pltpu.SemaphoreType.DMA((len(slide_weights),)),
             pltpu.SemaphoreType.DMA(()),
         ],
         compiler_params=pltpu.CompilerParams(vmem_limit_bytes=NORM_VMEM),
         cost_estimate=pl.CostEstimate(flops=0, bytes_accessed=0, transcendentals=0),
-    )(*in_hbm(tiles, gain, gate_weight, up_weight))
+    )(*in_hbm(tiles, gain, gate_weight, up_weight, *slide_weights))
 
 
 def after(value, *others):
@@ -182,10 +191,13 @@
         )
 
 
-def product(rows, weights, first, last):
-    return jnp.dot(
-        rows[:, first:last], weights[first:last, :], preferred_element_type=jnp.float32
-    )
+def product(out, rows, weights, first, last, more=None):
+    for at in range(0, rows.shape[0], MXU):
+        here = slice(at, at + MXU)
+        both = jnp.dot(
+            rows[here, first:last], weights[first:last, :], preferred_element_type=jnp.float32
+        )
+        out[here, :] = both if more is None else both + more[here, :]
 
 
 def early_kernel(layout, *refs):
@@ -205,7 +217,7 @@
     for i in range(2):
         for copy in row_loads[i]:
             copy.wait()
-        out_ref[i] = product(rows.at[i], weights, 0, layout.early)
+        product(out_ref.at[i], rows.at[i], weights, 0, layout.early)
 
 
 def early_mlp(layout, blocks, tiles):
@@ -254,14 +266,18 @@
     for i in range(3):
         for copy in waits[i]:
             copy.wait()
-        both = (even, odd)[i % 2]
-        if i < 2 and early:
-            both[...] = product(rows.at[i], weights, early, layout.width) + early_refs[0][i]
-        else:
-            both[...] = product(rows.at[i], weights, 0, layout.width)
-        if pending is not None:
-            gated_means(*pending, length)
-        pending = (both, out_ref, 2 * i)
+        for j in range(rows.shape[1] // length):
+            here = slice(j * length, (j + 1) * length)
+            tile = rows.shape[1] // length * i + j
+            both = (even, odd)[tile % 2]
+            if i < 2 and early:
+                more = early_refs[0].at[i, here]
+                product(both, rows.at[i, here], weights, early, layout.width, more)
+            else:
+                product(both, rows.at[i, here], weights, 0, layout.width)
+            if pending is not None:
+                gated_means(*pending, length)
+            pending = (both, out_ref, tile)
     gated_means(*pending, length)
 
 
@@ -281,8 +297,8 @@
         input_output_aliases={len(blocks) + 4: 1} if early else {},
         scratch_shapes=[
             pltpu.VMEM((3, n_rows, width), jnp.bfloat16),
-            pltpu.VMEM((n_rows, cols), jnp.float32),
-            pltpu.VMEM((n_rows, cols), jnp.float32),
+            pltpu.VMEM((length, cols), jnp.float32),
+            pltpu.VMEM((length, cols), jnp.float32),
             pltpu.SemaphoreType.DMA((len(blocks),)),
             pltpu.SemaphoreType.DMA((3, layout.nz)),
         ],
@@ -307,7 +323,7 @@
     half = n_rows // length
     for i in range(half):
         here = slice(i * length, (i + 1) * length)
-        both[i][...] = product(rows.at[here], weights, 0, layout.width)
+        product(both[i], rows.at[here], weights, 0, layout.width)
         if i:
             gated_means(both[i - 1], means, i - 1, length)
     gated_means(both[half - 1], means, half - 1, length)
@@ -455,13 +471,17 @@
     )
 
 
-def query_kernel(heads, mixed_ref, gain_ref, *refs):
-    n_in = (len(refs) - 1) // 2
-    weights, (out_ref, *kept), (wq, sems) = refs[:n_in], refs[n_in:-2], refs[-2:]
-    copies = [
-        pltpu.make_async_copy(weight, place, sems.at[k])
-        for k, (weight, place) in enumerate(zip(weights, [wq.at[0], wq.at[1], *kept]))
-    ]
+def query_kernel(heads, mixed_ref, gain_ref, far_ref, *refs):
+    near_refs, (many_ref, out_ref, many, *kept), (wq, sems) = refs[:4], refs[4:-2], refs[-2:]
+    places = [wq.at[0], wq.at[1], *kept]
+    copies = []
+    at = 0
+    for k, near in enumerate(near_refs):
+        far = far_ref.at[at : at + near.shape[0]]
+        at += near.shape[0]
+        for i, source in enumerate((near, far)):
+            copies.append(pltpu.make_async_copy(source, places[2 * k + i], sems.at[2 * k + i]))
+    copies.append(pltpu.make_async_copy(many_ref, many, sems.at[len(copies)]))
     for copy in copies:
         copy.start()
     hidden = normed(mixed_ref[...], gain_ref[...].reshape(1, -1))
@@ -556,17 +576,15 @@
     along_y = [(d, d ^ 1) for d in range(n_dev)]
 
     layout = Layout(n_dev, ny, gate_weight.shape[0])
-    first, *held = start_work(tiles, tile_gain, gate_weight, up_weight, layout.parts)
+    slide_weights = [slide_wq, slide_wk, slide_wv, slide_wo]
+    first, pack, *held = start_work(
+        tiles, tile_gain, gate_weight, up_weight, slide_weights, layout.parts
+    )
     second = lax.ppermute(first, "sub", to_sibling)
     pair_first = lax.ppermute(first, "grp", to_pair)
-
     proj_far = lax.ppermute(embed_proj, "sub", to_sibling)
-    wq_far = lax.ppermute(slide_wq, "sub", to_sibling)
-    wk_far = lax.ppermute(slide_wk, "sub", to_sibling)
-    wv_far = lax.ppermute(slide_wv, "sub", to_sibling)
+    pack_far = lax.ppermute(pack, "sub", to_sibling)
     out_cols = slide_wo.shape[1] // n_sub
-    wo_part = lax.dynamic_slice_in_dim(slide_wo, (1 - core) * out_cols, out_cols, 1)
-    wo_far = lax.ppermute(wo_part, "sub", to_sibling)
     smem = pl.BlockSpec(memory_space=pltpu.SMEM)
     vmem = pl.BlockSpec(memory_space=pltpu.VMEM)
     many = pl.pallas_call(
@@ -577,7 +595,7 @@
         compiler_params=pltpu.CompilerParams(vmem_limit_bytes=SMALL_VMEM),
     )(counts, slide_of, rates)
 
-    held[1] = after(held[1], proj_far, wq_far)
+    held[1] = after(held[1], proj_far, second)
     steps = []
     last = None
     for step in range(nz):
@@ -586,10 +604,8 @@
             if step:
                 arrived = lax.ppermute(held[part], "dev", along_z)
                 others = [steps[-1][len(held) + part]]
-                if (step, part) == (1, 1):
-                    others += [second]
                 if (step, part) == (nz - 1, 0):
-                    others += [many, wo_part]
+                    others += [many]
                 if last is not None:
                     others.append(last)
                 held[part] = last = after(arrived, *others)
@@ -624,21 +640,23 @@
     )(counts, *in_vmem(parts), slide_gain, embed_proj, proj_far)
     sent = lax.all_to_all(sent, "dev", split_axis=0, concat_axis=0, tiled=True)
     hbm = pl.BlockSpec(memory_space=pltpu.HBM)
-    weights = [slide_wk, wk_far, slide_wv, wv_far, slide_wo, wo_far, many]
-    query, *weights = pl.pallas_call(
+    far_shape = (slide_wo.shape[0], out_cols)
+    kept = [slide_wk.shape] * 4 + [slide_wo.shape, far_shape]
+    query, many, *weights = pl.pallas_call(
         functools.partial(query_kernel, heads),
-        in_specs=[vmem] * 2 + [hbm] * (2 + len(weights)),
-        out_specs=[vmem] * (1 + len(weights)),
+        in_specs=[vmem] * 2 + [hbm] * 6,
+        out_specs=[vmem] * (2 + len(kept)),
         out_shape=[
             pltpu.VMEM((heads * QROWS, out_width), jnp.bfloat16),
-            *[pltpu.VMEM(x.shape, x.dtype) for x in weights],
+            pltpu.VMEM(many.shape, many.dtype),
+            *[pltpu.VMEM(shape, jnp.bfloat16) for shape in kept],
         ],
         scratch_shapes=[
             pltpu.VMEM((2, *slide_wq.shape), jnp.bfloat16),
-            pltpu.SemaphoreType.DMA((2 + len(weights),)),
+            pltpu.SemaphoreType.DMA((3 + len(kept),)),
         ],
         compiler_params=small,
-    )(*in_vmem(mixed), slide_gain, *in_hbm(slide_wq, wq_far, *weights))
+    )(*in_vmem(mixed), slide_gain, *in_hbm(pack_far, *slide_weights, many))
     slide_out = pl.pallas_call(
         functools.partial(slide_kernel, heads),
         in_specs=[smem] + [vmem] * 10,
@@ -646,7 +664,7 @@
         out_shape=jax.ShapeDtypeStruct((slot_count, out_cols), jnp.bfloat16),
         scratch_shapes=[pltpu.VMEM((n_dev * slot_count, out_width), jnp.float32)],
         compiler_params=small,
-    )(counts, *in_vmem(sent, mixed, query, *weights))
+    )(counts, *in_vmem(sent, mixed, query, *weights, many))
     return (tile_embed, slide_out)
 
 

time: 89.3 us -> 78.1 us (0.87)
  starting transfers between devices: 26.8 us -> 17.4 us
  Pallas kernels: 32.6 us -> 23.7 us
  waiting for transfers between devices: 21.1 us -> 28.9 us
    pallas_call x1, Pallas kernels: 13.1 us -> 4.4 us  [start_work(): pl.pallas_call(functools.partial(start_kernel, parts), in_specs=[hbm] * (...]
    ppermute x8, waiting for transfers between devices: 2.71 us -> 8.77 us  [on_device(): sent.append(lax.ppermute(held[part], 'dev', along_y))]
    ppermute x8, starting transfers between devices: 12.1 us -> 6.65 us  [on_device(): sent.append(lax.ppermute(held[part], 'dev', along_y))]
    ppermute x6, waiting for transfers between devices: 13.3 us -> 15.5 us  [on_device(): arrived = lax.ppermute(held[part], 'dev', along_z)]
    all_to_all x1, starting transfers between devices: 5.16 us -> 3.54 us  [on_device(): sent = lax.all_to_all(sent, 'dev', split_axis=0, concat_axis=0, tiled=True)]
    ppermute x6, starting transfers between devices: 4.85 us -> 3.6 us  [on_device(): arrived = lax.ppermute(held[part], 'dev', along_z)]
    ppermute x4 -> x1, starting transfers between devices: 1 us -> 0.01 us  [on_device(): pack_far = lax.ppermute(pack, 'sub', to_sibling)]
  transfers between devices with their start and end apart: 23 -> 20, of which waited for: 11 -> 12; matrix products, arithmetic and copies ran while one was open for 1% -> 0% of each run, Pallas kernels for 34% -> 28%
where the time goes in v9:
time: 78.1 us; the launch traced here: 77.8 us
  waiting for transfers between devices  28.9 us (37%)
  Pallas kernels  23.7 us (30%)
  starting transfers between devices  17.4 us (22%)
  blocking collectives  6.21 us (8%)
  between operations  0.9 us (1%)
    ppermute x6, waiting for transfers between devices, on_device(): arrived = lax.ppermute(held[part], 'dev', along_z)  15.5 us
    ppermute x8, waiting for transfers between devices, on_device(): sent.append(lax.ppermute(held[part], 'dev', along_y))  8.77 us
    ppermute x8, starting transfers between devices, on_device(): sent.append(lax.ppermute(held[part], 'dev', along_y))  6.65 us
    all_to_all x1, blocking collectives, on_device(): lax.all_to_all(parts, ('grp', 'sub'), split_axis=0, concat_axis=0, tiled=...  6.21 us
    pallas_call x1, Pallas kernels, middle_mlp(): pl.pallas_call(functools.partial(middle_kernel, layout, length, len(block...  5.17 us
    pallas_call x1, Pallas kernels, early_mlp(): pl.pallas_call(functools.partial(early_kernel, layout), in_specs=[hbm] *...  5.14 us
    all_to_all x1, waiting for transfers between devices, on_device(): sent = lax.all_to_all(sent, 'dev', split_axis=0, concat_axis=0, tiled=True)  4.6 us
    pallas_call x1, Pallas kernels, start_work(): pl.pallas_call(functools.partial(start_kernel, parts), in_specs=[hbm] * (...  4.4 us
  transfers between devices with their start and end apart: 20, of which 12 were waited for; matrix products, arithmetic and copies ran while one was open for 0% of the time, Pallas kernels for 28%

profile of v9, /device:TPU:0, one launch (start us, length us, event | category | flops | bytes accessed | tf_op | source)
XLA Modules:
  0.0 77.8 jit_solution(15818047323846504736)
XLA Ops:
  1.2 4.4 %shard_map.140 = (bf16[512,1536]{1,0:T(8,128)(2,1)}, bf16[2688,384]{1,0:T(8,128)(2,1)S(1)}, bf16[96,1024]{1,0:T(8,128)(2,1)S(1)}, bf16[96,1024]{1,0:T(8,128)(2,1)S(1)}) custom-call(bf16[4,256,1536]{2,1,0:T(8,128)(2,1)} %refs_0_.2, f32[1536]{0:T(1024)} %refs_1_.2, bf16[192,1024]{1,0:T(8,128)(2,1)} %refs_2_.2, bf16[192,1024]{1,0:T(8,128)(2,1)} %refs_3_.2, ...), custom_call_target="tpu_custom_call" | custom-call | tf_op jit(solution)/shard_map/pallas_call | solution.py:99
  5.7 2.9 %collective-permute-start.16 = (bf16[512,1536]{1,0:T(8,128)(2,1)}, bf16[512,1536]{1,0:T(8,128)(2,1)S(1)}, u32[]{:S(2)}, u32[]{:S(2)}) collective-permute-start(bf16[512,1536]{1,0:T(8,128)(2,1)} %get-tuple-element.40.refs_12_.refs_4_), channel_id=1, source_target_pairs={{0,16},{16,0},{1,17},{17,1},{2,18},{18,2},{3,19},{19,3},{4,20},{20... | collective-permute-start | bytes 4718600 | tf_op jit(solution)/shard_map/ppermute | solution.py:584
  8.7 1.5 %collective-permute-start.1 = (bf16[96,1024]{1,0:T(8,128)(2,1)S(1)}, bf16[96,1024]{1,0:T(8,128)(2,1)S(1)}, u32[]{:S(2)}, u32[]{:S(2)}) collective-permute-start(bf16[96,1024]{1,0:T(8,128)(2,1)S(1)} %get-tuple-element.30.refs_0_), channel_id=1, source_target_pairs={{0,2},{2,0},{4,6},{6,4},{8,10},{10,8},{12,14},{14,12},{1,3},{3,1},... | collective-permute-start | bytes 589832 | tf_op jit(solution)/shard_map/ppermute | solution.py:612
  10.2 1.6 %collective-permute-start = (bf16[96,1024]{1,0:T(8,128)(2,1)S(1)}, bf16[96,1024]{1,0:T(8,128)(2,1)S(1)}, u32[]{:S(2)}, u32[]{:S(2)}) collective-permute-start(bf16[96,1024]{1,0:T(8,128)(2,1)S(1)} %get-tuple-element.30.refs_0_), channel_id=1, source_target_pairs={{0,4},{2,6},{4,8},{6,10},{8,12},{10,14},{12,0},{14,2},{1,5},{3,7},... | collective-permute-start | bytes 589832 | tf_op jit(solution)/shard_map/ppermute | solution.py:605
  12.4 1.6 %collective-permute-start.6 = (bf16[96,1024]{1,0:T(8,128)(2,1)S(1)}, bf16[96,1024]{1,0:T(8,128)(2,1)S(1)}, u32[]{:S(2)}, u32[]{:S(2)}) collective-permute-start(bf16[96,1024]{1,0:T(8,128)(2,1)S(1)} %get-tuple-element.34.refs_1_), channel_id=1, source_target_pairs={{0,4},{2,6},{4,8},{6,10},{8,12},{10,14},{12,0},{14,2},{1,5},{3,7},... | collective-permute-start | bytes 589832 | tf_op jit(solution)/shard_map/ppermute | solution.py:605
  13.9 2.5 %collective-permute-done.1.refs_2_ = bf16[96,1024]{1,0:T(8,128)(2,1)S(1)} collective-permute-done((bf16[96,1024]{1,0:T(8,128)(2,1)S(1)}, bf16[96,1024]{1,0:T(8,128)(2,1)S(1)}, u32[]{:S(2)}, u32[]{:S(2)}) %collective-permute-start.1) | collective-permute-done | bytes 196640 | tf_op jit(solution)/shard_map/ppermute | solution.py:612
  16.5 3.3 %collective-permute-done.refs_4_ = bf16[96,1024]{1,0:T(8,128)(2,1)S(1)} collective-permute-done((bf16[96,1024]{1,0:T(8,128)(2,1)S(1)}, bf16[96,1024]{1,0:T(8,128)(2,1)S(1)}, u32[]{:S(2)}, u32[]{:S(2)}) %collective-permute-start) | collective-permute-done | bytes 196640 | tf_op jit(solution)/shard_map/ppermute | solution.py:605
  20.3 3.1 %collective-permute-done.6.refs_5_ = bf16[96,1024]{1,0:T(8,128)(2,1)S(1)} collective-permute-done((bf16[96,1024]{1,0:T(8,128)(2,1)S(1)}, bf16[96,1024]{1,0:T(8,128)(2,1)S(1)}, u32[]{:S(2)}, u32[]{:S(2)}) %collective-permute-start.6) | collective-permute-done | bytes 196640 | tf_op jit(solution)/shard_map/ppermute | solution.py:605
  23.9 3.3 %collective-permute-done.3.refs_6_ = bf16[96,1024]{1,0:T(8,128)(2,1)S(1)} collective-permute-done((bf16[96,1024]{1,0:T(8,128)(2,1)S(1)}, bf16[96,1024]{1,0:T(8,128)(2,1)S(1)}, u32[]{:S(2)}, u32[]{:S(2)}) %collective-permute-start.3) | collective-permute-done | bytes 196640 | tf_op jit(solution)/shard_map/ppermute | solution.py:612
  27.2 2.5 %collective-permute-done.2.refs_8_ = bf16[96,1024]{1,0:T(8,128)(2,1)S(1)} collective-permute-done((bf16[96,1024]{1,0:T(8,128)(2,1)S(1)}, bf16[96,1024]{1,0:T(8,128)(2,1)S(1)}, u32[]{:S(2)}, u32[]{:S(2)}) %collective-permute-start.2) | collective-permute-done | bytes 196640 | tf_op jit(solution)/shard_map/ppermute | solution.py:605
  29.7 1.5 %collective-permute-start.9 = (bf16[96,1024]{1,0:T(8,128)(2,1)S(1)}, bf16[96,1024]{1,0:T(8,128)(2,1)S(1)}, u32[]{:S(2)}, u32[]{:S(2)}) collective-permute-start(bf16[96,1024]{1,0:T(8,128)(2,1)S(1)} %collective-permute-done.2.refs_8_), channel_id=1, source_target_pairs={{0,2},{2,0},{4,6},{6,4},{8,10},{10,8},{12,14},{14,12},{1,3},{3,1},... | collective-permute-start | bytes 589832 | tf_op jit(solution)/shard_map/ppermute | solution.py:612
  31.4 2.5 %collective-permute-done.10.refs_9_ = bf16[96,1024]{1,0:T(8,128)(2,1)S(1)} collective-permute-done((bf16[96,1024]{1,0:T(8,128)(2,1)S(1)}, bf16[96,1024]{1,0:T(8,128)(2,1)S(1)}, u32[]{:S(2)}, u32[]{:S(2)}) %collective-permute-start.10) | collective-permute-done | bytes 196640 | tf_op jit(solution)/shard_map/ppermute | solution.py:605
  35.4 1.6 %collective-permute-done.9.refs_10_ = bf16[96,1024]{1,0:T(8,128)(2,1)S(1)} collective-permute-done((bf16[96,1024]{1,0:T(8,128)(2,1)S(1)}, bf16[96,1024]{1,0:T(8,128)(2,1)S(1)}, u32[]{:S(2)}, u32[]{:S(2)}) %collective-permute-start.9) | collective-permute-done | bytes 196640 | tf_op jit(solution)/shard_map/ppermute | solution.py:612
  38.4 1.7 %collective-permute-done.8.refs_0_ = bf16[96,1024]{1,0:T(8,128)(2,1)S(1)} collective-permute-done((bf16[96,1024]{1,0:T(8,128)(2,1)S(1)}, bf16[96,1024]{1,0:T(8,128)(2,1)S(1)}, u32[]{:S(2)}, u32[]{:S(2)}) %collective-permute-start.8) | collective-permute-done | bytes 196640 | tf_op jit(solution)/shard_map/ppermute | solution.py:605
  40.6 2.4 %collective-permute-done.12.refs_1_ = bf16[96,1024]{1,0:T(8,128)(2,1)S(1)} collective-permute-done((bf16[96,1024]{1,0:T(8,128)(2,1)S(1)}, bf16[96,1024]{1,0:T(8,128)(2,1)S(1)}, u32[]{:S(2)}, u32[]{:S(2)}) %collective-permute-start.12) | collective-permute-done | bytes 196640 | tf_op jit(solution)/shard_map/ppermute | solution.py:605
  43.5 5.1 %shard_map.142 = (f32[2,512,1024]{2,1,0:T(8,128)S(1)}, bf16[1536,1024]{1,0:T(8,128)(2,1)S(1)}) custom-call(bf16[96,1024]{1,0:T(8,128)(2,1)} %copy-done.6, bf16[96,1024]{1,0:T(8,128)(2,1)} %copy-done.7, bf16[96,1024]{1,0:T(8,128)(2,1)} %copy-done.10, bf16[96,1024]{1,0:T(8,128)(2,1)} %copy-done.12, bf16[96,1024]{1,0:T(8,128)(2,1)} %copy-done.11, ...), custom_call_target="tpu_custom_call" | custom-call | flops 2147483648 | bytes 8388608 | tf_op jit(solution)/shard_map/pallas_call | solution.py:228
  49.9 5.2 %shard_map.143 = (f32[6,512]{1,0:T(8,128)S(1)}, bf16[1536,1024]{1,0:T(8,128)(2,1)S(1)}) custom-call(bf16[96,1024]{1,0:T(8,128)(2,1)S(1)} %collective-permute-done.8.refs_0_, bf16[96,1024]{1,0:T(8,128)(2,1)S(1)} %collective-permute-done.12.refs_1_, bf16[96,1024]{1,0:T(8,128)(2,1)S(1)} %collective-permute-done.14.refs_2_, ...), custom_call_target="tpu_custom_call", output_to_operand_aliasing={{1}: (8, {})} | custom-call | flops 3221225472 | bytes 7864320 | tf_op jit(solution)/shard_map/pallas_call | solution.py:289
  55.1 2.1 %shard_map.144 = bf16[4,16,128]{2,1,0:T(8,128)(2,1)S(1)} custom-call(f32[6,512]{1,0:T(8,128)S(1)} %get-tuple-element.44.means_ref, bf16[1536,1024]{1,0:T(8,128)(2,1)S(1)} %get-tuple-element.45.weights, bf16[512,1536]{1,0:T(8,128)(2,1)S(1)} %collective-permute-done.17.tiles_ref), custom_call_target="tpu_custom_call" | custom-call | flops 1610612736 | bytes 4718592 | tf_op jit(solution)/shard_map/pallas_call | solution.py:357
  57.2 6.2 %all_to_all.10.parts_ref = bf16[4,16,128]{2,1,0:T(8,128)(2,1)S(1)} all-to-all(bf16[4,16,128]{2,1,0:T(8,128)(2,1)S(1)} %shard_map.144), channel_id=1, replica_groups=mesh['grp'=2,'dev'=8,'sub'=2] {'grp','sub'}, dimensions={0} | all-to-all | bytes 32768 | tf_op jit(solution)/shard_map/all_to_all | solution.py:624
  63.4 1.9 %shard_map.145 = (bf16[4,1024]{1,0:T(4,128)(2,1)}, f32[8,768]{1,0:T(8,128)S(1)}, bf16[8,16,256]{2,1,0:T(8,128)(2,1)}) custom-call(s32[8]{0:T(128)S(1)} %copy-done.3, bf16[4,16,128]{2,1,0:T(8,128)(2,1)S(1)} %all_to_all.10.parts_ref, f32[768]{0:T(1024)S(1)} %copy-done.2, bf16[1024,768]{1,0:T(8,128)(2,1)S(1)} %copy-done, ...), custom_call_target="tpu_custom_call" | custom-call | tf_op jit(solution)/shard_map/pallas_call | solution.py:630
  65.3 3.5 %all-to-all-start.1 = ((bf16[8,16,256]{2,1,0:T(8,128)(2,1)}), bf16[8,16,256]{2,1,0:T(8,128)(2,1)S(1)}, u32[]{:S(2)}, u32[]{:S(2)}) async-start(bf16[8,16,256]{2,1,0:T(8,128)(2,1)} %get-tuple-element.47), calls=%async_computation.1 | async-start | bytes 131072 | tf_op jit(solution)/shard_map/all_to_all | solution.py:641
  68.8 2.3 %shard_map.146 = (bf16[96,768]{1,0:T(8,128)(2,1)S(1)}, f32[96,32]{1,0:T(8,128)S(1)}, bf16[768,384]{1,0:T(8,128)(2,1)S(1)}, bf16[768,384]{1,0:T(8,128)(2,1)S(1)},...) custom-call(f32[8,768]{1,0:T(8,128)S(1)} %get-tuple-element.48.mixed, ...), custom_call_target="tpu_custom_call" | custom-call | tf_op jit(solution)/shard_map/pallas_call | solution.py:645
  71.1 4.6 %all-to-all-done.1.sent_ref = bf16[8,16,256]{2,1,0:T(8,128)(2,1)S(1)} async-done(((bf16[8,16,256]{2,1,0:T(8,128)(2,1)}), bf16[8,16,256]{2,1,0:T(8,128)(2,1)S(1)}, u32[]{:S(2)}, u32[]{:S(2)}) %all-to-all-start.1) | async-done | bytes 65568 | tf_op jit(solution)/shard_map/all_to_all | solution.py:641
  75.7 2.1 %shard_map.147 = bf16[4,384]{1,0:T(4,128)(2,1)} custom-call(s32[8]{0:T(128)S(1)} %copy-done.3, bf16[8,16,256]{2,1,0:T(8,128)(2,1)S(1)} %all-to-all-done.1.sent_ref, f32[8,768]{1,0:T(8,128)S(1)} %get-tuple-element.48.mixed_ref, bf16[96,768]{1,0:T(8,128)(2,1)S(1)} %get-tuple-element.50.query_ref, bf16[768,384]{1,0:T(8,128)(2,1)S(1)} %get-tuple-element.51.wk_ref, ...), custom_call_target="tpu_custom_call" | custom-call | tf_op jit(solution)/shard_map/pallas_call | solution.py:660
  (65 shorter events, 7.5 us)
Async XLA Ops:
  0.6 36.4 %copy-start.3 = (s32[8]{0:T(128)S(1)}, s32[8]{0:T(128)}, u32[]{:S(2)}) copy-start(s32[8]{0:T(128)} %counts_ref.5) | copy-start | bytes 100
  0.6 36.4 %copy-start.5 = (s32[12]{0:T(128)S(1)}, s32[12]{0:T(128)}, u32[]{:S(2)}) copy-start(s32[12]{0:T(128)} %rates_ref.1) | copy-start | bytes 148
  0.7 11.1 %collective-permute-start.4 = (bf16[1024,768]{1,0:T(8,128)(2,1)}, bf16[1024,768]{1,0:T(8,128)(2,1)S(1)}, u32[]{:S(2)}, u32[]{:S(2)}) collective-permute-start(bf16[1024,768]{1,0:T(8,128)(2,1)} %near_ref.1), channel_id=1, source_target_pairs={{0,1},{1,0},{2,3},{3,2},{4,5},{5,4},{6,7},{7,6},{8,9},{9,8},{10,11... | collective-permute-start | bytes 4718600 | tf_op jit(solution)/shard_map/ppermute | solution.py:585
  5.6 37.8 %copy-start.6 = (bf16[96,1024]{1,0:T(8,128)(2,1)}, bf16[96,1024]{1,0:T(8,128)(2,1)S(1)}, u32[]{:S(2)}) copy-start(bf16[96,1024]{1,0:T(8,128)(2,1)S(1)} %get-tuple-element.30.refs_0_) | copy-start | bytes 589828
  5.6 37.8 %copy-start.7 = (bf16[96,1024]{1,0:T(8,128)(2,1)}, bf16[96,1024]{1,0:T(8,128)(2,1)S(1)}, u32[]{:S(2)}) copy-start(bf16[96,1024]{1,0:T(8,128)(2,1)S(1)} %get-tuple-element.34.refs_1_) | copy-start | bytes 589828
  5.6 6.2 %collective-permute-start.5 = (bf16[512,1536]{1,0:T(8,128)(2,1)}, bf16[512,1536]{1,0:T(8,128)(2,1)S(1)}, u32[]{:S(2)}, u32[]{:S(2)}) collective-permute-start(bf16[512,1536]{1,0:T(8,128)(2,1)} %get-tuple-element.40.refs_12_.refs_4_), channel_id=1, source_target_pairs={{0,1},{1,0},{2,3},{3,2},{4,5},{5,4},{6,7},{7,6},{8,9},{9,8},{10,11... | collective-permute-start | bytes 4718600 | tf_op jit(solution)/shard_map/ppermute | solution.py:583
  5.7 42.9 %collective-permute-start.16 = (bf16[512,1536]{1,0:T(8,128)(2,1)}, bf16[512,1536]{1,0:T(8,128)(2,1)S(1)}, u32[]{:S(2)}, u32[]{:S(2)}) collective-permute-start(bf16[512,1536]{1,0:T(8,128)(2,1)} %get-tuple-element.40.refs_12_.refs_4_), channel_id=1, source_target_pairs={{0,16},{16,0},{1,17},{17,1},{2,18},{18,2},{3,19},{19,3},{4,20},{20... | collective-permute-start | bytes 4718600 | tf_op jit(solution)/shard_map/ppermute | solution.py:584
  8.7 7.8 %collective-permute-start.1 = (bf16[96,1024]{1,0:T(8,128)(2,1)S(1)}, bf16[96,1024]{1,0:T(8,128)(2,1)S(1)}, u32[]{:S(2)}, u32[]{:S(2)}) collective-permute-start(bf16[96,1024]{1,0:T(8,128)(2,1)S(1)} %get-tuple-element.30.refs_0_), channel_id=1, source_target_pairs={{0,2},{2,0},{4,6},{6,4},{8,10},{10,8},{12,14},{14,12},{1,3},{3,1},... | collective-permute-start | bytes 589832 | tf_op jit(solution)/shard_map/ppermute | solution.py:612
  10.2 9.6 %collective-permute-start = (bf16[96,1024]{1,0:T(8,128)(2,1)S(1)}, bf16[96,1024]{1,0:T(8,128)(2,1)S(1)}, u32[]{:S(2)}, u32[]{:S(2)}) collective-permute-start(bf16[96,1024]{1,0:T(8,128)(2,1)S(1)} %get-tuple-element.30.refs_0_), channel_id=1, source_target_pairs={{0,4},{2,6},{4,8},{6,10},{8,12},{10,14},{12,0},{14,2},{1,5},{3,7},... | collective-permute-start | bytes 589832 | tf_op jit(solution)/shard_map/ppermute | solution.py:605
  11.8 8.6 %collective-permute-start.7 = (bf16[96,1024]{1,0:T(8,128)(2,1)S(1)}, bf16[96,1024]{1,0:T(8,128)(2,1)S(1)}, u32[]{:S(2)}, u32[]{:S(2)}) collective-permute-start(bf16[96,1024]{1,0:T(8,128)(2,1)S(1)} %get-tuple-element.34.refs_1_), channel_id=1, source_target_pairs={{0,2},{2,0},{4,6},{6,4},{8,10},{10,8},{12,14},{14,12},{1,3},{3,1},... | collective-permute-start | bytes 589832 | tf_op jit(solution)/shard_map/ppermute | solution.py:612
  12.4 11.1 %collective-permute-start.6 = (bf16[96,1024]{1,0:T(8,128)(2,1)S(1)}, bf16[96,1024]{1,0:T(8,128)(2,1)S(1)}, u32[]{:S(2)}, u32[]{:S(2)}) collective-permute-start(bf16[96,1024]{1,0:T(8,128)(2,1)S(1)} %get-tuple-element.34.refs_1_), channel_id=1, source_target_pairs={{0,4},{2,6},{4,8},{6,10},{8,12},{10,14},{12,0},{14,2},{1,5},{3,7},... | collective-permute-start | bytes 589832 | tf_op jit(solution)/shard_map/ppermute | solution.py:605
  19.8 7.4 %collective-permute-start.3 = (bf16[96,1024]{1,0:T(8,128)(2,1)S(1)}, bf16[96,1024]{1,0:T(8,128)(2,1)S(1)}, u32[]{:S(2)}, u32[]{:S(2)}) collective-permute-start(bf16[96,1024]{1,0:T(8,128)(2,1)S(1)} %collective-permute-done.refs_4_), channel_id=1, source_target_pairs={{0,2},{2,0},{4,6},{6,4},{8,10},{10,8},{12,14},{14,12},{1,3},{3,1},... | collective-permute-start | bytes 589832 | tf_op jit(solution)/shard_map/ppermute | solution.py:612
  20.3 9.4 %collective-permute-start.2 = (bf16[96,1024]{1,0:T(8,128)(2,1)S(1)}, bf16[96,1024]{1,0:T(8,128)(2,1)S(1)}, u32[]{:S(2)}, u32[]{:S(2)}) collective-permute-start(bf16[96,1024]{1,0:T(8,128)(2,1)S(1)} %collective-permute-done.refs_4_), channel_id=1, source_target_pairs={{0,4},{2,6},{4,8},{6,10},{8,12},{10,14},{12,0},{14,2},{1,5},{3,7},... | collective-permute-start | bytes 589832 | tf_op jit(solution)/shard_map/ppermute | solution.py:605
  23.4 8.0 %collective-permute-start.11 = (bf16[96,1024]{1,0:T(8,128)(2,1)S(1)}, bf16[96,1024]{1,0:T(8,128)(2,1)S(1)}, u32[]{:S(2)}, u32[]{:S(2)}) collective-permute-start(bf16[96,1024]{1,0:T(8,128)(2,1)S(1)} %collective-permute-done.6.refs_5_), channel_id=1, source_target_pairs={{0,2},{2,0},{4,6},{6,4},{8,10},{10,8},{12,14},{14,12},{1,3},{3,1},... | collective-permute-start | bytes 589832 | tf_op jit(solution)/shard_map/ppermute | solution.py:612
  23.4 10.5 %collective-permute-start.10 = (bf16[96,1024]{1,0:T(8,128)(2,1)S(1)}, bf16[96,1024]{1,0:T(8,128)(2,1)S(1)}, u32[]{:S(2)}, u32[]{:S(2)}) collective-permute-start(bf16[96,1024]{1,0:T(8,128)(2,1)S(1)} %collective-permute-done.6.refs_5_), channel_id=1, source_target_pairs={{0,4},{2,6},{4,8},{6,10},{8,12},{10,14},{12,0},{14,2},{1,5},{3,7},... | collective-permute-start | bytes 589832 | tf_op jit(solution)/shard_map/ppermute | solution.py:605
  29.7 7.3 %collective-permute-start.9 = (bf16[96,1024]{1,0:T(8,128)(2,1)S(1)}, bf16[96,1024]{1,0:T(8,128)(2,1)S(1)}, u32[]{:S(2)}, u32[]{:S(2)}) collective-permute-start(bf16[96,1024]{1,0:T(8,128)(2,1)S(1)} %collective-permute-done.2.refs_8_), channel_id=1, source_target_pairs={{0,2},{2,0},{4,6},{6,4},{8,10},{10,8},{12,14},{14,12},{1,3},{3,1},... | collective-permute-start | bytes 589832 | tf_op jit(solution)/shard_map/ppermute | solution.py:612
  31.2 8.8 %collective-permute-start.8 = (bf16[96,1024]{1,0:T(8,128)(2,1)S(1)}, bf16[96,1024]{1,0:T(8,128)(2,1)S(1)}, u32[]{:S(2)}, u32[]{:S(2)}) collective-permute-start(bf16[96,1024]{1,0:T(8,128)(2,1)S(1)} %collective-permute-done.2.refs_8_), channel_id=1, source_target_pairs={{0,4},{2,6},{4,8},{6,10},{8,12},{10,14},{12,0},{14,2},{1,5},{3,7},... | collective-permute-start | bytes 589832 | tf_op jit(solution)/shard_map/ppermute | solution.py:605
  33.9 6.6 %collective-permute-start.13 = (bf16[96,1024]{1,0:T(8,128)(2,1)S(1)}, bf16[96,1024]{1,0:T(8,128)(2,1)S(1)}, u32[]{:S(2)}, u32[]{:S(2)}) collective-permute-start(bf16[96,1024]{1,0:T(8,128)(2,1)S(1)} %collective-permute-done.10.refs_9_), channel_id=1, source_target_pairs={{0,2},{2,0},{4,6},{6,4},{8,10},{10,8},{12,14},{14,12},{1,3},{3,1},... | collective-permute-start | bytes 589832 | tf_op jit(solution)/shard_map/ppermute | solution.py:612
  35.4 7.5 %collective-permute-start.12 = (bf16[96,1024]{1,0:T(8,128)(2,1)S(1)}, bf16[96,1024]{1,0:T(8,128)(2,1)S(1)}, u32[]{:S(2)}, u32[]{:S(2)}) collective-permute-start(bf16[96,1024]{1,0:T(8,128)(2,1)S(1)} %collective-permute-done.10.refs_9_), channel_id=1, source_target_pairs={{0,4},{2,6},{4,8},{6,10},{8,12},{10,14},{12,0},{14,2},{1,5},{3,7},... | collective-permute-start | bytes 589832 | tf_op jit(solution)/shard_map/ppermute | solution.py:605
  37.0 31.8 %collective-permute-start.18 = (bf16[2688,384]{1,0:T(8,128)(2,1)S(1)}, bf16[2688,384]{1,0:T(8,128)(2,1)}, u32[]{:S(2)}, u32[]{:S(2)}) collective-permute-start(bf16[2688,384]{1,0:T(8,128)(2,1)S(1)} %get-tuple-element.49), channel_id=1, source_target_pairs={{0,1},{1,0},{2,3},{3,2},{4,5},{5,4},{6,7},{7,6},{8,9},{9,8},{10,11... | collective-permute-start | bytes 6193160 | tf_op jit(solution)/shard_map/ppermute | solution.py:586
  40.1 8.6 %collective-permute-start.14 = (bf16[96,1024]{1,0:T(8,128)(2,1)S(1)}, bf16[96,1024]{1,0:T(8,128)(2,1)S(1)}, u32[]{:S(2)}, u32[]{:S(2)}) collective-permute-start(bf16[96,1024]{1,0:T(8,128)(2,1)S(1)} %collective-permute-done.8.refs_0_), channel_id=1, source_target_pairs={{0,2},{2,0},{4,6},{6,4},{8,10},{10,8},{12,14},{14,12},{1,3},{3,1},... | collective-permute-start | bytes 589832 | tf_op jit(solution)/shard_map/ppermute | solution.py:612
  42.9 7.0 %collective-permute-start.15 = (bf16[96,1024]{1,0:T(8,128)(2,1)S(1)}, bf16[96,1024]{1,0:T(8,128)(2,1)S(1)}, u32[]{:S(2)}, u32[]{:S(2)}) collective-permute-start(bf16[96,1024]{1,0:T(8,128)(2,1)S(1)} %collective-permute-done.12.refs_1_), channel_id=1, source_target_pairs={{0,2},{2,0},{4,6},{6,4},{8,10},{10,8},{12,14},{14,12},{1,3},{3,1},... | collective-permute-start | bytes 589832 | tf_op jit(solution)/shard_map/ppermute | solution.py:612
  49.9 5.2 %collective-permute-start.17 = (bf16[512,1536]{1,0:T(8,128)(2,1)S(1)}, bf16[512,1536]{1,0:T(8,128)(2,1)S(1)}, u32[]{:S(2)}, u32[]{:S(2)}) collective-permute-start(bf16[512,1536]{1,0:T(8,128)(2,1)S(1)} %collective-permute-done.16.refs_6_), channel_id=1, source_target_pairs={{0,1},{1,0},{2,3},{3,2},{4,5},{5,4},{6,7},{7,6},{8,9},{9,8},{10,11... | collective-permute-start | bytes 4718600 | tf_op jit(solution)/shard_map/ppermute | solution.py:621
  65.3 10.4 %all-to-all-start.1 = ((bf16[8,16,256]{2,1,0:T(8,128)(2,1)}), bf16[8,16,256]{2,1,0:T(8,128)(2,1)S(1)}, u32[]{:S(2)}, u32[]{:S(2)}) async-start(bf16[8,16,256]{2,1,0:T(8,128)(2,1)} %get-tuple-element.47), calls=%async_computation.1 | async-start | bytes 131072 | tf_op jit(solution)/shard_map/all_to_all | solution.py:641
  (16 other events, 241.3 us)

commit v10 on v9

--- a/solution.py
+++ b/solution.py
@@ -13,6 +13,8 @@
 FLOOR = -1e30
 QROWS = 8
 NORM_ROWS = 16
+NORM_PIECE = 128
+NORM_UNROLL = 8
 LANES = 128
 UNIT_ROWS = 16
 ROW_TILE = 16
@@ -40,20 +42,34 @@
 def start_kernel(parts, *refs):
     tiles_ref, gain_ref, gate_ref, up_ref, *slide_refs = refs[:8]
     out_ref, pack_ref, *block_refs = refs[8 : 10 + len(parts)]
-    rows, hidden, gain, in_sems, out_sems, block_sems, slide_sems, gain_sem = refs[10 + len(parts) :]
+    (
+        rows,
+        hidden,
+        gain,
+        average,
+        scale,
+        in_sems,
+        out_sems,
+        block_sems,
+        slide_sems,
+        gain_sem,
+    ) = refs[10 + len(parts) :]
     core = lax.axis_index("sub")
-    half, length = rows.shape[:2]
+    pieces, piece = rows.shape[:2]
+    half, length = tiles_ref.shape[0] // 2, tiles_ref.shape[1]
     half_cols = gate_ref.shape[1] // 2
     gain_copy = pltpu.make_async_copy(gain_ref, gain, gain_sem)
     copies = [
-        pltpu.make_async_copy(tiles_ref.at[core * half + i], rows.at[i], in_sems.at[i])
-        for i in range(half)
+        pltpu.make_async_copy(
+            tiles_ref.at[core * half + i * piece // length, pl.ds(i * piece % length, piece)],
+            rows.at[i],
+            in_sems.at[i],
+        )
+        for i in range(pieces)
     ]
     stores = [
-        pltpu.make_async_copy(
-            hidden.at[i], out_ref.at[pl.ds(i * length, length)], out_sems.at[i]
-        )
-        for i in range(half)
+        pltpu.make_async_copy(hidden.at[i], out_ref.at[pl.ds(i * piece, piece)], out_sems.at[i])
+        for i in range(pieces)
     ]
     packs = []
     columns = pl.ds(pl.multiple_of(lax.rem(lax.axis_index("grp"), 2) * half_cols, LANES), half_cols)
@@ -75,15 +91,42 @@
         copy.start()
     gain_copy.wait()
     gains = gain[...].reshape(1, -1)
-    for i in range(half):
+    width = gains.shape[1]
+
+    def grouped(function):
+        def some_rows(j, carry):
+            function(pl.ds(pl.multiple_of(j * NORM_ROWS, NORM_ROWS), NORM_ROWS))
+            return carry
+
+        lax.fori_loop(0, rows.shape[1] // NORM_ROWS, some_rows, 0, unroll=NORM_UNROLL)
+
+    def lane_sum(values):
+        total = values[:, :LANES]
+        for k in range(LANES, width, LANES):
+            total = total + values[:, k : k + LANES]
+        return jnp.sum(total, axis=1, keepdims=True)
+
+    for i in range(rows.shape[0]):
         copies[i].wait()
 
-        def some_rows(j, carry):
-            here = pl.ds(pl.multiple_of(j * NORM_ROWS, NORM_ROWS), NORM_ROWS)
-            hidden[i, here, :] = normed(rows[i, here, :].astype(jnp.float32), gains)
-            return carry
-
-        lax.fori_loop(0, length // NORM_ROWS, some_rows, 0, unroll=4)
+        def sum_rows(here):
+            total = lane_sum(rows[i, here, :].astype(jnp.float32))
+            average[here, :] = jnp.broadcast_to(total * (1.0 / width), (NORM_ROWS, LANES))
+
+        def scale_rows(here):
+            centred = rows[i, here, :].astype(jnp.float32) - average[here, :1]
+            variance = lane_sum(centred * centred) * (1.0 / width)
+            scale[here, :] = jnp.broadcast_to(
+                lax.rsqrt(variance + EPSILON), (NORM_ROWS, LANES)
+            )
+
+        def norm_rows(here):
+            centred = rows[i, here, :].astype(jnp.float32) - average[here, :1]
+            hidden[i, here, :] = (centred * scale[here, :1] * gains).astype(jnp.bfloat16)
+
+        grouped(sum_rows)
+        grouped(scale_rows)
+        grouped(norm_rows)
         stores[i].start()
     for copy in packs + stores:
         copy.wait()
@@ -92,6 +135,7 @@
 def start_work(tiles, gain, gate_weight, up_weight, slide_weights, parts):
     slot_count, length, width = tiles.shape
     half = slot_count // 2
+    pieces = half * length // NORM_PIECE
     hbm = pl.BlockSpec(memory_space=pltpu.HBM)
     vmem = pl.BlockSpec(memory_space=pltpu.VMEM)
     cols = gate_weight.shape[1]
@@ -106,11 +150,13 @@
             *[pltpu.VMEM((part.stop - part.start, cols), jnp.bfloat16) for part in parts],
         ],
         scratch_shapes=[
-            pltpu.VMEM((half, length, width), jnp.bfloat16),
-            pltpu.VMEM((half, length, width), jnp.bfloat16),
+            pltpu.VMEM((pieces, NORM_PIECE, width), jnp.bfloat16),
+            pltpu.VMEM((pieces, NORM_PIECE, width), jnp.bfloat16),
             pltpu.VMEM((width,), jnp.float32),
-            pltpu.SemaphoreType.DMA((half,)),
-            pltpu.SemaphoreType.DMA((half,)),
+            pltpu.VMEM((NORM_PIECE, LANES), jnp.float32),
+            pltpu.VMEM((NORM_PIECE, LANES), jnp.float32),
+            pltpu.SemaphoreType.DMA((pieces,)),
+            pltpu.SemaphoreType.DMA((pieces,)),
             pltpu.SemaphoreType.DMA((len(parts), 2)),
             pltpu.SemaphoreType.DMA((len(slide_weights),)),
             pltpu.SemaphoreType.DMA(()),
@@ -210,7 +256,14 @@
         layout.row_copies(ref, rows.at[i], row_sems.at[i], steps)
         for i, ref in enumerate(tile_refs)
     ]
-    for copy in row_loads[0] + loads + row_loads[1]:
+    late_loads = [
+        copy
+        for i, ref in enumerate(tile_refs)
+        for copy in layout.row_copies(
+            ref, rows.at[i], row_sems.at[i], range(layout.early_steps, layout.nz)
+        )
+    ]
+    for copy in row_loads[0] + loads + row_loads[1] + late_loads:
         copy.start()
     for copy in loads:
         copy.wait()
@@ -218,6 +271,8 @@
         for copy in row_loads[i]:
             copy.wait()
         product(out_ref.at[i], rows.at[i], weights, 0, layout.early)
+    for copy in late_loads:
+        copy.wait()
 
 
 def early_mlp(layout, blocks, tiles):
@@ -228,13 +283,13 @@
     return pl.pallas_call(
         functools.partial(early_kernel, layout),
         in_specs=[hbm] * (len(blocks) + 2),
-        out_specs=(vmem, vmem),
+        out_specs=(vmem, vmem, vmem),
         out_shape=(
             pltpu.VMEM((2, n_rows, cols), jnp.float32),
             pltpu.VMEM((layout.width, cols), jnp.bfloat16),
+            pltpu.VMEM((2, n_rows, layout.width), jnp.bfloat16),
         ),
         scratch_shapes=[
-            pltpu.VMEM((2, n_rows, layout.early_steps * layout.pair), jnp.bfloat16),
             pltpu.SemaphoreType.DMA((len(blocks),)),
             pltpu.SemaphoreType.DMA((2, layout.nz)),
         ],
@@ -247,34 +302,34 @@
     )(*in_hbm(*blocks, *tiles))
 
 
-def middle_kernel(layout, length, n_blocks, *refs):
-    blocks, tile_refs = refs[:n_blocks], refs[n_blocks : n_blocks + 3]
-    early_refs = refs[n_blocks + 3 : -7]
+def middle_kernel(layout, length, n_blocks, n_tiles, *refs):
+    blocks, tile_refs = refs[:n_blocks], refs[n_blocks : n_blocks + n_tiles]
+    early_refs = refs[n_blocks + n_tiles : -7]
     out_ref, weights, rows, even, odd, weight_sems, row_sems = refs[-7:]
     early = layout.early
     loads = layout.block_copies(blocks, weights, weight_sems, layout.nz)
-    steps = [range(early // layout.pair, layout.nz)] * 2 + [range(layout.nz)]
     row_loads = [
-        layout.row_copies(ref, rows.at[i], row_sems.at[i], steps[i])
+        layout.row_copies(ref, rows.at[i], row_sems.at[i], range(layout.nz))
         for i, ref in enumerate(tile_refs)
     ]
-    waits = [row_loads[0] + loads, row_loads[1], row_loads[2]]
-    for copies in waits:
-        for copy in copies:
-            copy.start()
+    for copy in [copy for copies in [loads, *row_loads] for copy in copies]:
+        copy.start()
+    for copy in loads:
+        copy.wait()
+    units = [(early_refs[2].at[i], early_refs[0].at[i], []) for i in range(2)] if early else []
+    units += [(rows.at[i], None, row_loads[i]) for i in range(n_tiles)]
     pending = None
-    for i in range(3):
-        for copy in waits[i]:
+    for i, (unit, more, waits) in enumerate(units):
+        for copy in waits:
             copy.wait()
-        for j in range(rows.shape[1] // length):
+        for j in range(unit.shape[0] // length):
             here = slice(j * length, (j + 1) * length)
-            tile = rows.shape[1] // length * i + j
+            tile = unit.shape[0] // length * i + j
             both = (even, odd)[tile % 2]
-            if i < 2 and early:
-                more = early_refs[0].at[i, here]
-                product(both, rows.at[i, here], weights, early, layout.width, more)
+            if more is None:
+                product(both, unit.at[here], weights, 0, layout.width)
             else:
-                product(both, rows.at[i, here], weights, 0, layout.width)
+                product(both, unit.at[here], weights, early, layout.width, more.at[here])
             if pending is not None:
                 gated_means(*pending, length)
             pending = (both, out_ref, tile)
@@ -284,23 +339,24 @@
 def middle_mlp(layout, blocks, tiles, early, length):
     n_rows, width = tiles[0].shape
     cols = blocks[0].shape[1]
+    tiles = tiles[2:] if early else tiles
     hbm = pl.BlockSpec(memory_space=pltpu.HBM)
     vmem = pl.BlockSpec(memory_space=pltpu.VMEM)
     return pl.pallas_call(
-        functools.partial(middle_kernel, layout, length, len(blocks)),
-        in_specs=[hbm] * (len(blocks) + 3) + [vmem] * len(early),
+        functools.partial(middle_kernel, layout, length, len(blocks), len(tiles)),
+        in_specs=[hbm] * (len(blocks) + len(tiles)) + [vmem] * len(early),
         out_specs=(vmem, vmem),
         out_shape=(
             pltpu.VMEM((3 * n_rows // length, cols // 2), jnp.float32),
             pltpu.VMEM((width, cols), jnp.bfloat16),
         ),
-        input_output_aliases={len(blocks) + 4: 1} if early else {},
+        input_output_aliases={len(blocks) + len(tiles) + 1: 1} if early else {},
         scratch_shapes=[
-            pltpu.VMEM((3, n_rows, width), jnp.bfloat16),
+            pltpu.VMEM((len(tiles), n_rows, width), jnp.bfloat16),
             pltpu.VMEM((length, cols), jnp.float32),
             pltpu.VMEM((length, cols), jnp.float32),
             pltpu.SemaphoreType.DMA((len(blocks),)),
-            pltpu.SemaphoreType.DMA((3, layout.nz)),
+            pltpu.SemaphoreType.DMA((len(tiles), layout.nz)),
         ],
         compiler_params=pltpu.CompilerParams(vmem_limit_bytes=MLP_VMEM),
         cost_estimate=pl.CostEstimate(

time: 78.1 us -> 77.4 us (level)
  waiting for transfers between devices: 28.9 us -> 22.4 us
  starting transfers between devices: 17.4 us -> 22.5 us
  local copies, waits for them, and re-layouts: 0.69 us -> 1.74 us
    ppermute x8, waiting for transfers between devices: 8.77 us -> 3.76 us  [on_device(): sent.append(lax.ppermute(held[part], 'dev', along_y))]
    ppermute x8, starting transfers between devices: 6.65 us -> 10.9 us  [on_device(): sent.append(lax.ppermute(held[part], 'dev', along_y))]
    ppermute x6, waiting for transfers between devices: 15.5 us -> 14 us  [on_device(): arrived = lax.ppermute(held[part], 'dev', along_z)]
    unnamed x40, local copies, waits for them, and re-layouts: 0.69 us -> 1.74 us
    all_to_all x1, starting transfers between devices: 3.54 us -> 4.51 us  [on_device(): sent = lax.all_to_all(sent, 'dev', split_axis=0, concat_axis=0, tiled=True)]
  transfers between devices with their start and end apart: 20 -> 20, of which waited for: 12 -> 11; matrix products, arithmetic and copies ran while one was open for 0% -> 0% of each run, Pallas kernels for 28% -> 22%
where the time goes in v10:
time: 77.4 us; the launch traced here: 77.1 us
  Pallas kernels  23.3 us (30%)
  starting transfers between devices  22.5 us (29%)
  waiting for transfers between devices  22.4 us (29%)
  blocking collectives  6.21 us (8%)
  local copies, waits for them, and re-layouts  1.74 us (2%)
  between operations  0.92 us (1%)
    ppermute x6, waiting for transfers between devices, on_device(): arrived = lax.ppermute(held[part], 'dev', along_z)  14 us
    ppermute x8, starting transfers between devices, on_device(): sent.append(lax.ppermute(held[part], 'dev', along_y))  10.9 us
    all_to_all x1, blocking collectives, on_device(): lax.all_to_all(parts, ('grp', 'sub'), split_axis=0, concat_axis=0, tiled=...  6.21 us
    pallas_call x1, Pallas kernels, early_mlp(): pl.pallas_call(functools.partial(early_kernel, layout), in_specs=[hbm] *...  5.39 us
    all_to_all x1, waiting for transfers between devices, on_device(): sent = lax.all_to_all(sent, 'dev', split_axis=0, concat_axis=0, tiled=True)  4.6 us
    all_to_all x1, starting transfers between devices, on_device(): sent = lax.all_to_all(sent, 'dev', split_axis=0, concat_axis=0, tiled=True)  4.51 us
    pallas_call x1, Pallas kernels, start_work(): pl.pallas_call(functools.partial(start_kernel, parts), in_specs=[hbm] * (...  4.49 us
    pallas_call x1, Pallas kernels, middle_mlp(): pl.pallas_call(functools.partial(middle_kernel, layout, length, len(block...  4.45 us
  transfers between devices with their start and end apart: 20, of which 11 were waited for; matrix products, arithmetic and copies ran while one was open for 0% of the time, Pallas kernels for 22%

profile of v10, /device:TPU:0, one launch (start us, length us, event | category | flops | bytes accessed | tf_op | source)
XLA Modules:
  0.0 77.1 jit_solution(348938401659111113)
XLA Ops:
  0.7 4.5 %shard_map.140 = (bf16[512,1536]{1,0:T(8,128)(2,1)}, bf16[2688,384]{1,0:T(8,128)(2,1)S(1)}, bf16[96,1024]{1,0:T(8,128)(2,1)S(1)}, bf16[96,1024]{1,0:T(8,128)(2,1)S(1)}) custom-call(bf16[4,256,1536]{2,1,0:T(8,128)(2,1)} %refs_0_.2, f32[1536]{0:T(1024)} %refs_1_.2, bf16[192,1024]{1,0:T(8,128)(2,1)} %refs_2_.2, bf16[192,1024]{1,0:T(8,128)(2,1)} %refs_3_.2, ...), custom_call_target="tpu_custom_call" | custom-call | tf_op jit(solution)/shard_map/pallas_call | solution.py:143
  5.8 2.9 %collective-permute-start.16 = (bf16[512,1536]{1,0:T(8,128)(2,1)}, bf16[512,1536]{1,0:T(8,128)(2,1)S(1)}, u32[]{:S(2)}, u32[]{:S(2)}) collective-permute-start(bf16[512,1536]{1,0:T(8,128)(2,1)} %get-tuple-element.41.refs_12_), channel_id=1, source_target_pairs={{0,16},{16,0},{1,17},{17,1},{2,18},{18,2},{3,19},{19,3},{4,20},{20... | collective-permute-start | bytes 4718600 | tf_op jit(solution)/shard_map/ppermute | solution.py:640
  8.7 1.5 %collective-permute-start.1 = (bf16[96,1024]{1,0:T(8,128)(2,1)S(1)}, bf16[96,1024]{1,0:T(8,128)(2,1)S(1)}, u32[]{:S(2)}, u32[]{:S(2)}) collective-permute-start(bf16[96,1024]{1,0:T(8,128)(2,1)S(1)} %get-tuple-element.31.refs_0_), channel_id=1, source_target_pairs={{0,2},{2,0},{4,6},{6,4},{8,10},{10,8},{12,14},{14,12},{1,3},{3,1},... | collective-permute-start | bytes 589832 | tf_op jit(solution)/shard_map/ppermute | solution.py:668
  10.2 1.6 %collective-permute-start = (bf16[96,1024]{1,0:T(8,128)(2,1)S(1)}, bf16[96,1024]{1,0:T(8,128)(2,1)S(1)}, u32[]{:S(2)}, u32[]{:S(2)}) collective-permute-start(bf16[96,1024]{1,0:T(8,128)(2,1)S(1)} %get-tuple-element.31.refs_0_), channel_id=1, source_target_pairs={{0,4},{2,6},{4,8},{6,10},{8,12},{10,14},{12,0},{14,2},{1,5},{3,7},... | collective-permute-start | bytes 589832 | tf_op jit(solution)/shard_map/ppermute | solution.py:661
  11.8 2.1 %collective-permute-start.7 = (bf16[96,1024]{1,0:T(8,128)(2,1)S(1)}, bf16[96,1024]{1,0:T(8,128)(2,1)S(1)}, u32[]{:S(2)}, u32[]{:S(2)}) collective-permute-start(bf16[96,1024]{1,0:T(8,128)(2,1)S(1)} %get-tuple-element.35.refs_1_), channel_id=1, source_target_pairs={{0,2},{2,0},{4,6},{6,4},{8,10},{10,8},{12,14},{14,12},{1,3},{3,1},... | collective-permute-start | bytes 589832 | tf_op jit(solution)/shard_map/ppermute | solution.py:668
  13.9 1.6 %collective-permute-start.6 = (bf16[96,1024]{1,0:T(8,128)(2,1)S(1)}, bf16[96,1024]{1,0:T(8,128)(2,1)S(1)}, u32[]{:S(2)}, u32[]{:S(2)}) collective-permute-start(bf16[96,1024]{1,0:T(8,128)(2,1)S(1)} %get-tuple-element.35.refs_1_), channel_id=1, source_target_pairs={{0,4},{2,6},{4,8},{6,10},{8,12},{10,14},{12,0},{14,2},{1,5},{3,7},... | collective-permute-start | bytes 589832 | tf_op jit(solution)/shard_map/ppermute | solution.py:661
  15.7 2.9 %collective-permute-done.refs_4_ = bf16[96,1024]{1,0:T(8,128)(2,1)S(1)} collective-permute-done((bf16[96,1024]{1,0:T(8,128)(2,1)S(1)}, bf16[96,1024]{1,0:T(8,128)(2,1)S(1)}, u32[]{:S(2)}, u32[]{:S(2)}) %collective-permute-start) | collective-permute-done | bytes 196640 | tf_op jit(solution)/shard_map/ppermute | solution.py:661
  19.5 3.9 %collective-permute-done.6.refs_5_ = bf16[96,1024]{1,0:T(8,128)(2,1)S(1)} collective-permute-done((bf16[96,1024]{1,0:T(8,128)(2,1)S(1)}, bf16[96,1024]{1,0:T(8,128)(2,1)S(1)}, u32[]{:S(2)}, u32[]{:S(2)}) %collective-permute-start.6) | collective-permute-done | bytes 196640 | tf_op jit(solution)/shard_map/ppermute | solution.py:661
  24.2 2.6 %collective-permute-done.2.refs_8_ = bf16[96,1024]{1,0:T(8,128)(2,1)S(1)} collective-permute-done((bf16[96,1024]{1,0:T(8,128)(2,1)S(1)}, bf16[96,1024]{1,0:T(8,128)(2,1)S(1)}, u32[]{:S(2)}, u32[]{:S(2)}) %collective-permute-start.2) | collective-permute-done | bytes 196640 | tf_op jit(solution)/shard_map/ppermute | solution.py:661
  28.1 2.6 %collective-permute-done.11.refs_7_ = bf16[96,1024]{1,0:T(8,128)(2,1)S(1)} collective-permute-done((bf16[96,1024]{1,0:T(8,128)(2,1)S(1)}, bf16[96,1024]{1,0:T(8,128)(2,1)S(1)}, u32[]{:S(2)}, u32[]{:S(2)}) %collective-permute-start.11) | collective-permute-done | bytes 196640 | tf_op jit(solution)/shard_map/ppermute | solution.py:668
  30.6 2.0 %collective-permute-done.10.refs_9_ = bf16[96,1024]{1,0:T(8,128)(2,1)S(1)} collective-permute-done((bf16[96,1024]{1,0:T(8,128)(2,1)S(1)}, bf16[96,1024]{1,0:T(8,128)(2,1)S(1)}, u32[]{:S(2)}, u32[]{:S(2)}) %collective-permute-start.10) | collective-permute-done | bytes 196640 | tf_op jit(solution)/shard_map/ppermute | solution.py:661
  32.7 2.1 %collective-permute-start.13 = (bf16[96,1024]{1,0:T(8,128)(2,1)S(1)}, bf16[96,1024]{1,0:T(8,128)(2,1)S(1)}, u32[]{:S(2)}, u32[]{:S(2)}) collective-permute-start(bf16[96,1024]{1,0:T(8,128)(2,1)S(1)} %collective-permute-done.10.refs_9_), channel_id=1, source_target_pairs={{0,2},{2,0},{4,6},{6,4},{8,10},{10,8},{12,14},{14,12},{1,3},{3,1},... | collective-permute-start | bytes 589832 | tf_op jit(solution)/shard_map/ppermute | solution.py:668
  36.2 1.4 %collective-permute-done.8.refs_0_ = bf16[96,1024]{1,0:T(8,128)(2,1)S(1)} collective-permute-done((bf16[96,1024]{1,0:T(8,128)(2,1)S(1)}, bf16[96,1024]{1,0:T(8,128)(2,1)S(1)}, u32[]{:S(2)}, u32[]{:S(2)}) %collective-permute-start.8) | collective-permute-done | bytes 196640 | tf_op jit(solution)/shard_map/ppermute | solution.py:661
  37.6 1.4 %collective-permute-start.14 = (bf16[96,1024]{1,0:T(8,128)(2,1)S(1)}, bf16[96,1024]{1,0:T(8,128)(2,1)S(1)}, u32[]{:S(2)}, u32[]{:S(2)}) collective-permute-start(bf16[96,1024]{1,0:T(8,128)(2,1)S(1)} %collective-permute-done.8.refs_0_), channel_id=1, source_target_pairs={{0,2},{2,0},{4,6},{6,4},{8,10},{10,8},{12,14},{14,12},{1,3},{3,1},... | collective-permute-start | bytes 589832 | tf_op jit(solution)/shard_map/ppermute | solution.py:668
  40.2 2.1 %collective-permute-start.15 = (bf16[96,1024]{1,0:T(8,128)(2,1)S(1)}, bf16[96,1024]{1,0:T(8,128)(2,1)S(1)}, u32[]{:S(2)}, u32[]{:S(2)}) collective-permute-start(bf16[96,1024]{1,0:T(8,128)(2,1)S(1)} %collective-permute-done.12.refs_1_), channel_id=1, source_target_pairs={{0,2},{2,0},{4,6},{6,4},{8,10},{10,8},{12,14},{14,12},{1,3},{3,1},... | collective-permute-start | bytes 589832 | tf_op jit(solution)/shard_map/ppermute | solution.py:668
  42.4 5.4 %shard_map.142 = (f32[2,512,1024]{2,1,0:T(8,128)S(1)}, bf16[1536,1024]{1,0:T(8,128)(2,1)S(1)}, bf16[2,512,1536]{2,1,0:T(8,128)(2,1)S(1)}) custom-call(bf16[96,1024]{1,0:T(8,128)(2,1)} %copy-done.6, bf16[96,1024]{1,0:T(8,128)(2,1)} %copy-done.7, bf16[96,1024]{1,0:T(8,128)(2,1)} %copy-done.10, bf16[96,1024]{1,0:T(8,128)(2,1)} %copy-done.12, ...), custom_call_target="tpu_custom_call" | custom-call | flops 2147483648 | bytes 8388608 | tf_op jit(solution)/shard_map/pallas_call | solution.py:283
  48.9 4.5 %shard_map.143 = (f32[6,512]{1,0:T(8,128)S(1)}, bf16[1536,1024]{1,0:T(8,128)(2,1)S(1)}) custom-call(bf16[96,1024]{1,0:T(8,128)(2,1)S(1)} %collective-permute-done.8.refs_0_, bf16[96,1024]{1,0:T(8,128)(2,1)S(1)} %collective-permute-done.12.refs_1_, bf16[96,1024]{1,0:T(8,128)(2,1)S(1)} %collective-permute-done.14.refs_2_, ...), custom_call_target="tpu_custom_call", output_to_operand_aliasing={{1}: (6, {})} | custom-call | flops 3221225472 | bytes 7864320 | tf_op jit(solution)/shard_map/pallas_call | solution.py:345
  53.4 2.1 %shard_map.144 = bf16[4,16,128]{2,1,0:T(8,128)(2,1)S(1)} custom-call(f32[6,512]{1,0:T(8,128)S(1)} %get-tuple-element.46.means_ref, bf16[1536,1024]{1,0:T(8,128)(2,1)S(1)} %get-tuple-element.47.weights, bf16[512,1536]{1,0:T(8,128)(2,1)S(1)} %collective-permute-done.17.tiles_ref), custom_call_target="tpu_custom_call" | custom-call | flops 1610612736 | bytes 4718592 | tf_op jit(solution)/shard_map/pallas_call | solution.py:413
  55.5 6.2 %all_to_all.10.parts_ref = bf16[4,16,128]{2,1,0:T(8,128)(2,1)S(1)} all-to-all(bf16[4,16,128]{2,1,0:T(8,128)(2,1)S(1)} %shard_map.144), channel_id=1, replica_groups=mesh['grp'=2,'dev'=8,'sub'=2] {'grp','sub'}, dimensions={0} | all-to-all | bytes 32768 | tf_op jit(solution)/shard_map/all_to_all | solution.py:680
  61.7 1.9 %shard_map.145 = (bf16[4,1024]{1,0:T(4,128)(2,1)}, f32[8,768]{1,0:T(8,128)S(1)}, bf16[8,16,256]{2,1,0:T(8,128)(2,1)}) custom-call(s32[8]{0:T(128)S(1)} %copy-done.3, bf16[4,16,128]{2,1,0:T(8,128)(2,1)S(1)} %all_to_all.10.parts_ref, f32[768]{0:T(1024)S(1)} %copy-done.2, bf16[1024,768]{1,0:T(8,128)(2,1)S(1)} %copy-done, ...), custom_call_target="tpu_custom_call" | custom-call | tf_op jit(solution)/shard_map/pallas_call | solution.py:686
  63.6 4.5 %all-to-all-start.1 = ((bf16[8,16,256]{2,1,0:T(8,128)(2,1)}), bf16[8,16,256]{2,1,0:T(8,128)(2,1)S(1)}, u32[]{:S(2)}, u32[]{:S(2)}) async-start(bf16[8,16,256]{2,1,0:T(8,128)(2,1)} %get-tuple-element.49), calls=%async_computation.1 | async-start | bytes 131072 | tf_op jit(solution)/shard_map/all_to_all | solution.py:697
  68.1 2.3 %shard_map.146 = (bf16[96,768]{1,0:T(8,128)(2,1)S(1)}, f32[96,32]{1,0:T(8,128)S(1)}, bf16[768,384]{1,0:T(8,128)(2,1)S(1)}, bf16[768,384]{1,0:T(8,128)(2,1)S(1)},...) custom-call(f32[8,768]{1,0:T(8,128)S(1)} %get-tuple-element.50.mixed, ...), custom_call_target="tpu_custom_call" | custom-call | tf_op jit(solution)/shard_map/pallas_call | solution.py:701
  70.4 4.6 %all-to-all-done.1.sent_ref = bf16[8,16,256]{2,1,0:T(8,128)(2,1)S(1)} async-done(((bf16[8,16,256]{2,1,0:T(8,128)(2,1)}), bf16[8,16,256]{2,1,0:T(8,128)(2,1)S(1)}, u32[]{:S(2)}, u32[]{:S(2)}) %all-to-all-start.1) | async-done | bytes 65568 | tf_op jit(solution)/shard_map/all_to_all | solution.py:697
  75.0 2.1 %shard_map.147 = bf16[4,384]{1,0:T(4,128)(2,1)} custom-call(s32[8]{0:T(128)S(1)} %copy-done.3, bf16[8,16,256]{2,1,0:T(8,128)(2,1)S(1)} %all-to-all-done.1.sent_ref, f32[8,768]{1,0:T(8,128)S(1)} %get-tuple-element.50.mixed_ref, bf16[96,768]{1,0:T(8,128)(2,1)S(1)} %get-tuple-element.52.query_ref, bf16[768,384]{1,0:T(8,128)(2,1)S(1)} %get-tuple-element.53.wk_ref, ...), custom_call_target="tpu_custom_call" | custom-call | tf_op jit(solution)/shard_map/pallas_call | solution.py:716
  (65 shorter events, 7.5 us)
Async XLA Ops:
  0.6 34.2 %copy-start.3 = (s32[8]{0:T(128)S(1)}, s32[8]{0:T(128)}, u32[]{:S(2)}) copy-start(s32[8]{0:T(128)} %counts_ref.5) | copy-start | bytes 100
  0.7 34.2 %copy-start.4 = (s32[8]{0:T(128)S(1)}, s32[8]{0:T(128)}, u32[]{:S(2)}) copy-start(s32[8]{0:T(128)} %slide_ref.1) | copy-start | bytes 100
  5.2 37.1 %copy-start.6 = (bf16[96,1024]{1,0:T(8,128)(2,1)}, bf16[96,1024]{1,0:T(8,128)(2,1)S(1)}, u32[]{:S(2)}) copy-start(bf16[96,1024]{1,0:T(8,128)(2,1)S(1)} %get-tuple-element.31.refs_0_) | copy-start | bytes 589828
  5.2 37.1 %copy-start.7 = (bf16[96,1024]{1,0:T(8,128)(2,1)}, bf16[96,1024]{1,0:T(8,128)(2,1)S(1)}, u32[]{:S(2)}) copy-start(bf16[96,1024]{1,0:T(8,128)(2,1)S(1)} %get-tuple-element.35.refs_1_) | copy-start | bytes 589828
  5.2 6.6 %collective-permute-start.5 = (bf16[512,1536]{1,0:T(8,128)(2,1)}, bf16[512,1536]{1,0:T(8,128)(2,1)S(1)}, u32[]{:S(2)}, u32[]{:S(2)}) collective-permute-start(bf16[512,1536]{1,0:T(8,128)(2,1)} %get-tuple-element.41.refs_12_), channel_id=1, source_target_pairs={{0,1},{1,0},{2,3},{3,2},{4,5},{5,4},{6,7},{7,6},{8,9},{9,8},{10,11... | collective-permute-start | bytes 4718600 | tf_op jit(solution)/shard_map/ppermute | solution.py:639
  5.7 6.1 %collective-permute-start.4 = (bf16[1024,768]{1,0:T(8,128)(2,1)S(1)}, bf16[1024,768]{1,0:T(8,128)(2,1)S(1)}, u32[]{:S(2)}, u32[]{:S(2)}) collective-permute-start(bf16[1024,768]{1,0:T(8,128)(2,1)S(1)} %copy-done), channel_id=1, source_target_pairs={{0,1},{1,0},{2,3},{3,2},{4,5},{5,4},{6,7},{7,6},{8,9},{9,8},{10,11... | collective-permute-start | bytes 4718600 | tf_op jit(solution)/shard_map/ppermute | solution.py:641
  5.8 42.0 %collective-permute-start.16 = (bf16[512,1536]{1,0:T(8,128)(2,1)}, bf16[512,1536]{1,0:T(8,128)(2,1)S(1)}, u32[]{:S(2)}, u32[]{:S(2)}) collective-permute-start(bf16[512,1536]{1,0:T(8,128)(2,1)} %get-tuple-element.41.refs_12_), channel_id=1, source_target_pairs={{0,16},{16,0},{1,17},{17,1},{2,18},{18,2},{3,19},{19,3},{4,20},{20... | collective-permute-start | bytes 4718600 | tf_op jit(solution)/shard_map/ppermute | solution.py:640
  8.7 7.0 %collective-permute-start.1 = (bf16[96,1024]{1,0:T(8,128)(2,1)S(1)}, bf16[96,1024]{1,0:T(8,128)(2,1)S(1)}, u32[]{:S(2)}, u32[]{:S(2)}) collective-permute-start(bf16[96,1024]{1,0:T(8,128)(2,1)S(1)} %get-tuple-element.31.refs_0_), channel_id=1, source_target_pairs={{0,2},{2,0},{4,6},{6,4},{8,10},{10,8},{12,14},{14,12},{1,3},{3,1},... | collective-permute-start | bytes 589832 | tf_op jit(solution)/shard_map/ppermute | solution.py:668
  10.2 8.3 %collective-permute-start = (bf16[96,1024]{1,0:T(8,128)(2,1)S(1)}, bf16[96,1024]{1,0:T(8,128)(2,1)S(1)}, u32[]{:S(2)}, u32[]{:S(2)}) collective-permute-start(bf16[96,1024]{1,0:T(8,128)(2,1)S(1)} %get-tuple-element.31.refs_0_), channel_id=1, source_target_pairs={{0,4},{2,6},{4,8},{6,10},{8,12},{10,14},{12,0},{14,2},{1,5},{3,7},... | collective-permute-start | bytes 589832 | tf_op jit(solution)/shard_map/ppermute | solution.py:661
  11.8 7.7 %collective-permute-start.7 = (bf16[96,1024]{1,0:T(8,128)(2,1)S(1)}, bf16[96,1024]{1,0:T(8,128)(2,1)S(1)}, u32[]{:S(2)}, u32[]{:S(2)}) collective-permute-start(bf16[96,1024]{1,0:T(8,128)(2,1)S(1)} %get-tuple-element.35.refs_1_), channel_id=1, source_target_pairs={{0,2},{2,0},{4,6},{6,4},{8,10},{10,8},{12,14},{14,12},{1,3},{3,1},... | collective-permute-start | bytes 589832 | tf_op jit(solution)/shard_map/ppermute | solution.py:668
  13.9 9.6 %collective-permute-start.6 = (bf16[96,1024]{1,0:T(8,128)(2,1)S(1)}, bf16[96,1024]{1,0:T(8,128)(2,1)S(1)}, u32[]{:S(2)}, u32[]{:S(2)}) collective-permute-start(bf16[96,1024]{1,0:T(8,128)(2,1)S(1)} %get-tuple-element.35.refs_1_), channel_id=1, source_target_pairs={{0,4},{2,6},{4,8},{6,10},{8,12},{10,14},{12,0},{14,2},{1,5},{3,7},... | collective-permute-start | bytes 589832 | tf_op jit(solution)/shard_map/ppermute | solution.py:661
  18.6 5.7 %collective-permute-start.3 = (bf16[96,1024]{1,0:T(8,128)(2,1)S(1)}, bf16[96,1024]{1,0:T(8,128)(2,1)S(1)}, u32[]{:S(2)}, u32[]{:S(2)}) collective-permute-start(bf16[96,1024]{1,0:T(8,128)(2,1)S(1)} %collective-permute-done.refs_4_), channel_id=1, source_target_pairs={{0,2},{2,0},{4,6},{6,4},{8,10},{10,8},{12,14},{14,12},{1,3},{3,1},... | collective-permute-start | bytes 589832 | tf_op jit(solution)/shard_map/ppermute | solution.py:668
  19.1 7.8 %collective-permute-start.2 = (bf16[96,1024]{1,0:T(8,128)(2,1)S(1)}, bf16[96,1024]{1,0:T(8,128)(2,1)S(1)}, u32[]{:S(2)}, u32[]{:S(2)}) collective-permute-start(bf16[96,1024]{1,0:T(8,128)(2,1)S(1)} %collective-permute-done.refs_4_), channel_id=1, source_target_pairs={{0,4},{2,6},{4,8},{6,10},{8,12},{10,14},{12,0},{14,2},{1,5},{3,7},... | collective-permute-start | bytes 589832 | tf_op jit(solution)/shard_map/ppermute | solution.py:661
  23.5 7.2 %collective-permute-start.11 = (bf16[96,1024]{1,0:T(8,128)(2,1)S(1)}, bf16[96,1024]{1,0:T(8,128)(2,1)S(1)}, u32[]{:S(2)}, u32[]{:S(2)}) collective-permute-start(bf16[96,1024]{1,0:T(8,128)(2,1)S(1)} %collective-permute-done.6.refs_5_), channel_id=1, source_target_pairs={{0,2},{2,0},{4,6},{6,4},{8,10},{10,8},{12,14},{14,12},{1,3},{3,1},... | collective-permute-start | bytes 589832 | tf_op jit(solution)/shard_map/ppermute | solution.py:668
  23.5 9.2 %collective-permute-start.10 = (bf16[96,1024]{1,0:T(8,128)(2,1)S(1)}, bf16[96,1024]{1,0:T(8,128)(2,1)S(1)}, u32[]{:S(2)}, u32[]{:S(2)}) collective-permute-start(bf16[96,1024]{1,0:T(8,128)(2,1)S(1)} %collective-permute-done.6.refs_5_), channel_id=1, source_target_pairs={{0,4},{2,6},{4,8},{6,10},{8,12},{10,14},{12,0},{14,2},{1,5},{3,7},... | collective-permute-start | bytes 589832 | tf_op jit(solution)/shard_map/ppermute | solution.py:661
  26.8 8.0 %collective-permute-start.9 = (bf16[96,1024]{1,0:T(8,128)(2,1)S(1)}, bf16[96,1024]{1,0:T(8,128)(2,1)S(1)}, u32[]{:S(2)}, u32[]{:S(2)}) collective-permute-start(bf16[96,1024]{1,0:T(8,128)(2,1)S(1)} %collective-permute-done.2.refs_8_), channel_id=1, source_target_pairs={{0,2},{2,0},{4,6},{6,4},{8,10},{10,8},{12,14},{14,12},{1,3},{3,1},... | collective-permute-start | bytes 589832 | tf_op jit(solution)/shard_map/ppermute | solution.py:668
  28.1 9.5 %collective-permute-start.8 = (bf16[96,1024]{1,0:T(8,128)(2,1)S(1)}, bf16[96,1024]{1,0:T(8,128)(2,1)S(1)}, u32[]{:S(2)}, u32[]{:S(2)}) collective-permute-start(bf16[96,1024]{1,0:T(8,128)(2,1)S(1)} %collective-permute-done.2.refs_8_), channel_id=1, source_target_pairs={{0,4},{2,6},{4,8},{6,10},{8,12},{10,14},{12,0},{14,2},{1,5},{3,7},... | collective-permute-start | bytes 589832 | tf_op jit(solution)/shard_map/ppermute | solution.py:661
  32.7 7.5 %collective-permute-start.12 = (bf16[96,1024]{1,0:T(8,128)(2,1)S(1)}, bf16[96,1024]{1,0:T(8,128)(2,1)S(1)}, u32[]{:S(2)}, u32[]{:S(2)}) collective-permute-start(bf16[96,1024]{1,0:T(8,128)(2,1)S(1)} %collective-permute-done.10.refs_9_), channel_id=1, source_target_pairs={{0,4},{2,6},{4,8},{6,10},{8,12},{10,14},{12,0},{14,2},{1,5},{3,7},... | collective-permute-start | bytes 589832 | tf_op jit(solution)/shard_map/ppermute | solution.py:661
  32.7 7.5 %collective-permute-start.13 = (bf16[96,1024]{1,0:T(8,128)(2,1)S(1)}, bf16[96,1024]{1,0:T(8,128)(2,1)S(1)}, u32[]{:S(2)}, u32[]{:S(2)}) collective-permute-start(bf16[96,1024]{1,0:T(8,128)(2,1)S(1)} %collective-permute-done.10.refs_9_), channel_id=1, source_target_pairs={{0,2},{2,0},{4,6},{6,4},{8,10},{10,8},{12,14},{14,12},{1,3},{3,1},... | collective-permute-start | bytes 589832 | tf_op jit(solution)/shard_map/ppermute | solution.py:668
  34.8 33.3 %collective-permute-start.18 = (bf16[2688,384]{1,0:T(8,128)(2,1)S(1)}, bf16[2688,384]{1,0:T(8,128)(2,1)}, u32[]{:S(2)}, u32[]{:S(2)}) collective-permute-start(bf16[2688,384]{1,0:T(8,128)(2,1)S(1)} %get-tuple-element.51), channel_id=1, source_target_pairs={{0,1},{1,0},{2,3},{3,2},{4,5},{5,4},{6,7},{7,6},{8,9},{9,8},{10,11... | collective-permute-start | bytes 6193160 | tf_op jit(solution)/shard_map/ppermute | solution.py:642
  37.6 10.2 %collective-permute-start.14 = (bf16[96,1024]{1,0:T(8,128)(2,1)S(1)}, bf16[96,1024]{1,0:T(8,128)(2,1)S(1)}, u32[]{:S(2)}, u32[]{:S(2)}) collective-permute-start(bf16[96,1024]{1,0:T(8,128)(2,1)S(1)} %collective-permute-done.8.refs_0_), channel_id=1, source_target_pairs={{0,2},{2,0},{4,6},{6,4},{8,10},{10,8},{12,14},{14,12},{1,3},{3,1},... | collective-permute-start | bytes 589832 | tf_op jit(solution)/shard_map/ppermute | solution.py:668
  40.2 7.6 %collective-permute-start.15 = (bf16[96,1024]{1,0:T(8,128)(2,1)S(1)}, bf16[96,1024]{1,0:T(8,128)(2,1)S(1)}, u32[]{:S(2)}, u32[]{:S(2)}) collective-permute-start(bf16[96,1024]{1,0:T(8,128)(2,1)S(1)} %collective-permute-done.12.refs_1_), channel_id=1, source_target_pairs={{0,2},{2,0},{4,6},{6,4},{8,10},{10,8},{12,14},{14,12},{1,3},{3,1},... | collective-permute-start | bytes 589832 | tf_op jit(solution)/shard_map/ppermute | solution.py:668
  47.8 5.6 %collective-permute-start.17 = (bf16[512,1536]{1,0:T(8,128)(2,1)S(1)}, bf16[512,1536]{1,0:T(8,128)(2,1)S(1)}, u32[]{:S(2)}, u32[]{:S(2)}) collective-permute-start(bf16[512,1536]{1,0:T(8,128)(2,1)S(1)} %collective-permute-done.16.refs_4_), channel_id=1, source_target_pairs={{0,1},{1,0},{2,3},{3,2},{4,5},{5,4},{6,7},{7,6},{8,9},{9,8},{10,11... | collective-permute-start | bytes 4718600 | tf_op jit(solution)/shard_map/ppermute | solution.py:677
  63.6 11.4 %all-to-all-start.1 = ((bf16[8,16,256]{2,1,0:T(8,128)(2,1)}), bf16[8,16,256]{2,1,0:T(8,128)(2,1)S(1)}, u32[]{:S(2)}, u32[]{:S(2)}) async-start(bf16[8,16,256]{2,1,0:T(8,128)(2,1)} %get-tuple-element.49), calls=%async_computation.1 | async-start | bytes 131072 | tf_op jit(solution)/shard_map/all_to_all | solution.py:697
  (16 other events, 236.3 us)

commit v11 on v10

--- a/solution.py
+++ b/solution.py
@@ -20,7 +20,7 @@
 ROW_TILE = 16
 MXU = 256
 MLP_VMEM = 24 * 1024 * 1024
-NORM_VMEM = 8 * 1024 * 1024
+NORM_VMEM = 12 * 1024 * 1024
 SMALL_VMEM = 4 * 1024 * 1024
 
 
@@ -48,6 +48,8 @@
         gain,
         average,
         scale,
+        whole,
+        whole_slide,
         in_sems,
         out_sems,
         block_sems,
@@ -71,21 +73,25 @@
         pltpu.make_async_copy(hidden.at[i], out_ref.at[pl.ds(i * piece, piece)], out_sems.at[i])
         for i in range(pieces)
     ]
-    packs = []
+    packs = [
+        pltpu.make_async_copy(ref, whole.at[i], block_sems.at[i])
+        for i, ref in enumerate((gate_ref, up_ref))
+    ]
+    selects = []
     columns = pl.ds(pl.multiple_of(lax.rem(lax.axis_index("grp"), 2) * half_cols, LANES), half_cols)
     for k, (part, block_ref) in enumerate(zip(parts, block_refs)):
         for i, ref in enumerate((gate_ref, up_ref)):
-            place = block_ref.at[:, i * half_cols : (i + 1) * half_cols]
-            packs.append(
-                pltpu.make_async_copy(ref.at[part, columns], place, block_sems.at[k, i])
-            )
+            selects.append((block_ref, i * half_cols, whole.at[i, part, columns]))
     cols = pack_ref.shape[1]
     others = pl.ds(pl.multiple_of((1 - core) * cols, LANES), cols)
     at = 0
     for k, ref in enumerate(slide_refs):
         place = pack_ref.at[at : at + ref.shape[0]]
-        source = ref if ref.shape[1] == cols else ref.at[:, others]
-        packs.append(pltpu.make_async_copy(source, place, slide_sems.at[k]))
+        if ref.shape[1] == cols:
+            packs.append(pltpu.make_async_copy(ref, place, slide_sems.at[k]))
+        else:
+            packs.append(pltpu.make_async_copy(ref, whole_slide, slide_sems.at[k]))
+            selects.append((place, 0, whole_slide.at[:, others]))
         at += ref.shape[0]
     for copy in [gain_copy] + copies + packs:
         copy.start()
@@ -128,7 +134,11 @@
         grouped(scale_rows)
         grouped(norm_rows)
         stores[i].start()
-    for copy in packs + stores:
+    for copy in packs:
+        copy.wait()
+    for place, at, source in selects:
+        place[:, at : at + source.shape[1]] = source[...]
+    for copy in stores:
         copy.wait()
 
 
@@ -155,9 +165,11 @@
             pltpu.VMEM((width,), jnp.float32),
             pltpu.VMEM((NORM_PIECE, LANES), jnp.float32),
             pltpu.VMEM((NORM_PIECE, LANES), jnp.float32),
+            pltpu.VMEM((2, *gate_weight.shape), jnp.bfloat16),
+            pltpu.VMEM(slide_weights[-1].shape, jnp.bfloat16),
             pltpu.SemaphoreType.DMA((pieces,)),
             pltpu.SemaphoreType.DMA((pieces,)),
-            pltpu.SemaphoreType.DMA((len(parts), 2)),
+            pltpu.SemaphoreType.DMA((2,)),
             pltpu.SemaphoreType.DMA((len(slide_weights),)),
             pltpu.SemaphoreType.DMA(()),
         ],
@@ -302,10 +314,18 @@
     )(*in_hbm(*blocks, *tiles))
 
 
+def packed(mine, others):
+    low = lax.axis_index("sub") == 0
+    rows = jnp.concatenate([jnp.where(low, mine, others), jnp.where(low, others, mine)], axis=0)
+    return jnp.concatenate(
+        [rows[:, k : k + LANES] for k in range(0, rows.shape[1], LANES)], axis=0
+    ).astype(jnp.bfloat16)
+
+
 def middle_kernel(layout, length, n_blocks, n_tiles, *refs):
     blocks, tile_refs = refs[:n_blocks], refs[n_blocks : n_blocks + n_tiles]
-    early_refs = refs[n_blocks + n_tiles : -7]
-    out_ref, weights, rows, even, odd, weight_sems, row_sems = refs[-7:]
+    early_refs = refs[n_blocks + n_tiles : -9]
+    pair_ref, weights, own_ref, rows, even, odd, means, weight_sems, row_sems = refs[-9:]
     early = layout.early
     loads = layout.block_copies(blocks, weights, weight_sems, layout.nz)
     row_loads = [
@@ -332,29 +352,35 @@
                 product(both, unit.at[here], weights, early, layout.width, more.at[here])
             if pending is not None:
                 gated_means(*pending, length)
-            pending = (both, out_ref, tile)
+            pending = (both, means, tile)
     gated_means(*pending, length)
+    half = means.shape[0] // 3
+    own_ref[...] = packed(means[:half, :], means[half : 2 * half, :])
+    pair_ref[...] = means[2 * half :, :]
 
 
 def middle_mlp(layout, blocks, tiles, early, length):
     n_rows, width = tiles[0].shape
     cols = blocks[0].shape[1]
+    half = n_rows // length
     tiles = tiles[2:] if early else tiles
-    hbm = pl.BlockSpec(memory_space=pltpu.HBM)
     vmem = pl.BlockSpec(memory_space=pltpu.VMEM)
     return pl.pallas_call(
         functools.partial(middle_kernel, layout, length, len(blocks), len(tiles)),
-        in_specs=[hbm] * (len(blocks) + len(tiles)) + [vmem] * len(early),
-        out_specs=(vmem, vmem),
+        in_specs=[pl.BlockSpec(memory_space=pl.ANY)] * (len(blocks) + len(tiles))
+        + [vmem] * len(early),
+        out_specs=(vmem, vmem, vmem),
         out_shape=(
-            pltpu.VMEM((3 * n_rows // length, cols // 2), jnp.float32),
+            pltpu.VMEM((half, cols // 2), jnp.float32),
             pltpu.VMEM((width, cols), jnp.bfloat16),
+            jax.ShapeDtypeStruct((half * cols // LANES, LANES), jnp.bfloat16),
         ),
         input_output_aliases={len(blocks) + len(tiles) + 1: 1} if early else {},
         scratch_shapes=[
             pltpu.VMEM((len(tiles), n_rows, width), jnp.bfloat16),
             pltpu.VMEM((length, cols), jnp.float32),
             pltpu.VMEM((length, cols), jnp.float32),
+            pltpu.VMEM((3 * half, cols // 2), jnp.float32),
             pltpu.SemaphoreType.DMA((len(blocks),)),
             pltpu.SemaphoreType.DMA((len(tiles), layout.nz)),
         ],
@@ -364,59 +390,36 @@
             bytes_accessed=2 * (3 * n_rows * width + width * cols),
             transcendentals=0,
         ),
-    )(*blocks, *in_hbm(*tiles), *in_vmem(*early))
-
-
-def last_kernel(
-    layout, length, n_grp, n_sub, means_ref, weights, tiles_ref, out_ref, rows, both, means, row_sems
-):
+    )(*blocks, *(tiles if early else in_hbm(*tiles)), *in_vmem(*early))
+
+
+def last_kernel(layout, length, means_ref, weights, tiles_ref, out_ref, rows, both, means, row_sems):
     row_loads = layout.row_copies(tiles_ref, rows, row_sems, range(layout.nz))
     for copy in row_loads:
         copy.start()
     for copy in row_loads:
         copy.wait()
-    n_rows = rows.shape[0]
-    half = n_rows // length
+    half = rows.shape[0] // length
     for i in range(half):
         here = slice(i * length, (i + 1) * length)
         product(both[i], rows.at[here], weights, 0, layout.width)
         if i:
             gated_means(both[i - 1], means, i - 1, length)
     gated_means(both[half - 1], means, half - 1, length)
-
-    group, core = lax.axis_index("grp"), lax.axis_index("sub")
-    low = core == 0
-
-    def packed(mine, others):
-        rows = jnp.concatenate(
-            [jnp.where(low, mine, others), jnp.where(low, others, mine)], axis=0
-        )
-        return jnp.concatenate(
-            [rows[:, k : k + LANES] for k in range(0, rows.shape[1], LANES)], axis=0
-        )
-
-    before = means_ref[...]
-    own = packed(before[:half], before[half : 2 * half])
-    pair = packed(before[2 * half :], means[...])
-    for g in range(n_grp):
-        chosen = jnp.where(group == g, own, pair).astype(jnp.bfloat16)
-        for s in range(n_sub):
-            out_ref[g * n_sub + s] = chosen
-
-
-def last_mlp(layout, means, weights, tiles, length, n_grp, n_sub):
+    out_ref[...] = packed(means_ref[...], means[...])
+
+
+def last_mlp(layout, means, weights, tiles, length):
     n_rows, width = tiles.shape
     cols = weights.shape[1]
     half = n_rows // length
     any_spec = pl.BlockSpec(memory_space=pl.ANY)
     vmem = pl.BlockSpec(memory_space=pltpu.VMEM)
     return pl.pallas_call(
-        functools.partial(last_kernel, layout, length, n_grp, n_sub),
+        functools.partial(last_kernel, layout, length),
         in_specs=[vmem, vmem, any_spec],
         out_specs=vmem,
-        out_shape=jax.ShapeDtypeStruct(
-            (n_grp * n_sub, half * cols // LANES, LANES), jnp.bfloat16
-        ),
+        out_shape=jax.ShapeDtypeStruct((half * cols // LANES, LANES), jnp.bfloat16),
         scratch_shapes=[
             pltpu.VMEM((n_rows, width), jnp.bfloat16),
             [pltpu.VMEM((length, cols), jnp.float32) for _ in range(half)],
@@ -477,25 +480,38 @@
 
 
 def embed_kernel(
-    n_sub, counts_ref, parts_ref, gain_ref, near_ref, far_ref, embed_ref, mixed_ref, sent_ref
+    counts_ref,
+    own_ref,
+    own_far_ref,
+    pair_ref,
+    pair_far_ref,
+    gain_ref,
+    near_ref,
+    far_ref,
+    embed_ref,
+    mixed_ref,
+    sent_ref,
 ):
     slot_count, half = embed_ref.shape
     n_blocks = half // 2 // LANES
-    group, core = lax.axis_index("grp"), lax.axis_index("sub")
+    low = lax.rem(lax.axis_index("grp"), 2) == 0
     count = counts_ref[lax.axis_index("dev")]
-    base = group // 2 * 2
-    halves = []
-    for s in range(n_sub):
-        pieces = []
-        for x in range(2):
-            part = parts_ref[(base + x) * n_sub + s].astype(jnp.float32)
-            pieces += [part[k * slot_count : (k + 1) * slot_count] for k in range(n_blocks)]
-        rows = jnp.concatenate(pieces, axis=1)
+
+    def features(mine_ref, theirs_ref):
+        sides = []
+        for ref in (mine_ref, theirs_ref):
+            part = ref[...].astype(jnp.float32)
+            pieces = [part[k * slot_count : (k + 1) * slot_count] for k in range(n_blocks)]
+            sides.append(jnp.concatenate(pieces, axis=1))
+        mine, theirs = sides
+        rows = jnp.concatenate(
+            [jnp.where(low, mine, theirs), jnp.where(low, theirs, mine)], axis=1
+        )
         slot = lax.broadcasted_iota(jnp.int32, rows.shape, 0)
-        halves.append(jnp.where(slot < count, rows, 0.0))
-    low = core == 0
-    near = jnp.where(low, halves[0], halves[1]).astype(jnp.bfloat16)
-    far = jnp.where(low, halves[1], halves[0]).astype(jnp.bfloat16)
+        return jnp.where(slot < count, rows, 0.0).astype(jnp.bfloat16)
+
+    near = features(own_ref, pair_ref)
+    far = features(own_far_ref, pair_far_ref)
     embed_ref[...] = near
     mixed = jnp.dot(near, near_ref[...], preferred_element_type=jnp.float32) + jnp.dot(
         far, far_ref[...], preferred_element_type=jnp.float32
@@ -675,17 +691,24 @@
         blocks = blocks[n_early:]
     pair_first = after(pair_first, *steps[-1][-2:], *early)
     pair_second = lax.ppermute(pair_first, "sub", to_sibling)
-    means, weights = middle_mlp(layout, blocks, [first, second, pair_first], early, length)
-    parts = last_mlp(layout, means, weights, pair_second, length, n_grp, n_sub)
-    parts = lax.all_to_all(parts, ("grp", "sub"), split_axis=0, concat_axis=0, tiled=True)
+    means, weights, own = middle_mlp(
+        layout, blocks, [first, second, pair_first], early, length
+    )
+    own_far = lax.ppermute(own, "sub", to_sibling)
+    pair = last_mlp(layout, means, weights, pair_second, length)
+    across = [
+        (g * n_sub + s, (g ^ 1) * n_sub + (s ^ 1)) for g in range(n_grp) for s in range(n_sub)
+    ]
+    pair_far = lax.ppermute(pair, ("grp", "sub"), across)
+    pair = lax.ppermute(pair, "grp", to_pair)
 
     out_width = embed_proj.shape[1]
     sent_rows = 16
     sent_cols = 2 * LANES
     small = pltpu.CompilerParams(vmem_limit_bytes=SMALL_VMEM)
     tile_embed, mixed, sent = pl.pallas_call(
-        functools.partial(embed_kernel, n_sub),
-        in_specs=[smem] + [vmem] * 4,
+        embed_kernel,
+        in_specs=[smem] + [vmem] * 7,
         out_specs=(vmem, vmem, vmem),
         out_shape=(
             jax.ShapeDtypeStruct((slot_count, hidden_cols), jnp.bfloat16),
@@ -693,7 +716,7 @@
             pltpu.VMEM((n_dev, sent_rows, sent_cols), jnp.bfloat16),
         ),
         compiler_params=small,
-    )(counts, *in_vmem(parts), slide_gain, embed_proj, proj_far)
+    )(counts, *in_vmem(own, own_far, pair, pair_far), slide_gain, embed_proj, proj_far)
     sent = lax.all_to_all(sent, "dev", split_axis=0, concat_axis=0, tiled=True)
     hbm = pl.BlockSpec(memory_space=pltpu.HBM)
     far_shape = (slide_wo.shape[0], out_cols)

time: 77.4 us -> 75.8 us (0.979)
  blocking collectives: 6.21 us -> 0 us
  starting transfers between devices: 22.5 us -> 25.5 us
  waiting for transfers between devices: 22.4 us -> 25.4 us
  local copies, waits for them, and re-layouts: 1.74 us -> 0.07 us
    all_to_all x1 -> x0, blocking collectives: 6.21 us -> none  [on_device(): lax.all_to_all(parts, ('grp', 'sub'), split_axis=0, concat_axis=0, tiled=...]
    ppermute x0 -> x3, waiting for transfers between devices: none -> 2.42 us  [the longest x1 2.17 us: on_device(): pair = lax.ppermute(pair, 'grp', to_pair)]
    ppermute x0 -> x3, starting transfers between devices: none -> 1.99 us  [the longest x1 0.87 us: on_device(): pair = lax.ppermute(pair, 'grp', to_pair)]
    unnamed x40 -> x38, local copies, waits for them, and re-layouts: 1.74 us -> 0.07 us
    all_to_all x1, starting transfers between devices: 4.51 us -> 5.53 us  [on_device(): sent = lax.all_to_all(sent, 'dev', split_axis=0, concat_axis=0, tiled=True)]
  transfers between devices with their start and end apart: 20 -> 23, of which waited for: 11 -> 13; matrix products, arithmetic and copies ran while one was open for 0% -> 0% of each run, Pallas kernels for 22% -> 23%
where the time goes in v11:
time: 75.8 us; the launch traced here: 75.5 us
  starting transfers between devices  25.5 us (34%)
  waiting for transfers between devices  25.4 us (34%)
  Pallas kernels  23.6 us (31%)
  between operations  0.91 us (1%)
    ppermute x6, waiting for transfers between devices, on_device(): arrived = lax.ppermute(held[part], 'dev', along_z)  14.6 us
    ppermute x8, starting transfers between devices, on_device(): sent.append(lax.ppermute(held[part], 'dev', along_y))  10.9 us
    all_to_all x1, starting transfers between devices, on_device(): sent = lax.all_to_all(sent, 'dev', split_axis=0, concat_axis=0, tiled=True)  5.53 us
    pallas_call x1, Pallas kernels, early_mlp(): pl.pallas_call(functools.partial(early_kernel, layout), in_specs=[hbm] *...  5.39 us
    pallas_call x1, Pallas kernels, middle_mlp(): pl.pallas_call(functools.partial(middle_kernel, layout, length, len(block...  4.78 us
    all_to_all x1, waiting for transfers between devices, on_device(): sent = lax.all_to_all(sent, 'dev', split_axis=0, concat_axis=0, tiled=True)  4.6 us
    pallas_call x1, Pallas kernels, start_work(): pl.pallas_call(functools.partial(start_kernel, parts), in_specs=[hbm] * (...  4.48 us
    ppermute x8, waiting for transfers between devices, on_device(): sent.append(lax.ppermute(held[part], 'dev', along_y))  3.76 us
  transfers between devices with their start and end apart: 23, of which 13 were waited for; matrix products, arithmetic and copies ran while one was open for 0% of the time, Pallas kernels for 23%

profile of v11, /device:TPU:0, one launch (start us, length us, event | category | flops | bytes accessed | tf_op | source)
XLA Modules:
  0.0 75.5 jit_solution(9692378083435767248)
XLA Ops:
  0.7 4.5 %shard_map.140 = (bf16[512,1536]{1,0:T(8,128)(2,1)}, bf16[2688,384]{1,0:T(8,128)(2,1)S(1)}, bf16[96,1024]{1,0:T(8,128)(2,1)S(1)}, bf16[96,1024]{1,0:T(8,128)(2,1)S(1)}) custom-call(bf16[4,256,1536]{2,1,0:T(8,128)(2,1)} %refs_0_.2, f32[1536]{0:T(1024)} %refs_1_.2, bf16[192,1024]{1,0:T(8,128)(2,1)} %refs_2_.2, bf16[192,1024]{1,0:T(8,128)(2,1)} %refs_3_.2, ...), custom_call_target="tpu_custom_call" | custom-call | tf_op jit(solution)/shard_map/pallas_call | solution.py:153
  5.8 2.9 %collective-permute-start.16 = (bf16[512,1536]{1,0:T(8,128)(2,1)}, bf16[512,1536]{1,0:T(8,128)(2,1)S(1)}, u32[]{:S(2)}, u32[]{:S(2)}) collective-permute-start(bf16[512,1536]{1,0:T(8,128)(2,1)} %get-tuple-element.42.refs_12_), channel_id=1, source_target_pairs={{0,16},{16,0},{1,17},{17,1},{2,18},{18,2},{3,19},{19,3},{4,20},{20... | collective-permute-start | bytes 4718600 | tf_op jit(solution)/shard_map/ppermute | solution.py:656
  8.7 1.5 %collective-permute-start.1 = (bf16[96,1024]{1,0:T(8,128)(2,1)S(1)}, bf16[96,1024]{1,0:T(8,128)(2,1)S(1)}, u32[]{:S(2)}, u32[]{:S(2)}) collective-permute-start(bf16[96,1024]{1,0:T(8,128)(2,1)S(1)} %get-tuple-element.32.refs_0_), channel_id=1, source_target_pairs={{0,2},{2,0},{4,6},{6,4},{8,10},{10,8},{12,14},{14,12},{1,3},{3,1},... | collective-permute-start | bytes 589832 | tf_op jit(solution)/shard_map/ppermute | solution.py:684
  10.2 1.6 %collective-permute-start = (bf16[96,1024]{1,0:T(8,128)(2,1)S(1)}, bf16[96,1024]{1,0:T(8,128)(2,1)S(1)}, u32[]{:S(2)}, u32[]{:S(2)}) collective-permute-start(bf16[96,1024]{1,0:T(8,128)(2,1)S(1)} %get-tuple-element.32.refs_0_), channel_id=1, source_target_pairs={{0,4},{2,6},{4,8},{6,10},{8,12},{10,14},{12,0},{14,2},{1,5},{3,7},... | collective-permute-start | bytes 589832 | tf_op jit(solution)/shard_map/ppermute | solution.py:677
  11.8 2.1 %collective-permute-start.7 = (bf16[96,1024]{1,0:T(8,128)(2,1)S(1)}, bf16[96,1024]{1,0:T(8,128)(2,1)S(1)}, u32[]{:S(2)}, u32[]{:S(2)}) collective-permute-start(bf16[96,1024]{1,0:T(8,128)(2,1)S(1)} %get-tuple-element.36.refs_1_), channel_id=1, source_target_pairs={{0,2},{2,0},{4,6},{6,4},{8,10},{10,8},{12,14},{14,12},{1,3},{3,1},... | collective-permute-start | bytes 589832 | tf_op jit(solution)/shard_map/ppermute | solution.py:684
  13.9 1.6 %collective-permute-start.6 = (bf16[96,1024]{1,0:T(8,128)(2,1)S(1)}, bf16[96,1024]{1,0:T(8,128)(2,1)S(1)}, u32[]{:S(2)}, u32[]{:S(2)}) collective-permute-start(bf16[96,1024]{1,0:T(8,128)(2,1)S(1)} %get-tuple-element.36.refs_1_), channel_id=1, source_target_pairs={{0,4},{2,6},{4,8},{6,10},{8,12},{10,14},{12,0},{14,2},{1,5},{3,7},... | collective-permute-start | bytes 589832 | tf_op jit(solution)/shard_map/ppermute | solution.py:677
  15.7 2.9 %collective-permute-done.refs_4_ = bf16[96,1024]{1,0:T(8,128)(2,1)S(1)} collective-permute-done((bf16[96,1024]{1,0:T(8,128)(2,1)S(1)}, bf16[96,1024]{1,0:T(8,128)(2,1)S(1)}, u32[]{:S(2)}, u32[]{:S(2)}) %collective-permute-start) | collective-permute-done | bytes 196640 | tf_op jit(solution)/shard_map/ppermute | solution.py:677
  19.5 3.9 %collective-permute-done.6.refs_5_ = bf16[96,1024]{1,0:T(8,128)(2,1)S(1)} collective-permute-done((bf16[96,1024]{1,0:T(8,128)(2,1)S(1)}, bf16[96,1024]{1,0:T(8,128)(2,1)S(1)}, u32[]{:S(2)}, u32[]{:S(2)}) %collective-permute-start.6) | collective-permute-done | bytes 196640 | tf_op jit(solution)/shard_map/ppermute | solution.py:677
  24.2 2.6 %collective-permute-done.2.refs_8_ = bf16[96,1024]{1,0:T(8,128)(2,1)S(1)} collective-permute-done((bf16[96,1024]{1,0:T(8,128)(2,1)S(1)}, bf16[96,1024]{1,0:T(8,128)(2,1)S(1)}, u32[]{:S(2)}, u32[]{:S(2)}) %collective-permute-start.2) | collective-permute-done | bytes 196640 | tf_op jit(solution)/shard_map/ppermute | solution.py:677
  28.1 2.6 %collective-permute-done.11.refs_7_ = bf16[96,1024]{1,0:T(8,128)(2,1)S(1)} collective-permute-done((bf16[96,1024]{1,0:T(8,128)(2,1)S(1)}, bf16[96,1024]{1,0:T(8,128)(2,1)S(1)}, u32[]{:S(2)}, u32[]{:S(2)}) %collective-permute-start.11) | collective-permute-done | bytes 196640 | tf_op jit(solution)/shard_map/ppermute | solution.py:684
  30.6 2.0 %collective-permute-done.10.refs_9_ = bf16[96,1024]{1,0:T(8,128)(2,1)S(1)} collective-permute-done((bf16[96,1024]{1,0:T(8,128)(2,1)S(1)}, bf16[96,1024]{1,0:T(8,128)(2,1)S(1)}, u32[]{:S(2)}, u32[]{:S(2)}) %collective-permute-start.10) | collective-permute-done | bytes 196640 | tf_op jit(solution)/shard_map/ppermute | solution.py:677
  32.7 2.1 %collective-permute-start.13 = (bf16[96,1024]{1,0:T(8,128)(2,1)S(1)}, bf16[96,1024]{1,0:T(8,128)(2,1)S(1)}, u32[]{:S(2)}, u32[]{:S(2)}) collective-permute-start(bf16[96,1024]{1,0:T(8,128)(2,1)S(1)} %collective-permute-done.10.refs_9_), channel_id=1, source_target_pairs={{0,2},{2,0},{4,6},{6,4},{8,10},{10,8},{12,14},{14,12},{1,3},{3,1},... | collective-permute-start | bytes 589832 | tf_op jit(solution)/shard_map/ppermute | solution.py:684
  35.5 2.0 %collective-permute-done.8.refs_0_ = bf16[96,1024]{1,0:T(8,128)(2,1)S(1)} collective-permute-done((bf16[96,1024]{1,0:T(8,128)(2,1)S(1)}, bf16[96,1024]{1,0:T(8,128)(2,1)S(1)}, u32[]{:S(2)}, u32[]{:S(2)}) %collective-permute-start.8) | collective-permute-done | bytes 196640 | tf_op jit(solution)/shard_map/ppermute | solution.py:677
  37.6 1.4 %collective-permute-start.14 = (bf16[96,1024]{1,0:T(8,128)(2,1)S(1)}, bf16[96,1024]{1,0:T(8,128)(2,1)S(1)}, u32[]{:S(2)}, u32[]{:S(2)}) collective-permute-start(bf16[96,1024]{1,0:T(8,128)(2,1)S(1)} %collective-permute-done.8.refs_0_), channel_id=1, source_target_pairs={{0,2},{2,0},{4,6},{6,4},{8,10},{10,8},{12,14},{14,12},{1,3},{3,1},... | collective-permute-start | bytes 589832 | tf_op jit(solution)/shard_map/ppermute | solution.py:684
  40.2 2.1 %collective-permute-start.15 = (bf16[96,1024]{1,0:T(8,128)(2,1)S(1)}, bf16[96,1024]{1,0:T(8,128)(2,1)S(1)}, u32[]{:S(2)}, u32[]{:S(2)}) collective-permute-start(bf16[96,1024]{1,0:T(8,128)(2,1)S(1)} %collective-permute-done.12.refs_1_), channel_id=1, source_target_pairs={{0,2},{2,0},{4,6},{6,4},{8,10},{10,8},{12,14},{14,12},{1,3},{3,1},... | collective-permute-start | bytes 589832 | tf_op jit(solution)/shard_map/ppermute | solution.py:684
  42.4 5.4 %shard_map.142 = (f32[2,512,1024]{2,1,0:T(8,128)S(1)}, bf16[1536,1024]{1,0:T(8,128)(2,1)S(1)}, bf16[2,512,1536]{2,1,0:T(8,128)(2,1)S(1)}) custom-call(bf16[96,1024]{1,0:T(8,128)(2,1)} %copy-done.6, bf16[96,1024]{1,0:T(8,128)(2,1)} %copy-done.7, bf16[96,1024]{1,0:T(8,128)(2,1)} %copy-done.9, bf16[96,1024]{1,0:T(8,128)(2,1)} %copy-done.11, ...), custom_call_target="tpu_custom_call" | custom-call | flops 2147483648 | bytes 8388608 | tf_op jit(solution)/shard_map/pallas_call | solution.py:295
  47.9 4.8 %shard_map.143 = (f32[2,512]{1,0:T(2,128)S(1)}, bf16[1536,1024]{1,0:T(8,128)(2,1)S(1)}, bf16[16,128]{1,0:T(8,128)(2,1)S(1)}) custom-call(bf16[96,1024]{1,0:T(8,128)(2,1)S(1)} %collective-permute-done.8.refs_0_, bf16[96,1024]{1,0:T(8,128)(2,1)S(1)} %collective-permute-done.12.refs_1_, ...), custom_call_target="tpu_custom_call", output_to_operand_aliasing={{1}: (6, {})} | custom-call | flops 3221225472 | bytes 7864320 | tf_op jit(solution)/shard_map/pallas_call | solution.py:368
  53.2 2.1 %shard_map.144 = bf16[16,128]{1,0:T(8,128)(2,1)S(1)} custom-call(f32[2,512]{1,0:T(2,128)S(1)} %get-tuple-element.48.means_ref, bf16[1536,1024]{1,0:T(8,128)(2,1)S(1)} %get-tuple-element.49.weights, bf16[512,1536]{1,0:T(8,128)(2,1)S(1)} %collective-permute-done.18.tiles_ref), custom_call_target="tpu_custom_call" | custom-call | flops 1610612736 | bytes 4718592 | tf_op jit(solution)/shard_map/pallas_call | solution.py:418
  56.7 2.2 %collective-permute-done.19.pair_ref = bf16[16,128]{1,0:T(8,128)(2,1)S(1)} collective-permute-done((bf16[16,128]{1,0:T(8,128)(2,1)S(1)}, bf16[16,128]{1,0:T(8,128)(2,1)S(1)}, u32[]{:S(2)}, u32[]{:S(2)}) %collective-permute-start.19) | collective-permute-done | bytes 4128 | tf_op jit(solution)/shard_map/ppermute | solution.py:703
  59.2 1.9 %shard_map.145 = (bf16[4,1024]{1,0:T(4,128)(2,1)}, f32[8,768]{1,0:T(8,128)S(1)}, bf16[8,16,256]{2,1,0:T(8,128)(2,1)}) custom-call(s32[8]{0:T(128)S(1)} %copy-done.3, bf16[16,128]{1,0:T(8,128)(2,1)S(1)} %get-tuple-element.47.own_ref, bf16[16,128]{1,0:T(8,128)(2,1)S(1)} %collective-permute-done.17.own_far_ref, ...), custom_call_target="tpu_custom_call" | custom-call | tf_op jit(solution)/shard_map/pallas_call | solution.py:709
  61.0 5.5 %all-to-all-start = ((bf16[8,16,256]{2,1,0:T(8,128)(2,1)}), bf16[8,16,256]{2,1,0:T(8,128)(2,1)S(1)}, u32[]{:S(2)}, u32[]{:S(2)}) async-start(bf16[8,16,256]{2,1,0:T(8,128)(2,1)} %get-tuple-element.51), calls=%async_computation | async-start | bytes 131072 | tf_op jit(solution)/shard_map/all_to_all | solution.py:720
  66.6 2.3 %shard_map.146 = (bf16[96,768]{1,0:T(8,128)(2,1)S(1)}, f32[96,32]{1,0:T(8,128)S(1)}, bf16[768,384]{1,0:T(8,128)(2,1)S(1)}, bf16[768,384]{1,0:T(8,128)(2,1)S(1)},...) custom-call(f32[8,768]{1,0:T(8,128)S(1)} %get-tuple-element.52.mixed, ...), custom_call_target="tpu_custom_call" | custom-call | tf_op jit(solution)/shard_map/pallas_call | solution.py:724
  68.9 4.6 %all-to-all-done.sent_ref = bf16[8,16,256]{2,1,0:T(8,128)(2,1)S(1)} async-done(((bf16[8,16,256]{2,1,0:T(8,128)(2,1)}), bf16[8,16,256]{2,1,0:T(8,128)(2,1)S(1)}, u32[]{:S(2)}, u32[]{:S(2)}) %all-to-all-start) | async-done | bytes 65568 | tf_op jit(solution)/shard_map/all_to_all | solution.py:720
  73.5 2.1 %shard_map.147 = bf16[4,384]{1,0:T(4,128)(2,1)} custom-call(s32[8]{0:T(128)S(1)} %copy-done.3, bf16[8,16,256]{2,1,0:T(8,128)(2,1)S(1)} %all-to-all-done.sent_ref, f32[8,768]{1,0:T(8,128)S(1)} %get-tuple-element.52.mixed_ref, bf16[96,768]{1,0:T(8,128)(2,1)S(1)} %get-tuple-element.54.query_ref, bf16[768,384]{1,0:T(8,128)(2,1)S(1)} %get-tuple-element.55.wk_ref, ...), custom_call_target="tpu_custom_call" | custom-call | tf_op jit(solution)/shard_map/pallas_call | solution.py:739
  (68 shorter events, 8.1 us)
Async XLA Ops:
  5.2 37.1 %copy-start.6 = (bf16[96,1024]{1,0:T(8,128)(2,1)}, bf16[96,1024]{1,0:T(8,128)(2,1)S(1)}, u32[]{:S(2)}) copy-start(bf16[96,1024]{1,0:T(8,128)(2,1)S(1)} %get-tuple-element.32.refs_0_) | copy-start | bytes 589828
  5.2 6.6 %collective-permute-start.5 = (bf16[512,1536]{1,0:T(8,128)(2,1)}, bf16[512,1536]{1,0:T(8,128)(2,1)S(1)}, u32[]{:S(2)}, u32[]{:S(2)}) collective-permute-start(bf16[512,1536]{1,0:T(8,128)(2,1)} %get-tuple-element.42.refs_12_), channel_id=1, source_target_pairs={{0,1},{1,0},{2,3},{3,2},{4,5},{5,4},{6,7},{7,6},{8,9},{9,8},{10,11... | collective-permute-start | bytes 4718600 | tf_op jit(solution)/shard_map/ppermute | solution.py:655
  5.7 6.1 %collective-permute-start.4 = (bf16[1024,768]{1,0:T(8,128)(2,1)S(1)}, bf16[1024,768]{1,0:T(8,128)(2,1)S(1)}, u32[]{:S(2)}, u32[]{:S(2)}) collective-permute-start(bf16[1024,768]{1,0:T(8,128)(2,1)S(1)} %copy-done), channel_id=1, source_target_pairs={{0,1},{1,0},{2,3},{3,2},{4,5},{5,4},{6,7},{7,6},{8,9},{9,8},{10,11... | collective-permute-start | bytes 4718600 | tf_op jit(solution)/shard_map/ppermute | solution.py:657
  5.8 42.0 %collective-permute-start.16 = (bf16[512,1536]{1,0:T(8,128)(2,1)}, bf16[512,1536]{1,0:T(8,128)(2,1)S(1)}, u32[]{:S(2)}, u32[]{:S(2)}) collective-permute-start(bf16[512,1536]{1,0:T(8,128)(2,1)} %get-tuple-element.42.refs_12_), channel_id=1, source_target_pairs={{0,16},{16,0},{1,17},{17,1},{2,18},{18,2},{3,19},{19,3},{4,20},{20... | collective-permute-start | bytes 4718600 | tf_op jit(solution)/shard_map/ppermute | solution.py:656
  8.7 7.0 %collective-permute-start.1 = (bf16[96,1024]{1,0:T(8,128)(2,1)S(1)}, bf16[96,1024]{1,0:T(8,128)(2,1)S(1)}, u32[]{:S(2)}, u32[]{:S(2)}) collective-permute-start(bf16[96,1024]{1,0:T(8,128)(2,1)S(1)} %get-tuple-element.32.refs_0_), channel_id=1, source_target_pairs={{0,2},{2,0},{4,6},{6,4},{8,10},{10,8},{12,14},{14,12},{1,3},{3,1},... | collective-permute-start | bytes 589832 | tf_op jit(solution)/shard_map/ppermute | solution.py:684
  10.2 8.3 %collective-permute-start = (bf16[96,1024]{1,0:T(8,128)(2,1)S(1)}, bf16[96,1024]{1,0:T(8,128)(2,1)S(1)}, u32[]{:S(2)}, u32[]{:S(2)}) collective-permute-start(bf16[96,1024]{1,0:T(8,128)(2,1)S(1)} %get-tuple-element.32.refs_0_), channel_id=1, source_target_pairs={{0,4},{2,6},{4,8},{6,10},{8,12},{10,14},{12,0},{14,2},{1,5},{3,7},... | collective-permute-start | bytes 589832 | tf_op jit(solution)/shard_map/ppermute | solution.py:677
  11.8 7.7 %collective-permute-start.7 = (bf16[96,1024]{1,0:T(8,128)(2,1)S(1)}, bf16[96,1024]{1,0:T(8,128)(2,1)S(1)}, u32[]{:S(2)}, u32[]{:S(2)}) collective-permute-start(bf16[96,1024]{1,0:T(8,128)(2,1)S(1)} %get-tuple-element.36.refs_1_), channel_id=1, source_target_pairs={{0,2},{2,0},{4,6},{6,4},{8,10},{10,8},{12,14},{14,12},{1,3},{3,1},... | collective-permute-start | bytes 589832 | tf_op jit(solution)/shard_map/ppermute | solution.py:684
  13.9 9.6 %collective-permute-start.6 = (bf16[96,1024]{1,0:T(8,128)(2,1)S(1)}, bf16[96,1024]{1,0:T(8,128)(2,1)S(1)}, u32[]{:S(2)}, u32[]{:S(2)}) collective-permute-start(bf16[96,1024]{1,0:T(8,128)(2,1)S(1)} %get-tuple-element.36.refs_1_), channel_id=1, source_target_pairs={{0,4},{2,6},{4,8},{6,10},{8,12},{10,14},{12,0},{14,2},{1,5},{3,7},... | collective-permute-start | bytes 589832 | tf_op jit(solution)/shard_map/ppermute | solution.py:677
  18.6 5.7 %collective-permute-start.3 = (bf16[96,1024]{1,0:T(8,128)(2,1)S(1)}, bf16[96,1024]{1,0:T(8,128)(2,1)S(1)}, u32[]{:S(2)}, u32[]{:S(2)}) collective-permute-start(bf16[96,1024]{1,0:T(8,128)(2,1)S(1)} %collective-permute-done.refs_4_), channel_id=1, source_target_pairs={{0,2},{2,0},{4,6},{6,4},{8,10},{10,8},{12,14},{14,12},{1,3},{3,1},... | collective-permute-start | bytes 589832 | tf_op jit(solution)/shard_map/ppermute | solution.py:684
  19.1 7.8 %collective-permute-start.2 = (bf16[96,1024]{1,0:T(8,128)(2,1)S(1)}, bf16[96,1024]{1,0:T(8,128)(2,1)S(1)}, u32[]{:S(2)}, u32[]{:S(2)}) collective-permute-start(bf16[96,1024]{1,0:T(8,128)(2,1)S(1)} %collective-permute-done.refs_4_), channel_id=1, source_target_pairs={{0,4},{2,6},{4,8},{6,10},{8,12},{10,14},{12,0},{14,2},{1,5},{3,7},... | collective-permute-start | bytes 589832 | tf_op jit(solution)/shard_map/ppermute | solution.py:677
  23.5 7.2 %collective-permute-start.11 = (bf16[96,1024]{1,0:T(8,128)(2,1)S(1)}, bf16[96,1024]{1,0:T(8,128)(2,1)S(1)}, u32[]{:S(2)}, u32[]{:S(2)}) collective-permute-start(bf16[96,1024]{1,0:T(8,128)(2,1)S(1)} %collective-permute-done.6.refs_5_), channel_id=1, source_target_pairs={{0,2},{2,0},{4,6},{6,4},{8,10},{10,8},{12,14},{14,12},{1,3},{3,1},... | collective-permute-start | bytes 589832 | tf_op jit(solution)/shard_map/ppermute | solution.py:684
  23.5 9.2 %collective-permute-start.10 = (bf16[96,1024]{1,0:T(8,128)(2,1)S(1)}, bf16[96,1024]{1,0:T(8,128)(2,1)S(1)}, u32[]{:S(2)}, u32[]{:S(2)}) collective-permute-start(bf16[96,1024]{1,0:T(8,128)(2,1)S(1)} %collective-permute-done.6.refs_5_), channel_id=1, source_target_pairs={{0,4},{2,6},{4,8},{6,10},{8,12},{10,14},{12,0},{14,2},{1,5},{3,7},... | collective-permute-start | bytes 589832 | tf_op jit(solution)/shard_map/ppermute | solution.py:677
  26.8 8.0 %collective-permute-start.9 = (bf16[96,1024]{1,0:T(8,128)(2,1)S(1)}, bf16[96,1024]{1,0:T(8,128)(2,1)S(1)}, u32[]{:S(2)}, u32[]{:S(2)}) collective-permute-start(bf16[96,1024]{1,0:T(8,128)(2,1)S(1)} %collective-permute-done.2.refs_8_), channel_id=1, source_target_pairs={{0,2},{2,0},{4,6},{6,4},{8,10},{10,8},{12,14},{14,12},{1,3},{3,1},... | collective-permute-start | bytes 589832 | tf_op jit(solution)/shard_map/ppermute | solution.py:684
  28.1 9.5 %collective-permute-start.8 = (bf16[96,1024]{1,0:T(8,128)(2,1)S(1)}, bf16[96,1024]{1,0:T(8,128)(2,1)S(1)}, u32[]{:S(2)}, u32[]{:S(2)}) collective-permute-start(bf16[96,1024]{1,0:T(8,128)(2,1)S(1)} %collective-permute-done.2.refs_8_), channel_id=1, source_target_pairs={{0,4},{2,6},{4,8},{6,10},{8,12},{10,14},{12,0},{14,2},{1,5},{3,7},... | collective-permute-start | bytes 589832 | tf_op jit(solution)/shard_map/ppermute | solution.py:677
  32.7 7.5 %collective-permute-start.12 = (bf16[96,1024]{1,0:T(8,128)(2,1)S(1)}, bf16[96,1024]{1,0:T(8,128)(2,1)S(1)}, u32[]{:S(2)}, u32[]{:S(2)}) collective-permute-start(bf16[96,1024]{1,0:T(8,128)(2,1)S(1)} %collective-permute-done.10.refs_9_), channel_id=1, source_target_pairs={{0,4},{2,6},{4,8},{6,10},{8,12},{10,14},{12,0},{14,2},{1,5},{3,7},... | collective-permute-start | bytes 589832 | tf_op jit(solution)/shard_map/ppermute | solution.py:677
  32.7 7.5 %collective-permute-start.13 = (bf16[96,1024]{1,0:T(8,128)(2,1)S(1)}, bf16[96,1024]{1,0:T(8,128)(2,1)S(1)}, u32[]{:S(2)}, u32[]{:S(2)}) collective-permute-start(bf16[96,1024]{1,0:T(8,128)(2,1)S(1)} %collective-permute-done.10.refs_9_), channel_id=1, source_target_pairs={{0,2},{2,0},{4,6},{6,4},{8,10},{10,8},{12,14},{14,12},{1,3},{3,1},... | collective-permute-start | bytes 589832 | tf_op jit(solution)/shard_map/ppermute | solution.py:684
  34.8 31.8 %collective-permute-start.21 = (bf16[2688,384]{1,0:T(8,128)(2,1)S(1)}, bf16[2688,384]{1,0:T(8,128)(2,1)}, u32[]{:S(2)}, u32[]{:S(2)}) collective-permute-start(bf16[2688,384]{1,0:T(8,128)(2,1)S(1)} %get-tuple-element.53), channel_id=1, source_target_pairs={{0,1},{1,0},{2,3},{3,2},{4,5},{5,4},{6,7},{7,6},{8,9},{9,8},{10,11... | collective-permute-start | bytes 6193160 | tf_op jit(solution)/shard_map/ppermute | solution.py:658
  37.6 10.2 %collective-permute-start.14 = (bf16[96,1024]{1,0:T(8,128)(2,1)S(1)}, bf16[96,1024]{1,0:T(8,128)(2,1)S(1)}, u32[]{:S(2)}, u32[]{:S(2)}) collective-permute-start(bf16[96,1024]{1,0:T(8,128)(2,1)S(1)} %collective-permute-done.8.refs_0_), channel_id=1, source_target_pairs={{0,2},{2,0},{4,6},{6,4},{8,10},{10,8},{12,14},{14,12},{1,3},{3,1},... | collective-permute-start | bytes 589832 | tf_op jit(solution)/shard_map/ppermute | solution.py:684
  40.2 7.6 %collective-permute-start.15 = (bf16[96,1024]{1,0:T(8,128)(2,1)S(1)}, bf16[96,1024]{1,0:T(8,128)(2,1)S(1)}, u32[]{:S(2)}, u32[]{:S(2)}) collective-permute-start(bf16[96,1024]{1,0:T(8,128)(2,1)S(1)} %collective-permute-done.12.refs_1_), channel_id=1, source_target_pairs={{0,2},{2,0},{4,6},{6,4},{8,10},{10,8},{12,14},{14,12},{1,3},{3,1},... | collective-permute-start | bytes 589832 | tf_op jit(solution)/shard_map/ppermute | solution.py:684
  47.8 5.4 %collective-permute-start.18 = (bf16[512,1536]{1,0:T(8,128)(2,1)S(1)}, bf16[512,1536]{1,0:T(8,128)(2,1)S(1)}, u32[]{:S(2)}, u32[]{:S(2)}) collective-permute-start(bf16[512,1536]{1,0:T(8,128)(2,1)S(1)} %collective-permute-done.16.refs_4_), channel_id=1, source_target_pairs={{0,1},{1,0},{2,3},{3,2},{4,5},{5,4},{6,7},{7,6},{8,9},{9,8},{10,11... | collective-permute-start | bytes 4718600 | tf_op jit(solution)/shard_map/ppermute | solution.py:693
  52.7 4.1 %collective-permute-start.17 = (bf16[16,128]{1,0:T(8,128)(2,1)S(1)}, bf16[16,128]{1,0:T(8,128)(2,1)S(1)}, u32[]{:S(2)}, u32[]{:S(2)}) collective-permute-start(bf16[16,128]{1,0:T(8,128)(2,1)S(1)} %get-tuple-element.47.own_ref), channel_id=1, source_target_pairs={{0,1},{1,0},{2,3},{3,2},{4,5},{5,4},{6,7},{7,6},{8,9},{9,8},{10,11... | collective-permute-start | bytes 12296 | tf_op jit(solution)/shard_map/ppermute | solution.py:697
  55.2 3.7 %collective-permute-start.19 = (bf16[16,128]{1,0:T(8,128)(2,1)S(1)}, bf16[16,128]{1,0:T(8,128)(2,1)S(1)}, u32[]{:S(2)}, u32[]{:S(2)}) collective-permute-start(bf16[16,128]{1,0:T(8,128)(2,1)S(1)} %shard_map.144), channel_id=1, source_target_pairs={{0,16},{16,0},{1,17},{17,1},{2,18},{18,2},{3,19},{19,3},{4,20},{20... | collective-permute-start | bytes 12296 | tf_op jit(solution)/shard_map/ppermute | solution.py:703
  56.1 3.1 %collective-permute-start.20 = (bf16[16,128]{1,0:T(8,128)(2,1)S(1)}, bf16[16,128]{1,0:T(8,128)(2,1)S(1)}, u32[]{:S(2)}, u32[]{:S(2)}) collective-permute-start(bf16[16,128]{1,0:T(8,128)(2,1)S(1)} %shard_map.144), channel_id=1, source_target_pairs={{0,17},{1,16},{16,1},{17,0},{2,19},{3,18},{18,3},{19,2},{4,21},{5,... | collective-permute-start | bytes 12296 | tf_op jit(solution)/shard_map/ppermute | solution.py:702
  61.0 12.4 %all-to-all-start = ((bf16[8,16,256]{2,1,0:T(8,128)(2,1)}), bf16[8,16,256]{2,1,0:T(8,128)(2,1)S(1)}, u32[]{:S(2)}, u32[]{:S(2)}) async-start(bf16[8,16,256]{2,1,0:T(8,128)(2,1)} %get-tuple-element.51), calls=%async_computation | async-start | bytes 131072 | tf_op jit(solution)/shard_map/all_to_all | solution.py:720
  (18 other events, 349.8 us)

commit v12 on v11

--- a/solution.py
+++ b/solution.py
@@ -198,10 +198,15 @@
         my_z = me // self.ny
         return my_z, me - my_z * self.ny
 
+    def ring(self):
+        return [*range(0, self.nz, 2), *range(self.nz - 1, 0, -2)]
+
     def source(self, step):
         my_z, _ = self.place()
-        z = my_z - step
-        return jnp.where(z < 0, z + self.nz, z)
+        spot = jnp.where(my_z % 2 == 0, my_z // 2, self.nz - (my_z + 1) // 2)
+        spot = spot - step
+        spot = jnp.where(spot < 0, spot + self.nz, spot)
+        return jnp.where(spot < self.nz // 2, 2 * spot, 2 * (self.nz - spot) - 1)
 
     def block_copies(self, blocks, weights, sems, end=None):
         _, my_y = self.place()
@@ -644,10 +649,13 @@
 
     to_pair = [(g, g ^ 1) for g in range(n_grp)]
     to_sibling = [(s, s ^ 1) for s in range(n_sub)]
-    along_z = [(d, (d + ny) % n_dev) for d in range(n_dev)]
     along_y = [(d, d ^ 1) for d in range(n_dev)]
 
     layout = Layout(n_dev, ny, gate_weight.shape[0])
+    ring = layout.ring()
+    along_z = [
+        (z * ny + y, ring[(i + 1) % nz] * ny + y) for i, z in enumerate(ring) for y in range(ny)
+    ]
     slide_weights = [slide_wq, slide_wk, slide_wv, slide_wo]
     first, pack, *held = start_work(
         tiles, tile_gain, gate_weight, up_weight, slide_weights, layout.parts

time: 75.8 us -> 74.5 us (0.983)
  waiting for transfers between devices: 25.4 us -> 15.9 us
  starting transfers between devices: 25.5 us -> 33.2 us
    ppermute x6, starting transfers between devices: 3.45 us -> 17.3 us  [on_device(): arrived = lax.ppermute(held[part], 'dev', along_z)]
    ppermute x6, waiting for transfers between devices: 14.6 us -> 3.93 us  [on_device(): arrived = lax.ppermute(held[part], 'dev', along_z)]
    ppermute x8, starting transfers between devices: 10.9 us -> 6.97 us  [on_device(): sent.append(lax.ppermute(held[part], 'dev', along_y))]
    all_to_all x1, starting transfers between devices: 5.53 us -> 3.35 us  [on_device(): sent = lax.all_to_all(sent, 'dev', split_axis=0, concat_axis=0, tiled=True)]
    ppermute x8, waiting for transfers between devices: 3.76 us -> 4.57 us  [on_device(): sent.append(lax.ppermute(held[part], 'dev', along_y))]
  transfers between devices with their start and end apart: 23 -> 23, of which waited for: 13 -> 10; matrix products, arithmetic and copies ran while one was open for 0% -> 0% of each run, Pallas kernels for 23% -> 23%
where the time goes in v12:
time: 74.5 us; the launch traced here: 74.2 us
  starting transfers between devices  33.2 us (45%)
  Pallas kernels  23.6 us (32%)
  waiting for transfers between devices  15.9 us (21%)
  between operations  0.93 us (1%)
    ppermute x6, starting transfers between devices, on_device(): arrived = lax.ppermute(held[part], 'dev', along_z)  17.3 us
    ppermute x8, starting transfers between devices, on_device(): sent.append(lax.ppermute(held[part], 'dev', along_y))  6.97 us
    pallas_call x1, Pallas kernels, early_mlp(): pl.pallas_call(functools.partial(early_kernel, layout), in_specs=[hbm] *...  5.36 us
    pallas_call x1, Pallas kernels, middle_mlp(): pl.pallas_call(functools.partial(middle_kernel, layout, length, len(block...  4.73 us
    ppermute x8, waiting for transfers between devices, on_device(): sent.append(lax.ppermute(held[part], 'dev', along_y))  4.57 us
    all_to_all x1, waiting for transfers between devices, on_device(): sent = lax.all_to_all(sent, 'dev', split_axis=0, concat_axis=0, tiled=True)  4.53 us
    pallas_call x1, Pallas kernels, start_work(): pl.pallas_call(functools.partial(start_kernel, parts), in_specs=[hbm] * (...  4.48 us
    ppermute x6, waiting for transfers between devices, on_device(): arrived = lax.ppermute(held[part], 'dev', along_z)  3.93 us
  transfers between devices with their start and end apart: 23, of which 10 were waited for; matrix products, arithmetic and copies ran while one was open for 0% of the time, Pallas kernels for 23%

profile of v12, /device:TPU:0, one launch (start us, length us, event | category | flops | bytes accessed | tf_op | source)
XLA Modules:
  0.0 74.2 jit_solution(5769242809767904317)
XLA Ops:
  0.7 4.5 %shard_map.140 = (bf16[512,1536]{1,0:T(8,128)(2,1)}, bf16[2688,384]{1,0:T(8,128)(2,1)S(1)}, bf16[96,1024]{1,0:T(8,128)(2,1)S(1)}, bf16[96,1024]{1,0:T(8,128)(2,1)S(1)}) custom-call(bf16[4,256,1536]{2,1,0:T(8,128)(2,1)} %refs_0_.2, f32[1536]{0:T(1024)} %refs_1_.2, bf16[192,1024]{1,0:T(8,128)(2,1)} %refs_2_.2, bf16[192,1024]{1,0:T(8,128)(2,1)} %refs_3_.2, ...), custom_call_target="tpu_custom_call" | custom-call | tf_op jit(solution)/shard_map/pallas_call | solution.py:153
  5.8 2.9 %collective-permute-start.16 = (bf16[512,1536]{1,0:T(8,128)(2,1)}, bf16[512,1536]{1,0:T(8,128)(2,1)S(1)}, u32[]{:S(2)}, u32[]{:S(2)}) collective-permute-start(bf16[512,1536]{1,0:T(8,128)(2,1)} %get-tuple-element.42.refs_12_), channel_id=1, source_target_pairs={{0,16},{16,0},{1,17},{17,1},{2,18},{18,2},{3,19},{19,3},{4,20},{20... | collective-permute-start | bytes 4718600 | tf_op jit(solution)/shard_map/ppermute | solution.py:664
  8.7 1.5 %collective-permute-start.1 = (bf16[96,1024]{1,0:T(8,128)(2,1)S(1)}, bf16[96,1024]{1,0:T(8,128)(2,1)S(1)}, u32[]{:S(2)}, u32[]{:S(2)}) collective-permute-start(bf16[96,1024]{1,0:T(8,128)(2,1)S(1)} %get-tuple-element.32.refs_0_), channel_id=1, source_target_pairs={{0,2},{2,0},{4,6},{6,4},{8,10},{10,8},{12,14},{14,12},{1,3},{3,1},... | collective-permute-start | bytes 589832 | tf_op jit(solution)/shard_map/ppermute | solution.py:692
  10.2 2.6 %collective-permute-start = (bf16[96,1024]{1,0:T(8,128)(2,1)S(1)}, bf16[96,1024]{1,0:T(8,128)(2,1)S(1)}, u32[]{:S(2)}, u32[]{:S(2)}) collective-permute-start(bf16[96,1024]{1,0:T(8,128)(2,1)S(1)} %get-tuple-element.32.refs_0_), channel_id=1, source_target_pairs={{0,8},{2,10},{8,12},{10,14},{12,4},{14,6},{4,0},{6,2},{1,9},{3,11}... | collective-permute-start | bytes 589832 | tf_op jit(solution)/shard_map/ppermute | solution.py:685
  12.8 1.1 %collective-permute-start.7 = (bf16[96,1024]{1,0:T(8,128)(2,1)S(1)}, bf16[96,1024]{1,0:T(8,128)(2,1)S(1)}, u32[]{:S(2)}, u32[]{:S(2)}) collective-permute-start(bf16[96,1024]{1,0:T(8,128)(2,1)S(1)} %get-tuple-element.36.refs_1_), channel_id=1, source_target_pairs={{0,2},{2,0},{4,6},{6,4},{8,10},{10,8},{12,14},{14,12},{1,3},{3,1},... | collective-permute-start | bytes 589832 | tf_op jit(solution)/shard_map/ppermute | solution.py:692
  13.9 2.6 %collective-permute-start.6 = (bf16[96,1024]{1,0:T(8,128)(2,1)S(1)}, bf16[96,1024]{1,0:T(8,128)(2,1)S(1)}, u32[]{:S(2)}, u32[]{:S(2)}) collective-permute-start(bf16[96,1024]{1,0:T(8,128)(2,1)S(1)} %get-tuple-element.36.refs_1_), channel_id=1, source_target_pairs={{0,8},{2,10},{8,12},{10,14},{12,4},{14,6},{4,0},{6,2},{1,9},{3,11}... | collective-permute-start | bytes 589832 | tf_op jit(solution)/shard_map/ppermute | solution.py:685
  17.4 3.3 %collective-permute-start.2 = (bf16[96,1024]{1,0:T(8,128)(2,1)S(1)}, bf16[96,1024]{1,0:T(8,128)(2,1)S(1)}, u32[]{:S(2)}, u32[]{:S(2)}) collective-permute-start(bf16[96,1024]{1,0:T(8,128)(2,1)S(1)} %collective-permute-done.refs_4_), channel_id=1, source_target_pairs={{0,8},{2,10},{8,12},{10,14},{12,4},{14,6},{4,0},{6,2},{1,9},{3,11}... | collective-permute-start | bytes 589832 | tf_op jit(solution)/shard_map/ppermute | solution.py:685
  22.3 3.2 %collective-permute-start.10 = (bf16[96,1024]{1,0:T(8,128)(2,1)S(1)}, bf16[96,1024]{1,0:T(8,128)(2,1)S(1)}, u32[]{:S(2)}, u32[]{:S(2)}) collective-permute-start(bf16[96,1024]{1,0:T(8,128)(2,1)S(1)} %collective-permute-done.6.refs_5_), channel_id=1, source_target_pairs={{0,8},{2,10},{8,12},{10,14},{12,4},{14,6},{4,0},{6,2},{1,9},{3,11}... | collective-permute-start | bytes 589832 | tf_op jit(solution)/shard_map/ppermute | solution.py:685
  26.1 1.2 %collective-permute-start.9 = (bf16[96,1024]{1,0:T(8,128)(2,1)S(1)}, bf16[96,1024]{1,0:T(8,128)(2,1)S(1)}, u32[]{:S(2)}, u32[]{:S(2)}) collective-permute-start(bf16[96,1024]{1,0:T(8,128)(2,1)S(1)} %collective-permute-done.2.refs_8_), channel_id=1, source_target_pairs={{0,2},{2,0},{4,6},{6,4},{8,10},{10,8},{12,14},{14,12},{1,3},{3,1},... | collective-permute-start | bytes 589832 | tf_op jit(solution)/shard_map/ppermute | solution.py:692
  27.3 2.2 %collective-permute-start.8 = (bf16[96,1024]{1,0:T(8,128)(2,1)S(1)}, bf16[96,1024]{1,0:T(8,128)(2,1)S(1)}, u32[]{:S(2)}, u32[]{:S(2)}) collective-permute-start(bf16[96,1024]{1,0:T(8,128)(2,1)S(1)} %collective-permute-done.2.refs_8_), channel_id=1, source_target_pairs={{0,8},{2,10},{8,12},{10,14},{12,4},{14,6},{4,0},{6,2},{1,9},{3,11}... | collective-permute-start | bytes 589832 | tf_op jit(solution)/shard_map/ppermute | solution.py:685
  29.5 1.4 %collective-permute-done.10.refs_9_ = bf16[96,1024]{1,0:T(8,128)(2,1)S(1)} collective-permute-done((bf16[96,1024]{1,0:T(8,128)(2,1)S(1)}, bf16[96,1024]{1,0:T(8,128)(2,1)S(1)}, u32[]{:S(2)}, u32[]{:S(2)}) %collective-permute-start.10) | collective-permute-done | bytes 196640 | tf_op jit(solution)/shard_map/ppermute | solution.py:685
  30.9 3.4 %collective-permute-start.12 = (bf16[96,1024]{1,0:T(8,128)(2,1)S(1)}, bf16[96,1024]{1,0:T(8,128)(2,1)S(1)}, u32[]{:S(2)}, u32[]{:S(2)}) collective-permute-start(bf16[96,1024]{1,0:T(8,128)(2,1)S(1)} %collective-permute-done.10.refs_9_), channel_id=1, source_target_pairs={{0,8},{2,10},{8,12},{10,14},{12,4},{14,6},{4,0},{6,2},{1,9},{3,11}... | collective-permute-start | bytes 589832 | tf_op jit(solution)/shard_map/ppermute | solution.py:685
  35.4 1.7 %collective-permute-start.14 = (bf16[96,1024]{1,0:T(8,128)(2,1)S(1)}, bf16[96,1024]{1,0:T(8,128)(2,1)S(1)}, u32[]{:S(2)}, u32[]{:S(2)}) collective-permute-start(bf16[96,1024]{1,0:T(8,128)(2,1)S(1)} %collective-permute-done.8.refs_0_), channel_id=1, source_target_pairs={{0,2},{2,0},{4,6},{6,4},{8,10},{10,8},{12,14},{14,12},{1,3},{3,1},... | collective-permute-start | bytes 589832 | tf_op jit(solution)/shard_map/ppermute | solution.py:692
  37.7 3.7 %collective-permute-done.13.refs_11_ = bf16[96,1024]{1,0:T(8,128)(2,1)S(1)} collective-permute-done((bf16[96,1024]{1,0:T(8,128)(2,1)S(1)}, bf16[96,1024]{1,0:T(8,128)(2,1)S(1)}, u32[]{:S(2)}, u32[]{:S(2)}) %collective-permute-start.13) | collective-permute-done | bytes 196640 | tf_op jit(solution)/shard_map/ppermute | solution.py:692
  42.1 5.4 %shard_map.142 = (f32[2,512,1024]{2,1,0:T(8,128)S(1)}, bf16[1536,1024]{1,0:T(8,128)(2,1)S(1)}, bf16[2,512,1536]{2,1,0:T(8,128)(2,1)S(1)}) custom-call(bf16[96,1024]{1,0:T(8,128)(2,1)} %copy-done.6, bf16[96,1024]{1,0:T(8,128)(2,1)} %copy-done.7, bf16[96,1024]{1,0:T(8,128)(2,1)} %copy-done.9, bf16[96,1024]{1,0:T(8,128)(2,1)} %copy-done.11, ...), custom_call_target="tpu_custom_call" | custom-call | flops 2147483648 | bytes 8388608 | tf_op jit(solution)/shard_map/pallas_call | solution.py:300
  48.4 4.7 %shard_map.143 = (f32[2,512]{1,0:T(2,128)S(1)}, bf16[1536,1024]{1,0:T(8,128)(2,1)S(1)}, bf16[16,128]{1,0:T(8,128)(2,1)S(1)}) custom-call(bf16[96,1024]{1,0:T(8,128)(2,1)S(1)} %collective-permute-done.8.refs_0_, bf16[96,1024]{1,0:T(8,128)(2,1)S(1)} %collective-permute-done.12.refs_1_, ...), custom_call_target="tpu_custom_call", output_to_operand_aliasing={{1}: (6, {})} | custom-call | flops 3221225472 | bytes 7864320 | tf_op jit(solution)/shard_map/pallas_call | solution.py:373
  53.7 2.1 %shard_map.144 = bf16[16,128]{1,0:T(8,128)(2,1)S(1)} custom-call(f32[2,512]{1,0:T(2,128)S(1)} %get-tuple-element.48.means_ref, bf16[1536,1024]{1,0:T(8,128)(2,1)S(1)} %get-tuple-element.49.weights, bf16[512,1536]{1,0:T(8,128)(2,1)S(1)} %collective-permute-done.18.tiles_ref), custom_call_target="tpu_custom_call" | custom-call | flops 1610612736 | bytes 4718592 | tf_op jit(solution)/shard_map/pallas_call | solution.py:423
  55.7 1.3 %collective-permute-start.19 = (bf16[16,128]{1,0:T(8,128)(2,1)S(1)}, bf16[16,128]{1,0:T(8,128)(2,1)S(1)}, u32[]{:S(2)}, u32[]{:S(2)}) collective-permute-start(bf16[16,128]{1,0:T(8,128)(2,1)S(1)} %shard_map.144), channel_id=1, source_target_pairs={{0,16},{16,0},{1,17},{17,1},{2,18},{18,2},{3,19},{19,3},{4,20},{20... | collective-permute-start | bytes 12296 | tf_op jit(solution)/shard_map/ppermute | solution.py:711
  57.2 2.2 %collective-permute-done.19.pair_ref = bf16[16,128]{1,0:T(8,128)(2,1)S(1)} collective-permute-done((bf16[16,128]{1,0:T(8,128)(2,1)S(1)}, bf16[16,128]{1,0:T(8,128)(2,1)S(1)}, u32[]{:S(2)}, u32[]{:S(2)}) %collective-permute-start.19) | collective-permute-done | bytes 4128 | tf_op jit(solution)/shard_map/ppermute | solution.py:711
  60.1 1.9 %shard_map.145 = (bf16[4,1024]{1,0:T(4,128)(2,1)}, f32[8,768]{1,0:T(8,128)S(1)}, bf16[8,16,256]{2,1,0:T(8,128)(2,1)}) custom-call(s32[8]{0:T(128)S(1)} %copy-done.3, bf16[16,128]{1,0:T(8,128)(2,1)S(1)} %get-tuple-element.47.own_ref, bf16[16,128]{1,0:T(8,128)(2,1)S(1)} %collective-permute-done.17.own_far_ref, ...), custom_call_target="tpu_custom_call" | custom-call | tf_op jit(solution)/shard_map/pallas_call | solution.py:717
  61.9 3.3 %all-to-all-start = ((bf16[8,16,256]{2,1,0:T(8,128)(2,1)}), bf16[8,16,256]{2,1,0:T(8,128)(2,1)S(1)}, u32[]{:S(2)}, u32[]{:S(2)}) async-start(bf16[8,16,256]{2,1,0:T(8,128)(2,1)} %get-tuple-element.51), calls=%async_computation | async-start | bytes 131072 | tf_op jit(solution)/shard_map/all_to_all | solution.py:728
  65.3 2.3 %shard_map.146 = (bf16[96,768]{1,0:T(8,128)(2,1)S(1)}, f32[96,32]{1,0:T(8,128)S(1)}, bf16[768,384]{1,0:T(8,128)(2,1)S(1)}, bf16[768,384]{1,0:T(8,128)(2,1)S(1)},...) custom-call(f32[8,768]{1,0:T(8,128)S(1)} %get-tuple-element.52.mixed, ...), custom_call_target="tpu_custom_call" | custom-call | tf_op jit(solution)/shard_map/pallas_call | solution.py:732
  67.6 4.5 %all-to-all-done.sent_ref = bf16[8,16,256]{2,1,0:T(8,128)(2,1)S(1)} async-done(((bf16[8,16,256]{2,1,0:T(8,128)(2,1)}), bf16[8,16,256]{2,1,0:T(8,128)(2,1)S(1)}, u32[]{:S(2)}, u32[]{:S(2)}) %all-to-all-start) | async-done | bytes 65568 | tf_op jit(solution)/shard_map/all_to_all | solution.py:728
  72.1 2.1 %shard_map.147 = bf16[4,384]{1,0:T(4,128)(2,1)} custom-call(s32[8]{0:T(128)S(1)} %copy-done.3, bf16[8,16,256]{2,1,0:T(8,128)(2,1)S(1)} %all-to-all-done.sent_ref, f32[8,768]{1,0:T(8,128)S(1)} %get-tuple-element.52.mixed_ref, bf16[96,768]{1,0:T(8,128)(2,1)S(1)} %get-tuple-element.54.query_ref, bf16[768,384]{1,0:T(8,128)(2,1)S(1)} %get-tuple-element.55.wk_ref, ...), custom_call_target="tpu_custom_call" | custom-call | tf_op jit(solution)/shard_map/pallas_call | solution.py:747
  (68 shorter events, 8.3 us)
Async XLA Ops:
  5.2 36.2 %copy-start.6 = (bf16[96,1024]{1,0:T(8,128)(2,1)}, bf16[96,1024]{1,0:T(8,128)(2,1)S(1)}, u32[]{:S(2)}) copy-start(bf16[96,1024]{1,0:T(8,128)(2,1)S(1)} %get-tuple-element.32.refs_0_) | copy-start | bytes 589828
  5.2 7.6 %collective-permute-start.5 = (bf16[512,1536]{1,0:T(8,128)(2,1)}, bf16[512,1536]{1,0:T(8,128)(2,1)S(1)}, u32[]{:S(2)}, u32[]{:S(2)}) collective-permute-start(bf16[512,1536]{1,0:T(8,128)(2,1)} %get-tuple-element.42.refs_12_), channel_id=1, source_target_pairs={{0,1},{1,0},{2,3},{3,2},{4,5},{5,4},{6,7},{7,6},{8,9},{9,8},{10,11... | collective-permute-start | bytes 4718600 | tf_op jit(solution)/shard_map/ppermute | solution.py:663
  5.7 7.1 %collective-permute-start.4 = (bf16[1024,768]{1,0:T(8,128)(2,1)S(1)}, bf16[1024,768]{1,0:T(8,128)(2,1)S(1)}, u32[]{:S(2)}, u32[]{:S(2)}) collective-permute-start(bf16[1024,768]{1,0:T(8,128)(2,1)S(1)} %copy-done), channel_id=1, source_target_pairs={{0,1},{1,0},{2,3},{3,2},{4,5},{5,4},{6,7},{7,6},{8,9},{9,8},{10,11... | collective-permute-start | bytes 4718600 | tf_op jit(solution)/shard_map/ppermute | solution.py:665
  5.8 41.7 %collective-permute-start.16 = (bf16[512,1536]{1,0:T(8,128)(2,1)}, bf16[512,1536]{1,0:T(8,128)(2,1)S(1)}, u32[]{:S(2)}, u32[]{:S(2)}) collective-permute-start(bf16[512,1536]{1,0:T(8,128)(2,1)} %get-tuple-element.42.refs_12_), channel_id=1, source_target_pairs={{0,16},{16,0},{1,17},{17,1},{2,18},{18,2},{3,19},{19,3},{4,20},{20... | collective-permute-start | bytes 4718600 | tf_op jit(solution)/shard_map/ppermute | solution.py:664
  8.7 7.8 %collective-permute-start.1 = (bf16[96,1024]{1,0:T(8,128)(2,1)S(1)}, bf16[96,1024]{1,0:T(8,128)(2,1)S(1)}, u32[]{:S(2)}, u32[]{:S(2)}) collective-permute-start(bf16[96,1024]{1,0:T(8,128)(2,1)S(1)} %get-tuple-element.32.refs_0_), channel_id=1, source_target_pairs={{0,2},{2,0},{4,6},{6,4},{8,10},{10,8},{12,14},{14,12},{1,3},{3,1},... | collective-permute-start | bytes 589832 | tf_op jit(solution)/shard_map/ppermute | solution.py:692
  10.2 6.6 %collective-permute-start = (bf16[96,1024]{1,0:T(8,128)(2,1)S(1)}, bf16[96,1024]{1,0:T(8,128)(2,1)S(1)}, u32[]{:S(2)}, u32[]{:S(2)}) collective-permute-start(bf16[96,1024]{1,0:T(8,128)(2,1)S(1)} %get-tuple-element.32.refs_0_), channel_id=1, source_target_pairs={{0,8},{2,10},{8,12},{10,14},{12,4},{14,6},{4,0},{6,2},{1,9},{3,11}... | collective-permute-start | bytes 589832 | tf_op jit(solution)/shard_map/ppermute | solution.py:685
  12.8 7.9 %collective-permute-start.7 = (bf16[96,1024]{1,0:T(8,128)(2,1)S(1)}, bf16[96,1024]{1,0:T(8,128)(2,1)S(1)}, u32[]{:S(2)}, u32[]{:S(2)}) collective-permute-start(bf16[96,1024]{1,0:T(8,128)(2,1)S(1)} %get-tuple-element.36.refs_1_), channel_id=1, source_target_pairs={{0,2},{2,0},{4,6},{6,4},{8,10},{10,8},{12,14},{14,12},{1,3},{3,1},... | collective-permute-start | bytes 589832 | tf_op jit(solution)/shard_map/ppermute | solution.py:692
  13.9 7.9 %collective-permute-start.6 = (bf16[96,1024]{1,0:T(8,128)(2,1)S(1)}, bf16[96,1024]{1,0:T(8,128)(2,1)S(1)}, u32[]{:S(2)}, u32[]{:S(2)}) collective-permute-start(bf16[96,1024]{1,0:T(8,128)(2,1)S(1)} %get-tuple-element.36.refs_1_), channel_id=1, source_target_pairs={{0,8},{2,10},{8,12},{10,14},{12,4},{14,6},{4,0},{6,2},{1,9},{3,11}... | collective-permute-start | bytes 589832 | tf_op jit(solution)/shard_map/ppermute | solution.py:685
  16.8 8.7 %collective-permute-start.3 = (bf16[96,1024]{1,0:T(8,128)(2,1)S(1)}, bf16[96,1024]{1,0:T(8,128)(2,1)S(1)}, u32[]{:S(2)}, u32[]{:S(2)}) collective-permute-start(bf16[96,1024]{1,0:T(8,128)(2,1)S(1)} %collective-permute-done.refs_4_), channel_id=1, source_target_pairs={{0,2},{2,0},{4,6},{6,4},{8,10},{10,8},{12,14},{14,12},{1,3},{3,1},... | collective-permute-start | bytes 589832 | tf_op jit(solution)/shard_map/ppermute | solution.py:692
  17.4 8.7 %collective-permute-start.2 = (bf16[96,1024]{1,0:T(8,128)(2,1)S(1)}, bf16[96,1024]{1,0:T(8,128)(2,1)S(1)}, u32[]{:S(2)}, u32[]{:S(2)}) collective-permute-start(bf16[96,1024]{1,0:T(8,128)(2,1)S(1)} %collective-permute-done.refs_4_), channel_id=1, source_target_pairs={{0,8},{2,10},{8,12},{10,14},{12,4},{14,6},{4,0},{6,2},{1,9},{3,11}... | collective-permute-start | bytes 589832 | tf_op jit(solution)/shard_map/ppermute | solution.py:685
  21.8 7.7 %collective-permute-start.11 = (bf16[96,1024]{1,0:T(8,128)(2,1)S(1)}, bf16[96,1024]{1,0:T(8,128)(2,1)S(1)}, u32[]{:S(2)}, u32[]{:S(2)}) collective-permute-start(bf16[96,1024]{1,0:T(8,128)(2,1)S(1)} %collective-permute-done.6.refs_5_), channel_id=1, source_target_pairs={{0,2},{2,0},{4,6},{6,4},{8,10},{10,8},{12,14},{14,12},{1,3},{3,1},... | collective-permute-start | bytes 589832 | tf_op jit(solution)/shard_map/ppermute | solution.py:692
  22.3 8.6 %collective-permute-start.10 = (bf16[96,1024]{1,0:T(8,128)(2,1)S(1)}, bf16[96,1024]{1,0:T(8,128)(2,1)S(1)}, u32[]{:S(2)}, u32[]{:S(2)}) collective-permute-start(bf16[96,1024]{1,0:T(8,128)(2,1)S(1)} %collective-permute-done.6.refs_5_), channel_id=1, source_target_pairs={{0,8},{2,10},{8,12},{10,14},{12,4},{14,6},{4,0},{6,2},{1,9},{3,11}... | collective-permute-start | bytes 589832 | tf_op jit(solution)/shard_map/ppermute | solution.py:685
  26.1 8.6 %collective-permute-start.9 = (bf16[96,1024]{1,0:T(8,128)(2,1)S(1)}, bf16[96,1024]{1,0:T(8,128)(2,1)S(1)}, u32[]{:S(2)}, u32[]{:S(2)}) collective-permute-start(bf16[96,1024]{1,0:T(8,128)(2,1)S(1)} %collective-permute-done.2.refs_8_), channel_id=1, source_target_pairs={{0,2},{2,0},{4,6},{6,4},{8,10},{10,8},{12,14},{14,12},{1,3},{3,1},... | collective-permute-start | bytes 589832 | tf_op jit(solution)/shard_map/ppermute | solution.py:692
  27.3 8.1 %collective-permute-start.8 = (bf16[96,1024]{1,0:T(8,128)(2,1)S(1)}, bf16[96,1024]{1,0:T(8,128)(2,1)S(1)}, u32[]{:S(2)}, u32[]{:S(2)}) collective-permute-start(bf16[96,1024]{1,0:T(8,128)(2,1)S(1)} %collective-permute-done.2.refs_8_), channel_id=1, source_target_pairs={{0,8},{2,10},{8,12},{10,14},{12,4},{14,6},{4,0},{6,2},{1,9},{3,11}... | collective-permute-start | bytes 589832 | tf_op jit(solution)/shard_map/ppermute | solution.py:685
  30.9 6.8 %collective-permute-start.12 = (bf16[96,1024]{1,0:T(8,128)(2,1)S(1)}, bf16[96,1024]{1,0:T(8,128)(2,1)S(1)}, u32[]{:S(2)}, u32[]{:S(2)}) collective-permute-start(bf16[96,1024]{1,0:T(8,128)(2,1)S(1)} %collective-permute-done.10.refs_9_), channel_id=1, source_target_pairs={{0,8},{2,10},{8,12},{10,14},{12,4},{14,6},{4,0},{6,2},{1,9},{3,11}... | collective-permute-start | bytes 589832 | tf_op jit(solution)/shard_map/ppermute | solution.py:685
  34.3 7.1 %collective-permute-start.13 = (bf16[96,1024]{1,0:T(8,128)(2,1)S(1)}, bf16[96,1024]{1,0:T(8,128)(2,1)S(1)}, u32[]{:S(2)}, u32[]{:S(2)}) collective-permute-start(bf16[96,1024]{1,0:T(8,128)(2,1)S(1)} %collective-permute-done.10.refs_9_), channel_id=1, source_target_pairs={{0,2},{2,0},{4,6},{6,4},{8,10},{10,8},{12,14},{14,12},{1,3},{3,1},... | collective-permute-start | bytes 589832 | tf_op jit(solution)/shard_map/ppermute | solution.py:692
  34.6 30.6 %collective-permute-start.21 = (bf16[2688,384]{1,0:T(8,128)(2,1)S(1)}, bf16[2688,384]{1,0:T(8,128)(2,1)}, u32[]{:S(2)}, u32[]{:S(2)}) collective-permute-start(bf16[2688,384]{1,0:T(8,128)(2,1)S(1)} %get-tuple-element.53), channel_id=1, source_target_pairs={{0,1},{1,0},{2,3},{3,2},{4,5},{5,4},{6,7},{7,6},{8,9},{9,8},{10,11... | collective-permute-start | bytes 6193160 | tf_op jit(solution)/shard_map/ppermute | solution.py:666
  35.4 12.1 %collective-permute-start.14 = (bf16[96,1024]{1,0:T(8,128)(2,1)S(1)}, bf16[96,1024]{1,0:T(8,128)(2,1)S(1)}, u32[]{:S(2)}, u32[]{:S(2)}) collective-permute-start(bf16[96,1024]{1,0:T(8,128)(2,1)S(1)} %collective-permute-done.8.refs_0_), channel_id=1, source_target_pairs={{0,2},{2,0},{4,6},{6,4},{8,10},{10,8},{12,14},{14,12},{1,3},{3,1},... | collective-permute-start | bytes 589832 | tf_op jit(solution)/shard_map/ppermute | solution.py:692
  41.4 7.0 %collective-permute-start.15 = (bf16[96,1024]{1,0:T(8,128)(2,1)S(1)}, bf16[96,1024]{1,0:T(8,128)(2,1)S(1)}, u32[]{:S(2)}, u32[]{:S(2)}) collective-permute-start(bf16[96,1024]{1,0:T(8,128)(2,1)S(1)} %collective-permute-done.12.refs_1_), channel_id=1, source_target_pairs={{0,2},{2,0},{4,6},{6,4},{8,10},{10,8},{12,14},{14,12},{1,3},{3,1},... | collective-permute-start | bytes 589832 | tf_op jit(solution)/shard_map/ppermute | solution.py:692
  48.4 5.3 %collective-permute-start.18 = (bf16[512,1536]{1,0:T(8,128)(2,1)S(1)}, bf16[512,1536]{1,0:T(8,128)(2,1)S(1)}, u32[]{:S(2)}, u32[]{:S(2)}) collective-permute-start(bf16[512,1536]{1,0:T(8,128)(2,1)S(1)} %collective-permute-done.16.refs_4_), channel_id=1, source_target_pairs={{0,1},{1,0},{2,3},{3,2},{4,5},{5,4},{6,7},{7,6},{8,9},{9,8},{10,11... | collective-permute-start | bytes 4718600 | tf_op jit(solution)/shard_map/ppermute | solution.py:701
  53.1 4.1 %collective-permute-start.17 = (bf16[16,128]{1,0:T(8,128)(2,1)S(1)}, bf16[16,128]{1,0:T(8,128)(2,1)S(1)}, u32[]{:S(2)}, u32[]{:S(2)}) collective-permute-start(bf16[16,128]{1,0:T(8,128)(2,1)S(1)} %get-tuple-element.47.own_ref), channel_id=1, source_target_pairs={{0,1},{1,0},{2,3},{3,2},{4,5},{5,4},{6,7},{7,6},{8,9},{9,8},{10,11... | collective-permute-start | bytes 12296 | tf_op jit(solution)/shard_map/ppermute | solution.py:705
  55.7 3.7 %collective-permute-start.19 = (bf16[16,128]{1,0:T(8,128)(2,1)S(1)}, bf16[16,128]{1,0:T(8,128)(2,1)S(1)}, u32[]{:S(2)}, u32[]{:S(2)}) collective-permute-start(bf16[16,128]{1,0:T(8,128)(2,1)S(1)} %shard_map.144), channel_id=1, source_target_pairs={{0,16},{16,0},{1,17},{17,1},{2,18},{18,2},{3,19},{19,3},{4,20},{20... | collective-permute-start | bytes 12296 | tf_op jit(solution)/shard_map/ppermute | solution.py:711
  57.0 3.1 %collective-permute-start.20 = (bf16[16,128]{1,0:T(8,128)(2,1)S(1)}, bf16[16,128]{1,0:T(8,128)(2,1)S(1)}, u32[]{:S(2)}, u32[]{:S(2)}) collective-permute-start(bf16[16,128]{1,0:T(8,128)(2,1)S(1)} %shard_map.144), channel_id=1, source_target_pairs={{0,17},{1,16},{16,1},{17,0},{2,19},{3,18},{18,3},{19,2},{4,21},{5,... | collective-permute-start | bytes 12296 | tf_op jit(solution)/shard_map/ppermute | solution.py:710
  61.9 10.2 %all-to-all-start = ((bf16[8,16,256]{2,1,0:T(8,128)(2,1)}), bf16[8,16,256]{2,1,0:T(8,128)(2,1)S(1)}, u32[]{:S(2)}, u32[]{:S(2)}) async-start(bf16[8,16,256]{2,1,0:T(8,128)(2,1)} %get-tuple-element.51), calls=%async_computation | async-start | bytes 131072 | tf_op jit(solution)/shard_map/all_to_all | solution.py:728
  (18 other events, 341.7 us)

commit v13 on v12

--- a/solution.py
+++ b/solution.py
@@ -44,14 +44,12 @@
     out_ref, pack_ref, *block_refs = refs[8 : 10 + len(parts)]
     (
         rows,
-        hidden,
         gain,
         average,
         scale,
         whole,
         whole_slide,
         in_sems,
-        out_sems,
         block_sems,
         slide_sems,
         gain_sem,
@@ -67,10 +65,6 @@
             rows.at[i],
             in_sems.at[i],
         )
-        for i in range(pieces)
-    ]
-    stores = [
-        pltpu.make_async_copy(hidden.at[i], out_ref.at[pl.ds(i * piece, piece)], out_sems.at[i])
         for i in range(pieces)
     ]
     packs = [
@@ -128,18 +122,16 @@
 
         def norm_rows(here):
             centred = rows[i, here, :].astype(jnp.float32) - average[here, :1]
-            hidden[i, here, :] = (centred * scale[here, :1] * gains).astype(jnp.bfloat16)
+            place = pl.ds(pl.multiple_of(here.start + i * piece, NORM_ROWS), NORM_ROWS)
+            out_ref[place, :] = (centred * scale[here, :1] * gains).astype(jnp.bfloat16)
 
         grouped(sum_rows)
         grouped(scale_rows)
         grouped(norm_rows)
-        stores[i].start()
     for copy in packs:
         copy.wait()
     for place, at, source in selects:
         place[:, at : at + source.shape[1]] = source[...]
-    for copy in stores:
-        copy.wait()
 
 
 def start_work(tiles, gain, gate_weight, up_weight, slide_weights, parts):
@@ -153,21 +145,19 @@
     return pl.pallas_call(
         functools.partial(start_kernel, parts),
         in_specs=[hbm] * (4 + len(slide_weights)),
-        out_specs=[hbm] + [vmem] * (1 + len(parts)),
+        out_specs=[vmem] * (2 + len(parts)),
         out_shape=[
-            pltpu.HBM((half * length, width), jnp.bfloat16),
+            pltpu.VMEM((half * length, width), jnp.bfloat16),
             pltpu.VMEM(pack, jnp.bfloat16),
             *[pltpu.VMEM((part.stop - part.start, cols), jnp.bfloat16) for part in parts],
         ],
         scratch_shapes=[
-            pltpu.VMEM((pieces, NORM_PIECE, width), jnp.bfloat16),
             pltpu.VMEM((pieces, NORM_PIECE, width), jnp.bfloat16),
             pltpu.VMEM((width,), jnp.float32),
             pltpu.VMEM((NORM_PIECE, LANES), jnp.float32),
             pltpu.VMEM((NORM_PIECE, LANES), jnp.float32),
             pltpu.VMEM((2, *gate_weight.shape), jnp.bfloat16),
             pltpu.VMEM(slide_weights[-1].shape, jnp.bfloat16),
-            pltpu.SemaphoreType.DMA((pieces,)),
             pltpu.SemaphoreType.DMA((pieces,)),
             pltpu.SemaphoreType.DMA((2,)),
             pltpu.SemaphoreType.DMA((len(slide_weights),)),
@@ -244,10 +234,9 @@
     for tile in range(both.shape[0] // length):
         total = jnp.zeros((8, cols), jnp.float32)
         for first in range(tile * length, (tile + 1) * length, UNIT_ROWS):
-            gate = both[first : first + UNIT_ROWS, :cols]
+            half_gate = 0.5 * both[first : first + UNIT_ROWS, :cols]
             up_part = both[first : first + UNIT_ROWS, cols:]
-            silu = gate * (0.5 * jnp.tanh(0.5 * gate) + 0.5)
-            gated = (silu * up_part).astype(jnp.bfloat16).astype(jnp.float32)
+            gated = (half_gate * jnp.tanh(half_gate) + half_gate) * up_part
             total = total + jnp.sum(gated.reshape(UNIT_ROWS // 8, 8, cols), axis=0)
         out_ref[at + tile : at + tile + 1, :] = jnp.sum(total, axis=0, keepdims=True) * (
             1.0 / length
@@ -299,7 +288,7 @@
     vmem = pl.BlockSpec(memory_space=pltpu.VMEM)
     return pl.pallas_call(
         functools.partial(early_kernel, layout),
-        in_specs=[hbm] * (len(blocks) + 2),
+        in_specs=[hbm] * len(blocks) + [pl.BlockSpec(memory_space=pl.ANY)] * 2,
         out_specs=(vmem, vmem, vmem),
         out_shape=(
             pltpu.VMEM((2, n_rows, cols), jnp.float32),
@@ -316,7 +305,7 @@
             bytes_accessed=2 * layout.early * (cols + 2 * n_rows) + 8 * n_rows * cols,
             transcendentals=0,
         ),
-    )(*in_hbm(*blocks, *tiles))
+    )(*in_hbm(*blocks), *tiles)
 
 
 def packed(mine, others):

time: 74.5 us -> 73.8 us (level)
  Pallas kernels: 23.6 us -> 22 us
  waiting for transfers between devices: 15.9 us -> 16.7 us
    pallas_call x1, Pallas kernels: 5.36 us -> 4.51 us  [early_mlp(): pl.pallas_call(functools.partial(early_kernel, layout), in_specs=[hbm] *...]
    ppermute x8, waiting for transfers between devices: 4.57 us -> 5.41 us  [on_device(): sent.append(lax.ppermute(held[part], 'dev', along_y))]
  transfers between devices with their start and end apart: 23 -> 23, of which waited for: 10 -> 10; matrix products, arithmetic and copies ran while one was open for 0% -> 0% of each run, Pallas kernels for 23% -> 22%
where the time goes in v13:
time: 73.8 us; the launch traced here: 73.5 us
  starting transfers between devices  33.2 us (45%)
  Pallas kernels  22 us (30%)
  waiting for transfers between devices  16.7 us (23%)
  between operations  0.92 us (1%)
    ppermute x6, starting transfers between devices, on_device(): arrived = lax.ppermute(held[part], 'dev', along_z)  17.3 us
    ppermute x8, starting transfers between devices, on_device(): sent.append(lax.ppermute(held[part], 'dev', along_y))  6.97 us
    ppermute x8, waiting for transfers between devices, on_device(): sent.append(lax.ppermute(held[part], 'dev', along_y))  5.41 us
    pallas_call x1, Pallas kernels, middle_mlp(): pl.pallas_call(functools.partial(middle_kernel, layout, length, len(block...  4.74 us
    all_to_all x1, waiting for transfers between devices, on_device(): sent = lax.all_to_all(sent, 'dev', split_axis=0, concat_axis=0, tiled=True)  4.53 us
    pallas_call x1, Pallas kernels, early_mlp(): pl.pallas_call(functools.partial(early_kernel, layout), in_specs=[hbm] *...  4.51 us
    ppermute x6, waiting for transfers between devices, on_device(): arrived = lax.ppermute(held[part], 'dev', along_z)  3.93 us
    pallas_call x1, Pallas kernels, start_work(): pl.pallas_call(functools.partial(start_kernel, parts), in_specs=[hbm] * (...  3.76 us
  transfers between devices with their start and end apart: 23, of which 10 were waited for; matrix products, arithmetic and copies ran while one was open for 0% of the time, Pallas kernels for 22%

profile of v13, /device:TPU:0, one launch (start us, length us, event | category | flops | bytes accessed | tf_op | source)
XLA Modules:
  0.0 73.5 jit_solution(10883320326355486168)
XLA Ops:
  0.7 3.8 %shard_map.140 = (bf16[512,1536]{1,0:T(8,128)(2,1)S(1)}, bf16[2688,384]{1,0:T(8,128)(2,1)S(1)}, bf16[96,1024]{1,0:T(8,128)(2,1)S(1)}, bf16[96,1024]{1,0:T(8,128)(2,1)S(1)}) custom-call(bf16[4,256,1536]{2,1,0:T(8,128)(2,1)} %refs_0_.2, f32[1536]{0:T(1024)} %refs_1_.2, bf16[192,1024]{1,0:T(8,128)(2,1)} %refs_2_.2, bf16[192,1024]{1,0:T(8,128)(2,1)} %refs_3_.2, ...), custom_call_target="tpu_custom_call" | custom-call | tf_op jit(solution)/shard_map/pallas_call | solution.py:145
  5.1 2.9 %collective-permute-start.16 = (bf16[512,1536]{1,0:T(8,128)(2,1)S(1)}, bf16[512,1536]{1,0:T(8,128)(2,1)S(1)}, u32[]{:S(2)}, u32[]{:S(2)}) collective-permute-start(bf16[512,1536]{1,0:T(8,128)(2,1)S(1)} %get-tuple-element.42.refs_12_), channel_id=1, source_target_pairs={{0,16},{16,0},{1,17},{17,1},{2,18},{18,2},{3,19},{19,3},{4,20},{20... | collective-permute-start | bytes 4718600 | tf_op jit(solution)/shard_map/ppermute | solution.py:653
  8.0 1.5 %collective-permute-start.1 = (bf16[96,1024]{1,0:T(8,128)(2,1)S(1)}, bf16[96,1024]{1,0:T(8,128)(2,1)S(1)}, u32[]{:S(2)}, u32[]{:S(2)}) collective-permute-start(bf16[96,1024]{1,0:T(8,128)(2,1)S(1)} %get-tuple-element.32.refs_0_), channel_id=1, source_target_pairs={{0,2},{2,0},{4,6},{6,4},{8,10},{10,8},{12,14},{14,12},{1,3},{3,1},... | collective-permute-start | bytes 589832 | tf_op jit(solution)/shard_map/ppermute | solution.py:681
  9.5 2.6 %collective-permute-start = (bf16[96,1024]{1,0:T(8,128)(2,1)S(1)}, bf16[96,1024]{1,0:T(8,128)(2,1)S(1)}, u32[]{:S(2)}, u32[]{:S(2)}) collective-permute-start(bf16[96,1024]{1,0:T(8,128)(2,1)S(1)} %get-tuple-element.32.refs_0_), channel_id=1, source_target_pairs={{0,8},{2,10},{8,12},{10,14},{12,4},{14,6},{4,0},{6,2},{1,9},{3,11}... | collective-permute-start | bytes 589832 | tf_op jit(solution)/shard_map/ppermute | solution.py:674
  13.2 2.6 %collective-permute-start.6 = (bf16[96,1024]{1,0:T(8,128)(2,1)S(1)}, bf16[96,1024]{1,0:T(8,128)(2,1)S(1)}, u32[]{:S(2)}, u32[]{:S(2)}) collective-permute-start(bf16[96,1024]{1,0:T(8,128)(2,1)S(1)} %get-tuple-element.36.refs_1_), channel_id=1, source_target_pairs={{0,8},{2,10},{8,12},{10,14},{12,4},{14,6},{4,0},{6,2},{1,9},{3,11}... | collective-permute-start | bytes 589832 | tf_op jit(solution)/shard_map/ppermute | solution.py:674
  16.7 3.3 %collective-permute-start.2 = (bf16[96,1024]{1,0:T(8,128)(2,1)S(1)}, bf16[96,1024]{1,0:T(8,128)(2,1)S(1)}, u32[]{:S(2)}, u32[]{:S(2)}) collective-permute-start(bf16[96,1024]{1,0:T(8,128)(2,1)S(1)} %collective-permute-done.refs_4_), channel_id=1, source_target_pairs={{0,8},{2,10},{8,12},{10,14},{12,4},{14,6},{4,0},{6,2},{1,9},{3,11}... | collective-permute-start | bytes 589832 | tf_op jit(solution)/shard_map/ppermute | solution.py:674
  21.6 3.2 %collective-permute-start.10 = (bf16[96,1024]{1,0:T(8,128)(2,1)S(1)}, bf16[96,1024]{1,0:T(8,128)(2,1)S(1)}, u32[]{:S(2)}, u32[]{:S(2)}) collective-permute-start(bf16[96,1024]{1,0:T(8,128)(2,1)S(1)} %collective-permute-done.6.refs_5_), channel_id=1, source_target_pairs={{0,8},{2,10},{8,12},{10,14},{12,4},{14,6},{4,0},{6,2},{1,9},{3,11}... | collective-permute-start | bytes 589832 | tf_op jit(solution)/shard_map/ppermute | solution.py:674
  25.4 1.2 %collective-permute-start.9 = (bf16[96,1024]{1,0:T(8,128)(2,1)S(1)}, bf16[96,1024]{1,0:T(8,128)(2,1)S(1)}, u32[]{:S(2)}, u32[]{:S(2)}) collective-permute-start(bf16[96,1024]{1,0:T(8,128)(2,1)S(1)} %collective-permute-done.2.refs_8_), channel_id=1, source_target_pairs={{0,2},{2,0},{4,6},{6,4},{8,10},{10,8},{12,14},{14,12},{1,3},{3,1},... | collective-permute-start | bytes 589832 | tf_op jit(solution)/shard_map/ppermute | solution.py:681
  26.5 2.2 %collective-permute-start.8 = (bf16[96,1024]{1,0:T(8,128)(2,1)S(1)}, bf16[96,1024]{1,0:T(8,128)(2,1)S(1)}, u32[]{:S(2)}, u32[]{:S(2)}) collective-permute-start(bf16[96,1024]{1,0:T(8,128)(2,1)S(1)} %collective-permute-done.2.refs_8_), channel_id=1, source_target_pairs={{0,8},{2,10},{8,12},{10,14},{12,4},{14,6},{4,0},{6,2},{1,9},{3,11}... | collective-permute-start | bytes 589832 | tf_op jit(solution)/shard_map/ppermute | solution.py:674
  28.7 1.4 %collective-permute-done.10.refs_9_ = bf16[96,1024]{1,0:T(8,128)(2,1)S(1)} collective-permute-done((bf16[96,1024]{1,0:T(8,128)(2,1)S(1)}, bf16[96,1024]{1,0:T(8,128)(2,1)S(1)}, u32[]{:S(2)}, u32[]{:S(2)}) %collective-permute-start.10) | collective-permute-done | bytes 196640 | tf_op jit(solution)/shard_map/ppermute | solution.py:674
  30.2 3.4 %collective-permute-start.12 = (bf16[96,1024]{1,0:T(8,128)(2,1)S(1)}, bf16[96,1024]{1,0:T(8,128)(2,1)S(1)}, u32[]{:S(2)}, u32[]{:S(2)}) collective-permute-start(bf16[96,1024]{1,0:T(8,128)(2,1)S(1)} %collective-permute-done.10.refs_9_), channel_id=1, source_target_pairs={{0,8},{2,10},{8,12},{10,14},{12,4},{14,6},{4,0},{6,2},{1,9},{3,11}... | collective-permute-start | bytes 589832 | tf_op jit(solution)/shard_map/ppermute | solution.py:674
  34.7 1.7 %collective-permute-start.14 = (bf16[96,1024]{1,0:T(8,128)(2,1)S(1)}, bf16[96,1024]{1,0:T(8,128)(2,1)S(1)}, u32[]{:S(2)}, u32[]{:S(2)}) collective-permute-start(bf16[96,1024]{1,0:T(8,128)(2,1)S(1)} %collective-permute-done.8.refs_0_), channel_id=1, source_target_pairs={{0,2},{2,0},{4,6},{6,4},{8,10},{10,8},{12,14},{14,12},{1,3},{3,1},... | collective-permute-start | bytes 589832 | tf_op jit(solution)/shard_map/ppermute | solution.py:681
  37.0 3.7 %collective-permute-done.13.refs_11_ = bf16[96,1024]{1,0:T(8,128)(2,1)S(1)} collective-permute-done((bf16[96,1024]{1,0:T(8,128)(2,1)S(1)}, bf16[96,1024]{1,0:T(8,128)(2,1)S(1)}, u32[]{:S(2)}, u32[]{:S(2)}) %collective-permute-start.13) | collective-permute-done | bytes 196640 | tf_op jit(solution)/shard_map/ppermute | solution.py:681
  41.4 4.5 %shard_map.142 = (f32[2,512,1024]{2,1,0:T(8,128)S(1)}, bf16[1536,1024]{1,0:T(8,128)(2,1)S(1)}, bf16[2,512,1536]{2,1,0:T(8,128)(2,1)S(1)}) custom-call(bf16[96,1024]{1,0:T(8,128)(2,1)} %copy-done.6, bf16[96,1024]{1,0:T(8,128)(2,1)} %copy-done.7, bf16[96,1024]{1,0:T(8,128)(2,1)} %copy-done.8, bf16[96,1024]{1,0:T(8,128)(2,1)} %copy-done.10, ...), custom_call_target="tpu_custom_call" | custom-call | flops 2147483648 | bytes 8388608 | tf_op jit(solution)/shard_map/pallas_call | solution.py:289
  45.9 1.7 %collective-permute-done.15.refs_3_ = bf16[96,1024]{1,0:T(8,128)(2,1)S(1)} collective-permute-done((bf16[96,1024]{1,0:T(8,128)(2,1)S(1)}, bf16[96,1024]{1,0:T(8,128)(2,1)S(1)}, u32[]{:S(2)}, u32[]{:S(2)}) %collective-permute-start.15) | collective-permute-done | bytes 196640 | tf_op jit(solution)/shard_map/ppermute | solution.py:681
  47.6 4.7 %shard_map.143 = (f32[2,512]{1,0:T(2,128)S(1)}, bf16[1536,1024]{1,0:T(8,128)(2,1)S(1)}, bf16[16,128]{1,0:T(8,128)(2,1)S(1)}) custom-call(bf16[96,1024]{1,0:T(8,128)(2,1)S(1)} %collective-permute-done.8.refs_0_, bf16[96,1024]{1,0:T(8,128)(2,1)S(1)} %collective-permute-done.12.refs_1_, ...), custom_call_target="tpu_custom_call", output_to_operand_aliasing={{1}: (6, {})} | custom-call | flops 3221225472 | bytes 7864320 | tf_op jit(solution)/shard_map/pallas_call | solution.py:362
  53.0 2.1 %shard_map.144 = bf16[16,128]{1,0:T(8,128)(2,1)S(1)} custom-call(f32[2,512]{1,0:T(2,128)S(1)} %get-tuple-element.48.means_ref, bf16[1536,1024]{1,0:T(8,128)(2,1)S(1)} %get-tuple-element.49.weights, bf16[512,1536]{1,0:T(8,128)(2,1)S(1)} %collective-permute-done.18.tiles_ref), custom_call_target="tpu_custom_call" | custom-call | flops 1610612736 | bytes 4718592 | tf_op jit(solution)/shard_map/pallas_call | solution.py:412
  55.0 1.3 %collective-permute-start.19 = (bf16[16,128]{1,0:T(8,128)(2,1)S(1)}, bf16[16,128]{1,0:T(8,128)(2,1)S(1)}, u32[]{:S(2)}, u32[]{:S(2)}) collective-permute-start(bf16[16,128]{1,0:T(8,128)(2,1)S(1)} %shard_map.144), channel_id=1, source_target_pairs={{0,16},{16,0},{1,17},{17,1},{2,18},{18,2},{3,19},{19,3},{4,20},{20... | collective-permute-start | bytes 12296 | tf_op jit(solution)/shard_map/ppermute | solution.py:700
  56.5 2.2 %collective-permute-done.19.pair_ref = bf16[16,128]{1,0:T(8,128)(2,1)S(1)} collective-permute-done((bf16[16,128]{1,0:T(8,128)(2,1)S(1)}, bf16[16,128]{1,0:T(8,128)(2,1)S(1)}, u32[]{:S(2)}, u32[]{:S(2)}) %collective-permute-start.19) | collective-permute-done | bytes 4128 | tf_op jit(solution)/shard_map/ppermute | solution.py:700
  59.4 1.9 %shard_map.145 = (bf16[4,1024]{1,0:T(4,128)(2,1)}, f32[8,768]{1,0:T(8,128)S(1)}, bf16[8,16,256]{2,1,0:T(8,128)(2,1)}) custom-call(s32[8]{0:T(128)S(1)} %copy-done.3, bf16[16,128]{1,0:T(8,128)(2,1)S(1)} %get-tuple-element.47.own_ref, bf16[16,128]{1,0:T(8,128)(2,1)S(1)} %collective-permute-done.17.own_far_ref, ...), custom_call_target="tpu_custom_call" | custom-call | tf_op jit(solution)/shard_map/pallas_call | solution.py:706
  61.2 3.3 %all-to-all-start = ((bf16[8,16,256]{2,1,0:T(8,128)(2,1)}), bf16[8,16,256]{2,1,0:T(8,128)(2,1)S(1)}, u32[]{:S(2)}, u32[]{:S(2)}) async-start(bf16[8,16,256]{2,1,0:T(8,128)(2,1)} %get-tuple-element.51), calls=%async_computation | async-start | bytes 131072 | tf_op jit(solution)/shard_map/all_to_all | solution.py:717
  64.6 2.3 %shard_map.146 = (bf16[96,768]{1,0:T(8,128)(2,1)S(1)}, f32[96,32]{1,0:T(8,128)S(1)}, bf16[768,384]{1,0:T(8,128)(2,1)S(1)}, bf16[768,384]{1,0:T(8,128)(2,1)S(1)},...) custom-call(f32[8,768]{1,0:T(8,128)S(1)} %get-tuple-element.52.mixed, ...), custom_call_target="tpu_custom_call" | custom-call | tf_op jit(solution)/shard_map/pallas_call | solution.py:721
  66.9 4.5 %all-to-all-done.sent_ref = bf16[8,16,256]{2,1,0:T(8,128)(2,1)S(1)} async-done(((bf16[8,16,256]{2,1,0:T(8,128)(2,1)}), bf16[8,16,256]{2,1,0:T(8,128)(2,1)S(1)}, u32[]{:S(2)}, u32[]{:S(2)}) %all-to-all-start) | async-done | bytes 65568 | tf_op jit(solution)/shard_map/all_to_all | solution.py:717
  71.4 2.1 %shard_map.147 = bf16[4,384]{1,0:T(4,128)(2,1)} custom-call(s32[8]{0:T(128)S(1)} %copy-done.3, bf16[8,16,256]{2,1,0:T(8,128)(2,1)S(1)} %all-to-all-done.sent_ref, f32[8,768]{1,0:T(8,128)S(1)} %get-tuple-element.52.mixed_ref, bf16[96,768]{1,0:T(8,128)(2,1)S(1)} %get-tuple-element.54.query_ref, bf16[768,384]{1,0:T(8,128)(2,1)S(1)} %get-tuple-element.55.wk_ref, ...), custom_call_target="tpu_custom_call" | custom-call | tf_op jit(solution)/shard_map/pallas_call | solution.py:736
  (66 shorter events, 8.5 us)
Async XLA Ops:
  4.4 36.2 %copy-start.6 = (bf16[96,1024]{1,0:T(8,128)(2,1)}, bf16[96,1024]{1,0:T(8,128)(2,1)S(1)}, u32[]{:S(2)}) copy-start(bf16[96,1024]{1,0:T(8,128)(2,1)S(1)} %get-tuple-element.32.refs_0_) | copy-start | bytes 589828
  4.5 7.6 %collective-permute-start.5 = (bf16[512,1536]{1,0:T(8,128)(2,1)S(1)}, bf16[512,1536]{1,0:T(8,128)(2,1)S(1)}, u32[]{:S(2)}, u32[]{:S(2)}) collective-permute-start(bf16[512,1536]{1,0:T(8,128)(2,1)S(1)} %get-tuple-element.42.refs_12_), channel_id=1, source_target_pairs={{0,1},{1,0},{2,3},{3,2},{4,5},{5,4},{6,7},{7,6},{8,9},{9,8},{10,11... | collective-permute-start | bytes 4718600 | tf_op jit(solution)/shard_map/ppermute | solution.py:652
  5.0 7.1 %collective-permute-start.4 = (bf16[1024,768]{1,0:T(8,128)(2,1)S(1)}, bf16[1024,768]{1,0:T(8,128)(2,1)S(1)}, u32[]{:S(2)}, u32[]{:S(2)}) collective-permute-start(bf16[1024,768]{1,0:T(8,128)(2,1)S(1)} %copy-done), channel_id=1, source_target_pairs={{0,1},{1,0},{2,3},{3,2},{4,5},{5,4},{6,7},{7,6},{8,9},{9,8},{10,11... | collective-permute-start | bytes 4718600 | tf_op jit(solution)/shard_map/ppermute | solution.py:654
  5.1 40.8 %collective-permute-start.16 = (bf16[512,1536]{1,0:T(8,128)(2,1)S(1)}, bf16[512,1536]{1,0:T(8,128)(2,1)S(1)}, u32[]{:S(2)}, u32[]{:S(2)}) collective-permute-start(bf16[512,1536]{1,0:T(8,128)(2,1)S(1)} %get-tuple-element.42.refs_12_), channel_id=1, source_target_pairs={{0,16},{16,0},{1,17},{17,1},{2,18},{18,2},{3,19},{19,3},{4,20},{20... | collective-permute-start | bytes 4718600 | tf_op jit(solution)/shard_map/ppermute | solution.py:653
  8.0 7.8 %collective-permute-start.1 = (bf16[96,1024]{1,0:T(8,128)(2,1)S(1)}, bf16[96,1024]{1,0:T(8,128)(2,1)S(1)}, u32[]{:S(2)}, u32[]{:S(2)}) collective-permute-start(bf16[96,1024]{1,0:T(8,128)(2,1)S(1)} %get-tuple-element.32.refs_0_), channel_id=1, source_target_pairs={{0,2},{2,0},{4,6},{6,4},{8,10},{10,8},{12,14},{14,12},{1,3},{3,1},... | collective-permute-start | bytes 589832 | tf_op jit(solution)/shard_map/ppermute | solution.py:681
  9.5 6.6 %collective-permute-start = (bf16[96,1024]{1,0:T(8,128)(2,1)S(1)}, bf16[96,1024]{1,0:T(8,128)(2,1)S(1)}, u32[]{:S(2)}, u32[]{:S(2)}) collective-permute-start(bf16[96,1024]{1,0:T(8,128)(2,1)S(1)} %get-tuple-element.32.refs_0_), channel_id=1, source_target_pairs={{0,8},{2,10},{8,12},{10,14},{12,4},{14,6},{4,0},{6,2},{1,9},{3,11}... | collective-permute-start | bytes 589832 | tf_op jit(solution)/shard_map/ppermute | solution.py:674
  12.1 7.9 %collective-permute-start.7 = (bf16[96,1024]{1,0:T(8,128)(2,1)S(1)}, bf16[96,1024]{1,0:T(8,128)(2,1)S(1)}, u32[]{:S(2)}, u32[]{:S(2)}) collective-permute-start(bf16[96,1024]{1,0:T(8,128)(2,1)S(1)} %get-tuple-element.36.refs_1_), channel_id=1, source_target_pairs={{0,2},{2,0},{4,6},{6,4},{8,10},{10,8},{12,14},{14,12},{1,3},{3,1},... | collective-permute-start | bytes 589832 | tf_op jit(solution)/shard_map/ppermute | solution.py:681
  13.2 7.9 %collective-permute-start.6 = (bf16[96,1024]{1,0:T(8,128)(2,1)S(1)}, bf16[96,1024]{1,0:T(8,128)(2,1)S(1)}, u32[]{:S(2)}, u32[]{:S(2)}) collective-permute-start(bf16[96,1024]{1,0:T(8,128)(2,1)S(1)} %get-tuple-element.36.refs_1_), channel_id=1, source_target_pairs={{0,8},{2,10},{8,12},{10,14},{12,4},{14,6},{4,0},{6,2},{1,9},{3,11}... | collective-permute-start | bytes 589832 | tf_op jit(solution)/shard_map/ppermute | solution.py:674
  16.1 8.7 %collective-permute-start.3 = (bf16[96,1024]{1,0:T(8,128)(2,1)S(1)}, bf16[96,1024]{1,0:T(8,128)(2,1)S(1)}, u32[]{:S(2)}, u32[]{:S(2)}) collective-permute-start(bf16[96,1024]{1,0:T(8,128)(2,1)S(1)} %collective-permute-done.refs_4_), channel_id=1, source_target_pairs={{0,2},{2,0},{4,6},{6,4},{8,10},{10,8},{12,14},{14,12},{1,3},{3,1},... | collective-permute-start | bytes 589832 | tf_op jit(solution)/shard_map/ppermute | solution.py:681
  16.7 8.7 %collective-permute-start.2 = (bf16[96,1024]{1,0:T(8,128)(2,1)S(1)}, bf16[96,1024]{1,0:T(8,128)(2,1)S(1)}, u32[]{:S(2)}, u32[]{:S(2)}) collective-permute-start(bf16[96,1024]{1,0:T(8,128)(2,1)S(1)} %collective-permute-done.refs_4_), channel_id=1, source_target_pairs={{0,8},{2,10},{8,12},{10,14},{12,4},{14,6},{4,0},{6,2},{1,9},{3,11}... | collective-permute-start | bytes 589832 | tf_op jit(solution)/shard_map/ppermute | solution.py:674
  21.0 7.7 %collective-permute-start.11 = (bf16[96,1024]{1,0:T(8,128)(2,1)S(1)}, bf16[96,1024]{1,0:T(8,128)(2,1)S(1)}, u32[]{:S(2)}, u32[]{:S(2)}) collective-permute-start(bf16[96,1024]{1,0:T(8,128)(2,1)S(1)} %collective-permute-done.6.refs_5_), channel_id=1, source_target_pairs={{0,2},{2,0},{4,6},{6,4},{8,10},{10,8},{12,14},{14,12},{1,3},{3,1},... | collective-permute-start | bytes 589832 | tf_op jit(solution)/shard_map/ppermute | solution.py:681
  21.6 8.6 %collective-permute-start.10 = (bf16[96,1024]{1,0:T(8,128)(2,1)S(1)}, bf16[96,1024]{1,0:T(8,128)(2,1)S(1)}, u32[]{:S(2)}, u32[]{:S(2)}) collective-permute-start(bf16[96,1024]{1,0:T(8,128)(2,1)S(1)} %collective-permute-done.6.refs_5_), channel_id=1, source_target_pairs={{0,8},{2,10},{8,12},{10,14},{12,4},{14,6},{4,0},{6,2},{1,9},{3,11}... | collective-permute-start | bytes 589832 | tf_op jit(solution)/shard_map/ppermute | solution.py:674
  25.4 8.6 %collective-permute-start.9 = (bf16[96,1024]{1,0:T(8,128)(2,1)S(1)}, bf16[96,1024]{1,0:T(8,128)(2,1)S(1)}, u32[]{:S(2)}, u32[]{:S(2)}) collective-permute-start(bf16[96,1024]{1,0:T(8,128)(2,1)S(1)} %collective-permute-done.2.refs_8_), channel_id=1, source_target_pairs={{0,2},{2,0},{4,6},{6,4},{8,10},{10,8},{12,14},{14,12},{1,3},{3,1},... | collective-permute-start | bytes 589832 | tf_op jit(solution)/shard_map/ppermute | solution.py:681
  26.5 8.1 %collective-permute-start.8 = (bf16[96,1024]{1,0:T(8,128)(2,1)S(1)}, bf16[96,1024]{1,0:T(8,128)(2,1)S(1)}, u32[]{:S(2)}, u32[]{:S(2)}) collective-permute-start(bf16[96,1024]{1,0:T(8,128)(2,1)S(1)} %collective-permute-done.2.refs_8_), channel_id=1, source_target_pairs={{0,8},{2,10},{8,12},{10,14},{12,4},{14,6},{4,0},{6,2},{1,9},{3,11}... | collective-permute-start | bytes 589832 | tf_op jit(solution)/shard_map/ppermute | solution.py:674
  30.2 6.8 %collective-permute-start.12 = (bf16[96,1024]{1,0:T(8,128)(2,1)S(1)}, bf16[96,1024]{1,0:T(8,128)(2,1)S(1)}, u32[]{:S(2)}, u32[]{:S(2)}) collective-permute-start(bf16[96,1024]{1,0:T(8,128)(2,1)S(1)} %collective-permute-done.10.refs_9_), channel_id=1, source_target_pairs={{0,8},{2,10},{8,12},{10,14},{12,4},{14,6},{4,0},{6,2},{1,9},{3,11}... | collective-permute-start | bytes 589832 | tf_op jit(solution)/shard_map/ppermute | solution.py:674
  33.5 7.1 %collective-permute-start.13 = (bf16[96,1024]{1,0:T(8,128)(2,1)S(1)}, bf16[96,1024]{1,0:T(8,128)(2,1)S(1)}, u32[]{:S(2)}, u32[]{:S(2)}) collective-permute-start(bf16[96,1024]{1,0:T(8,128)(2,1)S(1)} %collective-permute-done.10.refs_9_), channel_id=1, source_target_pairs={{0,2},{2,0},{4,6},{6,4},{8,10},{10,8},{12,14},{14,12},{1,3},{3,1},... | collective-permute-start | bytes 589832 | tf_op jit(solution)/shard_map/ppermute | solution.py:681
  33.9 30.7 %collective-permute-start.21 = (bf16[2688,384]{1,0:T(8,128)(2,1)S(1)}, bf16[2688,384]{1,0:T(8,128)(2,1)}, u32[]{:S(2)}, u32[]{:S(2)}) collective-permute-start(bf16[2688,384]{1,0:T(8,128)(2,1)S(1)} %get-tuple-element.53), channel_id=1, source_target_pairs={{0,1},{1,0},{2,3},{3,2},{4,5},{5,4},{6,7},{7,6},{8,9},{9,8},{10,11... | collective-permute-start | bytes 6193160 | tf_op jit(solution)/shard_map/ppermute | solution.py:655
  34.7 11.2 %collective-permute-start.14 = (bf16[96,1024]{1,0:T(8,128)(2,1)S(1)}, bf16[96,1024]{1,0:T(8,128)(2,1)S(1)}, u32[]{:S(2)}, u32[]{:S(2)}) collective-permute-start(bf16[96,1024]{1,0:T(8,128)(2,1)S(1)} %collective-permute-done.8.refs_0_), channel_id=1, source_target_pairs={{0,2},{2,0},{4,6},{6,4},{8,10},{10,8},{12,14},{14,12},{1,3},{3,1},... | collective-permute-start | bytes 589832 | tf_op jit(solution)/shard_map/ppermute | solution.py:681
  40.7 7.0 %collective-permute-start.15 = (bf16[96,1024]{1,0:T(8,128)(2,1)S(1)}, bf16[96,1024]{1,0:T(8,128)(2,1)S(1)}, u32[]{:S(2)}, u32[]{:S(2)}) collective-permute-start(bf16[96,1024]{1,0:T(8,128)(2,1)S(1)} %collective-permute-done.12.refs_1_), channel_id=1, source_target_pairs={{0,2},{2,0},{4,6},{6,4},{8,10},{10,8},{12,14},{14,12},{1,3},{3,1},... | collective-permute-start | bytes 589832 | tf_op jit(solution)/shard_map/ppermute | solution.py:681
  47.6 5.3 %collective-permute-start.18 = (bf16[512,1536]{1,0:T(8,128)(2,1)S(1)}, bf16[512,1536]{1,0:T(8,128)(2,1)S(1)}, u32[]{:S(2)}, u32[]{:S(2)}) collective-permute-start(bf16[512,1536]{1,0:T(8,128)(2,1)S(1)} %collective-permute-done.16.refs_4_), channel_id=1, source_target_pairs={{0,1},{1,0},{2,3},{3,2},{4,5},{5,4},{6,7},{7,6},{8,9},{9,8},{10,11... | collective-permute-start | bytes 4718600 | tf_op jit(solution)/shard_map/ppermute | solution.py:690
  52.4 4.1 %collective-permute-start.17 = (bf16[16,128]{1,0:T(8,128)(2,1)S(1)}, bf16[16,128]{1,0:T(8,128)(2,1)S(1)}, u32[]{:S(2)}, u32[]{:S(2)}) collective-permute-start(bf16[16,128]{1,0:T(8,128)(2,1)S(1)} %get-tuple-element.47.own_ref), channel_id=1, source_target_pairs={{0,1},{1,0},{2,3},{3,2},{4,5},{5,4},{6,7},{7,6},{8,9},{9,8},{10,11... | collective-permute-start | bytes 12296 | tf_op jit(solution)/shard_map/ppermute | solution.py:694
  55.0 3.7 %collective-permute-start.19 = (bf16[16,128]{1,0:T(8,128)(2,1)S(1)}, bf16[16,128]{1,0:T(8,128)(2,1)S(1)}, u32[]{:S(2)}, u32[]{:S(2)}) collective-permute-start(bf16[16,128]{1,0:T(8,128)(2,1)S(1)} %shard_map.144), channel_id=1, source_target_pairs={{0,16},{16,0},{1,17},{17,1},{2,18},{18,2},{3,19},{19,3},{4,20},{20... | collective-permute-start | bytes 12296 | tf_op jit(solution)/shard_map/ppermute | solution.py:700
  56.3 3.1 %collective-permute-start.20 = (bf16[16,128]{1,0:T(8,128)(2,1)S(1)}, bf16[16,128]{1,0:T(8,128)(2,1)S(1)}, u32[]{:S(2)}, u32[]{:S(2)}) collective-permute-start(bf16[16,128]{1,0:T(8,128)(2,1)S(1)} %shard_map.144), channel_id=1, source_target_pairs={{0,17},{1,16},{16,1},{17,0},{2,19},{3,18},{18,3},{19,2},{4,21},{5,... | collective-permute-start | bytes 12296 | tf_op jit(solution)/shard_map/ppermute | solution.py:699
  61.2 10.2 %all-to-all-start = ((bf16[8,16,256]{2,1,0:T(8,128)(2,1)}), bf16[8,16,256]{2,1,0:T(8,128)(2,1)S(1)}, u32[]{:S(2)}, u32[]{:S(2)}) async-start(bf16[8,16,256]{2,1,0:T(8,128)(2,1)} %get-tuple-element.51), calls=%async_computation | async-start | bytes 131072 | tf_op jit(solution)/shard_map/all_to_all | solution.py:717
  (17 other events, 309.4 us)

commit v14 on v13

--- a/solution.py
+++ b/solution.py
@@ -670,15 +670,20 @@
     for step in range(nz):
         sent = []
         for part in range(len(held)):
+            over = None
             if step:
                 arrived = lax.ppermute(held[part], "dev", along_z)
-                others = [steps[-1][len(held) + part]]
+                others = [] if last is None else [last]
+                over = steps[-1][len(held) + part]
+                if (step, part) != (nz - 1, 1):
+                    others.append(over)
                 if (step, part) == (nz - 1, 0):
                     others += [many]
-                if last is not None:
-                    others.append(last)
                 held[part] = last = after(arrived, *others)
-            sent.append(lax.ppermute(held[part], "dev", along_y))
+            if (step, part) == (nz - 1, 0):
+                sent.append(lax.ppermute(after(over, last), "dev", along_z))
+            else:
+                sent.append(lax.ppermute(held[part], "dev", along_y))
         steps.append([*held, *sent])
     blocks = [block for step in steps for block in step]
     early = []

time: 73.8 us -> 71.9 us (0.974)
  waiting for transfers between devices: 16.7 us -> 11.3 us
  starting transfers between devices: 33.2 us -> 36.6 us
    ppermute x8 -> x7, waiting for transfers between devices: 5.41 us -> 0.91 us  [on_device(): sent.append(lax.ppermute(held[part], 'dev', along_y))]
    ppermute x0 -> x1, starting transfers between devices: none -> 3.09 us  [on_device(): sent.append(lax.ppermute(after(over, last), 'dev', along_z))]
    ppermute x8 -> x7, starting transfers between devices: 6.97 us -> 6.6 us  [on_device(): sent.append(lax.ppermute(held[part], 'dev', along_y))]
  transfers between devices with their start and end apart: 23 -> 23, of which waited for: 10 -> 9; matrix products, arithmetic and copies ran while one was open for 0% -> 0% of each run, Pallas kernels for 22% -> 23%
where the time goes in v14:
time: 71.9 us; the launch traced here: 71.7 us
  starting transfers between devices  36.6 us (51%)
  Pallas kernels  22.1 us (31%)
  waiting for transfers between devices  11.3 us (16%)
  between operations  0.92 us (1%)
  local copies, waits for them, and re-layouts  0.75 us (1%)
    ppermute x6, starting transfers between devices, on_device(): arrived = lax.ppermute(held[part], 'dev', along_z)  17.3 us
    ppermute x7, starting transfers between devices, on_device(): sent.append(lax.ppermute(held[part], 'dev', along_y))  6.6 us
    pallas_call x1, Pallas kernels, middle_mlp(): pl.pallas_call(functools.partial(middle_kernel, layout, length, len(block...  4.8 us
    all_to_all x1, waiting for transfers between devices, on_device(): sent = lax.all_to_all(sent, 'dev', split_axis=0, concat_axis=0, tiled=True)  4.6 us
    pallas_call x1, Pallas kernels, early_mlp(): pl.pallas_call(functools.partial(early_kernel, layout), in_specs=[hbm] *...  4.51 us
    all_to_all x1, starting transfers between devices, on_device(): sent = lax.all_to_all(sent, 'dev', split_axis=0, concat_axis=0, tiled=True)  4.01 us
    pallas_call x1, Pallas kernels, start_work(): pl.pallas_call(functools.partial(start_kernel, parts), in_specs=[hbm] * (...  3.76 us
    ppermute x6, waiting for transfers between devices, on_device(): arrived = lax.ppermute(held[part], 'dev', along_z)  3.56 us
  transfers between devices with their start and end apart: 23, of which 9 were waited for; matrix products, arithmetic and copies ran while one was open for 0% of the time, Pallas kernels for 23%

profile of v14, /device:TPU:0, one launch (start us, length us, event | category | flops | bytes accessed | tf_op | source)
XLA Modules:
  0.0 71.7 jit_solution(9159647784479868971)
XLA Ops:
  0.7 3.8 %shard_map.140 = (bf16[512,1536]{1,0:T(8,128)(2,1)S(1)}, bf16[2688,384]{1,0:T(8,128)(2,1)S(1)}, bf16[96,1024]{1,0:T(8,128)(2,1)S(1)}, bf16[96,1024]{1,0:T(8,128)(2,1)S(1)}) custom-call(bf16[4,256,1536]{2,1,0:T(8,128)(2,1)} %refs_0_.2, f32[1536]{0:T(1024)} %refs_1_.2, bf16[192,1024]{1,0:T(8,128)(2,1)} %refs_2_.2, bf16[192,1024]{1,0:T(8,128)(2,1)} %refs_3_.2, ...), custom_call_target="tpu_custom_call" | custom-call | tf_op jit(solution)/shard_map/pallas_call | solution.py:145
  5.1 2.9 %collective-permute-start.15 = (bf16[512,1536]{1,0:T(8,128)(2,1)S(1)}, bf16[512,1536]{1,0:T(8,128)(2,1)S(1)}, u32[]{:S(2)}, u32[]{:S(2)}) collective-permute-start(bf16[512,1536]{1,0:T(8,128)(2,1)S(1)} %get-tuple-element.44.refs_12_), channel_id=1, source_target_pairs={{0,16},{16,0},{1,17},{17,1},{2,18},{18,2},{3,19},{19,3},{4,20},{20... | collective-permute-start | bytes 4718600 | tf_op jit(solution)/shard_map/ppermute | solution.py:653
  8.0 1.5 %collective-permute-start.1 = (bf16[96,1024]{1,0:T(8,128)(2,1)S(1)}, bf16[96,1024]{1,0:T(8,128)(2,1)S(1)}, u32[]{:S(2)}, u32[]{:S(2)}) collective-permute-start(bf16[96,1024]{1,0:T(8,128)(2,1)S(1)} %get-tuple-element.33.refs_0_), channel_id=1, source_target_pairs={{0,2},{2,0},{4,6},{6,4},{8,10},{10,8},{12,14},{14,12},{1,3},{3,1},... | collective-permute-start | bytes 589832 | tf_op jit(solution)/shard_map/ppermute | solution.py:686
  9.5 2.6 %collective-permute-start = (bf16[96,1024]{1,0:T(8,128)(2,1)S(1)}, bf16[96,1024]{1,0:T(8,128)(2,1)S(1)}, u32[]{:S(2)}, u32[]{:S(2)}) collective-permute-start(bf16[96,1024]{1,0:T(8,128)(2,1)S(1)} %get-tuple-element.33.refs_0_), channel_id=1, source_target_pairs={{0,8},{2,10},{8,12},{10,14},{12,4},{14,6},{4,0},{6,2},{1,9},{3,11}... | collective-permute-start | bytes 589832 | tf_op jit(solution)/shard_map/ppermute | solution.py:675
  12.1 1.1 %collective-permute-start.6 = (bf16[96,1024]{1,0:T(8,128)(2,1)S(1)}, bf16[96,1024]{1,0:T(8,128)(2,1)S(1)}, u32[]{:S(2)}, u32[]{:S(2)}) collective-permute-start(bf16[96,1024]{1,0:T(8,128)(2,1)S(1)} %get-tuple-element.37.refs_1_), channel_id=1, source_target_pairs={{0,2},{2,0},{4,6},{6,4},{8,10},{10,8},{12,14},{14,12},{1,3},{3,1},... | collective-permute-start | bytes 589832 | tf_op jit(solution)/shard_map/ppermute | solution.py:686
  13.2 2.6 %collective-permute-start.5 = (bf16[96,1024]{1,0:T(8,128)(2,1)S(1)}, bf16[96,1024]{1,0:T(8,128)(2,1)S(1)}, u32[]{:S(2)}, u32[]{:S(2)}) collective-permute-start(bf16[96,1024]{1,0:T(8,128)(2,1)S(1)} %get-tuple-element.37.refs_1_), channel_id=1, source_target_pairs={{0,8},{2,10},{8,12},{10,14},{12,4},{14,6},{4,0},{6,2},{1,9},{3,11}... | collective-permute-start | bytes 589832 | tf_op jit(solution)/shard_map/ppermute | solution.py:675
  16.7 3.3 %collective-permute-start.2 = (bf16[96,1024]{1,0:T(8,128)(2,1)S(1)}, bf16[96,1024]{1,0:T(8,128)(2,1)S(1)}, u32[]{:S(2)}, u32[]{:S(2)}) collective-permute-start(bf16[96,1024]{1,0:T(8,128)(2,1)S(1)} %collective-permute-done.refs_4_), channel_id=1, source_target_pairs={{0,8},{2,10},{8,12},{10,14},{12,4},{14,6},{4,0},{6,2},{1,9},{3,11}... | collective-permute-start | bytes 589832 | tf_op jit(solution)/shard_map/ppermute | solution.py:675
  20.0 1.1 %collective-permute-done.5.refs_5_ = bf16[96,1024]{1,0:T(8,128)(2,1)S(1)} collective-permute-done((bf16[96,1024]{1,0:T(8,128)(2,1)S(1)}, bf16[96,1024]{1,0:T(8,128)(2,1)S(1)}, u32[]{:S(2)}, u32[]{:S(2)}) %collective-permute-start.5) | collective-permute-done | bytes 196640 | tf_op jit(solution)/shard_map/ppermute | solution.py:675
  21.6 3.2 %collective-permute-start.9 = (bf16[96,1024]{1,0:T(8,128)(2,1)S(1)}, bf16[96,1024]{1,0:T(8,128)(2,1)S(1)}, u32[]{:S(2)}, u32[]{:S(2)}) collective-permute-start(bf16[96,1024]{1,0:T(8,128)(2,1)S(1)} %collective-permute-done.5.refs_5_), channel_id=1, source_target_pairs={{0,8},{2,10},{8,12},{10,14},{12,4},{14,6},{4,0},{6,2},{1,9},{3,11}... | collective-permute-start | bytes 589832 | tf_op jit(solution)/shard_map/ppermute | solution.py:675
  25.4 1.2 %collective-permute-start.11 = (bf16[96,1024]{1,0:T(8,128)(2,1)S(1)}, bf16[96,1024]{1,0:T(8,128)(2,1)S(1)}, u32[]{:S(2)}, u32[]{:S(2)}) collective-permute-start(bf16[96,1024]{1,0:T(8,128)(2,1)S(1)} %collective-permute-done.2.refs_8_), channel_id=1, source_target_pairs={{0,2},{2,0},{4,6},{6,4},{8,10},{10,8},{12,14},{14,12},{1,3},{3,1},... | collective-permute-start | bytes 589832 | tf_op jit(solution)/shard_map/ppermute | solution.py:686
  26.5 2.2 %collective-permute-start.8 = (bf16[96,1024]{1,0:T(8,128)(2,1)S(1)}, bf16[96,1024]{1,0:T(8,128)(2,1)S(1)}, u32[]{:S(2)}, u32[]{:S(2)}) collective-permute-start(bf16[96,1024]{1,0:T(8,128)(2,1)S(1)} %collective-permute-done.2.refs_8_), channel_id=1, source_target_pairs={{0,8},{2,10},{8,12},{10,14},{12,4},{14,6},{4,0},{6,2},{1,9},{3,11}... | collective-permute-start | bytes 589832 | tf_op jit(solution)/shard_map/ppermute | solution.py:675
  28.7 1.4 %collective-permute-done.9.refs_9_ = bf16[96,1024]{1,0:T(8,128)(2,1)S(1)} collective-permute-done((bf16[96,1024]{1,0:T(8,128)(2,1)S(1)}, bf16[96,1024]{1,0:T(8,128)(2,1)S(1)}, u32[]{:S(2)}, u32[]{:S(2)}) %collective-permute-start.9) | collective-permute-done | bytes 196640 | tf_op jit(solution)/shard_map/ppermute | solution.py:675
  30.2 3.4 %collective-permute-start.12 = (bf16[96,1024]{1,0:T(8,128)(2,1)S(1)}, bf16[96,1024]{1,0:T(8,128)(2,1)S(1)}, u32[]{:S(2)}, u32[]{:S(2)}) collective-permute-start(bf16[96,1024]{1,0:T(8,128)(2,1)S(1)} %collective-permute-done.9.refs_9_), channel_id=1, source_target_pairs={{0,8},{2,10},{8,12},{10,14},{12,4},{14,6},{4,0},{6,2},{1,9},{3,11}... | collective-permute-start | bytes 589832 | tf_op jit(solution)/shard_map/ppermute | solution.py:675
  34.7 3.1 %collective-permute-start.13 = (bf16[96,1024]{1,0:T(8,128)(2,1)S(1)}, bf16[96,1024]{1,0:T(8,128)(2,1)S(1)}, u32[]{:S(2)}, u32[]{:S(2)}) collective-permute-start(bf16[96,1024]{1,0:T(8,128)(2,1)S(1)} %collective-permute-done.11.refs_10_), channel_id=1, source_target_pairs={{0,8},{2,10},{8,12},{10,14},{12,4},{14,6},{4,0},{6,2},{1,9},{3,11}... | collective-permute-start | bytes 589832 | tf_op jit(solution)/shard_map/ppermute | solution.py:684
  38.0 1.4 %collective-permute-start.14 = (bf16[96,1024]{1,0:T(8,128)(2,1)S(1)}, bf16[96,1024]{1,0:T(8,128)(2,1)S(1)}, u32[]{:S(2)}, u32[]{:S(2)}) collective-permute-start(bf16[96,1024]{1,0:T(8,128)(2,1)S(1)} %collective-permute-done.12.refs_1_), channel_id=1, source_target_pairs={{0,2},{2,0},{4,6},{6,4},{8,10},{10,8},{12,14},{14,12},{1,3},{3,1},... | collective-permute-start | bytes 589832 | tf_op jit(solution)/shard_map/ppermute | solution.py:686
  41.0 4.5 %shard_map.142 = (f32[2,512,1024]{2,1,0:T(8,128)S(1)}, bf16[1536,1024]{1,0:T(8,128)(2,1)S(1)}, bf16[2,512,1536]{2,1,0:T(8,128)(2,1)S(1)}) custom-call(bf16[96,1024]{1,0:T(8,128)(2,1)} %copy-done.6, bf16[96,1024]{1,0:T(8,128)(2,1)} %copy-done.7, bf16[96,1024]{1,0:T(8,128)(2,1)} %copy-done.8, bf16[96,1024]{1,0:T(8,128)(2,1)} %copy-done.10, ...), custom_call_target="tpu_custom_call" | custom-call | flops 2147483648 | bytes 8388608 | tf_op jit(solution)/shard_map/pallas_call | solution.py:289
  45.7 4.8 %shard_map.143 = (f32[2,512]{1,0:T(2,128)S(1)}, bf16[1536,1024]{1,0:T(8,128)(2,1)S(1)}, bf16[16,128]{1,0:T(8,128)(2,1)S(1)}) custom-call(bf16[96,1024]{1,0:T(8,128)(2,1)S(1)} %collective-permute-done.8.refs_0_, bf16[96,1024]{1,0:T(8,128)(2,1)S(1)} %collective-permute-done.12.refs_1_, ...), custom_call_target="tpu_custom_call", output_to_operand_aliasing={{1}: (6, {})} | custom-call | flops 3221225472 | bytes 7864320 | tf_op jit(solution)/shard_map/pallas_call | solution.py:362
  51.0 2.1 %shard_map.144 = bf16[16,128]{1,0:T(8,128)(2,1)S(1)} custom-call(f32[2,512]{1,0:T(2,128)S(1)} %get-tuple-element.50.means_ref, bf16[1536,1024]{1,0:T(8,128)(2,1)S(1)} %get-tuple-element.51.weights, bf16[512,1536]{1,0:T(8,128)(2,1)S(1)} %collective-permute-done.18.tiles_ref), custom_call_target="tpu_custom_call" | custom-call | flops 1610612736 | bytes 4718592 | tf_op jit(solution)/shard_map/pallas_call | solution.py:412
  54.6 2.2 %collective-permute-done.19.pair_ref = bf16[16,128]{1,0:T(8,128)(2,1)S(1)} collective-permute-done((bf16[16,128]{1,0:T(8,128)(2,1)S(1)}, bf16[16,128]{1,0:T(8,128)(2,1)S(1)}, u32[]{:S(2)}, u32[]{:S(2)}) %collective-permute-start.19) | collective-permute-done | bytes 4128 | tf_op jit(solution)/shard_map/ppermute | solution.py:705
  56.8 1.9 %shard_map.145 = (bf16[4,1024]{1,0:T(4,128)(2,1)}, f32[8,768]{1,0:T(8,128)S(1)}, bf16[8,16,256]{2,1,0:T(8,128)(2,1)}) custom-call(s32[8]{0:T(128)S(1)} %copy-done.3, bf16[16,128]{1,0:T(8,128)(2,1)S(1)} %get-tuple-element.49.own_ref, bf16[16,128]{1,0:T(8,128)(2,1)S(1)} %collective-permute-done.17.own_far_ref, ...), custom_call_target="tpu_custom_call" | custom-call | tf_op jit(solution)/shard_map/pallas_call | solution.py:711
  58.7 4.0 %all-to-all-start = ((bf16[8,16,256]{2,1,0:T(8,128)(2,1)}), bf16[8,16,256]{2,1,0:T(8,128)(2,1)S(1)}, u32[]{:S(2)}, u32[]{:S(2)}) async-start(bf16[8,16,256]{2,1,0:T(8,128)(2,1)} %get-tuple-element.53), calls=%async_computation | async-start | bytes 131072 | tf_op jit(solution)/shard_map/all_to_all | solution.py:722
  62.7 2.3 %shard_map.146 = (bf16[96,768]{1,0:T(8,128)(2,1)S(1)}, f32[96,32]{1,0:T(8,128)S(1)}, bf16[768,384]{1,0:T(8,128)(2,1)S(1)}, bf16[768,384]{1,0:T(8,128)(2,1)S(1)},...) custom-call(f32[8,768]{1,0:T(8,128)S(1)} %get-tuple-element.54.mixed, ...), custom_call_target="tpu_custom_call" | custom-call | tf_op jit(solution)/shard_map/pallas_call | solution.py:726
  65.0 4.6 %all-to-all-done.sent_ref = bf16[8,16,256]{2,1,0:T(8,128)(2,1)S(1)} async-done(((bf16[8,16,256]{2,1,0:T(8,128)(2,1)}), bf16[8,16,256]{2,1,0:T(8,128)(2,1)S(1)}, u32[]{:S(2)}, u32[]{:S(2)}) %all-to-all-start) | async-done | bytes 65568 | tf_op jit(solution)/shard_map/all_to_all | solution.py:722
  69.6 2.1 %shard_map.147 = bf16[4,384]{1,0:T(4,128)(2,1)} custom-call(s32[8]{0:T(128)S(1)} %copy-done.3, bf16[8,16,256]{2,1,0:T(8,128)(2,1)S(1)} %all-to-all-done.sent_ref, f32[8,768]{1,0:T(8,128)S(1)} %get-tuple-element.54.mixed_ref, bf16[96,768]{1,0:T(8,128)(2,1)S(1)} %get-tuple-element.56.query_ref, bf16[768,384]{1,0:T(8,128)(2,1)S(1)} %get-tuple-element.57.wk_ref, ...), custom_call_target="tpu_custom_call" | custom-call | tf_op jit(solution)/shard_map/pallas_call | solution.py:741
  (66 shorter events, 7.7 us)
Async XLA Ops:
  4.4 35.8 %copy-start.6 = (bf16[96,1024]{1,0:T(8,128)(2,1)}, bf16[96,1024]{1,0:T(8,128)(2,1)S(1)}, u32[]{:S(2)}) copy-start(bf16[96,1024]{1,0:T(8,128)(2,1)S(1)} %get-tuple-element.33.refs_0_) | copy-start | bytes 589828
  4.5 7.6 %collective-permute-start.4 = (bf16[512,1536]{1,0:T(8,128)(2,1)S(1)}, bf16[512,1536]{1,0:T(8,128)(2,1)S(1)}, u32[]{:S(2)}, u32[]{:S(2)}) collective-permute-start(bf16[512,1536]{1,0:T(8,128)(2,1)S(1)} %get-tuple-element.44.refs_12_), channel_id=1, source_target_pairs={{0,1},{1,0},{2,3},{3,2},{4,5},{5,4},{6,7},{7,6},{8,9},{9,8},{10,11... | collective-permute-start | bytes 4718600 | tf_op jit(solution)/shard_map/ppermute | solution.py:652
  5.0 7.1 %collective-permute-start.3 = (bf16[1024,768]{1,0:T(8,128)(2,1)S(1)}, bf16[1024,768]{1,0:T(8,128)(2,1)S(1)}, u32[]{:S(2)}, u32[]{:S(2)}) collective-permute-start(bf16[1024,768]{1,0:T(8,128)(2,1)S(1)} %copy-done), channel_id=1, source_target_pairs={{0,1},{1,0},{2,3},{3,2},{4,5},{5,4},{6,7},{7,6},{8,9},{9,8},{10,11... | collective-permute-start | bytes 4718600 | tf_op jit(solution)/shard_map/ppermute | solution.py:654
  5.1 40.5 %collective-permute-start.15 = (bf16[512,1536]{1,0:T(8,128)(2,1)S(1)}, bf16[512,1536]{1,0:T(8,128)(2,1)S(1)}, u32[]{:S(2)}, u32[]{:S(2)}) collective-permute-start(bf16[512,1536]{1,0:T(8,128)(2,1)S(1)} %get-tuple-element.44.refs_12_), channel_id=1, source_target_pairs={{0,16},{16,0},{1,17},{17,1},{2,18},{18,2},{3,19},{19,3},{4,20},{20... | collective-permute-start | bytes 4718600 | tf_op jit(solution)/shard_map/ppermute | solution.py:653
  8.0 7.8 %collective-permute-start.1 = (bf16[96,1024]{1,0:T(8,128)(2,1)S(1)}, bf16[96,1024]{1,0:T(8,128)(2,1)S(1)}, u32[]{:S(2)}, u32[]{:S(2)}) collective-permute-start(bf16[96,1024]{1,0:T(8,128)(2,1)S(1)} %get-tuple-element.33.refs_0_), channel_id=1, source_target_pairs={{0,2},{2,0},{4,6},{6,4},{8,10},{10,8},{12,14},{14,12},{1,3},{3,1},... | collective-permute-start | bytes 589832 | tf_op jit(solution)/shard_map/ppermute | solution.py:686
  9.5 6.6 %collective-permute-start = (bf16[96,1024]{1,0:T(8,128)(2,1)S(1)}, bf16[96,1024]{1,0:T(8,128)(2,1)S(1)}, u32[]{:S(2)}, u32[]{:S(2)}) collective-permute-start(bf16[96,1024]{1,0:T(8,128)(2,1)S(1)} %get-tuple-element.33.refs_0_), channel_id=1, source_target_pairs={{0,8},{2,10},{8,12},{10,14},{12,4},{14,6},{4,0},{6,2},{1,9},{3,11}... | collective-permute-start | bytes 589832 | tf_op jit(solution)/shard_map/ppermute | solution.py:675
  12.1 7.9 %collective-permute-start.6 = (bf16[96,1024]{1,0:T(8,128)(2,1)S(1)}, bf16[96,1024]{1,0:T(8,128)(2,1)S(1)}, u32[]{:S(2)}, u32[]{:S(2)}) collective-permute-start(bf16[96,1024]{1,0:T(8,128)(2,1)S(1)} %get-tuple-element.37.refs_1_), channel_id=1, source_target_pairs={{0,2},{2,0},{4,6},{6,4},{8,10},{10,8},{12,14},{14,12},{1,3},{3,1},... | collective-permute-start | bytes 589832 | tf_op jit(solution)/shard_map/ppermute | solution.py:686
  13.2 7.9 %collective-permute-start.5 = (bf16[96,1024]{1,0:T(8,128)(2,1)S(1)}, bf16[96,1024]{1,0:T(8,128)(2,1)S(1)}, u32[]{:S(2)}, u32[]{:S(2)}) collective-permute-start(bf16[96,1024]{1,0:T(8,128)(2,1)S(1)} %get-tuple-element.37.refs_1_), channel_id=1, source_target_pairs={{0,8},{2,10},{8,12},{10,14},{12,4},{14,6},{4,0},{6,2},{1,9},{3,11}... | collective-permute-start | bytes 589832 | tf_op jit(solution)/shard_map/ppermute | solution.py:675
  16.1 8.7 %collective-permute-start.7 = (bf16[96,1024]{1,0:T(8,128)(2,1)S(1)}, bf16[96,1024]{1,0:T(8,128)(2,1)S(1)}, u32[]{:S(2)}, u32[]{:S(2)}) collective-permute-start(bf16[96,1024]{1,0:T(8,128)(2,1)S(1)} %collective-permute-done.refs_4_), channel_id=1, source_target_pairs={{0,2},{2,0},{4,6},{6,4},{8,10},{10,8},{12,14},{14,12},{1,3},{3,1},... | collective-permute-start | bytes 589832 | tf_op jit(solution)/shard_map/ppermute | solution.py:686
  16.7 8.7 %collective-permute-start.2 = (bf16[96,1024]{1,0:T(8,128)(2,1)S(1)}, bf16[96,1024]{1,0:T(8,128)(2,1)S(1)}, u32[]{:S(2)}, u32[]{:S(2)}) collective-permute-start(bf16[96,1024]{1,0:T(8,128)(2,1)S(1)} %collective-permute-done.refs_4_), channel_id=1, source_target_pairs={{0,8},{2,10},{8,12},{10,14},{12,4},{14,6},{4,0},{6,2},{1,9},{3,11}... | collective-permute-start | bytes 589832 | tf_op jit(solution)/shard_map/ppermute | solution.py:675
  21.0 7.7 %collective-permute-start.10 = (bf16[96,1024]{1,0:T(8,128)(2,1)S(1)}, bf16[96,1024]{1,0:T(8,128)(2,1)S(1)}, u32[]{:S(2)}, u32[]{:S(2)}) collective-permute-start(bf16[96,1024]{1,0:T(8,128)(2,1)S(1)} %collective-permute-done.5.refs_5_), channel_id=1, source_target_pairs={{0,2},{2,0},{4,6},{6,4},{8,10},{10,8},{12,14},{14,12},{1,3},{3,1},... | collective-permute-start | bytes 589832 | tf_op jit(solution)/shard_map/ppermute | solution.py:686
  21.6 8.6 %collective-permute-start.9 = (bf16[96,1024]{1,0:T(8,128)(2,1)S(1)}, bf16[96,1024]{1,0:T(8,128)(2,1)S(1)}, u32[]{:S(2)}, u32[]{:S(2)}) collective-permute-start(bf16[96,1024]{1,0:T(8,128)(2,1)S(1)} %collective-permute-done.5.refs_5_), channel_id=1, source_target_pairs={{0,8},{2,10},{8,12},{10,14},{12,4},{14,6},{4,0},{6,2},{1,9},{3,11}... | collective-permute-start | bytes 589832 | tf_op jit(solution)/shard_map/ppermute | solution.py:675
  25.4 8.6 %collective-permute-start.11 = (bf16[96,1024]{1,0:T(8,128)(2,1)S(1)}, bf16[96,1024]{1,0:T(8,128)(2,1)S(1)}, u32[]{:S(2)}, u32[]{:S(2)}) collective-permute-start(bf16[96,1024]{1,0:T(8,128)(2,1)S(1)} %collective-permute-done.2.refs_8_), channel_id=1, source_target_pairs={{0,2},{2,0},{4,6},{6,4},{8,10},{10,8},{12,14},{14,12},{1,3},{3,1},... | collective-permute-start | bytes 589832 | tf_op jit(solution)/shard_map/ppermute | solution.py:686
  26.5 8.1 %collective-permute-start.8 = (bf16[96,1024]{1,0:T(8,128)(2,1)S(1)}, bf16[96,1024]{1,0:T(8,128)(2,1)S(1)}, u32[]{:S(2)}, u32[]{:S(2)}) collective-permute-start(bf16[96,1024]{1,0:T(8,128)(2,1)S(1)} %collective-permute-done.2.refs_8_), channel_id=1, source_target_pairs={{0,8},{2,10},{8,12},{10,14},{12,4},{14,6},{4,0},{6,2},{1,9},{3,11}... | collective-permute-start | bytes 589832 | tf_op jit(solution)/shard_map/ppermute | solution.py:675
  30.2 7.8 %collective-permute-start.12 = (bf16[96,1024]{1,0:T(8,128)(2,1)S(1)}, bf16[96,1024]{1,0:T(8,128)(2,1)S(1)}, u32[]{:S(2)}, u32[]{:S(2)}) collective-permute-start(bf16[96,1024]{1,0:T(8,128)(2,1)S(1)} %collective-permute-done.9.refs_9_), channel_id=1, source_target_pairs={{0,8},{2,10},{8,12},{10,14},{12,4},{14,6},{4,0},{6,2},{1,9},{3,11}... | collective-permute-start | bytes 589832 | tf_op jit(solution)/shard_map/ppermute | solution.py:675
  33.5 6.7 %collective-permute-start.16 = (bf16[96,1024]{1,0:T(8,128)(2,1)S(1)}, bf16[96,1024]{1,0:T(8,128)(2,1)S(1)}, u32[]{:S(2)}, u32[]{:S(2)}) collective-permute-start(bf16[96,1024]{1,0:T(8,128)(2,1)S(1)} %collective-permute-done.9.refs_9_), channel_id=1, source_target_pairs={{0,2},{2,0},{4,6},{6,4},{8,10},{10,8},{12,14},{14,12},{1,3},{3,1},... | collective-permute-start | bytes 589832 | tf_op jit(solution)/shard_map/ppermute | solution.py:686
  33.9 28.8 %collective-permute-start.21 = (bf16[2688,384]{1,0:T(8,128)(2,1)S(1)}, bf16[2688,384]{1,0:T(8,128)(2,1)}, u32[]{:S(2)}, u32[]{:S(2)}) collective-permute-start(bf16[2688,384]{1,0:T(8,128)(2,1)S(1)} %get-tuple-element.55), channel_id=1, source_target_pairs={{0,1},{1,0},{2,3},{3,2},{4,5},{5,4},{6,7},{7,6},{8,9},{9,8},{10,11... | collective-permute-start | bytes 6193160 | tf_op jit(solution)/shard_map/ppermute | solution.py:655
  34.7 10.9 %collective-permute-start.13 = (bf16[96,1024]{1,0:T(8,128)(2,1)S(1)}, bf16[96,1024]{1,0:T(8,128)(2,1)S(1)}, u32[]{:S(2)}, u32[]{:S(2)}) collective-permute-start(bf16[96,1024]{1,0:T(8,128)(2,1)S(1)} %collective-permute-done.11.refs_10_), channel_id=1, source_target_pairs={{0,8},{2,10},{8,12},{10,14},{12,4},{14,6},{4,0},{6,2},{1,9},{3,11}... | collective-permute-start | bytes 589832 | tf_op jit(solution)/shard_map/ppermute | solution.py:684
  38.0 7.6 %collective-permute-start.14 = (bf16[96,1024]{1,0:T(8,128)(2,1)S(1)}, bf16[96,1024]{1,0:T(8,128)(2,1)S(1)}, u32[]{:S(2)}, u32[]{:S(2)}) collective-permute-start(bf16[96,1024]{1,0:T(8,128)(2,1)S(1)} %collective-permute-done.12.refs_1_), channel_id=1, source_target_pairs={{0,2},{2,0},{4,6},{6,4},{8,10},{10,8},{12,14},{14,12},{1,3},{3,1},... | collective-permute-start | bytes 589832 | tf_op jit(solution)/shard_map/ppermute | solution.py:686
  45.6 5.4 %collective-permute-start.18 = (bf16[512,1536]{1,0:T(8,128)(2,1)S(1)}, bf16[512,1536]{1,0:T(8,128)(2,1)S(1)}, u32[]{:S(2)}, u32[]{:S(2)}) collective-permute-start(bf16[512,1536]{1,0:T(8,128)(2,1)S(1)} %collective-permute-done.15.refs_4_), channel_id=1, source_target_pairs={{0,1},{1,0},{2,3},{3,2},{4,5},{5,4},{6,7},{7,6},{8,9},{9,8},{10,11... | collective-permute-start | bytes 4718600 | tf_op jit(solution)/shard_map/ppermute | solution.py:695
  50.5 4.1 %collective-permute-start.17 = (bf16[16,128]{1,0:T(8,128)(2,1)S(1)}, bf16[16,128]{1,0:T(8,128)(2,1)S(1)}, u32[]{:S(2)}, u32[]{:S(2)}) collective-permute-start(bf16[16,128]{1,0:T(8,128)(2,1)S(1)} %get-tuple-element.49.own_ref), channel_id=1, source_target_pairs={{0,1},{1,0},{2,3},{3,2},{4,5},{5,4},{6,7},{7,6},{8,9},{9,8},{10,11... | collective-permute-start | bytes 12296 | tf_op jit(solution)/shard_map/ppermute | solution.py:699
  53.0 3.7 %collective-permute-start.19 = (bf16[16,128]{1,0:T(8,128)(2,1)S(1)}, bf16[16,128]{1,0:T(8,128)(2,1)S(1)}, u32[]{:S(2)}, u32[]{:S(2)}) collective-permute-start(bf16[16,128]{1,0:T(8,128)(2,1)S(1)} %shard_map.144), channel_id=1, source_target_pairs={{0,16},{16,0},{1,17},{17,1},{2,18},{18,2},{3,19},{19,3},{4,20},{20... | collective-permute-start | bytes 12296 | tf_op jit(solution)/shard_map/ppermute | solution.py:705
  53.7 3.1 %collective-permute-start.20 = (bf16[16,128]{1,0:T(8,128)(2,1)S(1)}, bf16[16,128]{1,0:T(8,128)(2,1)S(1)}, u32[]{:S(2)}, u32[]{:S(2)}) collective-permute-start(bf16[16,128]{1,0:T(8,128)(2,1)S(1)} %shard_map.144), channel_id=1, source_target_pairs={{0,17},{1,16},{16,1},{17,0},{2,19},{3,18},{18,3},{19,2},{4,21},{5,... | collective-permute-start | bytes 12296 | tf_op jit(solution)/shard_map/ppermute | solution.py:704
  58.7 10.9 %all-to-all-start = ((bf16[8,16,256]{2,1,0:T(8,128)(2,1)}), bf16[8,16,256]{2,1,0:T(8,128)(2,1)S(1)}, u32[]{:S(2)}, u32[]{:S(2)}) async-start(bf16[8,16,256]{2,1,0:T(8,128)(2,1)} %get-tuple-element.53), calls=%async_computation | async-start | bytes 131072 | tf_op jit(solution)/shard_map/all_to_all | solution.py:722
  (17 other events, 304.1 us)

commit v15 on v14

--- a/solution.py
+++ b/solution.py
@@ -12,9 +12,9 @@
 EPSILON = 1e-06
 FLOOR = -1e30
 QROWS = 8
-NORM_ROWS = 16
+NORM_ROWS = 32
 NORM_PIECE = 128
-NORM_UNROLL = 8
+NORM_UNROLL = 4
 LANES = 128
 UNIT_ROWS = 16
 ROW_TILE = 16
@@ -288,7 +288,7 @@
     vmem = pl.BlockSpec(memory_space=pltpu.VMEM)
     return pl.pallas_call(
         functools.partial(early_kernel, layout),
-        in_specs=[hbm] * len(blocks) + [pl.BlockSpec(memory_space=pl.ANY)] * 2,
+        in_specs=[hbm] * (len(blocks) - 4) + [pl.BlockSpec(memory_space=pl.ANY)] * 6,
         out_specs=(vmem, vmem, vmem),
         out_shape=(
             pltpu.VMEM((2, n_rows, cols), jnp.float32),
@@ -305,7 +305,7 @@
             bytes_accessed=2 * layout.early * (cols + 2 * n_rows) + 8 * n_rows * cols,
             transcendentals=0,
         ),
-    )(*in_hbm(*blocks), *tiles)
+    )(*in_hbm(*blocks[:-4]), *blocks[-4:], *tiles)
 
 
 def packed(mine, others):

time: 71.9 us -> 71.9 us (level)
  starting transfers between devices: 36.6 us -> 37.4 us
    all_to_all x1, starting transfers between devices: 4.01 us -> 4.84 us  [on_device(): sent = lax.all_to_all(sent, 'dev', split_axis=0, concat_axis=0, tiled=True)]
  transfers between devices with their start and end apart: 23 -> 23, of which waited for: 9 -> 9; matrix products, arithmetic and copies ran while one was open for 0% -> 0% of each run, Pallas kernels for 23% -> 22%
where the time goes in v15:
time: 71.9 us; the launch traced here: 71.6 us
  starting transfers between devices  37.4 us (52%)
  Pallas kernels  21.9 us (30%)
  waiting for transfers between devices  11.3 us (16%)
  between operations  0.87 us (1%)
    ppermute x6, starting transfers between devices, on_device(): arrived = lax.ppermute(held[part], 'dev', along_z)  17.3 us
    ppermute x7, starting transfers between devices, on_device(): sent.append(lax.ppermute(held[part], 'dev', along_y))  6.59 us
    all_to_all x1, starting transfers between devices, on_device(): sent = lax.all_to_all(sent, 'dev', split_axis=0, concat_axis=0, tiled=True)  4.84 us
    pallas_call x1, Pallas kernels, middle_mlp(): pl.pallas_call(functools.partial(middle_kernel, layout, length, len(block...  4.8 us
    all_to_all x1, waiting for transfers between devices, on_device(): sent = lax.all_to_all(sent, 'dev', split_axis=0, concat_axis=0, tiled=True)  4.6 us
    pallas_call x1, Pallas kernels, early_mlp(): pl.pallas_call(functools.partial(early_kernel, layout), in_specs=[hbm] *...  4.33 us
    pallas_call x1, Pallas kernels, start_work(): pl.pallas_call(functools.partial(start_kernel, parts), in_specs=[hbm] * (...  3.79 us
    ppermute x6, waiting for transfers between devices, on_device(): arrived = lax.ppermute(held[part], 'dev', along_z)  3.57 us
  transfers between devices with their start and end apart: 23, of which 9 were waited for; matrix products, arithmetic and copies ran while one was open for 0% of the time, Pallas kernels for 22%

profile of v15, /device:TPU:0, one launch (start us, length us, event | category | flops | bytes accessed | tf_op | source)
XLA Modules:
  0.0 71.6 jit_solution(12611961120415977673)
XLA Ops:
  0.7 3.8 %shard_map.140 = (bf16[512,1536]{1,0:T(8,128)(2,1)S(1)}, bf16[2688,384]{1,0:T(8,128)(2,1)S(1)}, bf16[96,1024]{1,0:T(8,128)(2,1)S(1)}, bf16[96,1024]{1,0:T(8,128)(2,1)S(1)}) custom-call(bf16[4,256,1536]{2,1,0:T(8,128)(2,1)} %refs_0_.2, f32[1536]{0:T(1024)} %refs_1_.2, bf16[192,1024]{1,0:T(8,128)(2,1)} %refs_2_.2, bf16[192,1024]{1,0:T(8,128)(2,1)} %refs_3_.2, ...), custom_call_target="tpu_custom_call" | custom-call | tf_op jit(solution)/shard_map/pallas_call | solution.py:145
  5.1 2.9 %collective-permute-start.15 = (bf16[512,1536]{1,0:T(8,128)(2,1)S(1)}, bf16[512,1536]{1,0:T(8,128)(2,1)S(1)}, u32[]{:S(2)}, u32[]{:S(2)}) collective-permute-start(bf16[512,1536]{1,0:T(8,128)(2,1)S(1)} %get-tuple-element.44.refs_12_), channel_id=1, source_target_pairs={{0,16},{16,0},{1,17},{17,1},{2,18},{18,2},{3,19},{19,3},{4,20},{20... | collective-permute-start | bytes 4718600 | tf_op jit(solution)/shard_map/ppermute | solution.py:653
  8.0 1.5 %collective-permute-start.1 = (bf16[96,1024]{1,0:T(8,128)(2,1)S(1)}, bf16[96,1024]{1,0:T(8,128)(2,1)S(1)}, u32[]{:S(2)}, u32[]{:S(2)}) collective-permute-start(bf16[96,1024]{1,0:T(8,128)(2,1)S(1)} %get-tuple-element.33.refs_0_), channel_id=1, source_target_pairs={{0,2},{2,0},{4,6},{6,4},{8,10},{10,8},{12,14},{14,12},{1,3},{3,1},... | collective-permute-start | bytes 589832 | tf_op jit(solution)/shard_map/ppermute | solution.py:686
  9.5 2.6 %collective-permute-start = (bf16[96,1024]{1,0:T(8,128)(2,1)S(1)}, bf16[96,1024]{1,0:T(8,128)(2,1)S(1)}, u32[]{:S(2)}, u32[]{:S(2)}) collective-permute-start(bf16[96,1024]{1,0:T(8,128)(2,1)S(1)} %get-tuple-element.33.refs_0_), channel_id=1, source_target_pairs={{0,8},{2,10},{8,12},{10,14},{12,4},{14,6},{4,0},{6,2},{1,9},{3,11}... | collective-permute-start | bytes 589832 | tf_op jit(solution)/shard_map/ppermute | solution.py:675
  12.1 1.1 %collective-permute-start.6 = (bf16[96,1024]{1,0:T(8,128)(2,1)S(1)}, bf16[96,1024]{1,0:T(8,128)(2,1)S(1)}, u32[]{:S(2)}, u32[]{:S(2)}) collective-permute-start(bf16[96,1024]{1,0:T(8,128)(2,1)S(1)} %get-tuple-element.37.refs_1_), channel_id=1, source_target_pairs={{0,2},{2,0},{4,6},{6,4},{8,10},{10,8},{12,14},{14,12},{1,3},{3,1},... | collective-permute-start | bytes 589832 | tf_op jit(solution)/shard_map/ppermute | solution.py:686
  13.2 2.6 %collective-permute-start.5 = (bf16[96,1024]{1,0:T(8,128)(2,1)S(1)}, bf16[96,1024]{1,0:T(8,128)(2,1)S(1)}, u32[]{:S(2)}, u32[]{:S(2)}) collective-permute-start(bf16[96,1024]{1,0:T(8,128)(2,1)S(1)} %get-tuple-element.37.refs_1_), channel_id=1, source_target_pairs={{0,8},{2,10},{8,12},{10,14},{12,4},{14,6},{4,0},{6,2},{1,9},{3,11}... | collective-permute-start | bytes 589832 | tf_op jit(solution)/shard_map/ppermute | solution.py:675
  16.7 3.3 %collective-permute-start.2 = (bf16[96,1024]{1,0:T(8,128)(2,1)S(1)}, bf16[96,1024]{1,0:T(8,128)(2,1)S(1)}, u32[]{:S(2)}, u32[]{:S(2)}) collective-permute-start(bf16[96,1024]{1,0:T(8,128)(2,1)S(1)} %collective-permute-done.refs_4_), channel_id=1, source_target_pairs={{0,8},{2,10},{8,12},{10,14},{12,4},{14,6},{4,0},{6,2},{1,9},{3,11}... | collective-permute-start | bytes 589832 | tf_op jit(solution)/shard_map/ppermute | solution.py:675
  20.0 1.1 %collective-permute-done.5.refs_5_ = bf16[96,1024]{1,0:T(8,128)(2,1)S(1)} collective-permute-done((bf16[96,1024]{1,0:T(8,128)(2,1)S(1)}, bf16[96,1024]{1,0:T(8,128)(2,1)S(1)}, u32[]{:S(2)}, u32[]{:S(2)}) %collective-permute-start.5) | collective-permute-done | bytes 196640 | tf_op jit(solution)/shard_map/ppermute | solution.py:675
  21.6 3.2 %collective-permute-start.9 = (bf16[96,1024]{1,0:T(8,128)(2,1)S(1)}, bf16[96,1024]{1,0:T(8,128)(2,1)S(1)}, u32[]{:S(2)}, u32[]{:S(2)}) collective-permute-start(bf16[96,1024]{1,0:T(8,128)(2,1)S(1)} %collective-permute-done.5.refs_5_), channel_id=1, source_target_pairs={{0,8},{2,10},{8,12},{10,14},{12,4},{14,6},{4,0},{6,2},{1,9},{3,11}... | collective-permute-start | bytes 589832 | tf_op jit(solution)/shard_map/ppermute | solution.py:675
  25.4 1.2 %collective-permute-start.11 = (bf16[96,1024]{1,0:T(8,128)(2,1)S(1)}, bf16[96,1024]{1,0:T(8,128)(2,1)S(1)}, u32[]{:S(2)}, u32[]{:S(2)}) collective-permute-start(bf16[96,1024]{1,0:T(8,128)(2,1)S(1)} %collective-permute-done.2.refs_8_), channel_id=1, source_target_pairs={{0,2},{2,0},{4,6},{6,4},{8,10},{10,8},{12,14},{14,12},{1,3},{3,1},... | collective-permute-start | bytes 589832 | tf_op jit(solution)/shard_map/ppermute | solution.py:686
  26.6 2.2 %collective-permute-start.8 = (bf16[96,1024]{1,0:T(8,128)(2,1)S(1)}, bf16[96,1024]{1,0:T(8,128)(2,1)S(1)}, u32[]{:S(2)}, u32[]{:S(2)}) collective-permute-start(bf16[96,1024]{1,0:T(8,128)(2,1)S(1)} %collective-permute-done.2.refs_8_), channel_id=1, source_target_pairs={{0,8},{2,10},{8,12},{10,14},{12,4},{14,6},{4,0},{6,2},{1,9},{3,11}... | collective-permute-start | bytes 589832 | tf_op jit(solution)/shard_map/ppermute | solution.py:675
  28.8 1.4 %collective-permute-done.9.refs_9_ = bf16[96,1024]{1,0:T(8,128)(2,1)S(1)} collective-permute-done((bf16[96,1024]{1,0:T(8,128)(2,1)S(1)}, bf16[96,1024]{1,0:T(8,128)(2,1)S(1)}, u32[]{:S(2)}, u32[]{:S(2)}) %collective-permute-start.9) | collective-permute-done | bytes 196640 | tf_op jit(solution)/shard_map/ppermute | solution.py:675
  30.2 3.4 %collective-permute-start.12 = (bf16[96,1024]{1,0:T(8,128)(2,1)S(1)}, bf16[96,1024]{1,0:T(8,128)(2,1)S(1)}, u32[]{:S(2)}, u32[]{:S(2)}) collective-permute-start(bf16[96,1024]{1,0:T(8,128)(2,1)S(1)} %collective-permute-done.9.refs_9_), channel_id=1, source_target_pairs={{0,8},{2,10},{8,12},{10,14},{12,4},{14,6},{4,0},{6,2},{1,9},{3,11}... | collective-permute-start | bytes 589832 | tf_op jit(solution)/shard_map/ppermute | solution.py:675
  34.7 3.1 %collective-permute-start.13 = (bf16[96,1024]{1,0:T(8,128)(2,1)S(1)}, bf16[96,1024]{1,0:T(8,128)(2,1)S(1)}, u32[]{:S(2)}, u32[]{:S(2)}) collective-permute-start(bf16[96,1024]{1,0:T(8,128)(2,1)S(1)} %collective-permute-done.11.refs_10_), channel_id=1, source_target_pairs={{0,8},{2,10},{8,12},{10,14},{12,4},{14,6},{4,0},{6,2},{1,9},{3,11}... | collective-permute-start | bytes 589832 | tf_op jit(solution)/shard_map/ppermute | solution.py:684
  38.0 1.4 %collective-permute-start.14 = (bf16[96,1024]{1,0:T(8,128)(2,1)S(1)}, bf16[96,1024]{1,0:T(8,128)(2,1)S(1)}, u32[]{:S(2)}, u32[]{:S(2)}) collective-permute-start(bf16[96,1024]{1,0:T(8,128)(2,1)S(1)} %collective-permute-done.12.refs_1_), channel_id=1, source_target_pairs={{0,2},{2,0},{4,6},{6,4},{8,10},{10,8},{12,14},{14,12},{1,3},{3,1},... | collective-permute-start | bytes 589832 | tf_op jit(solution)/shard_map/ppermute | solution.py:686
  40.3 4.3 %shard_map.142 = (f32[2,512,1024]{2,1,0:T(8,128)S(1)}, bf16[1536,1024]{1,0:T(8,128)(2,1)S(1)}, bf16[2,512,1536]{2,1,0:T(8,128)(2,1)S(1)}) custom-call(bf16[96,1024]{1,0:T(8,128)(2,1)} %copy-done.6, bf16[96,1024]{1,0:T(8,128)(2,1)} %copy-done.7, bf16[96,1024]{1,0:T(8,128)(2,1)} %copy-done.8, bf16[96,1024]{1,0:T(8,128)(2,1)} %copy-done.10, ...), custom_call_target="tpu_custom_call" | custom-call | flops 2147483648 | bytes 8388608 | tf_op jit(solution)/shard_map/pallas_call | solution.py:289
  44.8 4.8 %shard_map.143 = (f32[2,512]{1,0:T(2,128)S(1)}, bf16[1536,1024]{1,0:T(8,128)(2,1)S(1)}, bf16[16,128]{1,0:T(8,128)(2,1)S(1)}) custom-call(bf16[96,1024]{1,0:T(8,128)(2,1)S(1)} %collective-permute-done.8.refs_0_, bf16[96,1024]{1,0:T(8,128)(2,1)S(1)} %collective-permute-done.12.refs_1_, ...), custom_call_target="tpu_custom_call", output_to_operand_aliasing={{1}: (6, {})} | custom-call | flops 3221225472 | bytes 7864320 | tf_op jit(solution)/shard_map/pallas_call | solution.py:362
  50.1 2.1 %shard_map.144 = bf16[16,128]{1,0:T(8,128)(2,1)S(1)} custom-call(f32[2,512]{1,0:T(2,128)S(1)} %get-tuple-element.50.means_ref, bf16[1536,1024]{1,0:T(8,128)(2,1)S(1)} %get-tuple-element.51.weights, bf16[512,1536]{1,0:T(8,128)(2,1)S(1)} %collective-permute-done.18.tiles_ref), custom_call_target="tpu_custom_call" | custom-call | flops 1610612736 | bytes 4718592 | tf_op jit(solution)/shard_map/pallas_call | solution.py:412
  53.7 2.2 %collective-permute-done.19.pair_ref = bf16[16,128]{1,0:T(8,128)(2,1)S(1)} collective-permute-done((bf16[16,128]{1,0:T(8,128)(2,1)S(1)}, bf16[16,128]{1,0:T(8,128)(2,1)S(1)}, u32[]{:S(2)}, u32[]{:S(2)}) %collective-permute-start.19) | collective-permute-done | bytes 4128 | tf_op jit(solution)/shard_map/ppermute | solution.py:705
  55.9 1.9 %shard_map.145 = (bf16[4,1024]{1,0:T(4,128)(2,1)}, f32[8,768]{1,0:T(8,128)S(1)}, bf16[8,16,256]{2,1,0:T(8,128)(2,1)}) custom-call(s32[8]{0:T(128)S(1)} %copy-done.3, bf16[16,128]{1,0:T(8,128)(2,1)S(1)} %get-tuple-element.49.own_ref, bf16[16,128]{1,0:T(8,128)(2,1)S(1)} %collective-permute-done.17.own_far_ref, ...), custom_call_target="tpu_custom_call" | custom-call | tf_op jit(solution)/shard_map/pallas_call | solution.py:711
  57.8 4.8 %all-to-all-start = ((bf16[8,16,256]{2,1,0:T(8,128)(2,1)}), bf16[8,16,256]{2,1,0:T(8,128)(2,1)S(1)}, u32[]{:S(2)}, u32[]{:S(2)}) async-start(bf16[8,16,256]{2,1,0:T(8,128)(2,1)} %get-tuple-element.53), calls=%async_computation | async-start | bytes 131072 | tf_op jit(solution)/shard_map/all_to_all | solution.py:722
  62.6 2.3 %shard_map.146 = (bf16[96,768]{1,0:T(8,128)(2,1)S(1)}, f32[96,32]{1,0:T(8,128)S(1)}, bf16[768,384]{1,0:T(8,128)(2,1)S(1)}, bf16[768,384]{1,0:T(8,128)(2,1)S(1)},...) custom-call(f32[8,768]{1,0:T(8,128)S(1)} %get-tuple-element.54.mixed, ...), custom_call_target="tpu_custom_call" | custom-call | tf_op jit(solution)/shard_map/pallas_call | solution.py:726
  64.9 4.6 %all-to-all-done.sent_ref = bf16[8,16,256]{2,1,0:T(8,128)(2,1)S(1)} async-done(((bf16[8,16,256]{2,1,0:T(8,128)(2,1)}), bf16[8,16,256]{2,1,0:T(8,128)(2,1)S(1)}, u32[]{:S(2)}, u32[]{:S(2)}) %all-to-all-start) | async-done | bytes 65568 | tf_op jit(solution)/shard_map/all_to_all | solution.py:722
  69.5 2.1 %shard_map.147 = bf16[4,384]{1,0:T(4,128)(2,1)} custom-call(s32[8]{0:T(128)S(1)} %copy-done.3, bf16[8,16,256]{2,1,0:T(8,128)(2,1)S(1)} %all-to-all-done.sent_ref, f32[8,768]{1,0:T(8,128)S(1)} %get-tuple-element.54.mixed_ref, bf16[96,768]{1,0:T(8,128)(2,1)S(1)} %get-tuple-element.56.query_ref, bf16[768,384]{1,0:T(8,128)(2,1)S(1)} %get-tuple-element.57.wk_ref, ...), custom_call_target="tpu_custom_call" | custom-call | tf_op jit(solution)/shard_map/pallas_call | solution.py:741
  (58 shorter events, 7.0 us)
Async XLA Ops:
  4.5 35.8 %copy-start.6 = (bf16[96,1024]{1,0:T(8,128)(2,1)}, bf16[96,1024]{1,0:T(8,128)(2,1)S(1)}, u32[]{:S(2)}) copy-start(bf16[96,1024]{1,0:T(8,128)(2,1)S(1)} %get-tuple-element.33.refs_0_) | copy-start | bytes 589828
  4.5 7.6 %collective-permute-start.4 = (bf16[512,1536]{1,0:T(8,128)(2,1)S(1)}, bf16[512,1536]{1,0:T(8,128)(2,1)S(1)}, u32[]{:S(2)}, u32[]{:S(2)}) collective-permute-start(bf16[512,1536]{1,0:T(8,128)(2,1)S(1)} %get-tuple-element.44.refs_12_), channel_id=1, source_target_pairs={{0,1},{1,0},{2,3},{3,2},{4,5},{5,4},{6,7},{7,6},{8,9},{9,8},{10,11... | collective-permute-start | bytes 4718600 | tf_op jit(solution)/shard_map/ppermute | solution.py:652
  5.0 7.2 %collective-permute-start.3 = (bf16[1024,768]{1,0:T(8,128)(2,1)S(1)}, bf16[1024,768]{1,0:T(8,128)(2,1)S(1)}, u32[]{:S(2)}, u32[]{:S(2)}) collective-permute-start(bf16[1024,768]{1,0:T(8,128)(2,1)S(1)} %copy-done), channel_id=1, source_target_pairs={{0,1},{1,0},{2,3},{3,2},{4,5},{5,4},{6,7},{7,6},{8,9},{9,8},{10,11... | collective-permute-start | bytes 4718600 | tf_op jit(solution)/shard_map/ppermute | solution.py:654
  5.1 39.6 %collective-permute-start.15 = (bf16[512,1536]{1,0:T(8,128)(2,1)S(1)}, bf16[512,1536]{1,0:T(8,128)(2,1)S(1)}, u32[]{:S(2)}, u32[]{:S(2)}) collective-permute-start(bf16[512,1536]{1,0:T(8,128)(2,1)S(1)} %get-tuple-element.44.refs_12_), channel_id=1, source_target_pairs={{0,16},{16,0},{1,17},{17,1},{2,18},{18,2},{3,19},{19,3},{4,20},{20... | collective-permute-start | bytes 4718600 | tf_op jit(solution)/shard_map/ppermute | solution.py:653
  8.0 7.8 %collective-permute-start.1 = (bf16[96,1024]{1,0:T(8,128)(2,1)S(1)}, bf16[96,1024]{1,0:T(8,128)(2,1)S(1)}, u32[]{:S(2)}, u32[]{:S(2)}) collective-permute-start(bf16[96,1024]{1,0:T(8,128)(2,1)S(1)} %get-tuple-element.33.refs_0_), channel_id=1, source_target_pairs={{0,2},{2,0},{4,6},{6,4},{8,10},{10,8},{12,14},{14,12},{1,3},{3,1},... | collective-permute-start | bytes 589832 | tf_op jit(solution)/shard_map/ppermute | solution.py:686
  9.5 6.6 %collective-permute-start = (bf16[96,1024]{1,0:T(8,128)(2,1)S(1)}, bf16[96,1024]{1,0:T(8,128)(2,1)S(1)}, u32[]{:S(2)}, u32[]{:S(2)}) collective-permute-start(bf16[96,1024]{1,0:T(8,128)(2,1)S(1)} %get-tuple-element.33.refs_0_), channel_id=1, source_target_pairs={{0,8},{2,10},{8,12},{10,14},{12,4},{14,6},{4,0},{6,2},{1,9},{3,11}... | collective-permute-start | bytes 589832 | tf_op jit(solution)/shard_map/ppermute | solution.py:675
  12.1 7.9 %collective-permute-start.6 = (bf16[96,1024]{1,0:T(8,128)(2,1)S(1)}, bf16[96,1024]{1,0:T(8,128)(2,1)S(1)}, u32[]{:S(2)}, u32[]{:S(2)}) collective-permute-start(bf16[96,1024]{1,0:T(8,128)(2,1)S(1)} %get-tuple-element.37.refs_1_), channel_id=1, source_target_pairs={{0,2},{2,0},{4,6},{6,4},{8,10},{10,8},{12,14},{14,12},{1,3},{3,1},... | collective-permute-start | bytes 589832 | tf_op jit(solution)/shard_map/ppermute | solution.py:686
  13.2 7.9 %collective-permute-start.5 = (bf16[96,1024]{1,0:T(8,128)(2,1)S(1)}, bf16[96,1024]{1,0:T(8,128)(2,1)S(1)}, u32[]{:S(2)}, u32[]{:S(2)}) collective-permute-start(bf16[96,1024]{1,0:T(8,128)(2,1)S(1)} %get-tuple-element.37.refs_1_), channel_id=1, source_target_pairs={{0,8},{2,10},{8,12},{10,14},{12,4},{14,6},{4,0},{6,2},{1,9},{3,11}... | collective-permute-start | bytes 589832 | tf_op jit(solution)/shard_map/ppermute | solution.py:675
  16.1 8.7 %collective-permute-start.7 = (bf16[96,1024]{1,0:T(8,128)(2,1)S(1)}, bf16[96,1024]{1,0:T(8,128)(2,1)S(1)}, u32[]{:S(2)}, u32[]{:S(2)}) collective-permute-start(bf16[96,1024]{1,0:T(8,128)(2,1)S(1)} %collective-permute-done.refs_4_), channel_id=1, source_target_pairs={{0,2},{2,0},{4,6},{6,4},{8,10},{10,8},{12,14},{14,12},{1,3},{3,1},... | collective-permute-start | bytes 589832 | tf_op jit(solution)/shard_map/ppermute | solution.py:686
  16.7 8.7 %collective-permute-start.2 = (bf16[96,1024]{1,0:T(8,128)(2,1)S(1)}, bf16[96,1024]{1,0:T(8,128)(2,1)S(1)}, u32[]{:S(2)}, u32[]{:S(2)}) collective-permute-start(bf16[96,1024]{1,0:T(8,128)(2,1)S(1)} %collective-permute-done.refs_4_), channel_id=1, source_target_pairs={{0,8},{2,10},{8,12},{10,14},{12,4},{14,6},{4,0},{6,2},{1,9},{3,11}... | collective-permute-start | bytes 589832 | tf_op jit(solution)/shard_map/ppermute | solution.py:675
  21.1 7.7 %collective-permute-start.10 = (bf16[96,1024]{1,0:T(8,128)(2,1)S(1)}, bf16[96,1024]{1,0:T(8,128)(2,1)S(1)}, u32[]{:S(2)}, u32[]{:S(2)}) collective-permute-start(bf16[96,1024]{1,0:T(8,128)(2,1)S(1)} %collective-permute-done.5.refs_5_), channel_id=1, source_target_pairs={{0,2},{2,0},{4,6},{6,4},{8,10},{10,8},{12,14},{14,12},{1,3},{3,1},... | collective-permute-start | bytes 589832 | tf_op jit(solution)/shard_map/ppermute | solution.py:686
  21.6 8.6 %collective-permute-start.9 = (bf16[96,1024]{1,0:T(8,128)(2,1)S(1)}, bf16[96,1024]{1,0:T(8,128)(2,1)S(1)}, u32[]{:S(2)}, u32[]{:S(2)}) collective-permute-start(bf16[96,1024]{1,0:T(8,128)(2,1)S(1)} %collective-permute-done.5.refs_5_), channel_id=1, source_target_pairs={{0,8},{2,10},{8,12},{10,14},{12,4},{14,6},{4,0},{6,2},{1,9},{3,11}... | collective-permute-start | bytes 589832 | tf_op jit(solution)/shard_map/ppermute | solution.py:675
  25.4 8.6 %collective-permute-start.11 = (bf16[96,1024]{1,0:T(8,128)(2,1)S(1)}, bf16[96,1024]{1,0:T(8,128)(2,1)S(1)}, u32[]{:S(2)}, u32[]{:S(2)}) collective-permute-start(bf16[96,1024]{1,0:T(8,128)(2,1)S(1)} %collective-permute-done.2.refs_8_), channel_id=1, source_target_pairs={{0,2},{2,0},{4,6},{6,4},{8,10},{10,8},{12,14},{14,12},{1,3},{3,1},... | collective-permute-start | bytes 589832 | tf_op jit(solution)/shard_map/ppermute | solution.py:686
  26.6 8.1 %collective-permute-start.8 = (bf16[96,1024]{1,0:T(8,128)(2,1)S(1)}, bf16[96,1024]{1,0:T(8,128)(2,1)S(1)}, u32[]{:S(2)}, u32[]{:S(2)}) collective-permute-start(bf16[96,1024]{1,0:T(8,128)(2,1)S(1)} %collective-permute-done.2.refs_8_), channel_id=1, source_target_pairs={{0,8},{2,10},{8,12},{10,14},{12,4},{14,6},{4,0},{6,2},{1,9},{3,11}... | collective-permute-start | bytes 589832 | tf_op jit(solution)/shard_map/ppermute | solution.py:675
  30.2 7.8 %collective-permute-start.12 = (bf16[96,1024]{1,0:T(8,128)(2,1)S(1)}, bf16[96,1024]{1,0:T(8,128)(2,1)S(1)}, u32[]{:S(2)}, u32[]{:S(2)}) collective-permute-start(bf16[96,1024]{1,0:T(8,128)(2,1)S(1)} %collective-permute-done.9.refs_9_), channel_id=1, source_target_pairs={{0,8},{2,10},{8,12},{10,14},{12,4},{14,6},{4,0},{6,2},{1,9},{3,11}... | collective-permute-start | bytes 589832 | tf_op jit(solution)/shard_map/ppermute | solution.py:675
  33.6 6.7 %collective-permute-start.16 = (bf16[96,1024]{1,0:T(8,128)(2,1)S(1)}, bf16[96,1024]{1,0:T(8,128)(2,1)S(1)}, u32[]{:S(2)}, u32[]{:S(2)}) collective-permute-start(bf16[96,1024]{1,0:T(8,128)(2,1)S(1)} %collective-permute-done.9.refs_9_), channel_id=1, source_target_pairs={{0,2},{2,0},{4,6},{6,4},{8,10},{10,8},{12,14},{14,12},{1,3},{3,1},... | collective-permute-start | bytes 589832 | tf_op jit(solution)/shard_map/ppermute | solution.py:686
  33.9 28.7 %collective-permute-start.21 = (bf16[2688,384]{1,0:T(8,128)(2,1)S(1)}, bf16[2688,384]{1,0:T(8,128)(2,1)}, u32[]{:S(2)}, u32[]{:S(2)}) collective-permute-start(bf16[2688,384]{1,0:T(8,128)(2,1)S(1)} %get-tuple-element.55), channel_id=1, source_target_pairs={{0,1},{1,0},{2,3},{3,2},{4,5},{5,4},{6,7},{7,6},{8,9},{9,8},{10,11... | collective-permute-start | bytes 6193160 | tf_op jit(solution)/shard_map/ppermute | solution.py:655
  34.7 10.0 %collective-permute-start.13 = (bf16[96,1024]{1,0:T(8,128)(2,1)S(1)}, bf16[96,1024]{1,0:T(8,128)(2,1)S(1)}, u32[]{:S(2)}, u32[]{:S(2)}) collective-permute-start(bf16[96,1024]{1,0:T(8,128)(2,1)S(1)} %collective-permute-done.11.refs_10_), channel_id=1, source_target_pairs={{0,8},{2,10},{8,12},{10,14},{12,4},{14,6},{4,0},{6,2},{1,9},{3,11}... | collective-permute-start | bytes 589832 | tf_op jit(solution)/shard_map/ppermute | solution.py:684
  38.0 6.7 %collective-permute-start.14 = (bf16[96,1024]{1,0:T(8,128)(2,1)S(1)}, bf16[96,1024]{1,0:T(8,128)(2,1)S(1)}, u32[]{:S(2)}, u32[]{:S(2)}) collective-permute-start(bf16[96,1024]{1,0:T(8,128)(2,1)S(1)} %collective-permute-done.12.refs_1_), channel_id=1, source_target_pairs={{0,2},{2,0},{4,6},{6,4},{8,10},{10,8},{12,14},{14,12},{1,3},{3,1},... | collective-permute-start | bytes 589832 | tf_op jit(solution)/shard_map/ppermute | solution.py:686
  44.7 5.4 %collective-permute-start.18 = (bf16[512,1536]{1,0:T(8,128)(2,1)S(1)}, bf16[512,1536]{1,0:T(8,128)(2,1)S(1)}, u32[]{:S(2)}, u32[]{:S(2)}) collective-permute-start(bf16[512,1536]{1,0:T(8,128)(2,1)S(1)} %collective-permute-done.15.refs_4_), channel_id=1, source_target_pairs={{0,1},{1,0},{2,3},{3,2},{4,5},{5,4},{6,7},{7,6},{8,9},{9,8},{10,11... | collective-permute-start | bytes 4718600 | tf_op jit(solution)/shard_map/ppermute | solution.py:695
  49.6 4.1 %collective-permute-start.17 = (bf16[16,128]{1,0:T(8,128)(2,1)S(1)}, bf16[16,128]{1,0:T(8,128)(2,1)S(1)}, u32[]{:S(2)}, u32[]{:S(2)}) collective-permute-start(bf16[16,128]{1,0:T(8,128)(2,1)S(1)} %get-tuple-element.49.own_ref), channel_id=1, source_target_pairs={{0,1},{1,0},{2,3},{3,2},{4,5},{5,4},{6,7},{7,6},{8,9},{9,8},{10,11... | collective-permute-start | bytes 12296 | tf_op jit(solution)/shard_map/ppermute | solution.py:699
  52.2 3.7 %collective-permute-start.19 = (bf16[16,128]{1,0:T(8,128)(2,1)S(1)}, bf16[16,128]{1,0:T(8,128)(2,1)S(1)}, u32[]{:S(2)}, u32[]{:S(2)}) collective-permute-start(bf16[16,128]{1,0:T(8,128)(2,1)S(1)} %shard_map.144), channel_id=1, source_target_pairs={{0,16},{16,0},{1,17},{17,1},{2,18},{18,2},{3,19},{19,3},{4,20},{20... | collective-permute-start | bytes 12296 | tf_op jit(solution)/shard_map/ppermute | solution.py:705
  52.8 3.1 %collective-permute-start.20 = (bf16[16,128]{1,0:T(8,128)(2,1)S(1)}, bf16[16,128]{1,0:T(8,128)(2,1)S(1)}, u32[]{:S(2)}, u32[]{:S(2)}) collective-permute-start(bf16[16,128]{1,0:T(8,128)(2,1)S(1)} %shard_map.144), channel_id=1, source_target_pairs={{0,17},{1,16},{16,1},{17,0},{2,19},{3,18},{18,3},{19,2},{4,21},{5,... | collective-permute-start | bytes 12296 | tf_op jit(solution)/shard_map/ppermute | solution.py:704
  57.8 11.7 %all-to-all-start = ((bf16[8,16,256]{2,1,0:T(8,128)(2,1)}), bf16[8,16,256]{2,1,0:T(8,128)(2,1)S(1)}, u32[]{:S(2)}, u32[]{:S(2)}) async-start(bf16[8,16,256]{2,1,0:T(8,128)(2,1)} %get-tuple-element.53), calls=%async_computation | async-start | bytes 131072 | tf_op jit(solution)/shard_map/all_to_all | solution.py:722
  (13 other events, 271.0 us)

commit v16 on v15

--- a/solution.py
+++ b/solution.py
@@ -41,7 +41,7 @@
 
 def start_kernel(parts, *refs):
     tiles_ref, gain_ref, gate_ref, up_ref, *slide_refs = refs[:8]
-    out_ref, pack_ref, *block_refs = refs[8 : 10 + len(parts)]
+    out_ref, pack_ref, whole_ref, *block_refs = refs[8 : 11 + len(parts)]
     (
         rows,
         gain,
@@ -53,7 +53,7 @@
         block_sems,
         slide_sems,
         gain_sem,
-    ) = refs[10 + len(parts) :]
+    ) = refs[11 + len(parts) :]
     core = lax.axis_index("sub")
     pieces, piece = rows.shape[:2]
     half, length = tiles_ref.shape[0] // 2, tiles_ref.shape[1]
@@ -76,6 +76,8 @@
     for k, (part, block_ref) in enumerate(zip(parts, block_refs)):
         for i, ref in enumerate((gate_ref, up_ref)):
             selects.append((block_ref, i * half_cols, whole.at[i, part, columns]))
+    for i in range(2):
+        selects.append((whole_ref, i * half_cols, whole.at[i, :, columns]))
     cols = pack_ref.shape[1]
     others = pl.ds(pl.multiple_of((1 - core) * cols, LANES), cols)
     at = 0
@@ -145,10 +147,11 @@
     return pl.pallas_call(
         functools.partial(start_kernel, parts),
         in_specs=[hbm] * (4 + len(slide_weights)),
-        out_specs=[vmem] * (2 + len(parts)),
+        out_specs=[vmem] * (3 + len(parts)),
         out_shape=[
             pltpu.VMEM((half * length, width), jnp.bfloat16),
             pltpu.VMEM(pack, jnp.bfloat16),
+            pltpu.VMEM(gate_weight.shape, jnp.bfloat16),
             *[pltpu.VMEM((part.stop - part.start, cols), jnp.bfloat16) for part in parts],
         ],
         scratch_shapes=[
@@ -213,6 +216,10 @@
             copies.append(pltpu.make_async_copy(block, place, sems.at[k]))
         return copies
 
+    def halves(self, blocks):
+        n = len(self.parts)
+        return [*blocks[:n], *[blocks[n].at[part] for part in self.parts], *blocks[n + 1 :]]
+
     def row_copies(self, tiles_ref, rows, sems, steps):
         if not self.relative:
             return [pltpu.make_async_copy(tiles_ref, rows, sems.at[0])]
@@ -254,8 +261,8 @@
 
 def early_kernel(layout, *refs):
     steps = range(layout.early_steps)
-    n_blocks = len(steps) * layout.ny * len(layout.parts)
-    blocks, tile_refs = refs[:n_blocks], refs[n_blocks : n_blocks + 2]
+    n_blocks = len(steps) * layout.ny * len(layout.parts) - 1
+    blocks, tile_refs = layout.halves(refs[:n_blocks]), refs[n_blocks : n_blocks + 2]
     out_ref, weights, rows, weight_sems, row_sems = refs[n_blocks + 2 :]
     loads = layout.block_copies(blocks, weights, weight_sems)
     row_loads = [
@@ -296,7 +303,7 @@
             pltpu.VMEM((2, n_rows, layout.width), jnp.bfloat16),
         ),
         scratch_shapes=[
-            pltpu.SemaphoreType.DMA((len(blocks),)),
+            pltpu.SemaphoreType.DMA((len(blocks) + 1,)),
             pltpu.SemaphoreType.DMA((2, layout.nz)),
         ],
         compiler_params=pltpu.CompilerParams(vmem_limit_bytes=MLP_VMEM),
@@ -321,6 +328,8 @@
     early_refs = refs[n_blocks + n_tiles : -9]
     pair_ref, weights, own_ref, rows, even, odd, means, weight_sems, row_sems = refs[-9:]
     early = layout.early
+    if not early:
+        blocks = layout.halves(blocks)
     loads = layout.block_copies(blocks, weights, weight_sems, layout.nz)
     row_loads = [
         layout.row_copies(ref, rows.at[i], row_sems.at[i], range(layout.nz))
@@ -375,7 +384,7 @@
             pltpu.VMEM((length, cols), jnp.float32),
             pltpu.VMEM((length, cols), jnp.float32),
             pltpu.VMEM((3 * half, cols // 2), jnp.float32),
-            pltpu.SemaphoreType.DMA((len(blocks),)),
+            pltpu.SemaphoreType.DMA((len(blocks) + 1,)),
             pltpu.SemaphoreType.DMA((len(tiles), layout.nz)),
         ],
         compiler_params=pltpu.CompilerParams(vmem_limit_bytes=MLP_VMEM),
@@ -646,7 +655,7 @@
         (z * ny + y, ring[(i + 1) % nz] * ny + y) for i, z in enumerate(ring) for y in range(ny)
     ]
     slide_weights = [slide_wq, slide_wk, slide_wv, slide_wo]
-    first, pack, *held = start_work(
+    first, pack, whole, *held = start_work(
         tiles, tile_gain, gate_weight, up_weight, slide_weights, layout.parts
     )
     second = lax.ppermute(first, "sub", to_sibling)
@@ -674,21 +683,23 @@
             if step:
                 arrived = lax.ppermute(held[part], "dev", along_z)
                 others = [] if last is None else [last]
-                over = steps[-1][len(held) + part]
-                if (step, part) != (nz - 1, 1):
+                over = steps[-1][-1] if step == 1 else steps[-1][len(held) + part]
+                if (step, part) not in ((1, 0), (nz - 1, 1)):
                     others.append(over)
                 if (step, part) == (nz - 1, 0):
                     others += [many]
                 held[part] = last = after(arrived, *others)
             if (step, part) == (nz - 1, 0):
                 sent.append(lax.ppermute(after(over, last), "dev", along_z))
-            else:
+            elif step:
                 sent.append(lax.ppermute(held[part], "dev", along_y))
+        if step == 0:
+            sent.append(lax.ppermute(whole, "dev", along_y))
         steps.append([*held, *sent])
     blocks = [block for step in steps for block in step]
     early = []
     if layout.relative:
-        n_early = layout.early_steps * len(steps[0])
+        n_early = sum(len(step) for step in steps[: layout.early_steps])
         early = early_mlp(layout, blocks[:n_early], [after(first, last), second])
         blocks = blocks[n_early:]
     pair_first = after(pair_first, *steps[-1][-2:], *early)

time: 71.9 us -> 71.9 us (level)
    ppermute x0 -> x1, starting transfers between devices: none -> 1.52 us  [on_device(): sent.append(lax.ppermute(whole, 'dev', along_y))]
    ppermute x1, starting transfers between devices: 3.09 us -> 1.8 us  [on_device(): sent.append(lax.ppermute(after(over, last), 'dev', along_z))]
    ppermute x6, starting transfers between devices: 17.3 us -> 16 us  [on_device(): arrived = lax.ppermute(held[part], 'dev', along_z)]
    ppermute x7 -> x5, starting transfers between devices: 6.59 us -> 7.63 us  [on_device(): sent.append(lax.ppermute(held[part], 'dev', along_y))]
    ppermute x7 -> x5, waiting for transfers between devices: 0.91 us -> 0.15 us  [on_device(): sent.append(lax.ppermute(held[part], 'dev', along_y))]
  transfers between devices with their start and end apart: 23 -> 22, of which waited for: 9 -> 6; matrix products, arithmetic and copies ran while one was open for 0% -> 0% of each run, Pallas kernels for 22% -> 22%
where the time goes in v16:
time: 71.9 us; the launch traced here: 71.7 us
  starting transfers between devices  37.8 us (53%)
  Pallas kernels  21.9 us (30%)
  waiting for transfers between devices  11.1 us (15%)
  between operations  0.86 us (1%)
    ppermute x6, starting transfers between devices, on_device(): arrived = lax.ppermute(held[part], 'dev', along_z)  16 us
    ppermute x5, starting transfers between devices, on_device(): sent.append(lax.ppermute(held[part], 'dev', along_y))  7.63 us
    all_to_all x1, starting transfers between devices, on_device(): sent = lax.all_to_all(sent, 'dev', split_axis=0, concat_axis=0, tiled=True)  5.2 us
    pallas_call x1, Pallas kernels, middle_mlp(): pl.pallas_call(functools.partial(middle_kernel, layout, length, len(block...  4.76 us
    all_to_all x1, waiting for transfers between devices, on_device(): sent = lax.all_to_all(sent, 'dev', split_axis=0, concat_axis=0, tiled=True)  4.6 us
    pallas_call x1, Pallas kernels, early_mlp(): pl.pallas_call(functools.partial(early_kernel, layout), in_specs=[hbm] *...  4.33 us
    ppermute x6, waiting for transfers between devices, on_device(): arrived = lax.ppermute(held[part], 'dev', along_z)  4.12 us
    pallas_call x1, Pallas kernels, start_work(): pl.pallas_call(functools.partial(start_kernel, parts), in_specs=[hbm] * (...  3.83 us
  transfers between devices with their start and end apart: 22, of which 6 were waited for; matrix products, arithmetic and copies ran while one was open for 0% of the time, Pallas kernels for 22%

profile of v16, /device:TPU:0, one launch (start us, length us, event | category | flops | bytes accessed | tf_op | source)
XLA Modules:
  0.0 71.7 jit_solution(17194851350971731045)
XLA Ops:
  0.7 3.8 %shard_map.140 = (bf16[512,1536]{1,0:T(8,128)(2,1)S(1)}, bf16[2688,384]{1,0:T(8,128)(2,1)S(1)}, bf16[192,1024]{1,0:T(8,128)(2,1)S(1)}, bf16[96,1024]{1,0:T(8,128)(2,1)S(1)}, bf16[96,1024]{1,0:T(8,128)(2,1)S(1)}) custom-call(bf16[4,256,1536]{2,1,0:T(8,128)(2,1)} %refs_0_.2, f32[1536]{0:T(1024)} %refs_1_.2, bf16[192,1024]{1,0:T(8,128)(2,1)} %refs_2_.2, ...), custom_call_target="tpu_custom_call" | custom-call | tf_op jit(solution)/shard_map/pallas_call | solution.py:147
  5.1 2.9 %collective-permute-start.14 = (bf16[512,1536]{1,0:T(8,128)(2,1)S(1)}, bf16[512,1536]{1,0:T(8,128)(2,1)S(1)}, u32[]{:S(2)}, u32[]{:S(2)}) collective-permute-start(bf16[512,1536]{1,0:T(8,128)(2,1)S(1)} %get-tuple-element.44.refs_11_), channel_id=1, source_target_pairs={{0,16},{16,0},{1,17},{17,1},{2,18},{18,2},{3,19},{19,3},{4,20},{20... | collective-permute-start | bytes 4718600 | tf_op jit(solution)/shard_map/ppermute | solution.py:662
  8.0 1.5 %collective-permute-start.5 = (bf16[192,1024]{1,0:T(8,128)(2,1)S(1)}, bf16[192,1024]{1,0:T(8,128)(2,1)S(1)}, u32[]{:S(2)}, u32[]{:S(2)}) collective-permute-start(bf16[192,1024]{1,0:T(8,128)(2,1)S(1)} %get-tuple-element.37), channel_id=1, source_target_pairs={{0,2},{2,0},{4,6},{6,4},{8,10},{10,8},{12,14},{14,12},{1,3},{3,1},... | collective-permute-start | bytes 1179656 | tf_op jit(solution)/shard_map/ppermute | solution.py:697
  9.6 2.6 %collective-permute-start = (bf16[96,1024]{1,0:T(8,128)(2,1)S(1)}, bf16[96,1024]{1,0:T(8,128)(2,1)S(1)}, u32[]{:S(2)}, u32[]{:S(2)}) collective-permute-start(bf16[96,1024]{1,0:T(8,128)(2,1)S(1)} %get-tuple-element.33.refs_0_), channel_id=1, source_target_pairs={{0,8},{2,10},{8,12},{10,14},{12,4},{14,6},{4,0},{6,2},{1,9},{3,11}... | collective-permute-start | bytes 589832 | tf_op jit(solution)/shard_map/ppermute | solution.py:684
  12.2 2.1 %collective-permute-start.4 = (bf16[96,1024]{1,0:T(8,128)(2,1)S(1)}, bf16[96,1024]{1,0:T(8,128)(2,1)S(1)}, u32[]{:S(2)}, u32[]{:S(2)}) collective-permute-start(bf16[96,1024]{1,0:T(8,128)(2,1)S(1)} %get-tuple-element.36.refs_1_), channel_id=1, source_target_pairs={{0,8},{2,10},{8,12},{10,14},{12,4},{14,6},{4,0},{6,2},{1,9},{3,11}... | collective-permute-start | bytes 589832 | tf_op jit(solution)/shard_map/ppermute | solution.py:684
  14.3 3.1 %collective-permute-done.refs_3_ = bf16[96,1024]{1,0:T(8,128)(2,1)S(1)} collective-permute-done((bf16[96,1024]{1,0:T(8,128)(2,1)S(1)}, bf16[96,1024]{1,0:T(8,128)(2,1)S(1)}, u32[]{:S(2)}, u32[]{:S(2)}) %collective-permute-start) | collective-permute-done | bytes 196640 | tf_op jit(solution)/shard_map/ppermute | solution.py:684
  17.4 3.4 %collective-permute-start.1 = (bf16[96,1024]{1,0:T(8,128)(2,1)S(1)}, bf16[96,1024]{1,0:T(8,128)(2,1)S(1)}, u32[]{:S(2)}, u32[]{:S(2)}) collective-permute-start(bf16[96,1024]{1,0:T(8,128)(2,1)S(1)} %collective-permute-done.refs_3_), channel_id=1, source_target_pairs={{0,8},{2,10},{8,12},{10,14},{12,4},{14,6},{4,0},{6,2},{1,9},{3,11}... | collective-permute-start | bytes 589832 | tf_op jit(solution)/shard_map/ppermute | solution.py:684
  21.7 1.3 %collective-permute-start.9 = (bf16[96,1024]{1,0:T(8,128)(2,1)S(1)}, bf16[96,1024]{1,0:T(8,128)(2,1)S(1)}, u32[]{:S(2)}, u32[]{:S(2)}) collective-permute-start(bf16[96,1024]{1,0:T(8,128)(2,1)S(1)} %collective-permute-done.4.refs_4_), channel_id=1, source_target_pairs={{0,2},{2,0},{4,6},{6,4},{8,10},{10,8},{12,14},{14,12},{1,3},{3,1},... | collective-permute-start | bytes 589832 | tf_op jit(solution)/shard_map/ppermute | solution.py:695
  22.9 2.1 %collective-permute-start.8 = (bf16[96,1024]{1,0:T(8,128)(2,1)S(1)}, bf16[96,1024]{1,0:T(8,128)(2,1)S(1)}, u32[]{:S(2)}, u32[]{:S(2)}) collective-permute-start(bf16[96,1024]{1,0:T(8,128)(2,1)S(1)} %collective-permute-done.4.refs_4_), channel_id=1, source_target_pairs={{0,8},{2,10},{8,12},{10,14},{12,4},{14,6},{4,0},{6,2},{1,9},{3,11}... | collective-permute-start | bytes 589832 | tf_op jit(solution)/shard_map/ppermute | solution.py:684
  25.2 2.7 %collective-permute-start.10 = (bf16[96,1024]{1,0:T(8,128)(2,1)S(1)}, bf16[96,1024]{1,0:T(8,128)(2,1)S(1)}, u32[]{:S(2)}, u32[]{:S(2)}) collective-permute-start(bf16[96,1024]{1,0:T(8,128)(2,1)S(1)} %collective-permute-done.1.refs_7_), channel_id=1, source_target_pairs={{0,2},{2,0},{4,6},{6,4},{8,10},{10,8},{12,14},{14,12},{1,3},{3,1},... | collective-permute-start | bytes 589832 | tf_op jit(solution)/shard_map/ppermute | solution.py:695
  27.9 3.4 %collective-permute-start.7 = (bf16[96,1024]{1,0:T(8,128)(2,1)S(1)}, bf16[96,1024]{1,0:T(8,128)(2,1)S(1)}, u32[]{:S(2)}, u32[]{:S(2)}) collective-permute-start(bf16[96,1024]{1,0:T(8,128)(2,1)S(1)} %collective-permute-done.1.refs_7_), channel_id=1, source_target_pairs={{0,8},{2,10},{8,12},{10,14},{12,4},{14,6},{4,0},{6,2},{1,9},{3,11}... | collective-permute-start | bytes 589832 | tf_op jit(solution)/shard_map/ppermute | solution.py:684
  31.3 2.5 %collective-permute-start.11 = (bf16[96,1024]{1,0:T(8,128)(2,1)S(1)}, bf16[96,1024]{1,0:T(8,128)(2,1)S(1)}, u32[]{:S(2)}, u32[]{:S(2)}) collective-permute-start(bf16[96,1024]{1,0:T(8,128)(2,1)S(1)} %collective-permute-done.8.refs_8_), channel_id=1, source_target_pairs={{0,8},{2,10},{8,12},{10,14},{12,4},{14,6},{4,0},{6,2},{1,9},{3,11}... | collective-permute-start | bytes 589832 | tf_op jit(solution)/shard_map/ppermute | solution.py:684
  33.8 2.0 %collective-permute-start.15 = (bf16[96,1024]{1,0:T(8,128)(2,1)S(1)}, bf16[96,1024]{1,0:T(8,128)(2,1)S(1)}, u32[]{:S(2)}, u32[]{:S(2)}) collective-permute-start(bf16[96,1024]{1,0:T(8,128)(2,1)S(1)} %collective-permute-done.8.refs_8_), channel_id=1, source_target_pairs={{0,2},{2,0},{4,6},{6,4},{8,10},{10,8},{12,14},{14,12},{1,3},{3,1},... | collective-permute-start | bytes 589832 | tf_op jit(solution)/shard_map/ppermute | solution.py:695
  36.5 1.8 %collective-permute-start.12 = (bf16[96,1024]{1,0:T(8,128)(2,1)S(1)}, bf16[96,1024]{1,0:T(8,128)(2,1)S(1)}, u32[]{:S(2)}, u32[]{:S(2)}) collective-permute-start(bf16[96,1024]{1,0:T(8,128)(2,1)S(1)} %collective-permute-done.10.refs_9_), channel_id=1, source_target_pairs={{0,8},{2,10},{8,12},{10,14},{12,4},{14,6},{4,0},{6,2},{1,9},{3,11}... | collective-permute-start | bytes 589832 | tf_op jit(solution)/shard_map/ppermute | solution.py:693
  38.4 1.6 %collective-permute-start.13 = (bf16[96,1024]{1,0:T(8,128)(2,1)S(1)}, bf16[96,1024]{1,0:T(8,128)(2,1)S(1)}, u32[]{:S(2)}, u32[]{:S(2)}) collective-permute-start(bf16[96,1024]{1,0:T(8,128)(2,1)S(1)} %collective-permute-done.11.refs_1_), channel_id=1, source_target_pairs={{0,2},{2,0},{4,6},{6,4},{8,10},{10,8},{12,14},{14,12},{1,3},{3,1},... | collective-permute-start | bytes 589832 | tf_op jit(solution)/shard_map/ppermute | solution.py:695
  40.0 4.3 %shard_map.142 = (f32[2,512,1024]{2,1,0:T(8,128)S(1)}, bf16[1536,1024]{1,0:T(8,128)(2,1)S(1)}, bf16[2,512,1536]{2,1,0:T(8,128)(2,1)S(1)}) custom-call(bf16[96,1024]{1,0:T(8,128)(2,1)} %copy-done.6, bf16[96,1024]{1,0:T(8,128)(2,1)} %copy-done.7, bf16[192,1024]{1,0:T(8,128)(2,1)} %copy-done.8, bf16[96,1024]{1,0:T(8,128)(2,1)} %copy-done.9, ...), custom_call_target="tpu_custom_call" | custom-call | flops 2147483648 | bytes 8388608 | tf_op jit(solution)/shard_map/pallas_call | solution.py:296
  44.5 4.8 %shard_map.143 = (f32[2,512]{1,0:T(2,128)S(1)}, bf16[1536,1024]{1,0:T(8,128)(2,1)S(1)}, bf16[16,128]{1,0:T(8,128)(2,1)S(1)}) custom-call(bf16[96,1024]{1,0:T(8,128)(2,1)S(1)} %collective-permute-done.7.refs_0_, bf16[96,1024]{1,0:T(8,128)(2,1)S(1)} %collective-permute-done.11.refs_1_, ...), custom_call_target="tpu_custom_call", output_to_operand_aliasing={{1}: (6, {})} | custom-call | flops 3221225472 | bytes 7864320 | tf_op jit(solution)/shard_map/pallas_call | solution.py:371
  49.8 2.1 %shard_map.144 = bf16[16,128]{1,0:T(8,128)(2,1)S(1)} custom-call(f32[2,512]{1,0:T(2,128)S(1)} %get-tuple-element.50.means_ref, bf16[1536,1024]{1,0:T(8,128)(2,1)S(1)} %get-tuple-element.51.weights, bf16[512,1536]{1,0:T(8,128)(2,1)S(1)} %collective-permute-done.17.tiles_ref), custom_call_target="tpu_custom_call" | custom-call | flops 1610612736 | bytes 4718592 | tf_op jit(solution)/shard_map/pallas_call | solution.py:421
  53.4 2.2 %collective-permute-done.18.pair_ref = bf16[16,128]{1,0:T(8,128)(2,1)S(1)} collective-permute-done((bf16[16,128]{1,0:T(8,128)(2,1)S(1)}, bf16[16,128]{1,0:T(8,128)(2,1)S(1)}, u32[]{:S(2)}, u32[]{:S(2)}) %collective-permute-start.18) | collective-permute-done | bytes 4128 | tf_op jit(solution)/shard_map/ppermute | solution.py:716
  55.6 1.9 %shard_map.145 = (bf16[4,1024]{1,0:T(4,128)(2,1)}, f32[8,768]{1,0:T(8,128)S(1)}, bf16[8,16,256]{2,1,0:T(8,128)(2,1)}) custom-call(s32[8]{0:T(128)S(1)} %copy-done.3, bf16[16,128]{1,0:T(8,128)(2,1)S(1)} %get-tuple-element.49.own_ref, bf16[16,128]{1,0:T(8,128)(2,1)S(1)} %collective-permute-done.16.own_far_ref, ...), custom_call_target="tpu_custom_call" | custom-call | tf_op jit(solution)/shard_map/pallas_call | solution.py:722
  57.5 5.2 %all-to-all-start = ((bf16[8,16,256]{2,1,0:T(8,128)(2,1)}), bf16[8,16,256]{2,1,0:T(8,128)(2,1)S(1)}, u32[]{:S(2)}, u32[]{:S(2)}) async-start(bf16[8,16,256]{2,1,0:T(8,128)(2,1)} %get-tuple-element.53), calls=%async_computation | async-start | bytes 131072 | tf_op jit(solution)/shard_map/all_to_all | solution.py:733
  62.7 2.3 %shard_map.146 = (bf16[96,768]{1,0:T(8,128)(2,1)S(1)}, f32[96,32]{1,0:T(8,128)S(1)}, bf16[768,384]{1,0:T(8,128)(2,1)S(1)}, bf16[768,384]{1,0:T(8,128)(2,1)S(1)},...) custom-call(f32[8,768]{1,0:T(8,128)S(1)} %get-tuple-element.54.mixed, ...), custom_call_target="tpu_custom_call" | custom-call | tf_op jit(solution)/shard_map/pallas_call | solution.py:737
  65.0 4.6 %all-to-all-done.sent_ref = bf16[8,16,256]{2,1,0:T(8,128)(2,1)S(1)} async-done(((bf16[8,16,256]{2,1,0:T(8,128)(2,1)}), bf16[8,16,256]{2,1,0:T(8,128)(2,1)S(1)}, u32[]{:S(2)}, u32[]{:S(2)}) %all-to-all-start) | async-done | bytes 65568 | tf_op jit(solution)/shard_map/all_to_all | solution.py:733
  69.6 2.1 %shard_map.147 = bf16[4,384]{1,0:T(4,128)(2,1)} custom-call(s32[8]{0:T(128)S(1)} %copy-done.3, bf16[8,16,256]{2,1,0:T(8,128)(2,1)S(1)} %all-to-all-done.sent_ref, f32[8,768]{1,0:T(8,128)S(1)} %get-tuple-element.54.mixed_ref, bf16[96,768]{1,0:T(8,128)(2,1)S(1)} %get-tuple-element.56.query_ref, bf16[768,384]{1,0:T(8,128)(2,1)S(1)} %get-tuple-element.57.wk_ref, ...), custom_call_target="tpu_custom_call" | custom-call | tf_op jit(solution)/shard_map/pallas_call | solution.py:752
  (54 shorter events, 4.5 us)
Async XLA Ops:
  4.5 35.4 %copy-start.6 = (bf16[96,1024]{1,0:T(8,128)(2,1)}, bf16[96,1024]{1,0:T(8,128)(2,1)S(1)}, u32[]{:S(2)}) copy-start(bf16[96,1024]{1,0:T(8,128)(2,1)S(1)} %get-tuple-element.33.refs_0_) | copy-start | bytes 589828
  4.5 35.4 %copy-start.7 = (bf16[96,1024]{1,0:T(8,128)(2,1)}, bf16[96,1024]{1,0:T(8,128)(2,1)S(1)}, u32[]{:S(2)}) copy-start(bf16[96,1024]{1,0:T(8,128)(2,1)S(1)} %get-tuple-element.36.refs_1_) | copy-start | bytes 589828
  4.5 7.6 %collective-permute-start.3 = (bf16[512,1536]{1,0:T(8,128)(2,1)S(1)}, bf16[512,1536]{1,0:T(8,128)(2,1)S(1)}, u32[]{:S(2)}, u32[]{:S(2)}) collective-permute-start(bf16[512,1536]{1,0:T(8,128)(2,1)S(1)} %get-tuple-element.44.refs_11_), channel_id=1, source_target_pairs={{0,1},{1,0},{2,3},{3,2},{4,5},{5,4},{6,7},{7,6},{8,9},{9,8},{10,11... | collective-permute-start | bytes 4718600 | tf_op jit(solution)/shard_map/ppermute | solution.py:661
  5.0 7.2 %collective-permute-start.2 = (bf16[1024,768]{1,0:T(8,128)(2,1)S(1)}, bf16[1024,768]{1,0:T(8,128)(2,1)S(1)}, u32[]{:S(2)}, u32[]{:S(2)}) collective-permute-start(bf16[1024,768]{1,0:T(8,128)(2,1)S(1)} %copy-done), channel_id=1, source_target_pairs={{0,1},{1,0},{2,3},{3,2},{4,5},{5,4},{6,7},{7,6},{8,9},{9,8},{10,11... | collective-permute-start | bytes 4718600 | tf_op jit(solution)/shard_map/ppermute | solution.py:663
  5.1 39.3 %collective-permute-start.14 = (bf16[512,1536]{1,0:T(8,128)(2,1)S(1)}, bf16[512,1536]{1,0:T(8,128)(2,1)S(1)}, u32[]{:S(2)}, u32[]{:S(2)}) collective-permute-start(bf16[512,1536]{1,0:T(8,128)(2,1)S(1)} %get-tuple-element.44.refs_11_), channel_id=1, source_target_pairs={{0,16},{16,0},{1,17},{17,1},{2,18},{18,2},{3,19},{19,3},{4,20},{20... | collective-permute-start | bytes 4718600 | tf_op jit(solution)/shard_map/ppermute | solution.py:662
  8.0 12.8 %collective-permute-start.5 = (bf16[192,1024]{1,0:T(8,128)(2,1)S(1)}, bf16[192,1024]{1,0:T(8,128)(2,1)S(1)}, u32[]{:S(2)}, u32[]{:S(2)}) collective-permute-start(bf16[192,1024]{1,0:T(8,128)(2,1)S(1)} %get-tuple-element.37), channel_id=1, source_target_pairs={{0,2},{2,0},{4,6},{6,4},{8,10},{10,8},{12,14},{14,12},{1,3},{3,1},... | collective-permute-start | bytes 1179656 | tf_op jit(solution)/shard_map/ppermute | solution.py:697
  9.6 7.9 %collective-permute-start = (bf16[96,1024]{1,0:T(8,128)(2,1)S(1)}, bf16[96,1024]{1,0:T(8,128)(2,1)S(1)}, u32[]{:S(2)}, u32[]{:S(2)}) collective-permute-start(bf16[96,1024]{1,0:T(8,128)(2,1)S(1)} %get-tuple-element.33.refs_0_), channel_id=1, source_target_pairs={{0,8},{2,10},{8,12},{10,14},{12,4},{14,6},{4,0},{6,2},{1,9},{3,11}... | collective-permute-start | bytes 589832 | tf_op jit(solution)/shard_map/ppermute | solution.py:684
  12.2 9.5 %collective-permute-start.4 = (bf16[96,1024]{1,0:T(8,128)(2,1)S(1)}, bf16[96,1024]{1,0:T(8,128)(2,1)S(1)}, u32[]{:S(2)}, u32[]{:S(2)}) collective-permute-start(bf16[96,1024]{1,0:T(8,128)(2,1)S(1)} %get-tuple-element.36.refs_1_), channel_id=1, source_target_pairs={{0,8},{2,10},{8,12},{10,14},{12,4},{14,6},{4,0},{6,2},{1,9},{3,11}... | collective-permute-start | bytes 589832 | tf_op jit(solution)/shard_map/ppermute | solution.py:684
  17.4 7.6 %collective-permute-start.6 = (bf16[96,1024]{1,0:T(8,128)(2,1)S(1)}, bf16[96,1024]{1,0:T(8,128)(2,1)S(1)}, u32[]{:S(2)}, u32[]{:S(2)}) collective-permute-start(bf16[96,1024]{1,0:T(8,128)(2,1)S(1)} %collective-permute-done.refs_3_), channel_id=1, source_target_pairs={{0,2},{2,0},{4,6},{6,4},{8,10},{10,8},{12,14},{14,12},{1,3},{3,1},... | collective-permute-start | bytes 589832 | tf_op jit(solution)/shard_map/ppermute | solution.py:695
  17.4 7.7 %collective-permute-start.1 = (bf16[96,1024]{1,0:T(8,128)(2,1)S(1)}, bf16[96,1024]{1,0:T(8,128)(2,1)S(1)}, u32[]{:S(2)}, u32[]{:S(2)}) collective-permute-start(bf16[96,1024]{1,0:T(8,128)(2,1)S(1)} %collective-permute-done.refs_3_), channel_id=1, source_target_pairs={{0,8},{2,10},{8,12},{10,14},{12,4},{14,6},{4,0},{6,2},{1,9},{3,11}... | collective-permute-start | bytes 589832 | tf_op jit(solution)/shard_map/ppermute | solution.py:684
  21.7 9.6 %collective-permute-start.9 = (bf16[96,1024]{1,0:T(8,128)(2,1)S(1)}, bf16[96,1024]{1,0:T(8,128)(2,1)S(1)}, u32[]{:S(2)}, u32[]{:S(2)}) collective-permute-start(bf16[96,1024]{1,0:T(8,128)(2,1)S(1)} %collective-permute-done.4.refs_4_), channel_id=1, source_target_pairs={{0,2},{2,0},{4,6},{6,4},{8,10},{10,8},{12,14},{14,12},{1,3},{3,1},... | collective-permute-start | bytes 589832 | tf_op jit(solution)/shard_map/ppermute | solution.py:695
  22.9 8.4 %collective-permute-start.8 = (bf16[96,1024]{1,0:T(8,128)(2,1)S(1)}, bf16[96,1024]{1,0:T(8,128)(2,1)S(1)}, u32[]{:S(2)}, u32[]{:S(2)}) collective-permute-start(bf16[96,1024]{1,0:T(8,128)(2,1)S(1)} %collective-permute-done.4.refs_4_), channel_id=1, source_target_pairs={{0,8},{2,10},{8,12},{10,14},{12,4},{14,6},{4,0},{6,2},{1,9},{3,11}... | collective-permute-start | bytes 589832 | tf_op jit(solution)/shard_map/ppermute | solution.py:684
  25.2 10.6 %collective-permute-start.10 = (bf16[96,1024]{1,0:T(8,128)(2,1)S(1)}, bf16[96,1024]{1,0:T(8,128)(2,1)S(1)}, u32[]{:S(2)}, u32[]{:S(2)}) collective-permute-start(bf16[96,1024]{1,0:T(8,128)(2,1)S(1)} %collective-permute-done.1.refs_7_), channel_id=1, source_target_pairs={{0,2},{2,0},{4,6},{6,4},{8,10},{10,8},{12,14},{14,12},{1,3},{3,1},... | collective-permute-start | bytes 589832 | tf_op jit(solution)/shard_map/ppermute | solution.py:695
  27.9 8.6 %collective-permute-start.7 = (bf16[96,1024]{1,0:T(8,128)(2,1)S(1)}, bf16[96,1024]{1,0:T(8,128)(2,1)S(1)}, u32[]{:S(2)}, u32[]{:S(2)}) collective-permute-start(bf16[96,1024]{1,0:T(8,128)(2,1)S(1)} %collective-permute-done.1.refs_7_), channel_id=1, source_target_pairs={{0,8},{2,10},{8,12},{10,14},{12,4},{14,6},{4,0},{6,2},{1,9},{3,11}... | collective-permute-start | bytes 589832 | tf_op jit(solution)/shard_map/ppermute | solution.py:684
  31.3 7.0 %collective-permute-start.11 = (bf16[96,1024]{1,0:T(8,128)(2,1)S(1)}, bf16[96,1024]{1,0:T(8,128)(2,1)S(1)}, u32[]{:S(2)}, u32[]{:S(2)}) collective-permute-start(bf16[96,1024]{1,0:T(8,128)(2,1)S(1)} %collective-permute-done.8.refs_8_), channel_id=1, source_target_pairs={{0,8},{2,10},{8,12},{10,14},{12,4},{14,6},{4,0},{6,2},{1,9},{3,11}... | collective-permute-start | bytes 589832 | tf_op jit(solution)/shard_map/ppermute | solution.py:684
  33.8 6.2 %collective-permute-start.15 = (bf16[96,1024]{1,0:T(8,128)(2,1)S(1)}, bf16[96,1024]{1,0:T(8,128)(2,1)S(1)}, u32[]{:S(2)}, u32[]{:S(2)}) collective-permute-start(bf16[96,1024]{1,0:T(8,128)(2,1)S(1)} %collective-permute-done.8.refs_8_), channel_id=1, source_target_pairs={{0,2},{2,0},{4,6},{6,4},{8,10},{10,8},{12,14},{14,12},{1,3},{3,1},... | collective-permute-start | bytes 589832 | tf_op jit(solution)/shard_map/ppermute | solution.py:695
  35.8 26.9 %collective-permute-start.20 = (bf16[2688,384]{1,0:T(8,128)(2,1)S(1)}, bf16[2688,384]{1,0:T(8,128)(2,1)}, u32[]{:S(2)}, u32[]{:S(2)}) collective-permute-start(bf16[2688,384]{1,0:T(8,128)(2,1)S(1)} %get-tuple-element.55), channel_id=1, source_target_pairs={{0,1},{1,0},{2,3},{3,2},{4,5},{5,4},{6,7},{7,6},{8,9},{9,8},{10,11... | collective-permute-start | bytes 6193160 | tf_op jit(solution)/shard_map/ppermute | solution.py:664
  36.5 7.8 %collective-permute-start.12 = (bf16[96,1024]{1,0:T(8,128)(2,1)S(1)}, bf16[96,1024]{1,0:T(8,128)(2,1)S(1)}, u32[]{:S(2)}, u32[]{:S(2)}) collective-permute-start(bf16[96,1024]{1,0:T(8,128)(2,1)S(1)} %collective-permute-done.10.refs_9_), channel_id=1, source_target_pairs={{0,8},{2,10},{8,12},{10,14},{12,4},{14,6},{4,0},{6,2},{1,9},{3,11}... | collective-permute-start | bytes 589832 | tf_op jit(solution)/shard_map/ppermute | solution.py:693
  38.4 6.2 %collective-permute-start.13 = (bf16[96,1024]{1,0:T(8,128)(2,1)S(1)}, bf16[96,1024]{1,0:T(8,128)(2,1)S(1)}, u32[]{:S(2)}, u32[]{:S(2)}) collective-permute-start(bf16[96,1024]{1,0:T(8,128)(2,1)S(1)} %collective-permute-done.11.refs_1_), channel_id=1, source_target_pairs={{0,2},{2,0},{4,6},{6,4},{8,10},{10,8},{12,14},{14,12},{1,3},{3,1},... | collective-permute-start | bytes 589832 | tf_op jit(solution)/shard_map/ppermute | solution.py:695
  44.5 5.3 %collective-permute-start.17 = (bf16[512,1536]{1,0:T(8,128)(2,1)S(1)}, bf16[512,1536]{1,0:T(8,128)(2,1)S(1)}, u32[]{:S(2)}, u32[]{:S(2)}) collective-permute-start(bf16[512,1536]{1,0:T(8,128)(2,1)S(1)} %collective-permute-done.14.refs_4_), channel_id=1, source_target_pairs={{0,1},{1,0},{2,3},{3,2},{4,5},{5,4},{6,7},{7,6},{8,9},{9,8},{10,11... | collective-permute-start | bytes 4718600 | tf_op jit(solution)/shard_map/ppermute | solution.py:706
  49.3 4.1 %collective-permute-start.16 = (bf16[16,128]{1,0:T(8,128)(2,1)S(1)}, bf16[16,128]{1,0:T(8,128)(2,1)S(1)}, u32[]{:S(2)}, u32[]{:S(2)}) collective-permute-start(bf16[16,128]{1,0:T(8,128)(2,1)S(1)} %get-tuple-element.49.own_ref), channel_id=1, source_target_pairs={{0,1},{1,0},{2,3},{3,2},{4,5},{5,4},{6,7},{7,6},{8,9},{9,8},{10,11... | collective-permute-start | bytes 12296 | tf_op jit(solution)/shard_map/ppermute | solution.py:710
  51.9 3.7 %collective-permute-start.18 = (bf16[16,128]{1,0:T(8,128)(2,1)S(1)}, bf16[16,128]{1,0:T(8,128)(2,1)S(1)}, u32[]{:S(2)}, u32[]{:S(2)}) collective-permute-start(bf16[16,128]{1,0:T(8,128)(2,1)S(1)} %shard_map.144), channel_id=1, source_target_pairs={{0,16},{16,0},{1,17},{17,1},{2,18},{18,2},{3,19},{19,3},{4,20},{20... | collective-permute-start | bytes 12296 | tf_op jit(solution)/shard_map/ppermute | solution.py:716
  52.5 3.1 %collective-permute-start.19 = (bf16[16,128]{1,0:T(8,128)(2,1)S(1)}, bf16[16,128]{1,0:T(8,128)(2,1)S(1)}, u32[]{:S(2)}, u32[]{:S(2)}) collective-permute-start(bf16[16,128]{1,0:T(8,128)(2,1)S(1)} %shard_map.144), channel_id=1, source_target_pairs={{0,17},{1,16},{16,1},{17,0},{2,19},{3,18},{18,3},{19,2},{4,21},{5,... | collective-permute-start | bytes 12296 | tf_op jit(solution)/shard_map/ppermute | solution.py:715
  57.5 12.1 %all-to-all-start = ((bf16[8,16,256]{2,1,0:T(8,128)(2,1)}), bf16[8,16,256]{2,1,0:T(8,128)(2,1)S(1)}, u32[]{:S(2)}, u32[]{:S(2)}) async-start(bf16[8,16,256]{2,1,0:T(8,128)(2,1)} %get-tuple-element.53), calls=%async_computation | async-start | bytes 131072 | tf_op jit(solution)/shard_map/all_to_all | solution.py:733
  (11 other events, 207.1 us)
